TPU v7x, 512 devices: a whole 4x4x16 slice. The times are simulated.
512 devices in a mesh: gx: 16 (over x, y), gy: 32 (over z, core).
Axes of the slice: x: 4, y: 4, z: 16, core: 2. Of those that a mesh axis runs over, the one named last changes fastest.
Arguments:
- right_side: float32 [128, 256, 512], P('gx', 'gy'), may hold values from -6 to 6
- coefficient: float32 [128, 256, 512], P('gx', 'gy'), may hold values from 0.1 to 10
Outputs:
- correction: float32 [128, 256, 512], P('gx', 'gy')
- residual: float32 [128, 256, 512], P('gx', 'gy')
All inputs are finite; a program needn't handle non-finite values.
Results may differ from a plain program's by a relative error of at most 0.00016.
Values sent between devices are 32-bit elements; how exact they have to be, the bound alone decides.
No kernel may reach another device: no remote copies, remote signals or barrier semaphores. Data moves between devices by JAX's collectives and lax.ppermute only.
A program may use at most 128 MiB of HBM per device.

v0:
```python
import jax
import jax.numpy as jnp
from jax import lax
from jax.sharding import PartitionSpec as P

SWEEPS = 2
COARSE_SWEEPS = 8


absorption = 0.05
damping = 0.8


def with_halo(cells, sides, width):
    for axis, dim in sides:
        count = lax.axis_size(axis)
        head = lax.slice_in_dim(cells, 0, width, axis=dim)
        tail = lax.slice_in_dim(cells, cells.shape[dim] - width, cells.shape[dim], axis=dim)
        cells = jnp.concatenate(
            [
                lax.ppermute(tail, axis, [(i, (i + 1) % count) for i in range(count)]),
                cells,
                lax.ppermute(head, axis, [((i + 1) % count, i) for i in range(count)]),
            ],
            axis=dim,
        )
    return cells


def block_mean(field):
    shaped = field.reshape(field.shape[0] // 2, 2, field.shape[1] // 2, 2, field.shape[2] // 2, 2)
    return jnp.sum(shaped, axis=(1, 3, 5)) * 0.125


def prolong(field):
    return jnp.repeat(jnp.repeat(jnp.repeat(field, 2, 0), 2, 1), 2, 2)


def level_terms(coef_pad, scale):
    centre = coef_pad[1:-1, 1:-1]
    face_x = (coef_pad[:-1, 1:-1] + coef_pad[1:, 1:-1]) * 0.5
    face_y = (coef_pad[1:-1, :-1] + coef_pad[1:-1, 1:]) * 0.5
    right_z = (centre + jnp.roll(centre, -1, 2)) * 0.5
    left_z = jnp.roll(right_z, 1, 2)
    right_x = face_x[1:]
    left_x = face_x[:-1]
    right_y = face_y[:, 1:]
    left_y = face_y[:, :-1]
    diagonal = absorption + scale * (right_x + left_x + right_y + left_y + right_z + left_z)
    return (right_x, left_x, right_y, left_y, right_z, left_z, diagonal, scale)


def apply_padded(padded, terms):
    right_x, left_x, right_y, left_y, right_z, left_z, diagonal, scale = terms
    field = padded[1:-1, 1:-1]
    flux = right_x * (field - padded[2:, 1:-1]) + left_x * (field - padded[:-2, 1:-1])
    flux = flux + right_y * (field - padded[1:-1, 2:]) + left_y * (field - padded[1:-1, :-2])
    flux = (
        flux + right_z * (field - jnp.roll(field, -1, 2)) + left_z * (field - jnp.roll(field, 1, 2))
    )
    return absorption * field + scale * flux


def sweep(padded, source, terms):
    return padded[1:-1, 1:-1] + damping * (source - apply_padded(padded, terms)) / terms[6]


def first_sweep(source, terms):
    return damping * source / terms[6]


def fine_halo(field):
    return with_halo(field, (("gx", 0), ("gy", 1)), 1)


def middle_halo(field):
    return with_halo(field, (("gx", 0), ("gy", 1)), 1)


def coarse_halo(field):
    return with_halo(field, (("gx", 0), ("gy", 1)), 1)


def per_device(right_side, coefficient):
    coef_pad = with_halo(coefficient, (("gx", 0), ("gy", 1)), 4)
    fine_terms = level_terms(coef_pad[3:-3, 3:-3], 1.0)
    fine_iter = first_sweep(right_side, fine_terms)
    fine_iter = sweep(fine_halo(fine_iter), right_side, fine_terms)
    fine_padded = fine_halo(fine_iter)
    coef_half = block_mean(coef_pad)
    coef_quarter = block_mean(coef_half)
    middle_terms = level_terms(coef_half[1:-1, 1:-1], 0.25)
    middle_rhs = block_mean(right_side - apply_padded(fine_padded, fine_terms))
    middle_iter = first_sweep(middle_rhs, middle_terms)
    middle_iter = sweep(middle_halo(middle_iter), middle_rhs, middle_terms)
    middle_padded = middle_halo(middle_iter)
    coarse_rhs = block_mean(middle_rhs - apply_padded(middle_padded, middle_terms))
    coarse_terms = level_terms(coef_quarter, 0.0625)
    coarse_iter = first_sweep(coarse_rhs, coarse_terms)
    for sweep_index in range(COARSE_SWEEPS - 1):
        coarse_iter = sweep(coarse_halo(coarse_iter), coarse_rhs, coarse_terms)
    middle_iter = middle_iter + prolong(coarse_iter)
    for sweep_index in range(SWEEPS):
        middle_iter = sweep(middle_halo(middle_iter), middle_rhs, middle_terms)
    fine_padded = fine_halo(fine_iter + prolong(middle_iter))
    correction = sweep(fine_padded, right_side, fine_terms)
    correction = sweep(fine_halo(correction), right_side, fine_terms)
    residual = right_side - apply_padded(fine_halo(correction), fine_terms)
    return (correction, residual)


def solution(mesh):
    placed = (P("gx", "gy", None), P("gx", "gy", None))
    return jax.shard_map(
        per_device,
        mesh=mesh,
        in_specs=placed,
        out_specs=(P("gx", "gy", None), P("gx", "gy", None)),
        check_vma=False,
    )
```

profile of v0, /device:TPU:1, one launch (start us, length us, event | category | flops | bytes accessed | tf_op | source)
XLA Modules:
  0.0 349.1 jit_solution(7522477947064888428)
XLA Ops:
  5.6 5.6 %collective-permute-start.1 = (f32[4,8,512]{2,1,0:T(8,128)S(1)}, f32[4,8,512]{2,1,0:T(8,128)S(1)}, u32[]{:S(2)}, u32[]{:S(2)}) collective-permute-start(f32[4,8,512]{2,1,0:T(8,128)S(1)} %get-tuple-element.55), channel_id=1, source_target_pairs={{32,0},{64,32},{96,64},{128,96},{160,128},{192,160},{224,192},{256... | collective-permute-start | bytes 196616 | tf_op jit(solution)/shard_map/ppermute | solution.py:23
  14.0 6.5 %collective-permute-start.3 = (f32[16,4,512]{2,0,1:T(8,128)S(1)}, f32[16,4,512]{2,0,1:T(8,128)S(1)}, u32[]{:S(2)}, u32[]{:S(2)}) collective-permute-start(f32[16,4,512]{2,0,1:T(8,128)S(1)} %copy.608), channel_id=1, source_target_pairs={{1,0},{2,1},{3,2},{4,3},{5,4},{6,5},{7,6},{8,7},{9,8},{10,9},{11,1... | collective-permute-start | bytes 393224 | tf_op jit(solution)/shard_map/ppermute | solution.py:23
  26.0 34.8 %reshape.36 = f32[8,2,8,2,256,2]{5,4,3,2,1,0:T(8,128)} reshape(f32[16,16,512]{2,1,0:T(8,128)S(1)} %pad_maximum_fusion) | data formatting | bytes 1048576 | tf_op jit(solution)/shard_map/reshape | solution.py:31
  60.9 12.2 %reduce_sum.37 = f32[8,8,256]{2,1,0:T(8,128)S(1)} reduce(f32[8,2,8,2,256,2]{5,4,3,2,1,0:T(8,128)} %reshape.36, f32[]{:T(128)} %constant.11.clone.1), dimensions={1,3,5}, to_apply=%region_1.2 | reduce | flops 114688 | bytes 589828 | tf_op jit(solution)/shard_map/reduce_sum | solution.py:32
  73.2 5.5 %mul.563 = f32[4,2,4,2,128,2]{5,4,3,2,1,0:T(8,128)} reshape(f32[8,8,256]{2,1,0:T(8,128)S(1)} %broadcast_multiply_fusion) | data formatting | bytes 131072 | tf_op jit(solution)/shard_map/mul | solution.py:32
  78.8 5.5 %collective-permute-start.4 = (f32[1,8,512]{2,1,0:T(8,128)S(1)}, f32[1,8,512]{2,1,0:T(8,128)S(1)}, u32[]{:S(2)}, u32[]{:S(2)}) collective-permute-start(f32[1,8,512]{2,1,0:T(8,128)S(1)} %get-tuple-element.54), channel_id=1, source_target_pairs={{32,0},{64,32},{96,64},{128,96},{160,128},{192,160},{224,192},{256... | collective-permute-start | bytes 49160 | tf_op jit(solution)/shard_map/ppermute | solution.py:23
  104.8 5.1 %collective-permute-done.9 = f32[1,8,512]{2,1,0:T(8,128)S(1)} collective-permute-done((f32[1,8,512]{2,1,0:T(8,128)S(1)}, f32[1,8,512]{2,1,0:T(8,128)S(1)}, u32[]{:S(2)}, u32[]{:S(2)}) %collective-permute-start.9) | collective-permute-done | bytes 16416 | tf_op jit(solution)/shard_map/ppermute | solution.py:21
  110.3 4.7 %collective-permute-start.10 = (f32[10,1,512]{2,1,0:T(1,128)S(1)}, f32[10,1,512]{2,1,0:T(1,128)S(1)}, u32[]{:S(2)}, u32[]{:S(2)}) collective-permute-start(f32[10,1,512]{2,1,0:T(1,128)S(1)} %get-tuple-element.21), channel_id=1, source_target_pairs={{1,0},{2,1},{3,2},{4,3},{5,4},{6,5},{7,6},{8,7},{9,8},{10,9},{11,1... | collective-permute-start | bytes 61448 | tf_op jit(solution)/shard_map/ppermute | solution.py:23
  116.0 9.8 %reshape.35 = f32[4,2,4,2,256,2]{5,4,3,2,1,0:T(8,128)} reshape(f32[8,8,512]{2,1,0:T(8,128)S(1)} %fusion.61) | data formatting | bytes 262144 | tf_op jit(solution)/shard_map/reshape | solution.py:31
  139.6 4.7 %collective-permute-start.14 = (f32[6,1,256]{2,1,0:T(1,128)S(1)}, f32[6,1,256]{2,1,0:T(1,128)S(1)}, u32[]{:S(2)}, u32[]{:S(2)}) collective-permute-start(f32[6,1,256]{2,1,0:T(1,128)S(1)} %get-tuple-element.65), channel_id=1, source_target_pairs={{1,0},{2,1},{3,2},{4,3},{5,4},{6,5},{7,6},{8,7},{9,8},{10,9},{11,1... | collective-permute-start | bytes 18440 | tf_op jit(solution)/shard_map/ppermute | solution.py:23
  154.9 4.6 %collective-permute-start.18 = (f32[6,1,256]{2,1,0:T(1,128)S(1)}, f32[6,1,256]{2,1,0:T(1,128)S(1)}, u32[]{:S(2)}, u32[]{:S(2)}) collective-permute-start(f32[6,1,256]{2,1,0:T(1,128)S(1)} %get-tuple-element.63), channel_id=1, source_target_pairs={{1,0},{2,1},{3,2},{4,3},{5,4},{6,5},{7,6},{8,7},{9,8},{10,9},{11,1... | collective-permute-start | bytes 18440 | tf_op jit(solution)/shard_map/ppermute | solution.py:23
  171.3 4.6 %collective-permute-start.22 = (f32[4,1,128]{2,1,0:T(1,128)S(1)}, f32[4,1,128]{2,1,0:T(1,128)S(1)}, u32[]{:S(2)}, u32[]{:S(2)}) collective-permute-start(f32[4,1,128]{2,1,0:T(1,128)S(1)} %get-tuple-element.103), channel_id=1, source_target_pairs={{1,0},{2,1},{3,2},{4,3},{5,4},{6,5},{7,6},{8,7},{9,8},{10,9},{11,1... | collective-permute-start | bytes 6152 | tf_op jit(solution)/shard_map/ppermute | solution.py:23
  186.5 4.6 %collective-permute-start.26 = (f32[4,1,128]{2,1,0:T(1,128)S(1)}, f32[4,1,128]{2,1,0:T(1,128)S(1)}, u32[]{:S(2)}, u32[]{:S(2)}) collective-permute-start(f32[4,1,128]{2,1,0:T(1,128)S(1)} %get-tuple-element.101), channel_id=1, source_target_pairs={{1,0},{2,1},{3,2},{4,3},{5,4},{6,5},{7,6},{8,7},{9,8},{10,9},{11,1... | collective-permute-start | bytes 6152 | tf_op jit(solution)/shard_map/ppermute | solution.py:23
  201.6 4.6 %collective-permute-start.30 = (f32[4,1,128]{2,1,0:T(1,128)S(1)}, f32[4,1,128]{2,1,0:T(1,128)S(1)}, u32[]{:S(2)}, u32[]{:S(2)}) collective-permute-start(f32[4,1,128]{2,1,0:T(1,128)S(1)} %get-tuple-element.99), channel_id=1, source_target_pairs={{1,0},{2,1},{3,2},{4,3},{5,4},{6,5},{7,6},{8,7},{9,8},{10,9},{11,1... | collective-permute-start | bytes 6152 | tf_op jit(solution)/shard_map/ppermute | solution.py:23
  216.6 4.6 %collective-permute-start.34 = (f32[4,1,128]{2,1,0:T(1,128)S(1)}, f32[4,1,128]{2,1,0:T(1,128)S(1)}, u32[]{:S(2)}, u32[]{:S(2)}) collective-permute-start(f32[4,1,128]{2,1,0:T(1,128)S(1)} %get-tuple-element.97), channel_id=1, source_target_pairs={{1,0},{2,1},{3,2},{4,3},{5,4},{6,5},{7,6},{8,7},{9,8},{10,9},{11,1... | collective-permute-start | bytes 6152 | tf_op jit(solution)/shard_map/ppermute | solution.py:23
  231.7 4.6 %collective-permute-start.38 = (f32[4,1,128]{2,1,0:T(1,128)S(1)}, f32[4,1,128]{2,1,0:T(1,128)S(1)}, u32[]{:S(2)}, u32[]{:S(2)}) collective-permute-start(f32[4,1,128]{2,1,0:T(1,128)S(1)} %get-tuple-element.95), channel_id=1, source_target_pairs={{1,0},{2,1},{3,2},{4,3},{5,4},{6,5},{7,6},{8,7},{9,8},{10,9},{11,1... | collective-permute-start | bytes 6152 | tf_op jit(solution)/shard_map/ppermute | solution.py:23
  246.8 4.6 %collective-permute-start.42 = (f32[4,1,128]{2,1,0:T(1,128)S(1)}, f32[4,1,128]{2,1,0:T(1,128)S(1)}, u32[]{:S(2)}, u32[]{:S(2)}) collective-permute-start(f32[4,1,128]{2,1,0:T(1,128)S(1)} %get-tuple-element.93), channel_id=1, source_target_pairs={{1,0},{2,1},{3,2},{4,3},{5,4},{6,5},{7,6},{8,7},{9,8},{10,9},{11,1... | collective-permute-start | bytes 6152 | tf_op jit(solution)/shard_map/ppermute | solution.py:23
  261.9 4.6 %collective-permute-start.46 = (f32[4,1,128]{2,1,0:T(1,128)S(1)}, f32[4,1,128]{2,1,0:T(1,128)S(1)}, u32[]{:S(2)}, u32[]{:S(2)}) collective-permute-start(f32[4,1,128]{2,1,0:T(1,128)S(1)} %get-tuple-element.91), channel_id=1, source_target_pairs={{1,0},{2,1},{3,2},{4,3},{5,4},{6,5},{7,6},{8,7},{9,8},{10,9},{11,1... | collective-permute-start | bytes 6152 | tf_op jit(solution)/shard_map/ppermute | solution.py:23
  277.6 4.6 %collective-permute-start.50 = (f32[6,1,256]{2,1,0:T(1,128)S(1)}, f32[6,1,256]{2,1,0:T(1,128)S(1)}, u32[]{:S(2)}, u32[]{:S(2)}) collective-permute-start(f32[6,1,256]{2,1,0:T(1,128)S(1)} %get-tuple-element.61), channel_id=1, source_target_pairs={{1,0},{2,1},{3,2},{4,3},{5,4},{6,5},{7,6},{8,7},{9,8},{10,9},{11,1... | collective-permute-start | bytes 18440 | tf_op jit(solution)/shard_map/ppermute | solution.py:23
  292.8 4.6 %collective-permute-start.54 = (f32[6,1,256]{2,1,0:T(1,128)S(1)}, f32[6,1,256]{2,1,0:T(1,128)S(1)}, u32[]{:S(2)}, u32[]{:S(2)}) collective-permute-start(f32[6,1,256]{2,1,0:T(1,128)S(1)} %get-tuple-element.59), channel_id=1, source_target_pairs={{1,0},{2,1},{3,2},{4,3},{5,4},{6,5},{7,6},{8,7},{9,8},{10,9},{11,1... | collective-permute-start | bytes 18440 | tf_op jit(solution)/shard_map/ppermute | solution.py:23
  311.6 4.6 %collective-permute-start.58 = (f32[10,1,512]{2,1,0:T(1,128)S(1)}, f32[10,1,512]{2,1,0:T(1,128)S(1)}, u32[]{:S(2)}, u32[]{:S(2)}) collective-permute-start(f32[10,1,512]{2,1,0:T(1,128)S(1)} %get-tuple-element.19), channel_id=1, source_target_pairs={{1,0},{2,1},{3,2},{4,3},{5,4},{6,5},{7,6},{8,7},{9,8},{10,9},{11,1... | collective-permute-start | bytes 61448 | tf_op jit(solution)/shard_map/ppermute | solution.py:23
  327.1 4.7 %collective-permute-start.62 = (f32[10,1,512]{2,1,0:T(1,128)S(1)}, f32[10,1,512]{2,1,0:T(1,128)S(1)}, u32[]{:S(2)}, u32[]{:S(2)}) collective-permute-start(f32[10,1,512]{2,1,0:T(1,128)S(1)} %get-tuple-element.17), channel_id=1, source_target_pairs={{1,0},{2,1},{3,2},{4,3},{5,4},{6,5},{7,6},{8,7},{9,8},{10,9},{11,1... | collective-permute-start | bytes 61448 | tf_op jit(solution)/shard_map/ppermute | solution.py:23
  338.3 4.3 %collective-permute-done.65 = f32[1,8,512]{2,1,0:T(8,128)S(1)} collective-permute-done((f32[1,8,512]{2,1,0:T(8,128)S(1)}, f32[1,8,512]{2,1,0:T(8,128)S(1)}, u32[]{:S(2)}, u32[]{:S(2)}) %collective-permute-start.65) | collective-permute-done | bytes 16416 | tf_op jit(solution)/shard_map/ppermute | solution.py:21
  342.7 4.7 %collective-permute-start.66 = (f32[10,1,512]{2,1,0:T(1,128)S(1)}, f32[10,1,512]{2,1,0:T(1,128)S(1)}, u32[]{:S(2)}, u32[]{:S(2)}) collective-permute-start(f32[10,1,512]{2,1,0:T(1,128)S(1)} %get-tuple-element.15), channel_id=1, source_target_pairs={{1,0},{2,1},{3,2},{4,3},{5,4},{6,5},{7,6},{8,7},{9,8},{10,9},{11,1... | collective-permute-start | bytes 61448 | tf_op jit(solution)/shard_map/ppermute | solution.py:23
  (257 shorter events, 188.8 us)
Async XLA Ops:
  1.5 11.4 %collective-permute-start = (f32[4,8,512]{2,1,0:T(8,128)S(1)}, f32[4,8,512]{2,1,0:T(8,128)S(1)}, u32[]{:S(2)}, u32[]{:S(2)}) collective-permute-start(f32[4,8,512]{2,1,0:T(8,128)S(1)} %get-tuple-element.56), channel_id=1, source_target_pairs={{0,32},{32,64},{64,96},{96,128},{128,160},{160,192},{192,224},{224... | collective-permute-start | bytes 196616 | tf_op jit(solution)/shard_map/ppermute | solution.py:21
  5.6 8.3 %collective-permute-start.1 = (f32[4,8,512]{2,1,0:T(8,128)S(1)}, f32[4,8,512]{2,1,0:T(8,128)S(1)}, u32[]{:S(2)}, u32[]{:S(2)}) collective-permute-start(f32[4,8,512]{2,1,0:T(8,128)S(1)} %get-tuple-element.55), channel_id=1, source_target_pairs={{32,0},{64,32},{96,64},{128,96},{160,128},{192,160},{224,192},{256... | collective-permute-start | bytes 196616 | tf_op jit(solution)/shard_map/ppermute | solution.py:23
  14.0 7.6 %collective-permute-start.3 = (f32[16,4,512]{2,0,1:T(8,128)S(1)}, f32[16,4,512]{2,0,1:T(8,128)S(1)}, u32[]{:S(2)}, u32[]{:S(2)}) collective-permute-start(f32[16,4,512]{2,0,1:T(8,128)S(1)} %copy.608), channel_id=1, source_target_pairs={{1,0},{2,1},{3,2},{4,3},{5,4},{6,5},{7,6},{8,7},{9,8},{10,9},{11,1... | collective-permute-start | bytes 393224 | tf_op jit(solution)/shard_map/ppermute | solution.py:23
  78.8 10.2 %collective-permute-start.4 = (f32[1,8,512]{2,1,0:T(8,128)S(1)}, f32[1,8,512]{2,1,0:T(8,128)S(1)}, u32[]{:S(2)}, u32[]{:S(2)}) collective-permute-start(f32[1,8,512]{2,1,0:T(8,128)S(1)} %get-tuple-element.54), channel_id=1, source_target_pairs={{32,0},{64,32},{96,64},{128,96},{160,128},{192,160},{224,192},{256... | collective-permute-start | bytes 49160 | tf_op jit(solution)/shard_map/ppermute | solution.py:23
  84.3 7.8 %collective-permute-start.5 = (f32[1,8,512]{2,1,0:T(8,128)S(1)}, f32[1,8,512]{2,1,0:T(8,128)S(1)}, u32[]{:S(2)}, u32[]{:S(2)}) collective-permute-start(f32[1,8,512]{2,1,0:T(8,128)S(1)} %get-tuple-element.53), channel_id=1, source_target_pairs={{0,32},{32,64},{64,96},{96,128},{128,160},{160,192},{192,224},{224... | collective-permute-start | bytes 49160 | tf_op jit(solution)/shard_map/ppermute | solution.py:21
  92.1 6.9 %collective-permute-start.7 = (f32[10,1,512]{2,1,0:T(1,128)S(1)}, f32[10,1,512]{2,1,0:T(1,128)S(1)}, u32[]{:S(2)}, u32[]{:S(2)}) collective-permute-start(f32[10,1,512]{2,1,0:T(1,128)S(1)} %get-tuple-element.24), channel_id=1, source_target_pairs={{0,1},{1,2},{2,3},{3,4},{4,5},{5,6},{6,7},{7,8},{8,9},{9,10},{10,1... | collective-permute-start | bytes 61448 | tf_op jit(solution)/shard_map/ppermute | solution.py:21
  102.1 7.8 %collective-permute-start.9 = (f32[1,8,512]{2,1,0:T(8,128)S(1)}, f32[1,8,512]{2,1,0:T(8,128)S(1)}, u32[]{:S(2)}, u32[]{:S(2)}) collective-permute-start(f32[1,8,512]{2,1,0:T(8,128)S(1)} %get-tuple-element.47), channel_id=1, source_target_pairs={{0,32},{32,64},{64,96},{96,128},{128,160},{160,192},{192,224},{224... | collective-permute-start | bytes 49160 | tf_op jit(solution)/shard_map/ppermute | solution.py:21
  110.0 5.7 %collective-permute-start.11 = (f32[10,1,512]{2,1,0:T(1,128)S(1)}, f32[10,1,512]{2,1,0:T(1,128)S(1)}, u32[]{:S(2)}, u32[]{:S(2)}) collective-permute-start(f32[10,1,512]{2,1,0:T(1,128)S(1)} %get-tuple-element.22), channel_id=1, source_target_pairs={{0,1},{1,2},{2,3},{3,4},{4,5},{5,6},{6,7},{7,8},{8,9},{9,10},{10,1... | collective-permute-start | bytes 61448 | tf_op jit(solution)/shard_map/ppermute | solution.py:21
  131.9 7.7 %collective-permute-start.13 = (f32[1,4,256]{2,1,0:T(4,128)S(1)}, f32[1,4,256]{2,1,0:T(4,128)S(1)}, u32[]{:S(2)}, u32[]{:S(2)}) collective-permute-start(f32[1,4,256]{2,1,0:T(4,128)S(1)} %get-tuple-element.85), channel_id=1, source_target_pairs={{0,32},{32,64},{64,96},{96,128},{128,160},{160,192},{192,224},{224... | collective-permute-start | bytes 12296 | tf_op jit(solution)/shard_map/ppermute | solution.py:21
  147.2 7.7 %collective-permute-start.17 = (f32[1,4,256]{2,1,0:T(4,128)S(1)}, f32[1,4,256]{2,1,0:T(4,128)S(1)}, u32[]{:S(2)}, u32[]{:S(2)}) collective-permute-start(f32[1,4,256]{2,1,0:T(4,128)S(1)} %get-tuple-element.83), channel_id=1, source_target_pairs={{0,32},{32,64},{64,96},{96,128},{128,160},{160,192},{192,224},{224... | collective-permute-start | bytes 12296 | tf_op jit(solution)/shard_map/ppermute | solution.py:21
  163.7 7.6 %collective-permute-start.21 = (f32[1,2,128]{2,1,0:T(2,128)S(1)}, f32[1,2,128]{2,1,0:T(2,128)S(1)}, u32[]{:S(2)}, u32[]{:S(2)}) collective-permute-start(f32[1,2,128]{2,1,0:T(2,128)S(1)} %get-tuple-element.141), channel_id=1, source_target_pairs={{0,32},{32,64},{64,96},{96,128},{128,160},{160,192},{192,224},{224... | collective-permute-start | bytes 3080 | tf_op jit(solution)/shard_map/ppermute | solution.py:21
  178.8 7.6 %collective-permute-start.25 = (f32[1,2,128]{2,1,0:T(2,128)S(1)}, f32[1,2,128]{2,1,0:T(2,128)S(1)}, u32[]{:S(2)}, u32[]{:S(2)}) collective-permute-start(f32[1,2,128]{2,1,0:T(2,128)S(1)} %get-tuple-element.135), channel_id=1, source_target_pairs={{0,32},{32,64},{64,96},{96,128},{128,160},{160,192},{192,224},{224... | collective-permute-start | bytes 3080 | tf_op jit(solution)/shard_map/ppermute | solution.py:21
  193.9 7.6 %collective-permute-start.29 = (f32[1,2,128]{2,1,0:T(2,128)S(1)}, f32[1,2,128]{2,1,0:T(2,128)S(1)}, u32[]{:S(2)}, u32[]{:S(2)}) collective-permute-start(f32[1,2,128]{2,1,0:T(2,128)S(1)} %get-tuple-element.129), channel_id=1, source_target_pairs={{0,32},{32,64},{64,96},{96,128},{128,160},{160,192},{192,224},{224... | collective-permute-start | bytes 3080 | tf_op jit(solution)/shard_map/ppermute | solution.py:21
  209.0 7.6 %collective-permute-start.33 = (f32[1,2,128]{2,1,0:T(2,128)S(1)}, f32[1,2,128]{2,1,0:T(2,128)S(1)}, u32[]{:S(2)}, u32[]{:S(2)}) collective-permute-start(f32[1,2,128]{2,1,0:T(2,128)S(1)} %get-tuple-element.123), channel_id=1, source_target_pairs={{0,32},{32,64},{64,96},{96,128},{128,160},{160,192},{192,224},{224... | collective-permute-start | bytes 3080 | tf_op jit(solution)/shard_map/ppermute | solution.py:21
  224.1 7.6 %collective-permute-start.37 = (f32[1,2,128]{2,1,0:T(2,128)S(1)}, f32[1,2,128]{2,1,0:T(2,128)S(1)}, u32[]{:S(2)}, u32[]{:S(2)}) collective-permute-start(f32[1,2,128]{2,1,0:T(2,128)S(1)} %get-tuple-element.117), channel_id=1, source_target_pairs={{0,32},{32,64},{64,96},{96,128},{128,160},{160,192},{192,224},{224... | collective-permute-start | bytes 3080 | tf_op jit(solution)/shard_map/ppermute | solution.py:21
  239.2 7.6 %collective-permute-start.41 = (f32[1,2,128]{2,1,0:T(2,128)S(1)}, f32[1,2,128]{2,1,0:T(2,128)S(1)}, u32[]{:S(2)}, u32[]{:S(2)}) collective-permute-start(f32[1,2,128]{2,1,0:T(2,128)S(1)} %get-tuple-element.111), channel_id=1, source_target_pairs={{0,32},{32,64},{64,96},{96,128},{128,160},{160,192},{192,224},{224... | collective-permute-start | bytes 3080 | tf_op jit(solution)/shard_map/ppermute | solution.py:21
  254.2 7.6 %collective-permute-start.45 = (f32[1,2,128]{2,1,0:T(2,128)S(1)}, f32[1,2,128]{2,1,0:T(2,128)S(1)}, u32[]{:S(2)}, u32[]{:S(2)}) collective-permute-start(f32[1,2,128]{2,1,0:T(2,128)S(1)} %get-tuple-element.105), channel_id=1, source_target_pairs={{0,32},{32,64},{64,96},{96,128},{128,160},{160,192},{192,224},{224... | collective-permute-start | bytes 3080 | tf_op jit(solution)/shard_map/ppermute | solution.py:21
  269.9 7.7 %collective-permute-start.49 = (f32[1,4,256]{2,1,0:T(4,128)S(1)}, f32[1,4,256]{2,1,0:T(4,128)S(1)}, u32[]{:S(2)}, u32[]{:S(2)}) collective-permute-start(f32[1,4,256]{2,1,0:T(4,128)S(1)} %get-tuple-element.73), channel_id=1, source_target_pairs={{0,32},{32,64},{64,96},{96,128},{128,160},{160,192},{192,224},{224... | collective-permute-start | bytes 12296 | tf_op jit(solution)/shard_map/ppermute | solution.py:21
  285.1 7.7 %collective-permute-start.53 = (f32[1,4,256]{2,1,0:T(4,128)S(1)}, f32[1,4,256]{2,1,0:T(4,128)S(1)}, u32[]{:S(2)}, u32[]{:S(2)}) collective-permute-start(f32[1,4,256]{2,1,0:T(4,128)S(1)} %get-tuple-element.67), channel_id=1, source_target_pairs={{0,32},{32,64},{64,96},{96,128},{128,160},{160,192},{192,224},{224... | collective-permute-start | bytes 12296 | tf_op jit(solution)/shard_map/ppermute | solution.py:21
  303.8 7.8 %collective-permute-start.57 = (f32[1,8,512]{2,1,0:T(8,128)S(1)}, f32[1,8,512]{2,1,0:T(8,128)S(1)}, u32[]{:S(2)}, u32[]{:S(2)}) collective-permute-start(f32[1,8,512]{2,1,0:T(8,128)S(1)} %get-tuple-element.41), channel_id=1, source_target_pairs={{0,32},{32,64},{64,96},{96,128},{128,160},{160,192},{192,224},{224... | collective-permute-start | bytes 49160 | tf_op jit(solution)/shard_map/ppermute | solution.py:21
  319.2 7.8 %collective-permute-start.61 = (f32[1,8,512]{2,1,0:T(8,128)S(1)}, f32[1,8,512]{2,1,0:T(8,128)S(1)}, u32[]{:S(2)}, u32[]{:S(2)}) collective-permute-start(f32[1,8,512]{2,1,0:T(8,128)S(1)} %get-tuple-element.35), channel_id=1, source_target_pairs={{0,32},{32,64},{64,96},{96,128},{128,160},{160,192},{192,224},{224... | collective-permute-start | bytes 49160 | tf_op jit(solution)/shard_map/ppermute | solution.py:21
  327.1 5.6 %collective-permute-start.62 = (f32[10,1,512]{2,1,0:T(1,128)S(1)}, f32[10,1,512]{2,1,0:T(1,128)S(1)}, u32[]{:S(2)}, u32[]{:S(2)}) collective-permute-start(f32[10,1,512]{2,1,0:T(1,128)S(1)} %get-tuple-element.17), channel_id=1, source_target_pairs={{1,0},{2,1},{3,2},{4,3},{5,4},{6,5},{7,6},{8,7},{9,8},{10,9},{11,1... | collective-permute-start | bytes 61448 | tf_op jit(solution)/shard_map/ppermute | solution.py:23
  334.9 7.8 %collective-permute-start.65 = (f32[1,8,512]{2,1,0:T(8,128)S(1)}, f32[1,8,512]{2,1,0:T(8,128)S(1)}, u32[]{:S(2)}, u32[]{:S(2)}) collective-permute-start(f32[1,8,512]{2,1,0:T(8,128)S(1)} %get-tuple-element.29), channel_id=1, source_target_pairs={{0,32},{32,64},{64,96},{96,128},{128,160},{160,192},{192,224},{224... | collective-permute-start | bytes 49160 | tf_op jit(solution)/shard_map/ppermute | solution.py:21
  342.7 5.6 %collective-permute-start.66 = (f32[10,1,512]{2,1,0:T(1,128)S(1)}, f32[10,1,512]{2,1,0:T(1,128)S(1)}, u32[]{:S(2)}, u32[]{:S(2)}) collective-permute-start(f32[10,1,512]{2,1,0:T(1,128)S(1)} %get-tuple-element.15), channel_id=1, source_target_pairs={{1,0},{2,1},{3,2},{4,3},{5,4},{6,5},{7,6},{8,7},{9,8},{10,9},{11,1... | collective-permute-start | bytes 61448 | tf_op jit(solution)/shard_map/ppermute | solution.py:23
  (46 other events, 276.3 us)
where the time goes:
time: 351 us; the launch traced here: 349 us
  starting transfers between devices  179 us (51%)
  waiting for transfers between devices  82 us (23%)
  local copies, waits for them, and re-layouts  61.1 us (17%)
  other arithmetic  25.4 us (7%)
    ppermute x34, starting transfers between devices, with_halo(): lax.ppermute(head, axis, [((i + 1) % count, i) for i in range(count)])  120 us
    ppermute x34, waiting for transfers between devices, with_halo(): lax.ppermute(tail, axis, [(i, (i + 1) % count) for i in range(count)])  78.9 us
    ppermute x34, starting transfers between devices, with_halo(): lax.ppermute(tail, axis, [(i, (i + 1) % count) for i in range(count)])  59.1 us
    reshape x3, local copies, waits for them, and re-layouts, block_mean(): field.reshape(field.shape[0] // 2, 2, field.shape[1] // 2, 2, field.shape...  45.7 us
    reduce_sum x4, other arithmetic, block_mean(): return jnp.sum(shaped, axis=(1, 3, 5)) * 0.125  18.9 us
  transfers between devices with their start and end apart: 68, of which 49 were waited for; matrix products, arithmetic and copies ran while one was open for 3% of the time, Pallas kernels for 0%

commit v1 on v0

v1 whole, which is shorter than its diff:
```python
import jax
import jax.numpy as jnp
from jax import lax
from jax.experimental import pallas as pl
from jax.experimental.pallas import tpu as pltpu
from jax.sharding import PartitionSpec as P

ABSORPTION = 0.05
DAMPING = 0.8
F32 = jnp.float32
LANES = 128


def z_next(v):
    first = pltpu.roll(v[0], LANES - 1, 1)[None]
    return first if v.shape[0] == 1 else jnp.concatenate([v[1:], first], axis=0)


def z_prev(v):
    last = pltpu.roll(v[-1], 1, 1)[None]
    return last if v.shape[0] == 1 else jnp.concatenate([last, v[:-1]], axis=0)


def y_next(v):
    return pltpu.roll(v, v.shape[1] - 1, 1)


def y_prev(v):
    return pltpu.roll(v, 1, 1)


def flux_sum(u, u_next, flux_low, fx, fy, fz):
    flux_high = fx * (u - u_next)
    flux_y = fy * (u - y_next(u))
    flux_z = fz * (u - z_next(u))
    total = (flux_high - flux_low) + (flux_y - y_prev(flux_y)) + (flux_z - z_prev(flux_z))
    return ABSORPTION * u + total, flux_high


def loop(count, body, carry, unroll):
    return lax.fori_loop(0, count, body, carry, unroll=unroll)


def face_pass(count, k_ref, fx, fy, fz, w, scale, unroll):
    half = 0.5 * scale
    k0, k1 = k_ref[0], k_ref[1]
    low = half * (k0 + k1)
    fx[0] = low

    def body(i, carry):
        k, low = carry
        k_next = k_ref[i + 2]
        high = half * (k + k_next)
        face_y = half * (k + y_next(k))
        face_z = half * (k + z_next(k))
        diag = ABSORPTION + (high + low + face_y + y_prev(face_y) + face_z + z_prev(face_z))
        fx[i + 1] = high
        fy[i] = face_y
        fz[i] = face_z
        w[i] = DAMPING / diag
        return k_next, high

    loop(count, body, (k1, low), unroll)


def sweep_pass(count, u_ref, u_at, faces_at, g_ref, g_at, fx, fy, fz, w, out, out_at, unroll, last=False):
    u0, u1 = u_ref[u_at], u_ref[u_at + 1]
    low = fx[faces_at] * (u0 - u1)

    def body(i, carry):
        u, low = carry
        u_next = u_ref[u_at + 2 + i]
        f = faces_at + i
        applied, high = flux_sum(u, u_next, low, fx[f + 1], fy[f], fz[f])
        rest = g_ref[g_at + i] - applied
        out[out_at + i] = rest if last else u + w[f] * rest
        return u_next, high

    loop(count, body, (u1, low), unroll)


def permutation(inverse):
    z = lax.broadcasted_iota(jnp.int32, (512, 512), 1 if inverse else 0)
    at = lax.broadcasted_iota(jnp.int32, (512, 512), 0 if inverse else 1)
    return jnp.where(z == 4 * (at % LANES) + at // LANES, 1.0, 0.0).astype(F32)


def rearrange(rows, matrix):
    return lax.dot_general(rows, matrix, (((1,), (0,)), ((), ())), precision=lax.Precision.HIGHEST, preferred_element_type=F32)


def permute_kernel(g_ref, k_ref, own, high, low):
    matrix = permutation(False)
    for source, base in ((g_ref, 0), (k_ref, 8)):
        moved = rearrange(source[...].reshape(64, 512), matrix)
        for x in range(8):
            for r in range(4):
                own[base + x, r] = moved[8 * x : 8 * x + 8, LANES * r : LANES * r + LANES]
    high[0:4] = own[4:8]
    high[4:9] = own[11:16]
    low[0:4] = own[0:4]
    low[4:9] = own[8:13]


def wide_kernel(own, left, right, out):
    out[0:4] = left[0:4]
    out[4:12] = own[0:8]
    out[12:16] = right[0:4]
    out[16:21] = left[4:9]
    out[21:29] = own[8:16]
    out[29:34] = right[4:9]


def fine_kernel(own, left, right, piece, u_out, g_out, k_out, g, k, fx, fy, fz, w, uf, u0, res, s1, sc):
    for i in range(34):
        target = g.at[i] if i < 16 else k.at[i - 16]
        target[:, 0:8] = left[i]
        target[:, 8:16] = own[i]
        target[:, 16:24] = right[i]
    face_pass(16, k, fx, fy, fz, w, 1.0, 1)

    def first(i, carry):
        uf[i] = w[i] * g[i]
        return carry

    loop(16, first, 0, 1)
    sweep_pass(14, uf, 0, 1, g, 1, fx, fy, fz, w, u0, 0, 1)
    sweep_pass(8, u0, 2, 4, g, 4, fx, fy, fz, w, res, 0, 1, last=True)
    for x in range(4):
        both = res[2 * x] + res[2 * x + 1]
        s1[x, 0] = both[0] + both[1]
        s1[x, 1] = both[2] + both[3]
    for x in range(6):
        both = k[3 + 2 * x] + k[4 + 2 * x]
        sc[x, 0] = both[0] + both[1]
        sc[x, 1] = both[2] + both[3]

    def rows(ref, x, start):
        return jnp.stack(
            [ref[x, r, pl.ds(start, 8, 2), :] + ref[x, r, pl.ds(start + 1, 8, 2), :] for r in range(2)]
        ) * 0.125

    half = 0.5 * 0.25
    k_mid = [rows(sc, x, 4) for x in range(6)]
    for x in range(4):
        rhs = rows(s1, x, 4)
        here = k_mid[x + 1]
        face_z = half * (here + z_next(here))
        diag = ABSORPTION + (
            half * (here + k_mid[x]) + half * (here + k_mid[x + 2])
            + half * (here + rows(sc, x + 1, 2)) + half * (here + rows(sc, x + 1, 6))
            + face_z + z_prev(face_z)
        )
        piece[0, x] = DAMPING / diag * rhs
        piece[1, x] = here
    u_out[...] = u0[:, :, 4:20, :]
    g_out[...] = g[2:14, :, 4:20, :]
    k_out[...] = k[2:16, :, 4:20, :]


def middle_kernel(me, gathered, coarse, edge, u_out, rhs_out, fx_out, fy_out, fz_out, w_out,
                  uf, k, fx, fy, fz, w, rhs, u1, res, flat, flat_k, k2, r2):
    count = gathered.shape[0]
    for block in range(11):
        source = lax.rem(me[0] + (block - 5 + count * 5), count)
        uf[4 * block : 4 * block + 4] = gathered[source, 0]
        k[4 * block : 4 * block + 4] = gathered[source, 1]
    face_pass(42, k, fx, fy, fz, w, 0.25, 6)

    def right_side(i, carry):
        rhs[i] = uf[i + 1] / w[i]
        return carry

    loop(42, right_side, 0, 6)
    sweep_pass(42, uf, 0, 0, rhs, 0, fx, fy, fz, w, u1, 0, 6)
    sweep_pass(40, u1, 0, 1, rhs, 1, fx, fy, fz, w, res, 0, 5, last=True)

    def add_up(i, carry):
        both = res[2 * i] + res[2 * i + 1]
        flat[pl.ds(pl.multiple_of(8 * i, 8), 8), :] = both[0] + both[1]
        return carry

    loop(20, add_up, 0, 5)

    def add_up_k(i, carry):
        both = k[2 * i] + k[2 * i + 1]
        flat_k[pl.ds(pl.multiple_of(8 * i, 8), 8), :] = both[0] + both[1]
        return carry

    loop(22, add_up_k, 0, 2)
    flat[160:192] = jnp.zeros((32, LANES), F32)
    flat_k[176:256] = jnp.ones((80, LANES), F32)

    def row(ref, at, size):
        return (ref[pl.ds(at, size, 8), :] + ref[pl.ds(at + 1, size, 8), :]) * 0.125

    half = 0.5 * 0.0625
    for j in range(4):
        k2[j] = row(flat_k, 2 * j, 32)
    for j in range(2):
        here = k2[j + 1][0:32]
        face_x = half * (here + pltpu.roll(here, 31, 0))
        face_z = half * (here + pltpu.roll(here, LANES - 1, 1))
        diag = ABSORPTION + (
            face_x + pltpu.roll(face_x, 1, 0) + half * (here + k2[j]) + half * (here + k2[j + 2])
            + face_z + pltpu.roll(face_z, 1, 1)
        )
        r2[...] = DAMPING / diag
        coarse[2 * j] = r2[1:25] * row(flat, 2 * j + 2, 24)
        coarse[2 * j + 1] = k2[j + 1, 1:25]
    u_out[...] = u1[15:27]
    rhs_out[...] = rhs[16:26]
    fx_out[...] = fx[16:27]
    fy_out[...] = fy[16:26]
    fz_out[...] = fz[16:26]
    w_out[...] = w[16:26]
    uf[0:12] = u1[15:27]
    for x in range(12):
        for r in range(2):
            edge[0, 2 * x + r : 2 * x + r + 1, :] = uf[x, r, 4:5, :]
            edge[1, 2 * x + r : 2 * x + r + 1, :] = uf[x, r, 3:4, :]


def coarse_kernel(below, here, above, edge_low, edge_high, u_in, rhs, fx, fy, fz, w, v_out,
                  u, cx, cy, cz, cw, cr, v, va):
    half = 0.5 * 0.0625
    blocks = (below, here, above)

    def first(y):
        return blocks[y // 6][2 * (y % 6)]

    def coef(y):
        return blocks[y // 6][2 * (y % 6) + 1]

    for y in range(18):
        u[y] = first(y)
    cy[0] = half * (coef(0) + coef(1))
    for y in range(1, 17):
        k = coef(y)
        face_x = half * (k + pltpu.roll(k, 23, 0))
        face_z = half * (k + pltpu.roll(k, LANES - 1, 1))
        face_y = half * (k + coef(y + 1))
        diag = ABSORPTION + (
            face_x + pltpu.roll(face_x, 1, 0) + face_y + cy[y - 1] + face_z + pltpu.roll(face_z, 1, 1)
        )
        cx[y], cy[y], cz[y] = face_x, face_y, face_z
        cw[y] = DAMPING / diag
        cr[y] = first(y) * diag * (1.0 / DAMPING)
    for step in range(1, 8):
        now = u[step]
        low = cy[step - 1] * (u[step - 1] - now)
        for y in range(step, 18 - step):
            later = u[y + 1]
            high = cy[y] * (now - later)
            flux_x = cx[y] * (now - pltpu.roll(now, 23, 0))
            flux_z = cz[y] * (now - pltpu.roll(now, LANES - 1, 1))
            applied = ABSORPTION * now + (
                (high - low) + (flux_x - pltpu.roll(flux_x, 1, 0)) + (flux_z - pltpu.roll(flux_z, 1, 1))
            )
            u[y] = now + cw[y] * (cr[y] - applied)
            now, low = later, high
    v[...] = u_in[...]
    for x in range(12):
        for r in range(2):
            v[x, r, 0:1, :] = edge_low[2 * x + r : 2 * x + r + 1, :]
            v[x, r, 7:8, :] = edge_high[2 * x + r : 2 * x + r + 1, :]
    for x in range(6):
        rows = jnp.concatenate(
            [jnp.broadcast_to(u[7 + j, 7 + x : 8 + x, :], (2, LANES)) for j in range(4)], axis=0
        )
        for twin in range(2):
            for r in range(2):
                v[2 * x + twin, r] = v[2 * x + twin, r] + rows
    sweep_pass(10, v, 0, 0, rhs, 0, fx, fy, fz, w, va, 0, 5)
    sweep_pass(8, va, 0, 1, rhs, 1, fx, fy, fz, w, v_out, 0, 4)


def last_kernel(v_here, v_low, v_high, u0, g, k, correction, residual, fx, fy, fz, w, wide, ua, ub, res):
    for x in range(8):
        for r in range(2):
            rows = jnp.concatenate([v_low[x, r, 4:6], v_here[x, r, 2:6], v_high[x, r, 2:4]], axis=0)
            wide[x, r, pl.ds(0, 8, 2), :] = rows
            wide[x, r, pl.ds(1, 8, 2), :] = rows
    face_pass(12, k, fx, fy, fz, w, 1.0, 1)
    for i in range(14):
        fine = wide[(i + 1) // 2]
        ua[i] = u0[i] + jnp.stack([fine[0], fine[0], fine[1], fine[1]])
    sweep_pass(12, ua, 0, 0, g, 0, fx, fy, fz, w, ub, 0, 1)
    sweep_pass(10, ub, 0, 1, g, 1, fx, fy, fz, w, ua, 0, 1)
    sweep_pass(8, ua, 0, 2, g, 2, fx, fy, fz, w, res, 0, 1, last=True)
    matrix = permutation(True)
    for source, at, out in ((ua, 1, correction), (res, 0, residual)):
        rows = [
            jnp.concatenate([source[at + x, r, 4:12, :] for r in range(4)], axis=1) for x in range(8)
        ]
        out[...] = rearrange(jnp.concatenate(rows, axis=0), matrix).reshape(8, 8, 512)


VMEM = pl.BlockSpec(memory_space=pltpu.VMEM)
SMEM = pl.BlockSpec(memory_space=pltpu.SMEM)


def call(kernel, outs, scratch, *arrays, scalars=0):
    return pl.pallas_call(
        kernel,
        out_shape=[jax.ShapeDtypeStruct(shape, F32) for shape in outs],
        in_specs=[SMEM] * scalars + [VMEM] * (len(arrays) - scalars),
        out_specs=[VMEM] * len(outs),
        scratch_shapes=[pltpu.VMEM(shape, F32) for shape in scratch],
        compiler_params=pltpu.CompilerParams(vmem_limit_bytes=32 * 2**20),
    )(*arrays)


def shift(array, axis, by):
    count = lax.axis_size(axis)
    return lax.ppermute(array, axis, [(i, (i + by) % count) for i in range(count)])


def per_device(right_side, coefficient):
    own, high, low = call(
        permute_kernel, [(16, 4, 8, 128), (9, 4, 8, 128), (9, 4, 8, 128)], [], right_side, coefficient
    )
    left, right = shift(high, "gx", 1), shift(low, "gx", -1)
    (wide,) = call(wide_kernel, [(34, 4, 8, 128)], [], own, left, right)
    left, right = shift(wide, "gy", 1), shift(wide, "gy", -1)
    fine = (4, 24, 128)
    piece, u0, g, k = call(
        fine_kernel,
        [(2, 4, 2, 8, 128), (14, 4, 16, 128), (12, 4, 16, 128), (14, 4, 16, 128)],
        [(16, *fine), (18, *fine), (17, *fine), (16, *fine), (16, *fine), (16, *fine), (16, *fine), (14, *fine),
         (8, *fine), (4, 2, 24, 128), (6, 2, 24, 128)],
        wide, left, right,
    )
    count = lax.axis_size("gx")
    gathered = lax.all_to_all(jnp.broadcast_to(piece[None], (count, *piece.shape)), "gx", 0, 0)
    me = lax.axis_index("gx").astype(jnp.int32).reshape(1)
    mid = (2, 8, 128)
    coarse, edge, u1, rhs, fx, fy, fz, w = call(
        middle_kernel,
        [(4, 24, 128), (2, 24, 128), (12, *mid), (10, *mid), (11, *mid), (10, *mid), (10, *mid), (10, *mid)],
        [(44, *mid), (44, *mid), (43, *mid), (42, *mid), (42, *mid), (42, *mid), (42, *mid), (42, *mid), (40, *mid),
         (192, 128), (256, 128), (4, 32, 128), (32, 128)],
        me, gathered, scalars=1,
    )
    low = shift(jnp.concatenate([coarse, edge[0:1]]), "gy", 1)
    high = shift(jnp.concatenate([coarse, edge[1:2]]), "gy", -1)
    three = jnp.concatenate([low[0:4], coarse, high[0:4]])
    below, above = shift(three, "gy", 3), shift(three, "gy", -3)
    rows = (18, 24, 128)
    (v1,) = call(
        coarse_kernel, [(8, *mid)], [rows, rows, rows, rows, rows, rows, (12, *mid), (10, *mid)],
        below, three, above, low[4], high[4], u1, rhs, fx, fy, fz, w,
    )
    low, high = shift(v1, "gy", 1), shift(v1, "gy", -1)
    last = (4, 16, 128)
    return tuple(call(
        last_kernel, [(8, 8, 512), (8, 8, 512)],
        [(13, *last), (12, *last), (12, *last), (12, *last), (8, 2, 16, 128), (14, *last), (12, *last), (8, *last)],
        v1, low, high, u0, g, k,
    ))


def solution(mesh):
    placed = (P("gx", "gy", None), P("gx", "gy", None))
    return jax.shard_map(per_device, mesh=mesh, in_specs=placed, out_specs=placed, check_vma=False)
```

time: 351 us -> 102 us (0.29)
  starting transfers between devices: 179 us -> 42.9 us
  local copies, waits for them, and re-layouts: 61.1 us -> 4.35 us
  waiting for transfers between devices: 82 us -> 31.7 us
  other arithmetic: 25.4 us -> 0.02 us
  Pallas kernels: 0 us -> 21.3 us
    ppermute x68 -> x10, starting transfers between devices: 179 us -> 36 us  [shift(): lax.ppermute(array, axis, [(i, (i + by) % count) for i in range(count)])]
    ppermute x68 -> x10, waiting for transfers between devices: 82 us -> 19.8 us  [shift(): lax.ppermute(array, axis, [(i, (i + by) % count) for i in range(count)])]
    reshape x8 -> x0, local copies, waits for them, and re-layouts: 48 us -> none  [the longest x3 45.7 us: block_mean(): field.reshape(field.shape[0] // 2, 2, field.shape[1] // 2, 2, field.shape...]
    pallas_call x0 -> x6, Pallas kernels: none -> 21.3 us  [call(): pl.pallas_call(kernel, out_shape=[jax.ShapeDtypeStruct(shape, F32) for sh...]
    reduce_sum x4 -> x0, other arithmetic: 18.9 us -> none  [block_mean(): return jnp.sum(shaped, axis=(1, 3, 5)) * 0.125]
    all_to_all x0 -> x1, waiting for transfers between devices: none -> 11.9 us  [per_device(): lax.all_to_all(jnp.broadcast_to(piece[None], (count, *piece.shape)), 'gx'...]
    all_to_all x0 -> x1, starting transfers between devices: none -> 6.9 us  [per_device(): lax.all_to_all(jnp.broadcast_to(piece[None], (count, *piece.shape)), 'gx'...]
    mul x1 -> x0, local copies, waits for them, and re-layouts: 5.53 us -> none  [block_mean(): return jnp.sum(shaped, axis=(1, 3, 5)) * 0.125]
  transfers between devices with their start and end apart: 68 -> 11, of which waited for: 49 -> 11; matrix products, arithmetic and copies ran while one was open for 3% -> 0% of each run, Pallas kernels for 0% -> 0%
where the time goes in v1:
time: 102 us; the launch traced here: 101 us
  starting transfers between devices  42.9 us (42%)
  waiting for transfers between devices  31.7 us (31%)
  Pallas kernels  21.3 us (21%)
  local copies, waits for them, and re-layouts  4.35 us (4%)
    ppermute x10, starting transfers between devices, shift(): lax.ppermute(array, axis, [(i, (i + by) % count) for i in range(count)])  36 us
    pallas_call x6, Pallas kernels, call(): pl.pallas_call(kernel, out_shape=[jax.ShapeDtypeStruct(shape, F32) for sh...  21.3 us
    ppermute x10, waiting for transfers between devices, shift(): lax.ppermute(array, axis, [(i, (i + by) % count) for i in range(count)])  19.8 us
    all_to_all x1, waiting for transfers between devices, per_device(): lax.all_to_all(jnp.broadcast_to(piece[None], (count, *piece.shape)), 'gx'...  11.9 us
    all_to_all x1, starting transfers between devices, per_device(): lax.all_to_all(jnp.broadcast_to(piece[None], (count, *piece.shape)), 'gx'...  6.9 us
    unnamed x8, local copies, waits for them, and re-layouts  2.43 us
  transfers between devices with their start and end apart: 11, of which 11 were waited for; matrix products, arithmetic and copies ran while one was open for 0% of the time, Pallas kernels for 0%

profile of v1, /device:TPU:1, one launch (start us, length us, event | category | flops | bytes accessed | tf_op | source)
XLA Modules:
  0.0 101.1 jit_solution(10111319164743929968)
XLA Ops:
  2.4 1.3 %shard_map.41 = (f32[16,4,8,128]{3,2,1,0:T(8,128)S(1)}, f32[9,4,8,128]{3,2,1,0:T(8,128)S(1)}, f32[9,4,8,128]{3,2,1,0:T(8,128)S(1)}) custom-call(f32[8,8,512]{2,1,0:T(8,128)S(1)} %copy-done, f32[8,8,512]{2,1,0:T(8,128)S(1)} %copy-done.1), custom_call_target="tpu_custom_call" | custom-call | tf_op jit(solution)/shard_map/pallas_call | solution.py:304
  3.8 4.0 %collective-permute-start = (f32[9,4,8,128]{3,2,1,0:T(8,128)S(1)}, f32[9,4,8,128]{3,2,1,0:T(8,128)S(1)}, u32[]{:S(2)}, u32[]{:S(2)}) collective-permute-start(f32[9,4,8,128]{3,2,1,0:T(8,128)S(1)} %get-tuple-element.18), channel_id=1, source_target_pairs={{0,32},{32,64},{64,96},{96,128},{128,160},{160,192},{192,224},{224... | collective-permute-start | bytes 442376 | tf_op jit(solution)/shard_map/ppermute | solution.py:316
  7.8 5.5 %collective-permute-start.1 = (f32[9,4,8,128]{3,2,1,0:T(8,128)S(1)}, f32[9,4,8,128]{3,2,1,0:T(8,128)S(1)}, u32[]{:S(2)}, u32[]{:S(2)}) collective-permute-start(f32[9,4,8,128]{3,2,1,0:T(8,128)S(1)} %get-tuple-element.19), channel_id=1, source_target_pairs={{0,480},{32,0},{64,32},{96,64},{128,96},{160,128},{192,160},{224,1... | collective-permute-start | bytes 442376 | tf_op jit(solution)/shard_map/ppermute | solution.py:316
  14.0 1.5 %collective-permute-done.1.right = f32[9,4,8,128]{3,2,1,0:T(8,128)S(1)} collective-permute-done((f32[9,4,8,128]{3,2,1,0:T(8,128)S(1)}, f32[9,4,8,128]{3,2,1,0:T(8,128)S(1)}, u32[]{:S(2)}, u32[]{:S(2)}) %collective-permute-start.1) | collective-permute-done | bytes 147488 | tf_op jit(solution)/shard_map/ppermute | solution.py:316
  15.5 3.5 %collective-permute-start.2 = (f32[34,4,8,128]{3,2,1,0:T(8,128)S(1)}, f32[34,4,8,128]{3,2,1,0:T(8,128)S(1)}, u32[]{:S(2)}, u32[]{:S(2)}) collective-permute-start(f32[34,4,8,128]{3,2,1,0:T(8,128)S(1)} %shard_map.42.own), channel_id=1, source_target_pairs={{0,1},{1,2},{2,3},{3,4},{4,5},{5,6},{6,7},{7,8},{8,9},{9,10},{10,1... | collective-permute-start | bytes 1671176 | tf_op jit(solution)/shard_map/ppermute | solution.py:316
  19.0 3.6 %collective-permute-start.3 = (f32[34,4,8,128]{3,2,1,0:T(8,128)S(1)}, f32[34,4,8,128]{3,2,1,0:T(8,128)S(1)}, u32[]{:S(2)}, u32[]{:S(2)}) collective-permute-start(f32[34,4,8,128]{3,2,1,0:T(8,128)S(1)} %shard_map.42.own), channel_id=1, source_target_pairs={{0,31},{1,0},{2,1},{3,2},{4,3},{5,4},{6,5},{7,6},{8,7},{9,8},{10,9... | collective-permute-start | bytes 1671176 | tf_op jit(solution)/shard_map/ppermute | solution.py:316
  22.6 2.9 %collective-permute-done.2.left = f32[34,4,8,128]{3,2,1,0:T(8,128)S(1)} collective-permute-done((f32[34,4,8,128]{3,2,1,0:T(8,128)S(1)}, f32[34,4,8,128]{3,2,1,0:T(8,128)S(1)}, u32[]{:S(2)}, u32[]{:S(2)}) %collective-permute-start.2) | collective-permute-done | bytes 557088 | tf_op jit(solution)/shard_map/ppermute | solution.py:316
  25.5 2.8 %collective-permute-done.3.right = f32[34,4,8,128]{3,2,1,0:T(8,128)S(1)} collective-permute-done((f32[34,4,8,128]{3,2,1,0:T(8,128)S(1)}, f32[34,4,8,128]{3,2,1,0:T(8,128)S(1)}, u32[]{:S(2)}, u32[]{:S(2)}) %collective-permute-start.3) | collective-permute-done | bytes 557088 | tf_op jit(solution)/shard_map/ppermute | solution.py:316
  28.3 6.0 %shard_map.43 = (f32[2,4,2,8,128]{4,3,2,1,0:T(8,128)S(1)}, f32[14,4,16,128]{3,2,1,0:T(8,128)S(1)}, f32[12,4,16,128]{3,2,1,0:T(8,128)S(1)}, f32[14,4,16,128]{3,2,1,0:T(8,128)S(1)}) custom-call(f32[34,4,8,128]{3,2,1,0:T(8,128)S(1)} %shard_map.42.own, f32[34,4,8,128]{3,2,1,0:T(8,128)S(1)} %collective-permute-done.2.left, ...), custom_call_target="tpu_custom_call" | custom-call | tf_op jit(solution)/shard_map/pallas_call | solution.py:304
  34.3 1.1 %broadcast_in_dim.2 = f32[16,2,4,2,8,128]{5,4,3,2,1,0:T(8,128)} broadcast(f32[2,4,2,8,128]{4,3,2,1,0:T(8,128)S(1)} %get-tuple-element.20), dimensions={1,2,3,4,5} | broadcast | bytes 1114112 | tf_op jit(solution)/shard_map/broadcast_in_dim | solution.py:335
  35.4 6.9 %all-to-all-start = ((f32[16,2,4,2,8,128]{5,4,3,2,1,0:T(8,128)}), f32[16,2,4,2,8,128]{5,4,3,2,1,0:T(8,128)S(1)}, u32[]{:S(2)}, u32[]{:S(2)}) async-start(f32[16,2,4,2,8,128]{5,4,3,2,1,0:T(8,128)} %broadcast_in_dim.2), calls=%async_computation | async-start | bytes 2097152 | tf_op jit(solution)/shard_map/all_to_all | solution.py:335
  42.3 11.9 %all-to-all-done.gathered = f32[16,2,4,2,8,128]{5,4,3,2,1,0:T(8,128)S(1)} async-done(((f32[16,2,4,2,8,128]{5,4,3,2,1,0:T(8,128)}), f32[16,2,4,2,8,128]{5,4,3,2,1,0:T(8,128)S(1)}, u32[]{:S(2)}, u32[]{:S(2)}) %all-to-all-start) | async-done | bytes 1048608 | tf_op jit(solution)/shard_map/all_to_all | solution.py:335
  54.3 3.8 %shard_map.44 = (f32[4,24,128]{2,1,0:T(8,128)S(1)}, f32[2,24,128]{2,1,0:T(8,128)S(1)}, f32[12,2,8,128]{3,2,1,0:T(8,128)S(1)}, f32[10,2,8,128]{3,2,1,0:T(8,128)S(...) custom-call(s32[1]{0:T(128)} %bitcast.me, ...), custom_call_target="tpu_custom_call" | custom-call | tf_op jit(solution)/shard_map/pallas_call | solution.py:304
  58.1 6.0 %collective-permute-start.4 = (f32[5,24,128]{2,1,0:T(8,128)S(1)}, f32[5,24,128]{2,1,0:T(8,128)S(1)}, u32[]{:S(2)}, u32[]{:S(2)}) collective-permute-start(f32[5,24,128]{2,1,0:T(8,128)S(1)} %get-tuple-element.32), channel_id=1, source_target_pairs={{0,1},{1,2},{2,3},{3,4},{4,5},{5,6},{6,7},{7,8},{8,9},{9,10},{10,1... | collective-permute-start | bytes 184328 | tf_op jit(solution)/shard_map/ppermute | solution.py:316
  64.3 1.1 %collective-permute-done.4 = f32[5,24,128]{2,1,0:T(8,128)S(1)} collective-permute-done((f32[5,24,128]{2,1,0:T(8,128)S(1)}, f32[5,24,128]{2,1,0:T(8,128)S(1)}, u32[]{:S(2)}, u32[]{:S(2)}) %collective-permute-start.4) | collective-permute-done | bytes 61472 | tf_op jit(solution)/shard_map/ppermute | solution.py:316
  66.0 1.7 %collective-permute-done.5 = f32[5,24,128]{2,1,0:T(8,128)S(1)} collective-permute-done((f32[5,24,128]{2,1,0:T(8,128)S(1)}, f32[5,24,128]{2,1,0:T(8,128)S(1)}, u32[]{:S(2)}, u32[]{:S(2)}) %collective-permute-start.5) | collective-permute-done | bytes 61472 | tf_op jit(solution)/shard_map/ppermute | solution.py:316
  68.6 4.0 %collective-permute-start.6 = (f32[12,24,128]{2,1,0:T(8,128)S(1)}, f32[12,24,128]{2,1,0:T(8,128)S(1)}, u32[]{:S(2)}, u32[]{:S(2)}) collective-permute-start(f32[12,24,128]{2,1,0:T(8,128)S(1)} %pad_maximum_fusion.here), channel_id=1, source_target_pairs={{0,3},{1,4},{2,5},{3,6},{4,7},{5,8},{6,9},{7,10},{8,11},{9,12},{10... | collective-permute-start | bytes 442376 | tf_op jit(solution)/shard_map/ppermute | solution.py:316
  72.6 8.3 %collective-permute-start.7 = (f32[12,24,128]{2,1,0:T(8,128)S(1)}, f32[12,24,128]{2,1,0:T(8,128)S(1)}, u32[]{:S(2)}, u32[]{:S(2)}) collective-permute-start(f32[12,24,128]{2,1,0:T(8,128)S(1)} %pad_maximum_fusion.here), channel_id=1, source_target_pairs={{0,29},{1,30},{2,31},{3,0},{4,1},{5,2},{6,3},{7,4},{8,5},{9,6},{10... | collective-permute-start | bytes 442376 | tf_op jit(solution)/shard_map/ppermute | solution.py:316
  81.0 2.4 %collective-permute-done.6.below = f32[12,24,128]{2,1,0:T(8,128)S(1)} collective-permute-done((f32[12,24,128]{2,1,0:T(8,128)S(1)}, f32[12,24,128]{2,1,0:T(8,128)S(1)}, u32[]{:S(2)}, u32[]{:S(2)}) %collective-permute-start.6) | collective-permute-done | bytes 147488 | tf_op jit(solution)/shard_map/ppermute | solution.py:316
  83.4 3.1 %collective-permute-done.7.above = f32[12,24,128]{2,1,0:T(8,128)S(1)} collective-permute-done((f32[12,24,128]{2,1,0:T(8,128)S(1)}, f32[12,24,128]{2,1,0:T(8,128)S(1)}, u32[]{:S(2)}, u32[]{:S(2)}) %collective-permute-start.7) | collective-permute-done | bytes 147488 | tf_op jit(solution)/shard_map/ppermute | solution.py:316
  86.5 1.9 %shard_map.45.v_here = f32[8,2,8,128]{3,2,1,0:T(8,128)S(1)} custom-call(f32[12,24,128]{2,1,0:T(8,128)S(1)} %collective-permute-done.6.below, f32[12,24,128]{2,1,0:T(8,128)S(1)} %pad_maximum_fusion.here, f32[12,24,128]{2,1,0:T(8,128)S(1)} %collective-permute-done.7.above, f32[24,128]{1,0:T(8,128)S(1)} %slice_bitcast_fusion.1.edge_low, ...), custom_call_target="tpu_custom_call" | custom-call | tf_op jit(solution)/shard_map/pallas_call | solution.py:304
  89.2 1.3 %collective-permute-done.8.v_low = f32[8,2,8,128]{3,2,1,0:T(8,128)S(1)} collective-permute-done((f32[8,2,8,128]{3,2,1,0:T(8,128)S(1)}, f32[8,2,8,128]{3,2,1,0:T(8,128)S(1)}, u32[]{:S(2)}, u32[]{:S(2)}) %collective-permute-start.8) | collective-permute-done | bytes 65568 | tf_op jit(solution)/shard_map/ppermute | solution.py:316
  90.5 2.4 %collective-permute-done.9.v_high = f32[8,2,8,128]{3,2,1,0:T(8,128)S(1)} collective-permute-done((f32[8,2,8,128]{3,2,1,0:T(8,128)S(1)}, f32[8,2,8,128]{3,2,1,0:T(8,128)S(1)}, u32[]{:S(2)}, u32[]{:S(2)}) %collective-permute-start.9) | collective-permute-done | bytes 65568 | tf_op jit(solution)/shard_map/ppermute | solution.py:316
  92.8 8.2 %shard_map.46 = (f32[8,8,512]{2,1,0:T(8,128)}, f32[8,8,512]{2,1,0:T(8,128)}) custom-call(f32[8,2,8,128]{3,2,1,0:T(8,128)S(1)} %shard_map.45.v_here, f32[8,2,8,128]{3,2,1,0:T(8,128)S(1)} %collective-permute-done.8.v_low, f32[8,2,8,128]{3,2,1,0:T(8,128)S(1)} %collective-permute-done.9.v_high, f32[14,4,16,128]{3,2,1,0:T(8,128)S(1)} %get-tuple-element.29.u0, ...), custom_call_target="tpu_custom_call" | custom-call | tf_op jit(solution)/shard_map/pallas_call | solution.py:304
  (21 shorter events, 4.9 us)
Async XLA Ops:
  0.6 0.9 copy-start
  1.5 0.9 copy-start.1
  3.8 10.2 %collective-permute-start = (f32[9,4,8,128]{3,2,1,0:T(8,128)S(1)}, f32[9,4,8,128]{3,2,1,0:T(8,128)S(1)}, u32[]{:S(2)}, u32[]{:S(2)}) collective-permute-start(f32[9,4,8,128]{3,2,1,0:T(8,128)S(1)} %get-tuple-element.18), channel_id=1, source_target_pairs={{0,32},{32,64},{64,96},{96,128},{128,160},{160,192},{192,224},{224... | collective-permute-start | bytes 442376 | tf_op jit(solution)/shard_map/ppermute | solution.py:316
  7.8 7.6 %collective-permute-start.1 = (f32[9,4,8,128]{3,2,1,0:T(8,128)S(1)}, f32[9,4,8,128]{3,2,1,0:T(8,128)S(1)}, u32[]{:S(2)}, u32[]{:S(2)}) collective-permute-start(f32[9,4,8,128]{3,2,1,0:T(8,128)S(1)} %get-tuple-element.19), channel_id=1, source_target_pairs={{0,480},{32,0},{64,32},{96,64},{128,96},{160,128},{192,160},{224,1... | collective-permute-start | bytes 442376 | tf_op jit(solution)/shard_map/ppermute | solution.py:316
  15.5 10.0 %collective-permute-start.2 = (f32[34,4,8,128]{3,2,1,0:T(8,128)S(1)}, f32[34,4,8,128]{3,2,1,0:T(8,128)S(1)}, u32[]{:S(2)}, u32[]{:S(2)}) collective-permute-start(f32[34,4,8,128]{3,2,1,0:T(8,128)S(1)} %shard_map.42.own), channel_id=1, source_target_pairs={{0,1},{1,2},{2,3},{3,4},{4,5},{5,6},{6,7},{7,8},{8,9},{9,10},{10,1... | collective-permute-start | bytes 1671176 | tf_op jit(solution)/shard_map/ppermute | solution.py:316
  19.0 9.3 %collective-permute-start.3 = (f32[34,4,8,128]{3,2,1,0:T(8,128)S(1)}, f32[34,4,8,128]{3,2,1,0:T(8,128)S(1)}, u32[]{:S(2)}, u32[]{:S(2)}) collective-permute-start(f32[34,4,8,128]{3,2,1,0:T(8,128)S(1)} %shard_map.42.own), channel_id=1, source_target_pairs={{0,31},{1,0},{2,1},{3,2},{4,3},{5,4},{6,5},{7,6},{8,7},{9,8},{10,9... | collective-permute-start | bytes 1671176 | tf_op jit(solution)/shard_map/ppermute | solution.py:316
  35.4 18.9 %all-to-all-start = ((f32[16,2,4,2,8,128]{5,4,3,2,1,0:T(8,128)}), f32[16,2,4,2,8,128]{5,4,3,2,1,0:T(8,128)S(1)}, u32[]{:S(2)}, u32[]{:S(2)}) async-start(f32[16,2,4,2,8,128]{5,4,3,2,1,0:T(8,128)} %broadcast_in_dim.2), calls=%async_computation | async-start | bytes 2097152 | tf_op jit(solution)/shard_map/all_to_all | solution.py:335
  58.1 7.3 %collective-permute-start.4 = (f32[5,24,128]{2,1,0:T(8,128)S(1)}, f32[5,24,128]{2,1,0:T(8,128)S(1)}, u32[]{:S(2)}, u32[]{:S(2)}) collective-permute-start(f32[5,24,128]{2,1,0:T(8,128)S(1)} %get-tuple-element.32), channel_id=1, source_target_pairs={{0,1},{1,2},{2,3},{3,4},{4,5},{5,6},{6,7},{7,8},{8,9},{9,10},{10,1... | collective-permute-start | bytes 184328 | tf_op jit(solution)/shard_map/ppermute | solution.py:316
  64.1 3.6 %collective-permute-start.5 = (f32[5,24,128]{2,1,0:T(8,128)S(1)}, f32[5,24,128]{2,1,0:T(8,128)S(1)}, u32[]{:S(2)}, u32[]{:S(2)}) collective-permute-start(f32[5,24,128]{2,1,0:T(8,128)S(1)} %get-tuple-element.33), channel_id=1, source_target_pairs={{0,31},{1,0},{2,1},{3,2},{4,3},{5,4},{6,5},{7,6},{8,7},{9,8},{10,9... | collective-permute-start | bytes 184328 | tf_op jit(solution)/shard_map/ppermute | solution.py:316
  65.4 0.6 copy-start.2
  67.8 0.8 slice-start
  68.6 12.4 %copy-start.3 = (f32[5,24,128]{2,1,0:T(8,128)S(1)}, f32[5,24,128]{2,1,0:T(8,128)}, u32[]{:S(2)}) copy-start(f32[5,24,128]{2,1,0:T(8,128)} %copy-done.2) | copy-start | bytes 184324
  68.6 14.8 %collective-permute-start.6 = (f32[12,24,128]{2,1,0:T(8,128)S(1)}, f32[12,24,128]{2,1,0:T(8,128)S(1)}, u32[]{:S(2)}, u32[]{:S(2)}) collective-permute-start(f32[12,24,128]{2,1,0:T(8,128)S(1)} %pad_maximum_fusion.here), channel_id=1, source_target_pairs={{0,3},{1,4},{2,5},{3,6},{4,7},{5,8},{6,9},{7,10},{8,11},{9,12},{10... | collective-permute-start | bytes 442376 | tf_op jit(solution)/shard_map/ppermute | solution.py:316
  72.6 13.9 %collective-permute-start.7 = (f32[12,24,128]{2,1,0:T(8,128)S(1)}, f32[12,24,128]{2,1,0:T(8,128)S(1)}, u32[]{:S(2)}, u32[]{:S(2)}) collective-permute-start(f32[12,24,128]{2,1,0:T(8,128)S(1)} %pad_maximum_fusion.here), channel_id=1, source_target_pairs={{0,29},{1,30},{2,31},{3,0},{4,1},{5,2},{6,3},{7,4},{8,5},{9,6},{10... | collective-permute-start | bytes 442376 | tf_op jit(solution)/shard_map/ppermute | solution.py:316
  88.4 2.1 %collective-permute-start.8 = (f32[8,2,8,128]{3,2,1,0:T(8,128)S(1)}, f32[8,2,8,128]{3,2,1,0:T(8,128)S(1)}, u32[]{:S(2)}, u32[]{:S(2)}) collective-permute-start(f32[8,2,8,128]{3,2,1,0:T(8,128)S(1)} %shard_map.45.v_here), channel_id=1, source_target_pairs={{0,1},{1,2},{2,3},{3,4},{4,5},{5,6},{6,7},{7,8},{8,9},{9,10},{10,1... | collective-permute-start | bytes 196616 | tf_op jit(solution)/shard_map/ppermute | solution.py:316
  89.2 3.7 %collective-permute-start.9 = (f32[8,2,8,128]{3,2,1,0:T(8,128)S(1)}, f32[8,2,8,128]{3,2,1,0:T(8,128)S(1)}, u32[]{:S(2)}, u32[]{:S(2)}) collective-permute-start(f32[8,2,8,128]{3,2,1,0:T(8,128)S(1)} %shard_map.45.v_here), channel_id=1, source_target_pairs={{0,31},{1,0},{2,1},{3,2},{4,3},{5,4},{6,5},{7,6},{8,7},{9,8},{10,9... | collective-permute-start | bytes 196616 | tf_op jit(solution)/shard_map/ppermute | solution.py:316

commit v2 on v1

--- a/solution.py
+++ b/solution.py
@@ -82,20 +82,31 @@
 def permutation(inverse):
     z = lax.broadcasted_iota(jnp.int32, (512, 512), 1 if inverse else 0)
     at = lax.broadcasted_iota(jnp.int32, (512, 512), 0 if inverse else 1)
-    return jnp.where(z == 4 * (at % LANES) + at // LANES, 1.0, 0.0).astype(F32)
+    return jnp.where(z == 4 * (at % LANES) + at // LANES, 1.0, 0.0).astype(jnp.bfloat16)
 
 
 def rearrange(rows, matrix):
-    return lax.dot_general(rows, matrix, (((1,), (0,)), ((), ())), precision=lax.Precision.HIGHEST, preferred_element_type=F32)
-
-
-def permute_kernel(g_ref, k_ref, own, high, low):
+    count = rows.shape[0]
+    top = rows.astype(jnp.bfloat16)
+    rest = rows - top.astype(F32)
+    middle = rest.astype(jnp.bfloat16)
+    bottom = (rest - middle.astype(F32)).astype(jnp.bfloat16)
+    parts = jnp.concatenate([top, middle, bottom], axis=0)
+    moved = lax.dot_general(parts, matrix, (((1,), (0,)), ((), ())), preferred_element_type=F32)
+    return (moved[0:count] + moved[count : 2 * count]) + moved[2 * count :]
+
+
+def permute_kernel(g_ref, k_ref, own, high, low, held, arrived):
+    copies = [pltpu.make_async_copy(ref, held.at[i], arrived.at[i]) for i, ref in enumerate((g_ref, k_ref))]
+    for copy in copies:
+        copy.start()
     matrix = permutation(False)
-    for source, base in ((g_ref, 0), (k_ref, 8)):
-        moved = rearrange(source[...].reshape(64, 512), matrix)
-        for x in range(8):
-            for r in range(4):
-                own[base + x, r] = moved[8 * x : 8 * x + 8, LANES * r : LANES * r + LANES]
+    for copy in copies:
+        copy.wait()
+    moved = rearrange(held[...].reshape(128, 512), matrix)
+    for x in range(16):
+        for r in range(4):
+            own[x, r] = moved[8 * x : 8 * x + 8, LANES * r : LANES * r + LANES]
     high[0:4] = own[4:8]
     high[4:9] = own[11:16]
     low[0:4] = own[0:4]
@@ -117,15 +128,15 @@
         target[:, 0:8] = left[i]
         target[:, 8:16] = own[i]
         target[:, 16:24] = right[i]
-    face_pass(16, k, fx, fy, fz, w, 1.0, 1)
+    face_pass(16, k, fx, fy, fz, w, 1.0, 16)
 
     def first(i, carry):
         uf[i] = w[i] * g[i]
         return carry
 
-    loop(16, first, 0, 1)
-    sweep_pass(14, uf, 0, 1, g, 1, fx, fy, fz, w, u0, 0, 1)
-    sweep_pass(8, u0, 2, 4, g, 4, fx, fy, fz, w, res, 0, 1, last=True)
+    loop(16, first, 0, 16)
+    sweep_pass(14, uf, 0, 1, g, 1, fx, fy, fz, w, u0, 0, 14)
+    sweep_pass(8, u0, 2, 4, g, 4, fx, fy, fz, w, res, 0, 8, last=True)
     for x in range(4):
         both = res[2 * x] + res[2 * x + 1]
         s1[x, 0] = both[0] + both[1]
@@ -151,43 +162,45 @@
             + half * (here + rows(sc, x + 1, 2)) + half * (here + rows(sc, x + 1, 6))
             + face_z + z_prev(face_z)
         )
-        piece[0, x] = DAMPING / diag * rhs
-        piece[1, x] = here
+        first_sweep = DAMPING / diag * rhs
+        for to in range(piece.shape[0]):
+            piece[to, 0, x] = first_sweep
+            piece[to, 1, x] = here
     u_out[...] = u0[:, :, 4:20, :]
     g_out[...] = g[2:14, :, 4:20, :]
     k_out[...] = k[2:16, :, 4:20, :]
 
 
-def middle_kernel(me, gathered, coarse, edge, u_out, rhs_out, fx_out, fy_out, fz_out, w_out,
+def middle_kernel(me, gathered, send_high, send_low, u_out, rhs_out, fx_out, fy_out, fz_out, w_out,
                   uf, k, fx, fy, fz, w, rhs, u1, res, flat, flat_k, k2, r2):
     count = gathered.shape[0]
     for block in range(11):
         source = lax.rem(me[0] + (block - 5 + count * 5), count)
         uf[4 * block : 4 * block + 4] = gathered[source, 0]
         k[4 * block : 4 * block + 4] = gathered[source, 1]
-    face_pass(42, k, fx, fy, fz, w, 0.25, 6)
+    face_pass(42, k, fx, fy, fz, w, 0.25, 42)
 
     def right_side(i, carry):
         rhs[i] = uf[i + 1] / w[i]
         return carry
 
-    loop(42, right_side, 0, 6)
-    sweep_pass(42, uf, 0, 0, rhs, 0, fx, fy, fz, w, u1, 0, 6)
-    sweep_pass(40, u1, 0, 1, rhs, 1, fx, fy, fz, w, res, 0, 5, last=True)
+    loop(42, right_side, 0, 42)
+    sweep_pass(42, uf, 0, 0, rhs, 0, fx, fy, fz, w, u1, 0, 42)
+    sweep_pass(40, u1, 0, 1, rhs, 1, fx, fy, fz, w, res, 0, 40, last=True)
 
     def add_up(i, carry):
         both = res[2 * i] + res[2 * i + 1]
         flat[pl.ds(pl.multiple_of(8 * i, 8), 8), :] = both[0] + both[1]
         return carry
 
-    loop(20, add_up, 0, 5)
+    loop(20, add_up, 0, 20)
 
     def add_up_k(i, carry):
         both = k[2 * i] + k[2 * i + 1]
         flat_k[pl.ds(pl.multiple_of(8 * i, 8), 8), :] = both[0] + both[1]
         return carry
 
-    loop(22, add_up_k, 0, 2)
+    loop(22, add_up_k, 0, 22)
     flat[160:192] = jnp.zeros((32, LANES), F32)
     flat_k[176:256] = jnp.ones((80, LANES), F32)
 
@@ -206,8 +219,9 @@
             + face_z + pltpu.roll(face_z, 1, 1)
         )
         r2[...] = DAMPING / diag
-        coarse[2 * j] = r2[1:25] * row(flat, 2 * j + 2, 24)
-        coarse[2 * j + 1] = k2[j + 1, 1:25]
+        for coarse in (send_high, send_low):
+            coarse[2 * j] = r2[1:25] * row(flat, 2 * j + 2, 24)
+            coarse[2 * j + 1] = k2[j + 1, 1:25]
     u_out[...] = u1[15:27]
     rhs_out[...] = rhs[16:26]
     fx_out[...] = fx[16:27]
@@ -217,11 +231,17 @@
     uf[0:12] = u1[15:27]
     for x in range(12):
         for r in range(2):
-            edge[0, 2 * x + r : 2 * x + r + 1, :] = uf[x, r, 4:5, :]
-            edge[1, 2 * x + r : 2 * x + r + 1, :] = uf[x, r, 3:4, :]
-
-
-def coarse_kernel(below, here, above, edge_low, edge_high, u_in, rhs, fx, fy, fz, w, v_out,
+            send_high[4, 2 * x + r : 2 * x + r + 1, :] = uf[x, r, 4:5, :]
+            send_low[4, 2 * x + r : 2 * x + r + 1, :] = uf[x, r, 3:4, :]
+
+
+def three_kernel(here, low, high, out):
+    out[0:4] = low[0:4]
+    out[4:8] = here[0:4]
+    out[8:12] = high[0:4]
+
+
+def coarse_kernel(below, here, above, left, right, u_in, rhs, fx, fy, fz, w, v_out,
                   u, cx, cy, cz, cw, cr, v, va):
     half = 0.5 * 0.0625
     blocks = (below, here, above)
@@ -262,8 +282,8 @@
     v[...] = u_in[...]
     for x in range(12):
         for r in range(2):
-            v[x, r, 0:1, :] = edge_low[2 * x + r : 2 * x + r + 1, :]
-            v[x, r, 7:8, :] = edge_high[2 * x + r : 2 * x + r + 1, :]
+            v[x, r, 0:1, :] = left[4, 2 * x + r : 2 * x + r + 1, :]
+            v[x, r, 7:8, :] = right[4, 2 * x + r : 2 * x + r + 1, :]
     for x in range(6):
         rows = jnp.concatenate(
             [jnp.broadcast_to(u[7 + j, 7 + x : 8 + x, :], (2, LANES)) for j in range(4)], axis=0
@@ -271,8 +291,8 @@
         for twin in range(2):
             for r in range(2):
                 v[2 * x + twin, r] = v[2 * x + twin, r] + rows
-    sweep_pass(10, v, 0, 0, rhs, 0, fx, fy, fz, w, va, 0, 5)
-    sweep_pass(8, va, 0, 1, rhs, 1, fx, fy, fz, w, v_out, 0, 4)
+    sweep_pass(10, v, 0, 0, rhs, 0, fx, fy, fz, w, va, 0, 10)
+    sweep_pass(8, va, 0, 1, rhs, 1, fx, fy, fz, w, v_out, 0, 8)
 
 
 def last_kernel(v_here, v_low, v_high, u0, g, k, correction, residual, fx, fy, fz, w, wide, ua, ub, res):
@@ -281,13 +301,13 @@
             rows = jnp.concatenate([v_low[x, r, 4:6], v_here[x, r, 2:6], v_high[x, r, 2:4]], axis=0)
             wide[x, r, pl.ds(0, 8, 2), :] = rows
             wide[x, r, pl.ds(1, 8, 2), :] = rows
-    face_pass(12, k, fx, fy, fz, w, 1.0, 1)
+    face_pass(12, k, fx, fy, fz, w, 1.0, 12)
     for i in range(14):
         fine = wide[(i + 1) // 2]
         ua[i] = u0[i] + jnp.stack([fine[0], fine[0], fine[1], fine[1]])
-    sweep_pass(12, ua, 0, 0, g, 0, fx, fy, fz, w, ub, 0, 1)
-    sweep_pass(10, ub, 0, 1, g, 1, fx, fy, fz, w, ua, 0, 1)
-    sweep_pass(8, ua, 0, 2, g, 2, fx, fy, fz, w, res, 0, 1, last=True)
+    sweep_pass(12, ua, 0, 0, g, 0, fx, fy, fz, w, ub, 0, 12)
+    sweep_pass(10, ub, 0, 1, g, 1, fx, fy, fz, w, ua, 0, 10)
+    sweep_pass(8, ua, 0, 2, g, 2, fx, fy, fz, w, res, 0, 8, last=True)
     matrix = permutation(True)
     for source, at, out in ((ua, 1, correction), (res, 0, residual)):
         rows = [
@@ -298,15 +318,16 @@
 
 VMEM = pl.BlockSpec(memory_space=pltpu.VMEM)
 SMEM = pl.BlockSpec(memory_space=pltpu.SMEM)
-
-
-def call(kernel, outs, scratch, *arrays, scalars=0):
+HBM = pl.BlockSpec(memory_space=pltpu.HBM)
+
+
+def call(kernel, outs, scratch, *arrays, scalars=0, far=0, extra=()):
     return pl.pallas_call(
         kernel,
         out_shape=[jax.ShapeDtypeStruct(shape, F32) for shape in outs],
-        in_specs=[SMEM] * scalars + [VMEM] * (len(arrays) - scalars),
+        in_specs=[SMEM] * scalars + [HBM] * far + [VMEM] * (len(arrays) - scalars - far),
         out_specs=[VMEM] * len(outs),
-        scratch_shapes=[pltpu.VMEM(shape, F32) for shape in scratch],
+        scratch_shapes=[pltpu.VMEM(shape, F32) for shape in scratch] + list(extra),
         compiler_params=pltpu.CompilerParams(vmem_limit_bytes=32 * 2**20),
     )(*arrays)
 
@@ -318,38 +339,39 @@
 
 def per_device(right_side, coefficient):
     own, high, low = call(
-        permute_kernel, [(16, 4, 8, 128), (9, 4, 8, 128), (9, 4, 8, 128)], [], right_side, coefficient
+        permute_kernel, [(16, 4, 8, 128), (9, 4, 8, 128), (9, 4, 8, 128)], [(2, 8, 8, 512)], right_side, coefficient,
+        far=2, extra=[pltpu.SemaphoreType.DMA((2,))],
     )
     left, right = shift(high, "gx", 1), shift(low, "gx", -1)
     (wide,) = call(wide_kernel, [(34, 4, 8, 128)], [], own, left, right)
     left, right = shift(wide, "gy", 1), shift(wide, "gy", -1)
     fine = (4, 24, 128)
+    count = lax.axis_size("gx")
     piece, u0, g, k = call(
         fine_kernel,
-        [(2, 4, 2, 8, 128), (14, 4, 16, 128), (12, 4, 16, 128), (14, 4, 16, 128)],
+        [(count, 2, 4, 2, 8, 128), (14, 4, 16, 128), (12, 4, 16, 128), (14, 4, 16, 128)],
         [(16, *fine), (18, *fine), (17, *fine), (16, *fine), (16, *fine), (16, *fine), (16, *fine), (14, *fine),
          (8, *fine), (4, 2, 24, 128), (6, 2, 24, 128)],
         wide, left, right,
     )
-    count = lax.axis_size("gx")
-    gathered = lax.all_to_all(jnp.broadcast_to(piece[None], (count, *piece.shape)), "gx", 0, 0)
+    gathered = lax.all_to_all(piece, "gx", 0, 0)
     me = lax.axis_index("gx").astype(jnp.int32).reshape(1)
     mid = (2, 8, 128)
-    coarse, edge, u1, rhs, fx, fy, fz, w = call(
+    high, low, u1, rhs, fx, fy, fz, w = call(
         middle_kernel,
-        [(4, 24, 128), (2, 24, 128), (12, *mid), (10, *mid), (11, *mid), (10, *mid), (10, *mid), (10, *mid)],
+        [(5, 24, 128), (5, 24, 128), (12, *mid), (10, *mid), (11, *mid), (10, *mid), (10, *mid), (10, *mid)],
         [(44, *mid), (44, *mid), (43, *mid), (42, *mid), (42, *mid), (42, *mid), (42, *mid), (42, *mid), (40, *mid),
          (192, 128), (256, 128), (4, 32, 128), (32, 128)],
         me, gathered, scalars=1,
     )
-    low = shift(jnp.concatenate([coarse, edge[0:1]]), "gy", 1)
-    high = shift(jnp.concatenate([coarse, edge[1:2]]), "gy", -1)
-    three = jnp.concatenate([low[0:4], coarse, high[0:4]])
+    here = high
+    low, high = shift(high, "gy", 1), shift(low, "gy", -1)
+    (three,) = call(three_kernel, [(12, 24, 128)], [], here, low, high)
     below, above = shift(three, "gy", 3), shift(three, "gy", -3)
     rows = (18, 24, 128)
     (v1,) = call(
         coarse_kernel, [(8, *mid)], [rows, rows, rows, rows, rows, rows, (12, *mid), (10, *mid)],
-        below, three, above, low[4], high[4], u1, rhs, fx, fy, fz, w,
+        below, three, above, low, high, u1, rhs, fx, fy, fz, w,
     )
     low, high = shift(v1, "gy", 1), shift(v1, "gy", -1)
     last = (4, 16, 128)

time: 102 us -> 86.2 us (0.85)
  Pallas kernels: 21.3 us -> 8.12 us
  local copies, waits for them, and re-layouts: 4.35 us -> 1.8 us
  waiting for transfers between devices: 31.7 us -> 33 us
    pallas_call x6 -> x7, Pallas kernels: 21.3 us -> 8.12 us  [call(): pl.pallas_call(kernel, out_shape=[jax.ShapeDtypeStruct(shape, F32) for sh...]
    ppermute x10, waiting for transfers between devices: 19.8 us -> 21.1 us  [shift(): lax.ppermute(array, axis, [(i, (i + by) % count) for i in range(count)])]
    broadcast_in_dim x1 -> x0, local copies, waits for them, and re-layouts: 1.12 us -> none  [per_device(): jnp.broadcast_to(piece[None], (count, *piece.shape))]
    unnamed x8 -> x4, local copies, waits for them, and re-layouts: 2.43 us -> 1.8 us
where the time goes in v2:
time: 86.2 us; the launch traced here: 85.8 us
  starting transfers between devices  42.2 us (49%)
  waiting for transfers between devices  33 us (38%)
  Pallas kernels  8.12 us (9%)
  local copies, waits for them, and re-layouts  1.8 us (2%)
    ppermute x10, starting transfers between devices, shift(): lax.ppermute(array, axis, [(i, (i + by) % count) for i in range(count)])  35.3 us
    ppermute x10, waiting for transfers between devices, shift(): lax.ppermute(array, axis, [(i, (i + by) % count) for i in range(count)])  21.1 us
    all_to_all x1, waiting for transfers between devices, per_device(): gathered = lax.all_to_all(piece, 'gx', 0, 0)  11.9 us
    pallas_call x7, Pallas kernels, call(): pl.pallas_call(kernel, out_shape=[jax.ShapeDtypeStruct(shape, F32) for sh...  8.12 us
    all_to_all x1, starting transfers between devices, per_device(): gathered = lax.all_to_all(piece, 'gx', 0, 0)  6.9 us
    unnamed x4, local copies, waits for them, and re-layouts  1.8 us
  transfers between devices with their start and end apart: 11, of which 11 were waited for; matrix products, arithmetic and copies ran while one was open for 0% of the time, Pallas kernels for 0%

profile of v2, /device:TPU:1, one launch (start us, length us, event | category | flops | bytes accessed | tf_op | source)
XLA Modules:
  0.0 85.8 jit_solution(10444032667164992303)
XLA Ops:
  0.6 0.9 %copy-done = f32[8,8,512]{2,1,0:T(8,128)S(1)} copy-done((f32[8,8,512]{2,1,0:T(8,128)S(1)}, f32[8,8,512]{2,1,0:T(8,128)}, u32[]{:S(2)}) %copy-start) | copy-done | bytes 131096
  1.5 0.9 %copy-done.1 = f32[8,8,512]{2,1,0:T(8,128)S(1)} copy-done((f32[8,8,512]{2,1,0:T(8,128)S(1)}, f32[8,8,512]{2,1,0:T(8,128)}, u32[]{:S(2)}) %copy-start.1) | copy-done | bytes 131096
  2.4 0.8 shard_map.41
  3.3 4.0 %collective-permute-start = (f32[9,4,8,128]{3,2,1,0:T(8,128)S(1)}, f32[9,4,8,128]{3,2,1,0:T(8,128)S(1)}, u32[]{:S(2)}, u32[]{:S(2)}) collective-permute-start(f32[9,4,8,128]{3,2,1,0:T(8,128)S(1)} %get-tuple-element.18), channel_id=1, source_target_pairs={{0,32},{32,64},{64,96},{96,128},{128,160},{160,192},{192,224},{224... | collective-permute-start | bytes 442376 | tf_op jit(solution)/shard_map/ppermute | solution.py:337
  7.3 5.6 %collective-permute-start.1 = (f32[9,4,8,128]{3,2,1,0:T(8,128)S(1)}, f32[9,4,8,128]{3,2,1,0:T(8,128)S(1)}, u32[]{:S(2)}, u32[]{:S(2)}) collective-permute-start(f32[9,4,8,128]{3,2,1,0:T(8,128)S(1)} %get-tuple-element.19), channel_id=1, source_target_pairs={{0,480},{32,0},{64,32},{96,64},{128,96},{160,128},{192,160},{224,1... | collective-permute-start | bytes 442376 | tf_op jit(solution)/shard_map/ppermute | solution.py:337
  13.5 1.5 %collective-permute-done.1.right = f32[9,4,8,128]{3,2,1,0:T(8,128)S(1)} collective-permute-done((f32[9,4,8,128]{3,2,1,0:T(8,128)S(1)}, f32[9,4,8,128]{3,2,1,0:T(8,128)S(1)}, u32[]{:S(2)}, u32[]{:S(2)}) %collective-permute-start.1) | collective-permute-done | bytes 147488 | tf_op jit(solution)/shard_map/ppermute | solution.py:337
  15.0 3.5 %collective-permute-start.2 = (f32[34,4,8,128]{3,2,1,0:T(8,128)S(1)}, f32[34,4,8,128]{3,2,1,0:T(8,128)S(1)}, u32[]{:S(2)}, u32[]{:S(2)}) collective-permute-start(f32[34,4,8,128]{3,2,1,0:T(8,128)S(1)} %shard_map.42.own), channel_id=1, source_target_pairs={{0,1},{1,2},{2,3},{3,4},{4,5},{5,6},{6,7},{7,8},{8,9},{9,10},{10,1... | collective-permute-start | bytes 1671176 | tf_op jit(solution)/shard_map/ppermute | solution.py:337
  18.5 3.6 %collective-permute-start.3 = (f32[34,4,8,128]{3,2,1,0:T(8,128)S(1)}, f32[34,4,8,128]{3,2,1,0:T(8,128)S(1)}, u32[]{:S(2)}, u32[]{:S(2)}) collective-permute-start(f32[34,4,8,128]{3,2,1,0:T(8,128)S(1)} %shard_map.42.own), channel_id=1, source_target_pairs={{0,31},{1,0},{2,1},{3,2},{4,3},{5,4},{6,5},{7,6},{8,7},{9,8},{10,9... | collective-permute-start | bytes 1671176 | tf_op jit(solution)/shard_map/ppermute | solution.py:337
  22.1 2.9 %collective-permute-done.2.left = f32[34,4,8,128]{3,2,1,0:T(8,128)S(1)} collective-permute-done((f32[34,4,8,128]{3,2,1,0:T(8,128)S(1)}, f32[34,4,8,128]{3,2,1,0:T(8,128)S(1)}, u32[]{:S(2)}, u32[]{:S(2)}) %collective-permute-start.2) | collective-permute-done | bytes 557088 | tf_op jit(solution)/shard_map/ppermute | solution.py:337
  25.0 2.8 %collective-permute-done.3.right = f32[34,4,8,128]{3,2,1,0:T(8,128)S(1)} collective-permute-done((f32[34,4,8,128]{3,2,1,0:T(8,128)S(1)}, f32[34,4,8,128]{3,2,1,0:T(8,128)S(1)}, u32[]{:S(2)}, u32[]{:S(2)}) %collective-permute-start.3) | collective-permute-done | bytes 557088 | tf_op jit(solution)/shard_map/ppermute | solution.py:337
  27.8 2.8 %shard_map.43 = (f32[16,2,4,2,8,128]{5,4,3,2,1,0:T(8,128)}, f32[14,4,16,128]{3,2,1,0:T(8,128)S(1)}, f32[12,4,16,128]{3,2,1,0:T(8,128)S(1)}, f32[14,4,16,128]{3,2,1,0:T(8,128)S(1)}) custom-call(f32[34,4,8,128]{3,2,1,0:T(8,128)S(1)} %shard_map.42.own, f32[34,4,8,128]{3,2,1,0:T(8,128)S(1)} %collective-permute-done.2.left, ...), custom_call_target="tpu_custom_call" | custom-call | tf_op jit(solution)/shard_map/pallas_call | solution.py:325
  30.5 6.9 %all-to-all-start = ((f32[16,2,4,2,8,128]{5,4,3,2,1,0:T(8,128)}), f32[16,2,4,2,8,128]{5,4,3,2,1,0:T(8,128)S(1)}, u32[]{:S(2)}, u32[]{:S(2)}) async-start(f32[16,2,4,2,8,128]{5,4,3,2,1,0:T(8,128)} %get-tuple-element.20), calls=%async_computation | async-start | bytes 2097152 | tf_op jit(solution)/shard_map/all_to_all | solution.py:357
  37.4 11.9 %all-to-all-done.gathered = f32[16,2,4,2,8,128]{5,4,3,2,1,0:T(8,128)S(1)} async-done(((f32[16,2,4,2,8,128]{5,4,3,2,1,0:T(8,128)}), f32[16,2,4,2,8,128]{5,4,3,2,1,0:T(8,128)S(1)}, u32[]{:S(2)}, u32[]{:S(2)}) %all-to-all-start) | async-done | bytes 1048608 | tf_op jit(solution)/shard_map/all_to_all | solution.py:357
  50.2 6.0 %collective-permute-start.4 = (f32[5,24,128]{2,1,0:T(8,128)S(1)}, f32[5,24,128]{2,1,0:T(8,128)S(1)}, u32[]{:S(2)}, u32[]{:S(2)}) collective-permute-start(f32[5,24,128]{2,1,0:T(8,128)S(1)} %get-tuple-element.21.here), channel_id=1, source_target_pairs={{0,1},{1,2},{2,3},{3,4},{4,5},{5,6},{6,7},{7,8},{8,9},{9,10},{10,1... | collective-permute-start | bytes 184328 | tf_op jit(solution)/shard_map/ppermute | solution.py:337
  56.4 1.1 %collective-permute-done.4.low.left = f32[5,24,128]{2,1,0:T(8,128)S(1)} collective-permute-done((f32[5,24,128]{2,1,0:T(8,128)S(1)}, f32[5,24,128]{2,1,0:T(8,128)S(1)}, u32[]{:S(2)}, u32[]{:S(2)}) %collective-permute-start.4) | collective-permute-done | bytes 61472 | tf_op jit(solution)/shard_map/ppermute | solution.py:337
  57.5 2.4 %collective-permute-done.5.high.right = f32[5,24,128]{2,1,0:T(8,128)S(1)} collective-permute-done((f32[5,24,128]{2,1,0:T(8,128)S(1)}, f32[5,24,128]{2,1,0:T(8,128)S(1)}, u32[]{:S(2)}, u32[]{:S(2)}) %collective-permute-start.5) | collective-permute-done | bytes 61472 | tf_op jit(solution)/shard_map/ppermute | solution.py:337
  59.9 3.2 %collective-permute-start.6 = (f32[12,24,128]{2,1,0:T(8,128)S(1)}, f32[12,24,128]{2,1,0:T(8,128)S(1)}, u32[]{:S(2)}, u32[]{:S(2)}) collective-permute-start(f32[12,24,128]{2,1,0:T(8,128)S(1)} %shard_map.45.here), channel_id=1, source_target_pairs={{0,3},{1,4},{2,5},{3,6},{4,7},{5,8},{6,9},{7,10},{8,11},{9,12},{10... | collective-permute-start | bytes 442376 | tf_op jit(solution)/shard_map/ppermute | solution.py:337
  63.1 8.3 %collective-permute-start.7 = (f32[12,24,128]{2,1,0:T(8,128)S(1)}, f32[12,24,128]{2,1,0:T(8,128)S(1)}, u32[]{:S(2)}, u32[]{:S(2)}) collective-permute-start(f32[12,24,128]{2,1,0:T(8,128)S(1)} %shard_map.45.here), channel_id=1, source_target_pairs={{0,29},{1,30},{2,31},{3,0},{4,1},{5,2},{6,3},{7,4},{8,5},{9,6},{10... | collective-permute-start | bytes 442376 | tf_op jit(solution)/shard_map/ppermute | solution.py:337
  71.5 2.2 %collective-permute-done.6.below = f32[12,24,128]{2,1,0:T(8,128)S(1)} collective-permute-done((f32[12,24,128]{2,1,0:T(8,128)S(1)}, f32[12,24,128]{2,1,0:T(8,128)S(1)}, u32[]{:S(2)}, u32[]{:S(2)}) %collective-permute-start.6) | collective-permute-done | bytes 147488 | tf_op jit(solution)/shard_map/ppermute | solution.py:337
  73.7 3.9 %collective-permute-done.7.above = f32[12,24,128]{2,1,0:T(8,128)S(1)} collective-permute-done((f32[12,24,128]{2,1,0:T(8,128)S(1)}, f32[12,24,128]{2,1,0:T(8,128)S(1)}, u32[]{:S(2)}, u32[]{:S(2)}) %collective-permute-start.7) | collective-permute-done | bytes 147488 | tf_op jit(solution)/shard_map/ppermute | solution.py:337
  77.7 1.5 %shard_map.46.v_here = f32[8,2,8,128]{3,2,1,0:T(8,128)S(1)} custom-call(f32[12,24,128]{2,1,0:T(8,128)S(1)} %collective-permute-done.6.below, f32[12,24,128]{2,1,0:T(8,128)S(1)} %shard_map.45.here, f32[12,24,128]{2,1,0:T(8,128)S(1)} %collective-permute-done.7.above, f32[5,24,128]{2,1,0:T(8,128)S(1)} %collective-permute-done.4.low.left, ...), custom_call_target="tpu_custom_call" | custom-call | tf_op jit(solution)/shard_map/pallas_call | solution.py:325
  80.0 1.3 %collective-permute-done.8.v_low = f32[8,2,8,128]{3,2,1,0:T(8,128)S(1)} collective-permute-done((f32[8,2,8,128]{3,2,1,0:T(8,128)S(1)}, f32[8,2,8,128]{3,2,1,0:T(8,128)S(1)}, u32[]{:S(2)}, u32[]{:S(2)}) %collective-permute-start.8) | collective-permute-done | bytes 65568 | tf_op jit(solution)/shard_map/ppermute | solution.py:337
  81.3 2.4 %collective-permute-done.9.v_high = f32[8,2,8,128]{3,2,1,0:T(8,128)S(1)} collective-permute-done((f32[8,2,8,128]{3,2,1,0:T(8,128)S(1)}, f32[8,2,8,128]{3,2,1,0:T(8,128)S(1)}, u32[]{:S(2)}, u32[]{:S(2)}) %collective-permute-start.9) | collective-permute-done | bytes 65568 | tf_op jit(solution)/shard_map/ppermute | solution.py:337
  83.6 2.2 %shard_map.47 = (f32[8,8,512]{2,1,0:T(8,128)}, f32[8,8,512]{2,1,0:T(8,128)}) custom-call(f32[8,2,8,128]{3,2,1,0:T(8,128)S(1)} %shard_map.46.v_here, f32[8,2,8,128]{3,2,1,0:T(8,128)S(1)} %collective-permute-done.8.v_low, f32[8,2,8,128]{3,2,1,0:T(8,128)S(1)} %collective-permute-done.9.v_high, f32[14,4,16,128]{3,2,1,0:T(8,128)S(1)} %get-tuple-element.29.u0, ...), custom_call_target="tpu_custom_call" | custom-call | tf_op jit(solution)/shard_map/pallas_call | solution.py:325
  (9 shorter events, 2.5 us)
Async XLA Ops:
  0.6 0.9 %copy-start = (f32[8,8,512]{2,1,0:T(8,128)S(1)}, f32[8,8,512]{2,1,0:T(8,128)}, u32[]{:S(2)}) copy-start(f32[8,8,512]{2,1,0:T(8,128)} %g_ref.1) | copy-start | bytes 393220
  1.5 0.9 %copy-start.1 = (f32[8,8,512]{2,1,0:T(8,128)S(1)}, f32[8,8,512]{2,1,0:T(8,128)}, u32[]{:S(2)}) copy-start(f32[8,8,512]{2,1,0:T(8,128)} %k_ref.1) | copy-start | bytes 393220
  3.3 10.2 %collective-permute-start = (f32[9,4,8,128]{3,2,1,0:T(8,128)S(1)}, f32[9,4,8,128]{3,2,1,0:T(8,128)S(1)}, u32[]{:S(2)}, u32[]{:S(2)}) collective-permute-start(f32[9,4,8,128]{3,2,1,0:T(8,128)S(1)} %get-tuple-element.18), channel_id=1, source_target_pairs={{0,32},{32,64},{64,96},{96,128},{128,160},{160,192},{192,224},{224... | collective-permute-start | bytes 442376 | tf_op jit(solution)/shard_map/ppermute | solution.py:337
  7.3 7.6 %collective-permute-start.1 = (f32[9,4,8,128]{3,2,1,0:T(8,128)S(1)}, f32[9,4,8,128]{3,2,1,0:T(8,128)S(1)}, u32[]{:S(2)}, u32[]{:S(2)}) collective-permute-start(f32[9,4,8,128]{3,2,1,0:T(8,128)S(1)} %get-tuple-element.19), channel_id=1, source_target_pairs={{0,480},{32,0},{64,32},{96,64},{128,96},{160,128},{192,160},{224,1... | collective-permute-start | bytes 442376 | tf_op jit(solution)/shard_map/ppermute | solution.py:337
  15.0 10.0 %collective-permute-start.2 = (f32[34,4,8,128]{3,2,1,0:T(8,128)S(1)}, f32[34,4,8,128]{3,2,1,0:T(8,128)S(1)}, u32[]{:S(2)}, u32[]{:S(2)}) collective-permute-start(f32[34,4,8,128]{3,2,1,0:T(8,128)S(1)} %shard_map.42.own), channel_id=1, source_target_pairs={{0,1},{1,2},{2,3},{3,4},{4,5},{5,6},{6,7},{7,8},{8,9},{9,10},{10,1... | collective-permute-start | bytes 1671176 | tf_op jit(solution)/shard_map/ppermute | solution.py:337
  18.5 9.3 %collective-permute-start.3 = (f32[34,4,8,128]{3,2,1,0:T(8,128)S(1)}, f32[34,4,8,128]{3,2,1,0:T(8,128)S(1)}, u32[]{:S(2)}, u32[]{:S(2)}) collective-permute-start(f32[34,4,8,128]{3,2,1,0:T(8,128)S(1)} %shard_map.42.own), channel_id=1, source_target_pairs={{0,31},{1,0},{2,1},{3,2},{4,3},{5,4},{6,5},{7,6},{8,7},{9,8},{10,9... | collective-permute-start | bytes 1671176 | tf_op jit(solution)/shard_map/ppermute | solution.py:337
  30.5 18.9 %all-to-all-start = ((f32[16,2,4,2,8,128]{5,4,3,2,1,0:T(8,128)}), f32[16,2,4,2,8,128]{5,4,3,2,1,0:T(8,128)S(1)}, u32[]{:S(2)}, u32[]{:S(2)}) async-start(f32[16,2,4,2,8,128]{5,4,3,2,1,0:T(8,128)} %get-tuple-element.20), calls=%async_computation | async-start | bytes 2097152 | tf_op jit(solution)/shard_map/all_to_all | solution.py:357
  50.2 7.3 %collective-permute-start.4 = (f32[5,24,128]{2,1,0:T(8,128)S(1)}, f32[5,24,128]{2,1,0:T(8,128)S(1)}, u32[]{:S(2)}, u32[]{:S(2)}) collective-permute-start(f32[5,24,128]{2,1,0:T(8,128)S(1)} %get-tuple-element.21.here), channel_id=1, source_target_pairs={{0,1},{1,2},{2,3},{3,4},{4,5},{5,6},{6,7},{7,8},{8,9},{9,10},{10,1... | collective-permute-start | bytes 184328 | tf_op jit(solution)/shard_map/ppermute | solution.py:337
  56.2 3.6 %collective-permute-start.5 = (f32[5,24,128]{2,1,0:T(8,128)S(1)}, f32[5,24,128]{2,1,0:T(8,128)S(1)}, u32[]{:S(2)}, u32[]{:S(2)}) collective-permute-start(f32[5,24,128]{2,1,0:T(8,128)S(1)} %get-tuple-element.22), channel_id=1, source_target_pairs={{0,31},{1,0},{2,1},{3,2},{4,3},{5,4},{6,5},{7,6},{8,7},{9,8},{10,9... | collective-permute-start | bytes 184328 | tf_op jit(solution)/shard_map/ppermute | solution.py:337
  59.9 13.8 %collective-permute-start.6 = (f32[12,24,128]{2,1,0:T(8,128)S(1)}, f32[12,24,128]{2,1,0:T(8,128)S(1)}, u32[]{:S(2)}, u32[]{:S(2)}) collective-permute-start(f32[12,24,128]{2,1,0:T(8,128)S(1)} %shard_map.45.here), channel_id=1, source_target_pairs={{0,3},{1,4},{2,5},{3,6},{4,7},{5,8},{6,9},{7,10},{8,11},{9,12},{10... | collective-permute-start | bytes 442376 | tf_op jit(solution)/shard_map/ppermute | solution.py:337
  63.1 14.5 %collective-permute-start.7 = (f32[12,24,128]{2,1,0:T(8,128)S(1)}, f32[12,24,128]{2,1,0:T(8,128)S(1)}, u32[]{:S(2)}, u32[]{:S(2)}) collective-permute-start(f32[12,24,128]{2,1,0:T(8,128)S(1)} %shard_map.45.here), channel_id=1, source_target_pairs={{0,29},{1,30},{2,31},{3,0},{4,1},{5,2},{6,3},{7,4},{8,5},{9,6},{10... | collective-permute-start | bytes 442376 | tf_op jit(solution)/shard_map/ppermute | solution.py:337
  79.2 2.1 %collective-permute-start.8 = (f32[8,2,8,128]{3,2,1,0:T(8,128)S(1)}, f32[8,2,8,128]{3,2,1,0:T(8,128)S(1)}, u32[]{:S(2)}, u32[]{:S(2)}) collective-permute-start(f32[8,2,8,128]{3,2,1,0:T(8,128)S(1)} %shard_map.46.v_here), channel_id=1, source_target_pairs={{0,1},{1,2},{2,3},{3,4},{4,5},{5,6},{6,7},{7,8},{8,9},{9,10},{10,1... | collective-permute-start | bytes 196616 | tf_op jit(solution)/shard_map/ppermute | solution.py:337
  80.0 3.7 %collective-permute-start.9 = (f32[8,2,8,128]{3,2,1,0:T(8,128)S(1)}, f32[8,2,8,128]{3,2,1,0:T(8,128)S(1)}, u32[]{:S(2)}, u32[]{:S(2)}) collective-permute-start(f32[8,2,8,128]{3,2,1,0:T(8,128)S(1)} %shard_map.46.v_here), channel_id=1, source_target_pairs={{0,31},{1,0},{2,1},{3,2},{4,3},{5,4},{6,5},{7,6},{8,7},{9,8},{10,9... | collective-permute-start | bytes 196616 | tf_op jit(solution)/shard_map/ppermute | solution.py:337

commit v3 on v2

--- a/solution.py
+++ b/solution.py
@@ -35,6 +35,27 @@
     flux_z = fz * (u - z_next(u))
     total = (flux_high - flux_low) + (flux_y - y_prev(flux_y)) + (flux_z - z_prev(flux_z))
     return ABSORPTION * u + total, flux_high
+
+
+class Slabs:
+    def __init__(self, flat, rows):
+        self.flat, self.rows = flat, rows
+
+    def at(self, i):
+        return pl.ds(pl.multiple_of(i * (4 * self.rows), 8), 4 * self.rows)
+
+    def __getitem__(self, i):
+        return self.flat[self.at(i), :].reshape(4, self.rows, LANES)
+
+    def __setitem__(self, i, value):
+        self.flat[self.at(i), :] = value.reshape(4 * self.rows, LANES)
+
+    def part(self, i, start, size):
+        return jnp.stack([self.flat[pl.ds((4 * i + r) * self.rows + start, size), :] for r in range(4)])
+
+    def put(self, i, start, value):
+        for r in range(4):
+            self.flat[pl.ds((4 * i + r) * self.rows + start, value.shape[1]), :] = value[r]
 
 
 def loop(count, body, carry, unroll):
@@ -96,38 +117,69 @@
     return (moved[0:count] + moved[count : 2 * count]) + moved[2 * count :]
 
 
-def permute_kernel(g_ref, k_ref, own, high, low, held, arrived):
-    copies = [pltpu.make_async_copy(ref, held.at[i], arrived.at[i]) for i, ref in enumerate((g_ref, k_ref))]
-    for copy in copies:
-        copy.start()
+def permute_kernel(me, held, own, to_first, to_second):
     matrix = permutation(False)
-    for copy in copies:
-        copy.wait()
     moved = rearrange(held[...].reshape(128, 512), matrix)
     for x in range(16):
         for r in range(4):
             own[x, r] = moved[8 * x : 8 * x + 8, LANES * r : LANES * r + LANES]
-    high[0:4] = own[4:8]
-    high[4:9] = own[11:16]
-    low[0:4] = own[0:4]
-    low[4:9] = own[8:13]
-
-
-def wide_kernel(own, left, right, out):
-    out[0:4] = left[0:4]
-    out[4:12] = own[0:8]
-    out[12:16] = right[0:4]
-    out[16:21] = left[4:9]
-    out[21:29] = own[8:16]
-    out[29:34] = right[4:9]
-
-
-def fine_kernel(own, left, right, piece, u_out, g_out, k_out, g, k, fx, fy, fz, w, uf, u0, res, s1, sc):
+    even = lax.rem(me[0], 2) == 0
+    for take, high, low in ((even, to_second, to_first), (jnp.logical_not(even), to_first, to_second)):
+        @pl.when(take)
+        def _(high=high, low=low):
+            high[0:4] = own[4:8]
+            high[4:9] = own[11:16]
+            low[0:4] = own[0:4]
+            low[4:9] = own[8:13]
+
+
+G_REACH = (3, 2, 2, 2, 1, 0)
+K_REACH = (4, 3, 3, 3, 2, 1, 0)
+
+
+def row_parts():
+    at = 0
+    for array, reaches, border in ((0, G_REACH, 4), (1, K_REACH, 5)):
+        for d, reach in enumerate(reaches, 1):
+            size = 4 * (8 + 2 * reach)
+            yield array, d, border - reach, size, at
+            at += size
+
+
+ROWS = sum(part[3] for part in row_parts())
+
+
+def wide_kernel(me, own, first, second, flat, to_high, to_low):
+    out = Slabs(flat, 8)
+
+    def put(at, source, start, size):
+        for i in range(size):
+            out[at + i] = source[start + i]
+
+    put(4, own, 0, 8)
+    put(21, own, 8, 8)
+    even = lax.rem(me[0], 2) == 0
+    for take, left, right in ((even, first, second), (jnp.logical_not(even), second, first)):
+        @pl.when(take)
+        def _(left=left, right=right):
+            put(0, left, 0, 4)
+            put(12, right, 0, 4)
+            put(16, left, 4, 5)
+            put(29, right, 4, 5)
+    for array, d, column, size, at in row_parts():
+        base = (16 * array + column) * 32
+        to_high[at : at + size] = flat[pl.ds(base + 8 - d, size, 8), :]
+        to_low[at : at + size] = flat[pl.ds(base + d - 1, size, 8), :]
+
+
+def fine_kernel(own, low, high, piece, u0, g_flat, k_flat, fx, fy, fz, w, uf, res, s1, sc):
+    flats = g_flat, k_flat
+    own, g, k = Slabs(own, 8), Slabs(g_flat, 24), Slabs(k_flat, 24)
     for i in range(34):
-        target = g.at[i] if i < 16 else k.at[i - 16]
-        target[:, 0:8] = left[i]
-        target[:, 8:16] = own[i]
-        target[:, 16:24] = right[i]
+        (g if i < 16 else k).put(i if i < 16 else i - 16, 8, own[i])
+    for array, d, column, size, at in row_parts():
+        flats[array][pl.ds(column * 96 + 8 - d, size, 24), :] = low[at : at + size]
+        flats[array][pl.ds(column * 96 + 15 + d, size, 24), :] = high[at : at + size]
     face_pass(16, k, fx, fy, fz, w, 1.0, 16)
 
     def first(i, carry):
@@ -166,9 +218,16 @@
         for to in range(piece.shape[0]):
             piece[to, 0, x] = first_sweep
             piece[to, 1, x] = here
-    u_out[...] = u0[:, :, 4:20, :]
-    g_out[...] = g[2:14, :, 4:20, :]
-    k_out[...] = k[2:16, :, 4:20, :]
+
+
+def prepare_kernel(u0, g_flat, k_flat, u_out, g_out, fx, fy, fz, w, k_rows):
+    g, k = Slabs(g_flat, 24), Slabs(k_flat, 24)
+    for i in range(14):
+        u_out[i] = u0[i, :, 4:20, :]
+        k_rows[i] = k.part(i + 2, 4, 16)
+    for i in range(12):
+        g_out[i] = g.part(i + 2, 4, 16)
+    face_pass(12, k_rows, fx, fy, fz, w, 1.0, 12)
 
 
 def middle_kernel(me, gathered, send_high, send_low, u_out, rhs_out, fx_out, fy_out, fz_out, w_out,
@@ -235,25 +294,37 @@
             send_low[4, 2 * x + r : 2 * x + r + 1, :] = uf[x, r, 3:4, :]
 
 
-def three_kernel(here, low, high, out):
-    out[0:4] = low[0:4]
-    out[4:8] = here[0:4]
-    out[8:12] = high[0:4]
+def spread(j, upward):
+    d = j if upward else 5 - j
+    start, size = (2, 16) if d < 4 else (6, 8)
+    return start, size, 32 * d if d < 4 else 128 + 16 * (d - 4)
+
+
+def three_kernel(here, low, high, to_high, to_low):
+    blocks = (low, here, high)
+    for j in range(6):
+        source = blocks[j // 2]
+        for out, upward in ((to_high, False), (to_low, True)):
+            start, size, at = spread(j, upward)
+            for array in range(2):
+                out[at + size * array : at + size * array + size] = source[2 * (j % 2) + array, start : start + size]
 
 
 def coarse_kernel(below, here, above, left, right, u_in, rhs, fx, fy, fz, w, v_out,
-                  u, cx, cy, cz, cw, cr, v, va):
+                  u, c, cx, cy, cz, cw, cr, v, va):
     half = 0.5 * 0.0625
-    blocks = (below, here, above)
-
-    def first(y):
-        return blocks[y // 6][2 * (y % 6)]
+    for j in range(6):
+        for source, upward, y in ((below, False, j), (above, True, 12 + j)):
+            start, size, at = spread(j, upward)
+            u[y, start : start + size] = source[at : at + size]
+            c[y, start : start + size] = source[at + size : at + 2 * size]
+        block = (left, here, right)[j // 2]
+        u[6 + j] = block[2 * (j % 2)]
+        c[6 + j] = block[2 * (j % 2) + 1]
 
     def coef(y):
-        return blocks[y // 6][2 * (y % 6) + 1]
-
-    for y in range(18):
-        u[y] = first(y)
+        return c[y]
+
     cy[0] = half * (coef(0) + coef(1))
     for y in range(1, 17):
         k = coef(y)
@@ -265,7 +336,7 @@
         )
         cx[y], cy[y], cz[y] = face_x, face_y, face_z
         cw[y] = DAMPING / diag
-        cr[y] = first(y) * diag * (1.0 / DAMPING)
+        cr[y] = u[y] * diag * (1.0 / DAMPING)
     for step in range(1, 8):
         now = u[step]
         low = cy[step - 1] * (u[step - 1] - now)
@@ -295,25 +366,33 @@
     sweep_pass(8, va, 0, 1, rhs, 1, fx, fy, fz, w, v_out, 0, 8)
 
 
-def last_kernel(v_here, v_low, v_high, u0, g, k, correction, residual, fx, fy, fz, w, wide, ua, ub, res):
+def last_kernel(v_here, v_low, v_high, u0, g, fx, fy, fz, w, correction, residual, wide, ua, ub, res, held, left):
     for x in range(8):
         for r in range(2):
             rows = jnp.concatenate([v_low[x, r, 4:6], v_here[x, r, 2:6], v_high[x, r, 2:4]], axis=0)
             wide[x, r, pl.ds(0, 8, 2), :] = rows
             wide[x, r, pl.ds(1, 8, 2), :] = rows
-    face_pass(12, k, fx, fy, fz, w, 1.0, 12)
     for i in range(14):
         fine = wide[(i + 1) // 2]
         ua[i] = u0[i] + jnp.stack([fine[0], fine[0], fine[1], fine[1]])
     sweep_pass(12, ua, 0, 0, g, 0, fx, fy, fz, w, ub, 0, 12)
     sweep_pass(10, ub, 0, 1, g, 1, fx, fy, fz, w, ua, 0, 10)
-    sweep_pass(8, ua, 0, 2, g, 2, fx, fy, fz, w, res, 0, 8, last=True)
     matrix = permutation(True)
-    for source, at, out in ((ua, 1, correction), (res, 0, residual)):
+
+    def leave(index, source, at, out):
         rows = [
             jnp.concatenate([source[at + x, r, 4:12, :] for r in range(4)], axis=1) for x in range(8)
         ]
-        out[...] = rearrange(jnp.concatenate(rows, axis=0), matrix).reshape(8, 8, 512)
+        held[index] = rearrange(jnp.concatenate(rows, axis=0), matrix).reshape(8, 8, 512)
+        copy = pltpu.make_async_copy(held.at[index], out, left.at[index])
+        copy.start()
+        return copy
+
+    first = leave(0, ua, 1, correction)
+    sweep_pass(8, ua, 0, 2, g, 2, fx, fy, fz, w, res, 0, 8, last=True)
+    second = leave(1, res, 0, residual)
+    first.wait()
+    second.wait()
 
 
 VMEM = pl.BlockSpec(memory_space=pltpu.VMEM)
@@ -321,12 +400,12 @@
 HBM = pl.BlockSpec(memory_space=pltpu.HBM)
 
 
-def call(kernel, outs, scratch, *arrays, scalars=0, far=0, extra=()):
+def call(kernel, outs, scratch, *arrays, scalars=0, to_hbm=False, extra=()):
     return pl.pallas_call(
         kernel,
         out_shape=[jax.ShapeDtypeStruct(shape, F32) for shape in outs],
-        in_specs=[SMEM] * scalars + [HBM] * far + [VMEM] * (len(arrays) - scalars - far),
-        out_specs=[VMEM] * len(outs),
+        in_specs=[SMEM] * scalars + [VMEM] * (len(arrays) - scalars),
+        out_specs=[HBM if to_hbm else VMEM] * len(outs),
         scratch_shapes=[pltpu.VMEM(shape, F32) for shape in scratch] + list(extra),
         compiler_params=pltpu.CompilerParams(vmem_limit_bytes=32 * 2**20),
     )(*arrays)
@@ -337,25 +416,32 @@
     return lax.ppermute(array, axis, [(i, (i + by) % count) for i in range(count)])
 
 
+def swap(array, axis, start):
+    count = lax.axis_size(axis)
+    pairs = [(i, (i + 1) % count) for i in range(start, count, 2)]
+    return lax.ppermute(array, axis, pairs + [(j, i) for i, j in pairs])
+
+
 def per_device(right_side, coefficient):
-    own, high, low = call(
-        permute_kernel, [(16, 4, 8, 128), (9, 4, 8, 128), (9, 4, 8, 128)], [(2, 8, 8, 512)], right_side, coefficient,
-        far=2, extra=[pltpu.SemaphoreType.DMA((2,))],
+    me = lax.axis_index("gx").astype(jnp.int32).reshape(1)
+    own, first, second = call(
+        permute_kernel, [(16, 4, 8, 128), (9, 4, 8, 128), (9, 4, 8, 128)], [], me, jnp.stack([right_side, coefficient]),
+        scalars=1,
     )
-    left, right = shift(high, "gx", 1), shift(low, "gx", -1)
-    (wide,) = call(wide_kernel, [(34, 4, 8, 128)], [], own, left, right)
-    left, right = shift(wide, "gy", 1), shift(wide, "gy", -1)
+    first, second = swap(first, "gx", 1), swap(second, "gx", 0)
+    wide, high, low = call(wide_kernel, [(34 * 32, 128), (ROWS, 128), (ROWS, 128)], [], me, own, first, second, scalars=1)
+    low, high = shift(high, "gy", 1), shift(low, "gy", -1)
     fine = (4, 24, 128)
     count = lax.axis_size("gx")
     piece, u0, g, k = call(
         fine_kernel,
-        [(count, 2, 4, 2, 8, 128), (14, 4, 16, 128), (12, 4, 16, 128), (14, 4, 16, 128)],
-        [(16, *fine), (18, *fine), (17, *fine), (16, *fine), (16, *fine), (16, *fine), (16, *fine), (14, *fine),
-         (8, *fine), (4, 2, 24, 128), (6, 2, 24, 128)],
-        wide, left, right,
+        [(count, 2, 4, 2, 8, 128), (14, *fine), (16 * 96, 128), (18 * 96, 128)],
+        [(17, *fine), (16, *fine), (16, *fine), (16, *fine), (16, *fine), (8, *fine), (4, 2, 24, 128), (6, 2, 24, 128)],
+        wide, low, high,
     )
+    piece, u0, g, k, me = lax.optimization_barrier((piece, u0, g, k, me))
     gathered = lax.all_to_all(piece, "gx", 0, 0)
-    me = lax.axis_index("gx").astype(jnp.int32).reshape(1)
+    gathered, u0, g, k, me = lax.optimization_barrier((gathered, u0, g, k, me))
     mid = (2, 8, 128)
     high, low, u1, rhs, fx, fy, fz, w = call(
         middle_kernel,
@@ -366,19 +452,22 @@
     )
     here = high
     low, high = shift(high, "gy", 1), shift(low, "gy", -1)
-    (three,) = call(three_kernel, [(12, 24, 128)], [], here, low, high)
-    below, above = shift(three, "gy", 3), shift(three, "gy", -3)
+    far_high, far_low = call(three_kernel, [(160, 128), (160, 128)], [], here, low, high)
+    below, above = shift(far_high, "gy", 3), shift(far_low, "gy", -3)
+    last = (4, 16, 128)
+    u0, g, *faces = call(
+        prepare_kernel, [(14, *last), (12, *last), (13, *last), (12, *last), (12, *last), (12, *last)], [(14, *last)], u0, g, k
+    )
     rows = (18, 24, 128)
     (v1,) = call(
-        coarse_kernel, [(8, *mid)], [rows, rows, rows, rows, rows, rows, (12, *mid), (10, *mid)],
-        below, three, above, low, high, u1, rhs, fx, fy, fz, w,
+        coarse_kernel, [(8, *mid)], [rows, rows, rows, rows, rows, rows, rows, (12, *mid), (10, *mid)],
+        below, here, above, low, high, u1, rhs, fx, fy, fz, w,
     )
     low, high = shift(v1, "gy", 1), shift(v1, "gy", -1)
-    last = (4, 16, 128)
     return tuple(call(
         last_kernel, [(8, 8, 512), (8, 8, 512)],
-        [(13, *last), (12, *last), (12, *last), (12, *last), (8, 2, 16, 128), (14, *last), (12, *last), (8, *last)],
-        v1, low, high, u0, g, k,
+        [(8, 2, 16, 128), (14, *last), (12, *last), (8, *last), (2, 8, 8, 512)],
+        v1, low, high, u0, g, *faces, to_hbm=True, extra=[pltpu.SemaphoreType.DMA((2,))],
     ))
 
 

time: 86.2 us -> 76.6 us (0.89)
  the two profiles are of different devices: /device:TPU:1 before, /device:TPU:8 now
where the time goes in v3:
time: 76.6 us; the launch traced here: 76.3 us
  starting transfers between devices  32.2 us (42%)
  waiting for transfers between devices  19.5 us (25%)
  blocking collectives  16.2 us (21%)
  Pallas kernels  6.68 us (9%)
  other arithmetic  0.99 us (1%)
    ppermute x8, starting transfers between devices, shift(): lax.ppermute(array, axis, [(i, (i + by) % count) for i in range(count)])  22.6 us
    all_to_all x1, blocking collectives, per_device(): gathered = lax.all_to_all(piece, 'gx', 0, 0)  16.2 us
    ppermute x8, waiting for transfers between devices, shift(): lax.ppermute(array, axis, [(i, (i + by) % count) for i in range(count)])  16.2 us
    ppermute x2, starting transfers between devices, swap(): return lax.ppermute(array, axis, pairs + [(j, i) for i, j in pairs])  9.65 us
    pallas_call x8, Pallas kernels, call(): pl.pallas_call(kernel, out_shape=[jax.ShapeDtypeStruct(shape, F32) for sh...  6.68 us
    ppermute x2, waiting for transfers between devices, swap(): return lax.ppermute(array, axis, pairs + [(j, i) for i, j in pairs])  3.36 us
  transfers between devices with their start and end apart: 10, of which 8 were waited for; matrix products, arithmetic and copies ran while one was open for 0% of the time, Pallas kernels for 0%

profile of v3, /device:TPU:8, one launch (start us, length us, event | category | flops | bytes accessed | tf_op | source)
XLA Modules:
  0.0 76.3 jit_solution(11582890304618419501)
XLA Ops:
  0.6 1.0 %pad_maximum_fusion.held = f32[2,8,8,512]{3,2,1,0:T(8,128)S(1)} fusion(f32[1,8,8,512]{3,2,1,0:T(8,128)} %bitcast.3, f32[1,8,8,512]{3,2,1,0:T(8,128)} %bitcast.4), kind=kLoop, calls=%fused_computation | loop fusion | flops 65536 | bytes 524288 | tf_op jit(solution)/shard_map/stack | solution.py:428
  1.6 0.4 shard_map.41
  2.0 3.5 %collective-permute-start = (f32[9,4,8,128]{3,2,1,0:T(8,128)S(1)}, f32[9,4,8,128]{3,2,1,0:T(8,128)S(1)}, u32[]{:S(2)}, u32[]{:S(2)}) collective-permute-start(f32[9,4,8,128]{3,2,1,0:T(8,128)S(1)} %get-tuple-element.39), channel_id=1, source_target_pairs={{32,64},{96,128},{160,192},{224,256},{288,320},{352,384},{416,448}... | collective-permute-start | bytes 442376 | tf_op jit(solution)/shard_map/ppermute | solution.py:422
  5.5 6.2 %collective-permute-start.1 = (f32[9,4,8,128]{3,2,1,0:T(8,128)S(1)}, f32[9,4,8,128]{3,2,1,0:T(8,128)S(1)}, u32[]{:S(2)}, u32[]{:S(2)}) collective-permute-start(f32[9,4,8,128]{3,2,1,0:T(8,128)S(1)} %get-tuple-element.40), channel_id=1, source_target_pairs={{0,32},{64,96},{128,160},{192,224},{256,288},{320,352},{384,416},{... | collective-permute-start | bytes 442376 | tf_op jit(solution)/shard_map/ppermute | solution.py:422
  11.7 3.4 %collective-permute-done.1.second = f32[9,4,8,128]{3,2,1,0:T(8,128)S(1)} collective-permute-done((f32[9,4,8,128]{3,2,1,0:T(8,128)S(1)}, f32[9,4,8,128]{3,2,1,0:T(8,128)S(1)}, u32[]{:S(2)}, u32[]{:S(2)}) %collective-permute-start.1) | collective-permute-done | bytes 147488 | tf_op jit(solution)/shard_map/ppermute | solution.py:422
  15.1 0.1 shard_map.42
  15.2 8.1 %collective-permute-start.3 = (f32[624,128]{1,0:T(8,128)S(1)}, f32[624,128]{1,0:T(8,128)S(1)}, u32[]{:S(2)}, u32[]{:S(2)}) collective-permute-start(f32[624,128]{1,0:T(8,128)S(1)} %get-tuple-element.43), channel_id=1, source_target_pairs={{0,31},{1,0},{2,1},{3,2},{4,3},{5,4},{6,5},{7,6},{8,7},{9,8},{10,9... | collective-permute-start | bytes 958472 | tf_op jit(solution)/shard_map/ppermute | solution.py:416
  23.3 4.6 %collective-permute-done.2.low = f32[624,128]{1,0:T(8,128)S(1)} collective-permute-done((f32[624,128]{1,0:T(8,128)S(1)}, f32[624,128]{1,0:T(8,128)S(1)}, u32[]{:S(2)}, u32[]{:S(2)}) %collective-permute-start.2) | collective-permute-done | bytes 319520 | tf_op jit(solution)/shard_map/ppermute | solution.py:416
  28.0 1.7 %shard_map.43 = (f32[16,2,4,2,8,128]{5,4,3,2,1,0:T(8,128)S(1)}, f32[14,4,24,128]{3,2,1,0:T(8,128)S(1)}, f32[1536,128]{1,0:T(8,128)S(1)}, f32[1728,128]{1,0:T(8,128)S(1)}) custom-call(f32[1088,128]{1,0:T(8,128)S(1)} %get-tuple-element.41.own, f32[624,128]{1,0:T(8,128)S(1)} %collective-permute-done.2.low, f32[624,128]{1,0:T(8,128)S(1)} %collective-permute-done.3.high), custom_call_target="tpu_custom_call" | custom-call | tf_op jit(solution)/shard_map/pallas_call | solution.py:404
  29.7 16.2 %all_to_all.5.gathered = f32[16,2,4,2,8,128]{5,4,3,2,1,0:T(8,128)S(1)} all-to-all(f32[16,2,4,2,8,128]{5,4,3,2,1,0:T(8,128)S(1)} %get-tuple-element.48), channel_id=1, replica_groups=mesh['gx'=16,'gy'=32] {'gx'}, dimensions={0} | all-to-all | bytes 2097152 | tf_op jit(solution)/shard_map/all_to_all | solution.py:443
  45.8 0.8 %shard_map.44 = (f32[5,24,128]{2,1,0:T(8,128)S(1)}, f32[5,24,128]{2,1,0:T(8,128)S(1)}, f32[12,2,8,128]{3,2,1,0:T(8,128)S(1)}, f32[10,2,8,128]{3,2,1,0:T(8,128)S(...) custom-call(s32[1]{0:T(128)} %bitcast.me, ...), custom_call_target="tpu_custom_call" | custom-call | tf_op jit(solution)/shard_map/pallas_call | solution.py:404
  46.7 5.8 %collective-permute-start.5 = (f32[5,24,128]{2,1,0:T(8,128)S(1)}, f32[5,24,128]{2,1,0:T(8,128)S(1)}, u32[]{:S(2)}, u32[]{:S(2)}) collective-permute-start(f32[5,24,128]{2,1,0:T(8,128)S(1)} %get-tuple-element.56), channel_id=1, source_target_pairs={{0,31},{1,0},{2,1},{3,2},{4,3},{5,4},{6,5},{7,6},{8,7},{9,8},{10,9... | collective-permute-start | bytes 184328 | tf_op jit(solution)/shard_map/ppermute | solution.py:416
  52.5 1.9 %collective-permute-done.5.high.right = f32[5,24,128]{2,1,0:T(8,128)S(1)} collective-permute-done((f32[5,24,128]{2,1,0:T(8,128)S(1)}, f32[5,24,128]{2,1,0:T(8,128)S(1)}, u32[]{:S(2)}, u32[]{:S(2)}) %collective-permute-start.5) | collective-permute-done | bytes 61472 | tf_op jit(solution)/shard_map/ppermute | solution.py:416
  54.3 3.0 %collective-permute-done.4.low.left = f32[5,24,128]{2,1,0:T(8,128)S(1)} collective-permute-done((f32[5,24,128]{2,1,0:T(8,128)S(1)}, f32[5,24,128]{2,1,0:T(8,128)S(1)}, u32[]{:S(2)}, u32[]{:S(2)}) %collective-permute-start.4) | collective-permute-done | bytes 61472 | tf_op jit(solution)/shard_map/ppermute | solution.py:416
  57.3 1.9 %collective-permute-start.6 = (f32[160,128]{1,0:T(8,128)S(1)}, f32[160,128]{1,0:T(8,128)S(1)}, u32[]{:S(2)}, u32[]{:S(2)}) collective-permute-start(f32[160,128]{1,0:T(8,128)S(1)} %get-tuple-element.57), channel_id=1, source_target_pairs={{0,3},{1,4},{2,5},{3,6},{4,7},{5,8},{6,9},{7,10},{8,11},{9,12},{10... | collective-permute-start | bytes 245768 | tf_op jit(solution)/shard_map/ppermute | solution.py:416
  59.3 5.8 %collective-permute-start.7 = (f32[160,128]{1,0:T(8,128)S(1)}, f32[160,128]{1,0:T(8,128)S(1)}, u32[]{:S(2)}, u32[]{:S(2)}) collective-permute-start(f32[160,128]{1,0:T(8,128)S(1)} %get-tuple-element.58), channel_id=1, source_target_pairs={{0,29},{1,30},{2,31},{3,0},{4,1},{5,2},{6,3},{7,4},{8,5},{9,6},{10... | collective-permute-start | bytes 245768 | tf_op jit(solution)/shard_map/ppermute | solution.py:416
  65.0 0.5 collective-permute-done.6.below
  65.5 1.5 %collective-permute-done.7.above = f32[160,128]{1,0:T(8,128)S(1)} collective-permute-done((f32[160,128]{1,0:T(8,128)S(1)}, f32[160,128]{1,0:T(8,128)S(1)}, u32[]{:S(2)}, u32[]{:S(2)}) %collective-permute-start.7) | collective-permute-done | bytes 81952 | tf_op jit(solution)/shard_map/ppermute | solution.py:416
  67.1 1.5 %shard_map.46.v_here = f32[8,2,8,128]{3,2,1,0:T(8,128)S(1)} custom-call(f32[160,128]{1,0:T(8,128)S(1)} %collective-permute-done.6.below, f32[5,24,128]{2,1,0:T(8,128)S(1)} %get-tuple-element.55.here, f32[160,128]{1,0:T(8,128)S(1)} %collective-permute-done.7.above, f32[5,24,128]{2,1,0:T(8,128)S(1)} %collective-permute-done.4.low.left, ...), custom_call_target="tpu_custom_call" | custom-call | tf_op jit(solution)/shard_map/pallas_call | solution.py:404
  68.5 1.1 %collective-permute-start.9 = (f32[8,2,8,128]{3,2,1,0:T(8,128)S(1)}, f32[8,2,8,128]{3,2,1,0:T(8,128)S(1)}, u32[]{:S(2)}, u32[]{:S(2)}) collective-permute-start(f32[8,2,8,128]{3,2,1,0:T(8,128)S(1)} %shard_map.46.v_here), channel_id=1, source_target_pairs={{0,31},{1,0},{2,1},{3,2},{4,3},{5,4},{6,5},{7,6},{8,7},{9,8},{10,9... | collective-permute-start | bytes 196616 | tf_op jit(solution)/shard_map/ppermute | solution.py:416
  69.6 0.3 shard_map.47
  69.9 1.6 %collective-permute-done.9.v_high = f32[8,2,8,128]{3,2,1,0:T(8,128)S(1)} collective-permute-done((f32[8,2,8,128]{3,2,1,0:T(8,128)S(1)}, f32[8,2,8,128]{3,2,1,0:T(8,128)S(1)}, u32[]{:S(2)}, u32[]{:S(2)}) %collective-permute-start.9) | collective-permute-done | bytes 65568 | tf_op jit(solution)/shard_map/ppermute | solution.py:416
  71.5 3.0 %collective-permute-done.8.v_low = f32[8,2,8,128]{3,2,1,0:T(8,128)S(1)} collective-permute-done((f32[8,2,8,128]{3,2,1,0:T(8,128)S(1)}, f32[8,2,8,128]{3,2,1,0:T(8,128)S(1)}, u32[]{:S(2)}, u32[]{:S(2)}) %collective-permute-start.8) | collective-permute-done | bytes 65568 | tf_op jit(solution)/shard_map/ppermute | solution.py:416
  74.5 1.8 %shard_map.48 = (f32[8,8,512]{2,1,0:T(8,128)}, f32[8,8,512]{2,1,0:T(8,128)}) custom-call(f32[8,2,8,128]{3,2,1,0:T(8,128)S(1)} %shard_map.46.v_here, f32[8,2,8,128]{3,2,1,0:T(8,128)S(1)} %collective-permute-done.8.v_low, f32[8,2,8,128]{3,2,1,0:T(8,128)S(1)} %collective-permute-done.9.v_high, f32[14,4,16,128]{3,2,1,0:T(8,128)S(1)} %get-tuple-element.68.u0, ...), custom_call_target="tpu_custom_call" | custom-call | tf_op jit(solution)/shard_map/pallas_call | solution.py:404
  (6 shorter events, 0.0 us)
Async XLA Ops:
  2.0 9.7 %collective-permute-start = (f32[9,4,8,128]{3,2,1,0:T(8,128)S(1)}, f32[9,4,8,128]{3,2,1,0:T(8,128)S(1)}, u32[]{:S(2)}, u32[]{:S(2)}) collective-permute-start(f32[9,4,8,128]{3,2,1,0:T(8,128)S(1)} %get-tuple-element.39), channel_id=1, source_target_pairs={{32,64},{96,128},{160,192},{224,256},{288,320},{352,384},{416,448}... | collective-permute-start | bytes 442376 | tf_op jit(solution)/shard_map/ppermute | solution.py:422
  5.5 9.5 %collective-permute-start.1 = (f32[9,4,8,128]{3,2,1,0:T(8,128)S(1)}, f32[9,4,8,128]{3,2,1,0:T(8,128)S(1)}, u32[]{:S(2)}, u32[]{:S(2)}) collective-permute-start(f32[9,4,8,128]{3,2,1,0:T(8,128)S(1)} %get-tuple-element.40), channel_id=1, source_target_pairs={{0,32},{64,96},{128,160},{192,224},{256,288},{320,352},{384,416},{... | collective-permute-start | bytes 442376 | tf_op jit(solution)/shard_map/ppermute | solution.py:422
  15.2 12.7 %collective-permute-start.2 = (f32[624,128]{1,0:T(8,128)S(1)}, f32[624,128]{1,0:T(8,128)S(1)}, u32[]{:S(2)}, u32[]{:S(2)}) collective-permute-start(f32[624,128]{1,0:T(8,128)S(1)} %get-tuple-element.42), channel_id=1, source_target_pairs={{0,1},{1,2},{2,3},{3,4},{4,5},{5,6},{6,7},{7,8},{8,9},{9,10},{10,1... | collective-permute-start | bytes 958472 | tf_op jit(solution)/shard_map/ppermute | solution.py:416
  15.2 12.7 %collective-permute-start.3 = (f32[624,128]{1,0:T(8,128)S(1)}, f32[624,128]{1,0:T(8,128)S(1)}, u32[]{:S(2)}, u32[]{:S(2)}) collective-permute-start(f32[624,128]{1,0:T(8,128)S(1)} %get-tuple-element.43), channel_id=1, source_target_pairs={{0,31},{1,0},{2,1},{3,2},{4,3},{5,4},{6,5},{7,6},{8,7},{9,8},{10,9... | collective-permute-start | bytes 958472 | tf_op jit(solution)/shard_map/ppermute | solution.py:416
  46.7 7.6 %collective-permute-start.5 = (f32[5,24,128]{2,1,0:T(8,128)S(1)}, f32[5,24,128]{2,1,0:T(8,128)S(1)}, u32[]{:S(2)}, u32[]{:S(2)}) collective-permute-start(f32[5,24,128]{2,1,0:T(8,128)S(1)} %get-tuple-element.56), channel_id=1, source_target_pairs={{0,31},{1,0},{2,1},{3,2},{4,3},{5,4},{6,5},{7,6},{8,7},{9,8},{10,9... | collective-permute-start | bytes 184328 | tf_op jit(solution)/shard_map/ppermute | solution.py:416
  52.5 4.9 %collective-permute-start.4 = (f32[5,24,128]{2,1,0:T(8,128)S(1)}, f32[5,24,128]{2,1,0:T(8,128)S(1)}, u32[]{:S(2)}, u32[]{:S(2)}) collective-permute-start(f32[5,24,128]{2,1,0:T(8,128)S(1)} %get-tuple-element.55.here), channel_id=1, source_target_pairs={{0,1},{1,2},{2,3},{3,4},{4,5},{5,6},{6,7},{7,8},{8,9},{9,10},{10,1... | collective-permute-start | bytes 184328 | tf_op jit(solution)/shard_map/ppermute | solution.py:416
  57.3 8.2 %collective-permute-start.6 = (f32[160,128]{1,0:T(8,128)S(1)}, f32[160,128]{1,0:T(8,128)S(1)}, u32[]{:S(2)}, u32[]{:S(2)}) collective-permute-start(f32[160,128]{1,0:T(8,128)S(1)} %get-tuple-element.57), channel_id=1, source_target_pairs={{0,3},{1,4},{2,5},{3,6},{4,7},{5,8},{6,9},{7,10},{8,11},{9,12},{10... | collective-permute-start | bytes 245768 | tf_op jit(solution)/shard_map/ppermute | solution.py:416
  59.3 7.8 %collective-permute-start.7 = (f32[160,128]{1,0:T(8,128)S(1)}, f32[160,128]{1,0:T(8,128)S(1)}, u32[]{:S(2)}, u32[]{:S(2)}) collective-permute-start(f32[160,128]{1,0:T(8,128)S(1)} %get-tuple-element.58), channel_id=1, source_target_pairs={{0,29},{1,30},{2,31},{3,0},{4,1},{5,2},{6,3},{7,4},{8,5},{9,6},{10... | collective-permute-start | bytes 245768 | tf_op jit(solution)/shard_map/ppermute | solution.py:416
  68.5 3.0 %collective-permute-start.9 = (f32[8,2,8,128]{3,2,1,0:T(8,128)S(1)}, f32[8,2,8,128]{3,2,1,0:T(8,128)S(1)}, u32[]{:S(2)}, u32[]{:S(2)}) collective-permute-start(f32[8,2,8,128]{3,2,1,0:T(8,128)S(1)} %shard_map.46.v_here), channel_id=1, source_target_pairs={{0,31},{1,0},{2,1},{3,2},{4,3},{5,4},{6,5},{7,6},{8,7},{9,8},{10,9... | collective-permute-start | bytes 196616 | tf_op jit(solution)/shard_map/ppermute | solution.py:416
  69.6 4.9 %collective-permute-start.8 = (f32[8,2,8,128]{3,2,1,0:T(8,128)S(1)}, f32[8,2,8,128]{3,2,1,0:T(8,128)S(1)}, u32[]{:S(2)}, u32[]{:S(2)}) collective-permute-start(f32[8,2,8,128]{3,2,1,0:T(8,128)S(1)} %shard_map.46.v_here), channel_id=1, source_target_pairs={{0,1},{1,2},{2,3},{3,4},{4,5},{5,6},{6,7},{7,8},{8,9},{9,10},{10,1... | collective-permute-start | bytes 196616 | tf_op jit(solution)/shard_map/ppermute | solution.py:416

commit v4 on v3

v4 whole, which is shorter than its diff:
```python
import jax
import jax.numpy as jnp
from jax import lax
from jax.experimental import pallas as pl
from jax.experimental.pallas import tpu as pltpu
from jax.sharding import PartitionSpec as P

ABSORPTION = 0.05
DAMPING = 0.8
F32 = jnp.float32
LANES = 128


def z_next(v):
    first = pltpu.roll(v[0], LANES - 1, 1)[None]
    return first if v.shape[0] == 1 else jnp.concatenate([v[1:], first], axis=0)


def z_prev(v):
    last = pltpu.roll(v[-1], 1, 1)[None]
    return last if v.shape[0] == 1 else jnp.concatenate([last, v[:-1]], axis=0)


def y_next(v):
    return pltpu.roll(v, v.shape[1] - 1, 1)


def y_prev(v):
    return pltpu.roll(v, 1, 1)


def flux_sum(u, u_next, flux_low, fx, fy, fz):
    flux_high = fx * (u - u_next)
    flux_y = fy * (u - y_next(u))
    flux_z = fz * (u - z_next(u))
    total = (flux_high - flux_low) + (flux_y - y_prev(flux_y)) + (flux_z - z_prev(flux_z))
    return ABSORPTION * u + total, flux_high


class Slabs:
    def __init__(self, flat, rows, parts=4):
        self.flat, self.rows, self.parts = flat, rows, parts

    def at(self, i):
        size = self.parts * self.rows
        return pl.ds(pl.multiple_of(i * size, 8), size)

    def __getitem__(self, i):
        return self.flat[self.at(i), :].reshape(self.parts, self.rows, LANES)

    def __setitem__(self, i, value):
        self.flat[self.at(i), :] = value.reshape(self.parts * self.rows, LANES)

    def part(self, i, start, size, step=1):
        where = lambda r: pl.ds((self.parts * i + r) * self.rows + start, size, step)
        return jnp.stack([self.flat[where(r), :] for r in range(self.parts)])

    def put(self, i, start, value):
        for r in range(self.parts):
            self.flat[pl.ds((self.parts * i + r) * self.rows + start, value.shape[1]), :] = value[r]


def loop(count, body, carry, unroll):
    return lax.fori_loop(0, count, body, carry, unroll=unroll)


def face_pass(count, k_ref, fx, fy, fz, w, scale, unroll, k_at=0):
    half = 0.5 * scale
    k0, k1 = k_ref[k_at], k_ref[k_at + 1]
    low = half * (k0 + k1)
    fx[0] = low

    def body(i, carry):
        k, low = carry
        k_next = k_ref[k_at + 2 + i]
        high = half * (k + k_next)
        face_y = half * (k + y_next(k))
        face_z = half * (k + z_next(k))
        diag = ABSORPTION + (high + low + face_y + y_prev(face_y) + face_z + z_prev(face_z))
        fx[i + 1] = high
        fy[i] = face_y
        fz[i] = face_z
        w[i] = DAMPING / diag
        return k_next, high

    loop(count, body, (k1, low), unroll)


def sweep_pass(count, u_ref, u_at, faces_at, g_ref, g_at, fx, fy, fz, w, out, out_at, unroll, last=False):
    u0, u1 = u_ref[u_at], u_ref[u_at + 1]
    low = fx[faces_at] * (u0 - u1)

    def body(i, carry):
        u, low = carry
        u_next = u_ref[u_at + 2 + i]
        f = faces_at + i
        applied, high = flux_sum(u, u_next, low, fx[f + 1], fy[f], fz[f])
        rest = g_ref[g_at + i] - applied
        out[out_at + i] = rest if last else u + w[f] * rest
        return u_next, high

    loop(count, body, (u1, low), unroll)


def permutation(inverse):
    z = lax.broadcasted_iota(jnp.int32, (512, 512), 1 if inverse else 0)
    at = lax.broadcasted_iota(jnp.int32, (512, 512), 0 if inverse else 1)
    return jnp.where(z == 4 * (at % LANES) + at // LANES, 1.0, 0.0).astype(jnp.bfloat16)


def rearrange(rows, matrix):
    count = rows.shape[0]
    top = rows.astype(jnp.bfloat16)
    rest = rows - top.astype(F32)
    middle = rest.astype(jnp.bfloat16)
    bottom = (rest - middle.astype(F32)).astype(jnp.bfloat16)
    parts = jnp.concatenate([top, middle, bottom], axis=0)
    moved = lax.dot_general(parts, matrix, (((1,), (0,)), ((), ())), preferred_element_type=F32)
    return (moved[0:count] + moved[count : 2 * count]) + moved[2 * count :]


def permute_kernel(me, held, own, to_first, to_second):
    matrix = permutation(False)
    moved = rearrange(held[...].reshape(128, 512), matrix)
    for x in range(16):
        for r in range(4):
            own[x, r] = moved[8 * x : 8 * x + 8, LANES * r : LANES * r + LANES]
    even = lax.rem(me[0], 2) == 0
    for take, high, low in ((even, to_second, to_first), (jnp.logical_not(even), to_first, to_second)):
        @pl.when(take)
        def _(high=high, low=low):
            high[0:6] = own[2:8]
            low[0:6] = own[0:6]
            high[6:14] = own[8:16]
            low[6:14] = own[8:16]


G_BORDER, K_BORDER = 6, 8
G_SLABS, K_SLABS = 8 + 2 * G_BORDER, 8 + 2 * K_BORDER
G_REACH = (5, 4, 3, 2, 1, 0)
K_REACH = (6, 6, 4, 4, 2, 1, 0)


def row_parts():
    at = 0
    for array, reaches, border in ((0, G_REACH, G_BORDER), (1, K_REACH, K_BORDER)):
        for d, reach in enumerate(reaches, 1):
            size = 4 * (8 + 2 * reach)
            yield array, d, border - reach, size, at
            at += size


ROWS = sum(part[3] for part in row_parts())


def wide_kernel(me, own, first, second, flat, to_high, to_low):
    out = Slabs(flat, 8)

    def put(at, source, start, size):
        for i in range(size):
            out[at + i] = source[start + i]

    put(6, own, 0, 8)
    put(28, own, 8, 8)
    even = lax.rem(me[0], 2) == 0
    for take, left, right in ((even, first, second), (jnp.logical_not(even), second, first)):
        @pl.when(take)
        def _(left=left, right=right):
            put(0, left, 0, 6)
            put(14, right, 0, 6)
            put(20, left, 6, 8)
            put(36, right, 6, 8)
    for array, d, column, size, at in row_parts():
        base = (G_SLABS * array + column) * 32
        to_high[at : at + size] = flat[pl.ds(base + 8 - d, size, 8), :]
        to_low[at : at + size] = flat[pl.ds(base + d - 1, size, 8), :]


def fine_kernel(me, own, low, high, piece, u0, g_flat, k_flat, u1, rhs, fx, fy, fz, w, uf, res, s1, sc,
                mx, my, mz, mw, mf, mr, ck):
    flats = g_flat, k_flat
    own, g, k = Slabs(own, 8), Slabs(g_flat, 24), Slabs(k_flat, 24)
    for i in range(G_SLABS):
        g.put(i, 8, own[i])
    for i in range(K_SLABS):
        k.put(i, 8, own[G_SLABS + i])
    for array, d, column, size, at in row_parts():
        flats[array][pl.ds(column * 96 + 8 - d, size, 24), :] = low[at : at + size]
        flats[array][pl.ds(column * 96 + 15 + d, size, 24), :] = high[at : at + size]
    face_pass(20, k, fx, fy, fz, w, 1.0, 20, k_at=1)

    def first(i, carry):
        uf[i] = w[i] * g[i]
        return carry

    loop(20, first, 0, 20)
    sweep_pass(18, uf, 0, 1, g, 1, fx, fy, fz, w, u0, 0, 18)
    sweep_pass(16, u0, 0, 2, g, 2, fx, fy, fz, w, res, 0, 16, last=True)
    for x in range(8):
        both = res[2 * x] + res[2 * x + 1]
        s1[x, 0] = both[0] + both[1]
        s1[x, 1] = both[2] + both[3]
    for x in range(10):
        both = k[2 + 2 * x] + k[3 + 2 * x]
        sc[x, 0] = both[0] + both[1]
        sc[x, 1] = both[2] + both[3]

    def rows(ref, x, start):
        return jnp.stack(
            [ref[x, r, pl.ds(start, 8, 2), :] + ref[x, r, pl.ds(start + 1, 8, 2), :] for r in range(2)]
        ) * 0.125

    half = 0.5 * 0.25
    k_mid = [rows(sc, x, 4) for x in range(10)]
    mx[0] = half * (k_mid[0] + k_mid[1])
    for x in range(8):
        here = k_mid[x + 1]
        face_x = half * (here + k_mid[x + 2])
        face_y = half * (here + rows(sc, x + 1, 6))
        face_z = half * (here + z_next(here))
        diag = ABSORPTION + (
            mx[x] + face_x + face_y + half * (here + rows(sc, x + 1, 2)) + face_z + z_prev(face_z)
        )
        mx[x + 1], my[x], mz[x] = face_x, face_y, face_z
        mw[x] = DAMPING / diag
        rhs[x] = rows(s1, x, 4)
        mf[x] = mw[x] * rhs[x]
    sweep_pass(6, mf, 0, 1, rhs, 1, mx, my, mz, mw, u1, 0, 6)
    sweep_pass(4, u1, 0, 2, rhs, 2, mx, my, mz, mw, mr, 0, 4, last=True)
    for x in range(4):
        both = k_mid[2 * x + 1] + k_mid[2 * x + 2]
        ck[x] = both[0] + both[1]
    k2 = [(ck[x, pl.ds(0, 4, 2), :] + ck[x, pl.ds(1, 4, 2), :]) * 0.125 for x in range(4)]
    half = 0.5 * 0.0625
    for x in range(2):
        here = k2[x + 1][1:3]
        face_z = half * (here + pltpu.roll(here, LANES - 1, 1))
        diag = ABSORPTION + (
            half * (here + k2[x][1:3]) + half * (here + k2[x + 2][1:3])
            + half * (here + k2[x + 1][0:2]) + half * (here + k2[x + 1][2:4])
            + face_z + pltpu.roll(face_z, 1, 1)
        )
        both = mr[2 * x] + mr[2 * x + 1]
        ck[x] = both[0] + both[1]
        first_sweep = DAMPING / diag * ((ck[x, pl.ds(2, 2, 2), :] + ck[x, pl.ds(3, 2, 2), :]) * 0.125)
        for to in range(piece.shape[0]):
            for j in range(2):
                piece[to, 2 * j + x : 2 * j + x + 1, :] = first_sweep[j : j + 1]
                piece[to, 4 + 2 * j + x : 5 + 2 * j + x, :] = here[j : j + 1]
    count = piece.shape[0]
    for to, column in ((lax.rem(me[0] + 1, count), 0), (lax.rem(me[0] + count - 1, count), 1)):
        for r in range(2):
            for x in range(3):
                at = 8 + 4 * (2 * x + r)
                piece[to, at : at + 4, :] = u1[column + x + 1, r, 2:6, :]
            piece[to, 32 + 4 * r : 36 + 4 * r, :] = rhs[column + 3, r, 2:6, :]


def prepare_middle_kernel(k_flat, fx, fy, fz, w, k_mid, sums):
    k = Slabs(k_flat, 24)
    for x in range(12):
        both = k[2 * x] + k[2 * x + 1]
        for r in range(2):
            sums[r] = both[2 * r] + both[2 * r + 1]
            k_mid[x, r] = (sums[r, pl.ds(4, 8, 2), :] + sums[r, pl.ds(5, 8, 2), :]) * 0.125
    face_pass(10, k_mid, fx, fy, fz, w, 0.25, 10)


def prepare_kernel(u0, g_flat, k_flat, u_out, g_out, fx, fy, fz, w, k_rows):
    g, k = Slabs(g_flat, 24), Slabs(k_flat, 24)
    for i in range(14):
        u_out[i] = u0[i + 2, :, 4:20, :]
        k_rows[i] = k.part(i + 5, 4, 16)
    for i in range(12):
        g_out[i] = g.part(i + 4, 4, 16)
    face_pass(12, k_rows, fx, fy, fz, w, 1.0, 12)


def middle_kernel(me, gathered, u1, rhs, send_high, send_low, u_flat, r_flat):
    count = gathered.shape[0]
    for block in range(11):
        source = lax.rem(me[0] + (block - 5 + count * 5), count)
        for j in range(2):
            for array in range(2):
                at = 4 * array + 2 * j
                pair = gathered[source, at : at + 2, :]
                for out in (send_high, send_low):
                    out[2 * j + array, 2 * block : 2 * block + 2, :] = pair
    u, g = Slabs(u_flat, 8, 2), Slabs(r_flat, 8, 2)
    for x in range(6):
        u[3 + x] = u1[x]
    for x in range(8):
        g[1 + x] = rhs[x]
    for source, column, edge in ((lax.rem(me[0] + count - 1, count), 0, 0), (lax.rem(me[0] + 1, count), 9, 9)):
        for r in range(2):
            for x in range(3):
                at = 8 + 4 * (2 * x + r)
                to = 8 * (2 * (column + x) + r) + 2
                u_flat[to : to + 4, :] = gathered[source, at : at + 4, :]
            to = 8 * (2 * edge + r) + 2
            r_flat[to : to + 4, :] = gathered[source, 32 + 4 * r : 36 + 4 * r, :]
    for out, row, rhs_row in ((send_high, 4, 5), (send_low, 2, 2)):
        out[4] = u_flat[pl.ds(row, 24, 8), :]
        out[5] = u_flat[pl.ds(row + 1, 24, 8), :]
        out[6, 0:20] = r_flat[pl.ds(rhs_row, 20, 8), :]


def spread(j, upward):
    d = j if upward else 5 - j
    start, size = (3, 16) if d < 4 else (7, 8)
    return start, size, 32 * d if d < 4 else 128 + 16 * (d - 4)


def three_kernel(me, here, low, high, to_first, to_second):
    blocks = (low, here, high)
    even = lax.rem(me[0], 2) == 0
    for take, to_high, to_low in ((even, to_second, to_first), (jnp.logical_not(even), to_first, to_second)):
        @pl.when(take)
        def _(to_high=to_high, to_low=to_low):
            for j in range(6):
                source = blocks[j // 2]
                for out, upward in ((to_high, False), (to_low, True)):
                    start, size, at = spread(j, upward)
                    for array in range(2):
                        out[at + size * array : at + size * array + size] = source[2 * (j % 2) + array, start : start + size]


def coarse_kernel(me, first, here, second, left, right, u_in, r_in, fx, fy, fz, w, v_out,
                  u, c, cx, cy, cz, cw, cr, v_flat, r_flat, va):
    half = 0.5 * 0.0625
    even = lax.rem(me[0], 2) == 0
    for take, below, above in ((even, first, second), (jnp.logical_not(even), second, first)):
        @pl.when(take)
        def _(below=below, above=above):
            for j in range(6):
                for source, upward, y in ((below, False, j), (above, True, 12 + j)):
                    start, size, at = spread(j, upward)
                    u[y, start : start + size] = source[at : at + size]
                    c[y, start : start + size] = source[at + size : at + 2 * size]
    for j in range(6):
        block = (left, here, right)[j // 2]
        u[6 + j] = block[2 * (j % 2)]
        c[6 + j] = block[2 * (j % 2) + 1]

    def coef(y):
        return c[y]

    cy[0] = half * (coef(0) + coef(1))
    for y in range(1, 17):
        k = coef(y)
        face_x = half * (k + pltpu.roll(k, 23, 0))
        face_z = half * (k + pltpu.roll(k, LANES - 1, 1))
        face_y = half * (k + coef(y + 1))
        diag = ABSORPTION + (
            face_x + pltpu.roll(face_x, 1, 0) + face_y + cy[y - 1] + face_z + pltpu.roll(face_z, 1, 1)
        )
        cx[y], cy[y], cz[y] = face_x, face_y, face_z
        cw[y] = DAMPING / diag
        cr[y] = u[y] * diag * (1.0 / DAMPING)
    for step in range(1, 8):
        now = u[step]
        low = cy[step - 1] * (u[step - 1] - now)
        for y in range(step, 18 - step):
            later = u[y + 1]
            high = cy[y] * (now - later)
            flux_x = cx[y] * (now - pltpu.roll(now, 23, 0))
            flux_z = cz[y] * (now - pltpu.roll(now, LANES - 1, 1))
            applied = ABSORPTION * now + (
                (high - low) + (flux_x - pltpu.roll(flux_x, 1, 0)) + (flux_z - pltpu.roll(flux_z, 1, 1))
            )
            u[y] = now + cw[y] * (cr[y] - applied)
            now, low = later, high
    v_flat[...] = u_in[...]
    r_flat[...] = r_in[...]
    for source, row, rhs_row in ((left, 0, 1), (right, 6, 6)):
        v_flat[pl.ds(row, 24, 8), :] = source[4]
        v_flat[pl.ds(row + 1, 24, 8), :] = source[5]
        r_flat[pl.ds(rhs_row, 20, 8), :] = source[6, 0:20]
    v, rhs = Slabs(v_flat, 8, 2), Slabs(r_flat, 8, 2)
    for x in range(6):
        rows = jnp.concatenate(
            [jnp.broadcast_to(u[7 + j, 8 + x : 9 + x, :], (2, LANES)) for j in range(4)], axis=0
        )
        for twin in range(2):
            v[2 * x + twin] = v[2 * x + twin] + rows[None]
    sweep_pass(10, v, 0, 0, rhs, 0, fx, fy, fz, w, va, 0, 10)
    sweep_pass(8, va, 0, 1, rhs, 1, fx, fy, fz, w, v_out, 0, 8)


def last_kernel(v_here, v_low, v_high, u0, g, fx, fy, fz, w, correction, residual, wide, ua, ub, res, held, left):
    for x in range(8):
        for r in range(2):
            rows = jnp.concatenate([v_low[x, r, 4:6], v_here[x, r, 2:6], v_high[x, r, 2:4]], axis=0)
            wide[x, r, pl.ds(0, 8, 2), :] = rows
            wide[x, r, pl.ds(1, 8, 2), :] = rows
    for i in range(14):
        fine = wide[(i + 1) // 2]
        ua[i] = u0[i] + jnp.stack([fine[0], fine[0], fine[1], fine[1]])
    sweep_pass(12, ua, 0, 0, g, 0, fx, fy, fz, w, ub, 0, 12)
    sweep_pass(10, ub, 0, 1, g, 1, fx, fy, fz, w, ua, 0, 10)
    matrix = permutation(True)

    def leave(index, source, at, out):
        rows = [
            jnp.concatenate([source[at + x, r, 4:12, :] for r in range(4)], axis=1) for x in range(8)
        ]
        held[index] = rearrange(jnp.concatenate(rows, axis=0), matrix).reshape(8, 8, 512)
        copy = pltpu.make_async_copy(held.at[index], out, left.at[index])
        copy.start()
        return copy

    first = leave(0, ua, 1, correction)
    sweep_pass(8, ua, 0, 2, g, 2, fx, fy, fz, w, res, 0, 8, last=True)
    second = leave(1, res, 0, residual)
    first.wait()
    second.wait()


VMEM = pl.BlockSpec(memory_space=pltpu.VMEM)
SMEM = pl.BlockSpec(memory_space=pltpu.SMEM)
HBM = pl.BlockSpec(memory_space=pltpu.HBM)


def call(kernel, outs, scratch, *arrays, scalars=0, to_hbm=False, extra=()):
    return pl.pallas_call(
        kernel,
        out_shape=[jax.ShapeDtypeStruct(shape, F32) for shape in outs],
        in_specs=[SMEM] * scalars + [VMEM] * (len(arrays) - scalars),
        out_specs=[HBM if to_hbm else VMEM] * len(outs),
        scratch_shapes=[pltpu.VMEM(shape, F32) for shape in scratch] + list(extra),
        compiler_params=pltpu.CompilerParams(vmem_limit_bytes=32 * 2**20),
    )(*arrays)


def shift(array, axis, by):
    count = lax.axis_size(axis)
    return lax.ppermute(array, axis, [(i, (i + by) % count) for i in range(count)])


def swap(array, axis, start, by=1):
    count = lax.axis_size(axis)
    pairs = [(i, (i + by) % count) for i in range(start, count, 2)]
    return lax.ppermute(array, axis, pairs + [(j, i) for i, j in pairs])


def per_device(right_side, coefficient):
    me_x = lax.axis_index("gx").astype(jnp.int32).reshape(1)
    me_y = lax.axis_index("gy").astype(jnp.int32).reshape(1)
    count = lax.axis_size("gx")
    border = (G_BORDER + K_BORDER, 4, 8, 128)
    own, first, second = call(
        permute_kernel, [(16, 4, 8, 128), border, border], [], me_x, jnp.stack([right_side, coefficient]), scalars=1
    )
    first, second = swap(first, "gx", 1), swap(second, "gx", 0)
    wide, high, low = call(
        wide_kernel, [((G_SLABS + K_SLABS) * 32, 128), (ROWS, 128), (ROWS, 128)], [], me_x, own, first, second, scalars=1
    )
    low, high = shift(high, "gy", 1), shift(low, "gy", -1)
    fine, mid, last = (4, 24, 128), (2, 8, 128), (4, 16, 128)
    piece, u0, g, k, u1, rhs = call(
        fine_kernel,
        [(count, 40, 128), (18, *fine), (G_SLABS * 96, 128), (K_SLABS * 96, 128), (6, *mid), (8, *mid)],
        [(21, *fine), (20, *fine), (20, *fine), (20, *fine), (20, *fine), (16, *fine), (8, 2, 24, 128), (10, 2, 24, 128),
         (9, *mid), (8, *mid), (8, *mid), (8, *mid), (8, *mid), (4, *mid), (4, 8, 128)],
        me_x, wide, low, high, scalars=1,
    )
    piece, u0, g, k, u1, rhs = lax.optimization_barrier((piece, u0, g, k, u1, rhs))
    gathered = lax.all_to_all(piece, "gx", 0, 0)
    gathered, u0, g, k, u1, rhs = lax.optimization_barrier((gathered, u0, g, k, u1, rhs))
    high, low, u1, rhs = call(
        middle_kernel, [(7, 24, 128), (7, 24, 128), (192, 128), (160, 128)], [], me_x, gathered, u1, rhs, scalars=1
    )
    here = high
    low, high = shift(high, "gy", 1), shift(low, "gy", -1)
    first, second = call(three_kernel, [(160, 128), (160, 128)], [], me_y, here, low, high, scalars=1)
    first, second = swap(first, "gy", 1, 3), swap(second, "gy", 0, 3)
    faces = call(
        prepare_middle_kernel, [(11, *mid), (10, *mid), (10, *mid), (10, *mid)], [(12, *mid), (2, 24, 128)], k
    )
    rows = (18, 24, 128)
    (v1,) = call(
        coarse_kernel, [(8, *mid)], [rows, rows, rows, rows, rows, rows, rows, (192, 128), (160, 128), (10, *mid)],
        me_y, first, here, second, low, high, u1, rhs, *faces, scalars=1,
    )
    u0, g, *faces = call(
        prepare_kernel, [(14, *last), (12, *last), (13, *last), (12, *last), (12, *last), (12, *last)], [(14, *last)], u0, g, k
    )
    low, high = shift(v1, "gy", 1), shift(v1, "gy", -1)
    return tuple(call(
        last_kernel, [(8, 8, 512), (8, 8, 512)],
        [(8, 2, 16, 128), (14, *last), (12, *last), (8, *last), (2, 8, 8, 512)],
        v1, low, high, u0, g, *faces, to_hbm=True, extra=[pltpu.SemaphoreType.DMA((2,))],
    ))


def solution(mesh):
    placed = (P("gx", "gy", None), P("gx", "gy", None))
    return jax.shard_map(per_device, mesh=mesh, in_specs=placed, out_specs=placed, check_vma=False)
```

time: 76.6 us -> 72.5 us (0.946)
  the two profiles are of different devices: /device:TPU:8 before, /device:TPU:1 now
where the time goes in v4:
time: 72.5 us; the launch traced here: 72.2 us
  starting transfers between devices  33.3 us (46%)
  waiting for transfers between devices  19.5 us (27%)
  blocking collectives  10.3 us (14%)
  Pallas kernels  7.51 us (10%)
  other arithmetic  0.99 us (1%)
  between operations  0.73 us (1%)
    ppermute x4, starting transfers between devices, swap(): return lax.ppermute(array, axis, pairs + [(j, i) for i, j in pairs])  23.2 us
    ppermute x6, waiting for transfers between devices, shift(): lax.ppermute(array, axis, [(i, (i + by) % count) for i in range(count)])  11.7 us
    all_to_all x1, blocking collectives, per_device(): gathered = lax.all_to_all(piece, 'gx', 0, 0)  10.3 us
    ppermute x6, starting transfers between devices, shift(): lax.ppermute(array, axis, [(i, (i + by) % count) for i in range(count)])  10.1 us
    ppermute x4, waiting for transfers between devices, swap(): return lax.ppermute(array, axis, pairs + [(j, i) for i, j in pairs])  7.79 us
    pallas_call x9, Pallas kernels, call(): pl.pallas_call(kernel, out_shape=[jax.ShapeDtypeStruct(shape, F32) for sh...  7.51 us
  transfers between devices with their start and end apart: 10, of which 9 were waited for; matrix products, arithmetic and copies ran while one was open for 0% of the time, Pallas kernels for 1%

profile of v4, /device:TPU:1, one launch (start us, length us, event | category | flops | bytes accessed | tf_op | source)
XLA Modules:
  0.0 72.2 jit_solution(1544165973541486211)
XLA Ops:
  0.6 1.0 %pad_maximum_fusion.held = f32[2,8,8,512]{3,2,1,0:T(8,128)S(1)} fusion(f32[1,8,8,512]{3,2,1,0:T(8,128)} %bitcast.4, f32[1,8,8,512]{3,2,1,0:T(8,128)} %bitcast.5), kind=kLoop, calls=%fused_computation | loop fusion | flops 65536 | bytes 524288 | tf_op jit(solution)/shard_map/stack | solution.py:452
  1.6 0.4 shard_map.41
  2.0 7.7 %collective-permute-start = (f32[14,4,8,128]{3,2,1,0:T(8,128)S(1)}, f32[14,4,8,128]{3,2,1,0:T(8,128)S(1)}, u32[]{:S(2)}, u32[]{:S(2)}) collective-permute-start(f32[14,4,8,128]{3,2,1,0:T(8,128)S(1)} %get-tuple-element.37), channel_id=1, source_target_pairs={{32,64},{96,128},{160,192},{224,256},{288,320},{352,384},{416,448}... | collective-permute-start | bytes 688136 | tf_op jit(solution)/shard_map/ppermute | solution.py:443
  9.7 1.9 %collective-permute-start.1 = (f32[14,4,8,128]{3,2,1,0:T(8,128)S(1)}, f32[14,4,8,128]{3,2,1,0:T(8,128)S(1)}, u32[]{:S(2)}, u32[]{:S(2)}) collective-permute-start(f32[14,4,8,128]{3,2,1,0:T(8,128)S(1)} %get-tuple-element.38), channel_id=1, source_target_pairs={{0,32},{64,96},{128,160},{192,224},{256,288},{320,352},{384,416},{... | collective-permute-start | bytes 688136 | tf_op jit(solution)/shard_map/ppermute | solution.py:443
  11.6 2.1 %collective-permute-done.first = f32[14,4,8,128]{3,2,1,0:T(8,128)S(1)} collective-permute-done((f32[14,4,8,128]{3,2,1,0:T(8,128)S(1)}, f32[14,4,8,128]{3,2,1,0:T(8,128)S(1)}, u32[]{:S(2)}, u32[]{:S(2)}) %collective-permute-start) | collective-permute-done | bytes 229408 | tf_op jit(solution)/shard_map/ppermute | solution.py:443
  13.8 3.8 %collective-permute-done.1.second = f32[14,4,8,128]{3,2,1,0:T(8,128)S(1)} collective-permute-done((f32[14,4,8,128]{3,2,1,0:T(8,128)S(1)}, f32[14,4,8,128]{3,2,1,0:T(8,128)S(1)}, u32[]{:S(2)}, u32[]{:S(2)}) %collective-permute-start.1) | collective-permute-done | bytes 229408 | tf_op jit(solution)/shard_map/ppermute | solution.py:443
  17.7 3.6 %collective-permute-start.2 = (f32[720,128]{1,0:T(8,128)S(1)}, f32[720,128]{1,0:T(8,128)S(1)}, u32[]{:S(2)}, u32[]{:S(2)}) collective-permute-start(f32[720,128]{1,0:T(8,128)S(1)} %get-tuple-element.40), channel_id=1, source_target_pairs={{0,1},{1,2},{2,3},{3,4},{4,5},{5,6},{6,7},{7,8},{8,9},{9,10},{10,1... | collective-permute-start | bytes 1105928 | tf_op jit(solution)/shard_map/ppermute | solution.py:437
  21.3 4.5 %collective-permute-done.2.low = f32[720,128]{1,0:T(8,128)S(1)} collective-permute-done((f32[720,128]{1,0:T(8,128)S(1)}, f32[720,128]{1,0:T(8,128)S(1)}, u32[]{:S(2)}, u32[]{:S(2)}) %collective-permute-start.2) | collective-permute-done | bytes 368672 | tf_op jit(solution)/shard_map/ppermute | solution.py:437
  25.8 2.8 %collective-permute-done.3.high = f32[720,128]{1,0:T(8,128)S(1)} collective-permute-done((f32[720,128]{1,0:T(8,128)S(1)}, f32[720,128]{1,0:T(8,128)S(1)}, u32[]{:S(2)}, u32[]{:S(2)}) %collective-permute-start.3) | collective-permute-done | bytes 368672 | tf_op jit(solution)/shard_map/ppermute | solution.py:437
  28.6 2.4 %shard_map.43 = (f32[16,40,128]{2,1,0:T(8,128)S(1)}, f32[18,4,24,128]{3,2,1,0:T(8,128)S(1)}, f32[1920,128]{1,0:T(8,128)S(1)}, f32[2304,128]{1,0:T(8,128)S(1)}, f...) custom-call(s32[1]{0:T(128)} %bitcast.1.me, f32[1408,128]{1,0:T(8,128)S(1)} %get-tuple-element.39.own, ...), custom_call_target="tpu_custom_call" | custom-call | tf_op jit(solution)/shard_map/pallas_call | solution.py:425
  31.0 10.3 %all_to_all.5.gathered = f32[16,40,128]{2,1,0:T(8,128)S(1)} all-to-all(f32[16,40,128]{2,1,0:T(8,128)S(1)} %get-tuple-element.42), channel_id=1, replica_groups=mesh['gx'=16,'gy'=32] {'gx'}, dimensions={0} | all-to-all | bytes 655360 | tf_op jit(solution)/shard_map/all_to_all | solution.py:468
  41.3 0.7 shard_map.44
  42.0 1.8 %collective-permute-start.4 = (f32[7,24,128]{2,1,0:T(8,128)S(1)}, f32[7,24,128]{2,1,0:T(8,128)S(1)}, u32[]{:S(2)}, u32[]{:S(2)}) collective-permute-start(f32[7,24,128]{2,1,0:T(8,128)S(1)} %get-tuple-element.51.here), channel_id=1, source_target_pairs={{0,1},{1,2},{2,3},{3,4},{4,5},{5,6},{6,7},{7,8},{8,9},{9,10},{10,1... | collective-permute-start | bytes 258056 | tf_op jit(solution)/shard_map/ppermute | solution.py:437
  43.7 4.2 %collective-permute-start.5 = (f32[7,24,128]{2,1,0:T(8,128)}, f32[7,24,128]{2,1,0:T(8,128)S(1)}, u32[]{:S(2)}, u32[]{:S(2)}) collective-permute-start(f32[7,24,128]{2,1,0:T(8,128)} %get-tuple-element.52), channel_id=1, source_target_pairs={{0,31},{1,0},{2,1},{3,2},{4,3},{5,4},{6,5},{7,6},{8,7},{9,8},{10,9... | collective-permute-start | bytes 258056 | tf_op jit(solution)/shard_map/ppermute | solution.py:437
  47.9 0.8 %collective-permute-done.4.low.left = f32[7,24,128]{2,1,0:T(8,128)S(1)} collective-permute-done((f32[7,24,128]{2,1,0:T(8,128)S(1)}, f32[7,24,128]{2,1,0:T(8,128)S(1)}, u32[]{:S(2)}, u32[]{:S(2)}) %collective-permute-start.4) | collective-permute-done | bytes 86048 | tf_op jit(solution)/shard_map/ppermute | solution.py:437
  48.7 0.4 collective-permute-done.5.high.right
  49.1 2.1 %collective-permute-start.6 = (f32[160,128]{1,0:T(8,128)S(1)}, f32[160,128]{1,0:T(8,128)S(1)}, u32[]{:S(2)}, u32[]{:S(2)}) collective-permute-start(f32[160,128]{1,0:T(8,128)S(1)} %get-tuple-element.53), channel_id=1, source_target_pairs={{1,4},{3,6},{5,8},{7,10},{9,12},{11,14},{13,16},{15,18},{17,20},{1... | collective-permute-start | bytes 245768 | tf_op jit(solution)/shard_map/ppermute | solution.py:443
  51.2 11.5 %collective-permute-start.7 = (f32[160,128]{1,0:T(8,128)S(1)}, f32[160,128]{1,0:T(8,128)S(1)}, u32[]{:S(2)}, u32[]{:S(2)}) collective-permute-start(f32[160,128]{1,0:T(8,128)S(1)} %get-tuple-element.54), channel_id=1, source_target_pairs={{0,3},{2,5},{4,7},{6,9},{8,11},{10,13},{12,15},{14,17},{16,19},{18... | collective-permute-start | bytes 245768 | tf_op jit(solution)/shard_map/ppermute | solution.py:443
  63.0 1.9 %collective-permute-done.7.second = f32[160,128]{1,0:T(8,128)S(1)} collective-permute-done((f32[160,128]{1,0:T(8,128)S(1)}, f32[160,128]{1,0:T(8,128)S(1)}, u32[]{:S(2)}, u32[]{:S(2)}) %collective-permute-start.7) | collective-permute-done | bytes 81952 | tf_op jit(solution)/shard_map/ppermute | solution.py:443
  64.8 1.4 %shard_map.47.v_here = f32[8,2,8,128]{3,2,1,0:T(8,128)S(1)} custom-call(s32[1]{0:T(128)} %bitcast.me, f32[160,128]{1,0:T(8,128)S(1)} %collective-permute-done.6.first, f32[7,24,128]{2,1,0:T(8,128)S(1)} %get-tuple-element.51.here, f32[160,128]{1,0:T(8,128)S(1)} %collective-permute-done.7.second, f32[7,24,128]{2,1,0:T(8,128)S(1)} %collective-permute-done.4.low.left, ...), custom_call_target="tpu_custom_call" | custom-call | tf_op jit(solution)/shard_map/pallas_call | solution.py:425
  66.4 0.4 collective-permute-start.9
  67.1 0.7 collective-permute-done.8.v_low
  67.7 2.7 %collective-permute-done.9.v_high = f32[8,2,8,128]{3,2,1,0:T(8,128)S(1)} collective-permute-done((f32[8,2,8,128]{3,2,1,0:T(8,128)S(1)}, f32[8,2,8,128]{3,2,1,0:T(8,128)S(1)}, u32[]{:S(2)}, u32[]{:S(2)}) %collective-permute-start.9) | collective-permute-done | bytes 65568 | tf_op jit(solution)/shard_map/ppermute | solution.py:437
  70.4 1.8 %shard_map.49 = (f32[8,8,512]{2,1,0:T(8,128)}, f32[8,8,512]{2,1,0:T(8,128)}) custom-call(f32[8,2,8,128]{3,2,1,0:T(8,128)S(1)} %shard_map.47.v_here, f32[8,2,8,128]{3,2,1,0:T(8,128)S(1)} %collective-permute-done.8.v_low, f32[8,2,8,128]{3,2,1,0:T(8,128)S(1)} %collective-permute-done.9.v_high, f32[14,4,16,128]{3,2,1,0:T(8,128)S(1)} %get-tuple-element.64.u0, ...), custom_call_target="tpu_custom_call" | custom-call | tf_op jit(solution)/shard_map/pallas_call | solution.py:425
  (7 shorter events, 0.8 us)
Async XLA Ops:
  2.0 11.7 %collective-permute-start = (f32[14,4,8,128]{3,2,1,0:T(8,128)S(1)}, f32[14,4,8,128]{3,2,1,0:T(8,128)S(1)}, u32[]{:S(2)}, u32[]{:S(2)}) collective-permute-start(f32[14,4,8,128]{3,2,1,0:T(8,128)S(1)} %get-tuple-element.37), channel_id=1, source_target_pairs={{32,64},{96,128},{160,192},{224,256},{288,320},{352,384},{416,448}... | collective-permute-start | bytes 688136 | tf_op jit(solution)/shard_map/ppermute | solution.py:443
  9.7 7.8 %collective-permute-start.1 = (f32[14,4,8,128]{3,2,1,0:T(8,128)S(1)}, f32[14,4,8,128]{3,2,1,0:T(8,128)S(1)}, u32[]{:S(2)}, u32[]{:S(2)}) collective-permute-start(f32[14,4,8,128]{3,2,1,0:T(8,128)S(1)} %get-tuple-element.38), channel_id=1, source_target_pairs={{0,32},{64,96},{128,160},{192,224},{256,288},{320,352},{384,416},{... | collective-permute-start | bytes 688136 | tf_op jit(solution)/shard_map/ppermute | solution.py:443
  17.7 8.1 %collective-permute-start.2 = (f32[720,128]{1,0:T(8,128)S(1)}, f32[720,128]{1,0:T(8,128)S(1)}, u32[]{:S(2)}, u32[]{:S(2)}) collective-permute-start(f32[720,128]{1,0:T(8,128)S(1)} %get-tuple-element.40), channel_id=1, source_target_pairs={{0,1},{1,2},{2,3},{3,4},{4,5},{5,6},{6,7},{7,8},{8,9},{9,10},{10,1... | collective-permute-start | bytes 1105928 | tf_op jit(solution)/shard_map/ppermute | solution.py:437
  21.3 7.2 %collective-permute-start.3 = (f32[720,128]{1,0:T(8,128)S(1)}, f32[720,128]{1,0:T(8,128)S(1)}, u32[]{:S(2)}, u32[]{:S(2)}) collective-permute-start(f32[720,128]{1,0:T(8,128)S(1)} %get-tuple-element.41), channel_id=1, source_target_pairs={{0,31},{1,0},{2,1},{3,2},{4,3},{5,4},{6,5},{7,6},{8,7},{9,8},{10,9... | collective-permute-start | bytes 1105928 | tf_op jit(solution)/shard_map/ppermute | solution.py:437
  42.0 6.7 %collective-permute-start.4 = (f32[7,24,128]{2,1,0:T(8,128)S(1)}, f32[7,24,128]{2,1,0:T(8,128)S(1)}, u32[]{:S(2)}, u32[]{:S(2)}) collective-permute-start(f32[7,24,128]{2,1,0:T(8,128)S(1)} %get-tuple-element.51.here), channel_id=1, source_target_pairs={{0,1},{1,2},{2,3},{3,4},{4,5},{5,6},{6,7},{7,8},{8,9},{9,10},{10,1... | collective-permute-start | bytes 258056 | tf_op jit(solution)/shard_map/ppermute | solution.py:437
  43.7 5.3 %collective-permute-start.5 = (f32[7,24,128]{2,1,0:T(8,128)}, f32[7,24,128]{2,1,0:T(8,128)S(1)}, u32[]{:S(2)}, u32[]{:S(2)}) collective-permute-start(f32[7,24,128]{2,1,0:T(8,128)} %get-tuple-element.52), channel_id=1, source_target_pairs={{0,31},{1,0},{2,1},{3,2},{4,3},{5,4},{6,5},{7,6},{8,7},{9,8},{10,9... | collective-permute-start | bytes 258056 | tf_op jit(solution)/shard_map/ppermute | solution.py:437
  49.1 13.9 %collective-permute-start.6 = (f32[160,128]{1,0:T(8,128)S(1)}, f32[160,128]{1,0:T(8,128)S(1)}, u32[]{:S(2)}, u32[]{:S(2)}) collective-permute-start(f32[160,128]{1,0:T(8,128)S(1)} %get-tuple-element.53), channel_id=1, source_target_pairs={{1,4},{3,6},{5,8},{7,10},{9,12},{11,14},{13,16},{15,18},{17,20},{1... | collective-permute-start | bytes 245768 | tf_op jit(solution)/shard_map/ppermute | solution.py:443
  51.2 13.6 %collective-permute-start.7 = (f32[160,128]{1,0:T(8,128)S(1)}, f32[160,128]{1,0:T(8,128)S(1)}, u32[]{:S(2)}, u32[]{:S(2)}) collective-permute-start(f32[160,128]{1,0:T(8,128)S(1)} %get-tuple-element.54), channel_id=1, source_target_pairs={{0,3},{2,5},{4,7},{6,9},{8,11},{10,13},{12,15},{14,17},{16,19},{18... | collective-permute-start | bytes 245768 | tf_op jit(solution)/shard_map/ppermute | solution.py:443
  66.3 1.5 %collective-permute-start.8 = (f32[8,2,8,128]{3,2,1,0:T(8,128)S(1)}, f32[8,2,8,128]{3,2,1,0:T(8,128)S(1)}, u32[]{:S(2)}, u32[]{:S(2)}) collective-permute-start(f32[8,2,8,128]{3,2,1,0:T(8,128)S(1)} %shard_map.47.v_here), channel_id=1, source_target_pairs={{0,1},{1,2},{2,3},{3,4},{4,5},{5,6},{6,7},{7,8},{8,9},{9,10},{10,1... | collective-permute-start | bytes 196616 | tf_op jit(solution)/shard_map/ppermute | solution.py:437
  66.4 4.0 %collective-permute-start.9 = (f32[8,2,8,128]{3,2,1,0:T(8,128)S(1)}, f32[8,2,8,128]{3,2,1,0:T(8,128)S(1)}, u32[]{:S(2)}, u32[]{:S(2)}) collective-permute-start(f32[8,2,8,128]{3,2,1,0:T(8,128)S(1)} %shard_map.47.v_here), channel_id=1, source_target_pairs={{0,31},{1,0},{2,1},{3,2},{4,3},{5,4},{6,5},{7,6},{8,7},{9,8},{10,9... | collective-permute-start | bytes 196616 | tf_op jit(solution)/shard_map/ppermute | solution.py:437

commit v5 on v4

--- a/solution.py
+++ b/solution.py
@@ -119,20 +119,23 @@
     return (moved[0:count] + moved[count : 2 * count]) + moved[2 * count :]
 
 
-def permute_kernel(me, held, own, to_first, to_second):
+def permute_kernel(me, held, own_flat, to_first, to_second):
     matrix = permutation(False)
     moved = rearrange(held[...].reshape(128, 512), matrix)
     for x in range(16):
         for r in range(4):
-            own[x, r] = moved[8 * x : 8 * x + 8, LANES * r : LANES * r + LANES]
+            own_flat[32 * x + 8 * r : 32 * x + 8 * r + 8] = moved[8 * x : 8 * x + 8, LANES * r : LANES * r + LANES]
+    own = Slabs(own_flat, 8)
     even = lax.rem(me[0], 2) == 0
     for take, high, low in ((even, to_second, to_first), (jnp.logical_not(even), to_first, to_second)):
         @pl.when(take)
         def _(high=high, low=low):
-            high[0:6] = own[2:8]
-            low[0:6] = own[0:6]
-            high[6:14] = own[8:16]
-            low[6:14] = own[8:16]
+            for i in range(6):
+                high[i] = own[2 + i]
+                low[i] = own[i]
+            for i in range(6, 14):
+                high[i] = own[2 + i]
+                low[i] = own[2 + i]
 
 
 G_BORDER, K_BORDER = 6, 8
@@ -142,19 +145,32 @@
 
 
 def row_parts():
-    at = 0
     for array, reaches, border in ((0, G_REACH, G_BORDER), (1, K_REACH, K_BORDER)):
         for d, reach in enumerate(reaches, 1):
-            size = 4 * (8 + 2 * reach)
-            yield array, d, border - reach, size, at
-            at += size
-
-
-ROWS = sum(part[3] for part in row_parts())
+            yield array, d, reach, border
+
+
+FACE_ROWS = 32 * (len(G_REACH) + len(K_REACH))
+CORNER_ROWS = 8 * (sum(G_REACH) + sum(K_REACH))
+
+
+def face_kernel(own, to_high, to_low):
+    for i, (array, d, _, _) in enumerate(row_parts()):
+        for out, y in ((to_high, 8 - d), (to_low, d - 1)):
+            out[32 * i : 32 * i + 32] = own[pl.ds(256 * array + y, 32, 8), :]
+
+
+def corners():
+    at = 0
+    for array, d, reach, border in row_parts():
+        for column in (border - reach, border + 8):
+            if reach:
+                yield array, d, column, 4 * reach, at
+                at += 4 * reach
 
 
 def wide_kernel(me, own, first, second, flat, to_high, to_low):
-    out = Slabs(flat, 8)
+    out, own = Slabs(flat, 8), Slabs(own, 8)
 
     def put(at, source, start, size):
         for i in range(size):
@@ -170,13 +186,13 @@
             put(14, right, 0, 6)
             put(20, left, 6, 8)
             put(36, right, 6, 8)
-    for array, d, column, size, at in row_parts():
+    for array, d, column, size, at in corners():
         base = (G_SLABS * array + column) * 32
         to_high[at : at + size] = flat[pl.ds(base + 8 - d, size, 8), :]
         to_low[at : at + size] = flat[pl.ds(base + d - 1, size, 8), :]
 
 
-def fine_kernel(me, own, low, high, piece, u0, g_flat, k_flat, u1, rhs, fx, fy, fz, w, uf, res, s1, sc,
+def fine_kernel(me, own, low, high, low_corners, high_corners, piece, u0, g_flat, k_flat, u1, rhs, fx, fy, fz, w, uf, res, s1, sc,
                 mx, my, mz, mw, mf, mr, ck):
     flats = g_flat, k_flat
     own, g, k = Slabs(own, 8), Slabs(g_flat, 24), Slabs(k_flat, 24)
@@ -184,9 +200,12 @@
         g.put(i, 8, own[i])
     for i in range(K_SLABS):
         k.put(i, 8, own[G_SLABS + i])
-    for array, d, column, size, at in row_parts():
-        flats[array][pl.ds(column * 96 + 8 - d, size, 24), :] = low[at : at + size]
-        flats[array][pl.ds(column * 96 + 15 + d, size, 24), :] = high[at : at + size]
+    for i, (array, d, _, border) in enumerate(row_parts()):
+        flats[array][pl.ds(border * 96 + 8 - d, 32, 24), :] = low[32 * i : 32 * i + 32]
+        flats[array][pl.ds(border * 96 + 15 + d, 32, 24), :] = high[32 * i : 32 * i + 32]
+    for array, d, column, size, at in corners():
+        flats[array][pl.ds(column * 96 + 8 - d, size, 24), :] = low_corners[at : at + size]
+        flats[array][pl.ds(column * 96 + 15 + d, size, 24), :] = high_corners[at : at + size]
     face_pass(20, k, fx, fy, fz, w, 1.0, 20, k_at=1)
 
     def first(i, carry):
@@ -243,10 +262,12 @@
         both = mr[2 * x] + mr[2 * x + 1]
         ck[x] = both[0] + both[1]
         first_sweep = DAMPING / diag * ((ck[x, pl.ds(2, 2, 2), :] + ck[x, pl.ds(3, 2, 2), :]) * 0.125)
-        for to in range(piece.shape[0]):
-            for j in range(2):
-                piece[to, 2 * j + x : 2 * j + x + 1, :] = first_sweep[j : j + 1]
-                piece[to, 4 + 2 * j + x : 5 + 2 * j + x, :] = here[j : j + 1]
+        for j in range(2):
+            ck[3, 2 * j + x : 2 * j + x + 1, :] = first_sweep[j : j + 1]
+            ck[3, 4 + 2 * j + x : 5 + 2 * j + x, :] = here[j : j + 1]
+    level_2 = ck[3]
+    for to in range(piece.shape[0]):
+        piece[to, 0:8, :] = level_2
     count = piece.shape[0]
     for to, column in ((lax.rem(me[0] + 1, count), 0), (lax.rem(me[0] + count - 1, count), 1)):
         for r in range(2):
@@ -276,16 +297,15 @@
     face_pass(12, k_rows, fx, fy, fz, w, 1.0, 12)
 
 
-def middle_kernel(me, gathered, u1, rhs, send_high, send_low, u_flat, r_flat):
+def middle_kernel(me, gathered, u1, rhs, send, level_1):
     count = gathered.shape[0]
     for block in range(11):
         source = lax.rem(me[0] + (block - 5 + count * 5), count)
         for j in range(2):
             for array in range(2):
                 at = 4 * array + 2 * j
-                pair = gathered[source, at : at + 2, :]
-                for out in (send_high, send_low):
-                    out[2 * j + array, 2 * block : 2 * block + 2, :] = pair
+                send[2 * j + array, 2 * block : 2 * block + 2, :] = gathered[source, at : at + 2, :]
+    u_flat, r_flat = level_1.at[0:192], level_1.at[192:352]
     u, g = Slabs(u_flat, 8, 2), Slabs(r_flat, 8, 2)
     for x in range(6):
         u[3 + x] = u1[x]
@@ -299,16 +319,18 @@
                 u_flat[to : to + 4, :] = gathered[source, at : at + 4, :]
             to = 8 * (2 * edge + r) + 2
             r_flat[to : to + 4, :] = gathered[source, 32 + 4 * r : 36 + 4 * r, :]
-    for out, row, rhs_row in ((send_high, 4, 5), (send_low, 2, 2)):
-        out[4] = u_flat[pl.ds(row, 24, 8), :]
-        out[5] = u_flat[pl.ds(row + 1, 24, 8), :]
-        out[6, 0:20] = r_flat[pl.ds(rhs_row, 20, 8), :]
+    for row in range(4):
+        send[4 + row] = u_flat[pl.ds(2 + row, 24, 8), :]
+    send[8, 0:20] = r_flat[pl.ds(2, 20, 8), :]
+    send[9, 0:20] = r_flat[pl.ds(5, 20, 8), :]
+
+
+SPREAD = (16, 14, 12, 10, 8, 6)
 
 
 def spread(j, upward):
     d = j if upward else 5 - j
-    start, size = (3, 16) if d < 4 else (7, 8)
-    return start, size, 32 * d if d < 4 else 128 + 16 * (d - 4)
+    return 3 + d, SPREAD[d], 2 * sum(SPREAD[:d])
 
 
 def three_kernel(me, here, low, high, to_first, to_second):
@@ -325,8 +347,8 @@
                         out[at + size * array : at + size * array + size] = source[2 * (j % 2) + array, start : start + size]
 
 
-def coarse_kernel(me, first, here, second, left, right, u_in, r_in, fx, fy, fz, w, v_out,
-                  u, c, cx, cy, cz, cw, cr, v_flat, r_flat, va):
+def coarse_kernel(me, first, here, second, left, right, level_1, fx, fy, fz, w, v_flat_out, to_high, to_low,
+                  u, c, start, cy, weights, v_flat, r_flat, va):
     half = 0.5 * 0.0625
     even = lax.rem(me[0], 2) == 0
     for take, below, above in ((even, first, second), (jnp.logical_not(even), second, first)):
@@ -334,48 +356,41 @@
         def _(below=below, above=above):
             for j in range(6):
                 for source, upward, y in ((below, False, j), (above, True, 12 + j)):
-                    start, size, at = spread(j, upward)
-                    u[y, start : start + size] = source[at : at + size]
-                    c[y, start : start + size] = source[at + size : at + 2 * size]
+                    column, size, at = spread(j, upward)
+                    start[y, column : column + size] = source[at : at + size]
+                    c[y, column : column + size] = source[at + size : at + 2 * size]
     for j in range(6):
         block = (left, here, right)[j // 2]
-        u[6 + j] = block[2 * (j % 2)]
+        start[6 + j] = block[2 * (j % 2)]
         c[6 + j] = block[2 * (j % 2) + 1]
-
-    def coef(y):
-        return c[y]
-
-    cy[0] = half * (coef(0) + coef(1))
+    cy[0] = half * (c[0] + c[1])
+    for y in range(18):
+        u[y] = start[y]
     for y in range(1, 17):
-        k = coef(y)
-        face_x = half * (k + pltpu.roll(k, 23, 0))
-        face_z = half * (k + pltpu.roll(k, LANES - 1, 1))
-        face_y = half * (k + coef(y + 1))
-        diag = ABSORPTION + (
-            face_x + pltpu.roll(face_x, 1, 0) + face_y + cy[y - 1] + face_z + pltpu.roll(face_z, 1, 1)
-        )
-        cx[y], cy[y], cz[y] = face_x, face_y, face_z
-        cw[y] = DAMPING / diag
-        cr[y] = u[y] * diag * (1.0 / DAMPING)
+        k = c[y]
+        right_x = half * (k + pltpu.roll(k, 23, 0))
+        right_z = half * (k + pltpu.roll(k, LANES - 1, 1))
+        right_y = half * (k + c[y + 1])
+        left_x, left_z, left_y = pltpu.roll(right_x, 1, 0), pltpu.roll(right_z, 1, 1), cy[y - 1]
+        cy[y] = right_y
+        scale = DAMPING / (ABSORPTION + (right_x + left_x + right_y + left_y + right_z + left_z))
+        for i, face in enumerate((right_x, left_x, right_y, left_y, right_z, left_z)):
+            weights[i, y] = scale * face
     for step in range(1, 8):
-        now = u[step]
-        low = cy[step - 1] * (u[step - 1] - now)
+        before, now = u[step - 1], u[step]
         for y in range(step, 18 - step):
             later = u[y + 1]
-            high = cy[y] * (now - later)
-            flux_x = cx[y] * (now - pltpu.roll(now, 23, 0))
-            flux_z = cz[y] * (now - pltpu.roll(now, LANES - 1, 1))
-            applied = ABSORPTION * now + (
-                (high - low) + (flux_x - pltpu.roll(flux_x, 1, 0)) + (flux_z - pltpu.roll(flux_z, 1, 1))
-            )
-            u[y] = now + cw[y] * (cr[y] - applied)
-            now, low = later, high
-    v_flat[...] = u_in[...]
-    r_flat[...] = r_in[...]
-    for source, row, rhs_row in ((left, 0, 1), (right, 6, 6)):
-        v_flat[pl.ds(row, 24, 8), :] = source[4]
-        v_flat[pl.ds(row + 1, 24, 8), :] = source[5]
-        r_flat[pl.ds(rhs_row, 20, 8), :] = source[6, 0:20]
+            along_x = weights[0, y] * pltpu.roll(now, 23, 0) + weights[1, y] * pltpu.roll(now, 1, 0)
+            along_y = weights[2, y] * later + weights[3, y] * before
+            along_z = weights[4, y] * pltpu.roll(now, LANES - 1, 1) + weights[5, y] * pltpu.roll(now, 1, 1)
+            u[y] = ((1.0 - DAMPING) * now + start[y]) + along_y + (along_x + along_z)
+            before, now = now, later
+    v_flat[...] = level_1[0:192]
+    r_flat[...] = level_1[192:352]
+    for source, row, slab, rhs_row, rhs_slab in ((left, 0, 6, 1, 9), (right, 6, 4, 6, 8)):
+        v_flat[pl.ds(row, 24, 8), :] = source[slab]
+        v_flat[pl.ds(row + 1, 24, 8), :] = source[slab + 1]
+        r_flat[pl.ds(rhs_row, 20, 8), :] = source[rhs_slab, 0:20]
     v, rhs = Slabs(v_flat, 8, 2), Slabs(r_flat, 8, 2)
     for x in range(6):
         rows = jnp.concatenate(
@@ -384,13 +399,20 @@
         for twin in range(2):
             v[2 * x + twin] = v[2 * x + twin] + rows[None]
     sweep_pass(10, v, 0, 0, rhs, 0, fx, fy, fz, w, va, 0, 10)
-    sweep_pass(8, va, 0, 1, rhs, 1, fx, fy, fz, w, v_out, 0, 8)
-
-
-def last_kernel(v_here, v_low, v_high, u0, g, fx, fy, fz, w, correction, residual, wide, ua, ub, res, held, left):
+    sweep_pass(8, va, 0, 1, rhs, 1, fx, fy, fz, w, Slabs(v_flat_out, 8, 2), 0, 8)
+    for out, row in ((to_high, 4), (to_low, 2)):
+        for i in range(2):
+            out[16 * i : 16 * i + 16] = v_flat_out[pl.ds(row + i, 16, 8), :]
+
+
+def last_kernel(v_here, v_low, v_high, u0, g, fx, fy, fz, w, correction, residual, v_flat, wide, ua, ub, res, held, left):
+    v_flat[...] = v_here[...]
+    for source, row in ((v_low, 0), (v_high, 6)):
+        for i in range(2):
+            v_flat[pl.ds(row + i, 16, 8), :] = source[16 * i : 16 * i + 16]
     for x in range(8):
         for r in range(2):
-            rows = jnp.concatenate([v_low[x, r, 4:6], v_here[x, r, 2:6], v_high[x, r, 2:4]], axis=0)
+            rows = v_flat[8 * (2 * x + r) : 8 * (2 * x + r) + 8]
             wide[x, r, pl.ds(0, 8, 2), :] = rows
             wide[x, r, pl.ds(1, 8, 2), :] = rows
     for i in range(14):
@@ -449,46 +471,49 @@
     count = lax.axis_size("gx")
     border = (G_BORDER + K_BORDER, 4, 8, 128)
     own, first, second = call(
-        permute_kernel, [(16, 4, 8, 128), border, border], [], me_x, jnp.stack([right_side, coefficient]), scalars=1
+        permute_kernel, [(512, 128), border, border], [], me_x, jnp.stack([right_side, coefficient]), scalars=1
     )
     first, second = swap(first, "gx", 1), swap(second, "gx", 0)
-    wide, high, low = call(
-        wide_kernel, [((G_SLABS + K_SLABS) * 32, 128), (ROWS, 128), (ROWS, 128)], [], me_x, own, first, second, scalars=1
-    )
+    high, low = call(face_kernel, [(FACE_ROWS, 128), (FACE_ROWS, 128)], [], own)
     low, high = shift(high, "gy", 1), shift(low, "gy", -1)
+    wide, high_corners, low_corners = call(
+        wide_kernel, [((G_SLABS + K_SLABS) * 32, 128), (CORNER_ROWS, 128), (CORNER_ROWS, 128)], [],
+        me_x, own, first, second, scalars=1,
+    )
+    low_corners, high_corners = shift(high_corners, "gy", 1), shift(low_corners, "gy", -1)
     fine, mid, last = (4, 24, 128), (2, 8, 128), (4, 16, 128)
     piece, u0, g, k, u1, rhs = call(
         fine_kernel,
         [(count, 40, 128), (18, *fine), (G_SLABS * 96, 128), (K_SLABS * 96, 128), (6, *mid), (8, *mid)],
         [(21, *fine), (20, *fine), (20, *fine), (20, *fine), (20, *fine), (16, *fine), (8, 2, 24, 128), (10, 2, 24, 128),
          (9, *mid), (8, *mid), (8, *mid), (8, *mid), (8, *mid), (4, *mid), (4, 8, 128)],
-        me_x, wide, low, high, scalars=1,
+        me_x, wide, low, high, low_corners, high_corners, scalars=1,
     )
     piece, u0, g, k, u1, rhs = lax.optimization_barrier((piece, u0, g, k, u1, rhs))
     gathered = lax.all_to_all(piece, "gx", 0, 0)
     gathered, u0, g, k, u1, rhs = lax.optimization_barrier((gathered, u0, g, k, u1, rhs))
-    high, low, u1, rhs = call(
-        middle_kernel, [(7, 24, 128), (7, 24, 128), (192, 128), (160, 128)], [], me_x, gathered, u1, rhs, scalars=1
-    )
-    here = high
-    low, high = shift(high, "gy", 1), shift(low, "gy", -1)
-    first, second = call(three_kernel, [(160, 128), (160, 128)], [], me_y, here, low, high, scalars=1)
+    here, level_1 = call(
+        middle_kernel, [(10, 24, 128), (352, 128)], [], me_x, gathered, u1, rhs, scalars=1
+    )
+    low, high = shift(here, "gy", 1), shift(here, "gy", -1)
+    first, second = call(three_kernel, [(136, 128), (136, 128)], [], me_y, here, low, high, scalars=1)
     first, second = swap(first, "gy", 1, 3), swap(second, "gy", 0, 3)
     faces = call(
         prepare_middle_kernel, [(11, *mid), (10, *mid), (10, *mid), (10, *mid)], [(12, *mid), (2, 24, 128)], k
     )
     rows = (18, 24, 128)
-    (v1,) = call(
-        coarse_kernel, [(8, *mid)], [rows, rows, rows, rows, rows, rows, rows, (192, 128), (160, 128), (10, *mid)],
-        me_y, first, here, second, low, high, u1, rhs, *faces, scalars=1,
+    v1, high_rows, low_rows = call(
+        coarse_kernel, [(128, 128), (32, 128), (32, 128)],
+        [rows, rows, rows, rows, (6, *rows), (192, 128), (160, 128), (10, *mid)],
+        me_y, first, here, second, low, high, level_1, *faces, scalars=1,
     )
     u0, g, *faces = call(
         prepare_kernel, [(14, *last), (12, *last), (13, *last), (12, *last), (12, *last), (12, *last)], [(14, *last)], u0, g, k
     )
-    low, high = shift(v1, "gy", 1), shift(v1, "gy", -1)
+    low, high = shift(high_rows, "gy", 1), shift(low_rows, "gy", -1)
     return tuple(call(
         last_kernel, [(8, 8, 512), (8, 8, 512)],
-        [(8, 2, 16, 128), (14, *last), (12, *last), (8, *last), (2, 8, 8, 512)],
+        [(128, 128), (8, 2, 16, 128), (14, *last), (12, *last), (8, *last), (2, 8, 8, 512)],
         v1, low, high, u0, g, *faces, to_hbm=True, extra=[pltpu.SemaphoreType.DMA((2,))],
     ))
 

time: 72.5 us -> 69.6 us (0.960)
  waiting for transfers between devices: 19.5 us -> 13.3 us
  starting transfers between devices: 33.3 us -> 36.6 us
    ppermute x6 -> x8, waiting for transfers between devices: 11.7 us -> 8.19 us  [shift(): lax.ppermute(array, axis, [(i, (i + by) % count) for i in range(count)])]
    ppermute x6 -> x8, starting transfers between devices: 10.1 us -> 13.1 us  [shift(): lax.ppermute(array, axis, [(i, (i + by) % count) for i in range(count)])]
    ppermute x4, waiting for transfers between devices: 7.79 us -> 5.11 us  [swap(): return lax.ppermute(array, axis, pairs + [(j, i) for i, j in pairs])]
    pallas_call x9 -> x10, Pallas kernels: 7.51 us -> 6.8 us  [call(): pl.pallas_call(kernel, out_shape=[jax.ShapeDtypeStruct(shape, F32) for sh...]
  transfers between devices with their start and end apart: 10 -> 12, of which waited for: 9 -> 8; matrix products, arithmetic and copies ran while one was open for 0% -> 0% of each run, Pallas kernels for 1% -> 1%
where the time goes in v5:
time: 69.6 us; the launch traced here: 69.4 us
  starting transfers between devices  36.6 us (53%)
  waiting for transfers between devices  13.3 us (19%)
  blocking collectives  10.3 us (15%)
  Pallas kernels  6.8 us (10%)
  other arithmetic  0.99 us (1%)
  between operations  0.75 us (1%)
    ppermute x4, starting transfers between devices, swap(): return lax.ppermute(array, axis, pairs + [(j, i) for i, j in pairs])  23.6 us
    ppermute x8, starting transfers between devices, shift(): lax.ppermute(array, axis, [(i, (i + by) % count) for i in range(count)])  13.1 us
    all_to_all x1, blocking collectives, per_device(): gathered = lax.all_to_all(piece, 'gx', 0, 0)  10.3 us
    ppermute x8, waiting for transfers between devices, shift(): lax.ppermute(array, axis, [(i, (i + by) % count) for i in range(count)])  8.19 us
    pallas_call x10, Pallas kernels, call(): pl.pallas_call(kernel, out_shape=[jax.ShapeDtypeStruct(shape, F32) for sh...  6.8 us
    ppermute x4, waiting for transfers between devices, swap(): return lax.ppermute(array, axis, pairs + [(j, i) for i, j in pairs])  5.11 us
  transfers between devices with their start and end apart: 12, of which 8 were waited for; matrix products, arithmetic and copies ran while one was open for 0% of the time, Pallas kernels for 1%

profile of v5, /device:TPU:1, one launch (start us, length us, event | category | flops | bytes accessed | tf_op | source)
XLA Modules:
  0.0 69.4 jit_solution(17931852071414880225)
XLA Ops:
  0.6 1.0 %pad_maximum_fusion.held = f32[2,8,8,512]{3,2,1,0:T(8,128)S(1)} fusion(f32[1,8,8,512]{3,2,1,0:T(8,128)} %bitcast.4, f32[1,8,8,512]{3,2,1,0:T(8,128)} %bitcast.5), kind=kLoop, calls=%fused_computation | loop fusion | flops 65536 | bytes 524288 | tf_op jit(solution)/shard_map/stack | solution.py:474
  1.6 0.4 shard_map.41
  2.0 7.7 %collective-permute-start = (f32[14,4,8,128]{3,2,1,0:T(8,128)S(1)}, f32[14,4,8,128]{3,2,1,0:T(8,128)S(1)}, u32[]{:S(2)}, u32[]{:S(2)}) collective-permute-start(f32[14,4,8,128]{3,2,1,0:T(8,128)S(1)} %get-tuple-element.40), channel_id=1, source_target_pairs={{32,64},{96,128},{160,192},{224,256},{288,320},{352,384},{416,448}... | collective-permute-start | bytes 688136 | tf_op jit(solution)/shard_map/ppermute | solution.py:465
  9.7 1.9 %collective-permute-start.1 = (f32[14,4,8,128]{3,2,1,0:T(8,128)S(1)}, f32[14,4,8,128]{3,2,1,0:T(8,128)S(1)}, u32[]{:S(2)}, u32[]{:S(2)}) collective-permute-start(f32[14,4,8,128]{3,2,1,0:T(8,128)S(1)} %get-tuple-element.41), channel_id=1, source_target_pairs={{0,32},{64,96},{128,160},{192,224},{256,288},{320,352},{384,416},{... | collective-permute-start | bytes 688136 | tf_op jit(solution)/shard_map/ppermute | solution.py:465
  11.7 2.5 %collective-permute-start.2 = (f32[416,128]{1,0:T(8,128)S(1)}, f32[416,128]{1,0:T(8,128)S(1)}, u32[]{:S(2)}, u32[]{:S(2)}) collective-permute-start(f32[416,128]{1,0:T(8,128)S(1)} %get-tuple-element.43), channel_id=1, source_target_pairs={{0,1},{1,2},{2,3},{3,4},{4,5},{5,6},{6,7},{7,8},{8,9},{9,10},{10,1... | collective-permute-start | bytes 638984 | tf_op jit(solution)/shard_map/ppermute | solution.py:459
  14.2 3.4 %collective-permute-done.1.second = f32[14,4,8,128]{3,2,1,0:T(8,128)S(1)} collective-permute-done((f32[14,4,8,128]{3,2,1,0:T(8,128)S(1)}, f32[14,4,8,128]{3,2,1,0:T(8,128)S(1)}, u32[]{:S(2)}, u32[]{:S(2)}) %collective-permute-start.1) | collective-permute-done | bytes 229408 | tf_op jit(solution)/shard_map/ppermute | solution.py:465
  17.7 3.6 %collective-permute-start.4 = (f32[304,128]{1,0:T(8,128)S(1)}, f32[304,128]{1,0:T(8,128)S(1)}, u32[]{:S(2)}, u32[]{:S(2)}) collective-permute-start(f32[304,128]{1,0:T(8,128)S(1)} %get-tuple-element.45), channel_id=1, source_target_pairs={{0,1},{1,2},{2,3},{3,4},{4,5},{5,6},{6,7},{7,8},{8,9},{9,10},{10,1... | collective-permute-start | bytes 466952 | tf_op jit(solution)/shard_map/ppermute | solution.py:459
  21.5 1.9 %collective-permute-done.4.low_corners = f32[304,128]{1,0:T(8,128)S(1)} collective-permute-done((f32[304,128]{1,0:T(8,128)S(1)}, f32[304,128]{1,0:T(8,128)S(1)}, u32[]{:S(2)}, u32[]{:S(2)}) %collective-permute-start.4) | collective-permute-done | bytes 155680 | tf_op jit(solution)/shard_map/ppermute | solution.py:459
  23.5 2.5 %collective-permute-done.5.high_corners = f32[304,128]{1,0:T(8,128)S(1)} collective-permute-done((f32[304,128]{1,0:T(8,128)S(1)}, f32[304,128]{1,0:T(8,128)S(1)}, u32[]{:S(2)}, u32[]{:S(2)}) %collective-permute-start.5) | collective-permute-done | bytes 155680 | tf_op jit(solution)/shard_map/ppermute | solution.py:459
  25.9 2.4 %shard_map.44 = (f32[16,40,128]{2,1,0:T(8,128)S(1)}, f32[18,4,24,128]{3,2,1,0:T(8,128)S(1)}, f32[1920,128]{1,0:T(8,128)S(1)}, f32[2304,128]{1,0:T(8,128)S(1)}, f...) custom-call(s32[1]{0:T(128)} %bitcast.1.me, f32[1408,128]{1,0:T(8,128)S(1)} %get-tuple-element.42.own, ...), custom_call_target="tpu_custom_call" | custom-call | tf_op jit(solution)/shard_map/pallas_call | solution.py:447
  28.4 10.3 %all_to_all.5.gathered = f32[16,40,128]{2,1,0:T(8,128)S(1)} all-to-all(f32[16,40,128]{2,1,0:T(8,128)S(1)} %get-tuple-element.47), channel_id=1, replica_groups=mesh['gx'=16,'gy'=32] {'gx'}, dimensions={0} | all-to-all | bytes 655360 | tf_op jit(solution)/shard_map/all_to_all | solution.py:493
  38.7 0.7 copy-done
  39.3 2.1 %collective-permute-start.6 = (f32[10,24,128]{2,1,0:T(8,128)S(1)}, f32[10,24,128]{2,1,0:T(8,128)S(1)}, u32[]{:S(2)}, u32[]{:S(2)}) collective-permute-start(f32[10,24,128]{2,1,0:T(8,128)S(1)} %get-tuple-element.56.here), channel_id=1, source_target_pairs={{0,1},{1,2},{2,3},{3,4},{4,5},{5,6},{6,7},{7,8},{8,9},{9,10},{10,1... | collective-permute-start | bytes 368648 | tf_op jit(solution)/shard_map/ppermute | solution.py:459
  41.4 4.2 %collective-permute-start.7 = (f32[10,24,128]{2,1,0:T(8,128)S(1)}, f32[10,24,128]{2,1,0:T(8,128)S(1)}, u32[]{:S(2)}, u32[]{:S(2)}) collective-permute-start(f32[10,24,128]{2,1,0:T(8,128)S(1)} %get-tuple-element.56.here), channel_id=1, source_target_pairs={{0,31},{1,0},{2,1},{3,2},{4,3},{5,4},{6,5},{7,6},{8,7},{9,8},{10,9... | collective-permute-start | bytes 368648 | tf_op jit(solution)/shard_map/ppermute | solution.py:459
  45.6 0.8 %collective-permute-done.6.low.left = f32[10,24,128]{2,1,0:T(8,128)S(1)} collective-permute-done((f32[10,24,128]{2,1,0:T(8,128)S(1)}, f32[10,24,128]{2,1,0:T(8,128)S(1)}, u32[]{:S(2)}, u32[]{:S(2)}) %collective-permute-start.6) | collective-permute-done | bytes 122912 | tf_op jit(solution)/shard_map/ppermute | solution.py:459
  46.6 2.4 %collective-permute-start.8 = (f32[136,128]{1,0:T(8,128)S(1)}, f32[136,128]{1,0:T(8,128)S(1)}, u32[]{:S(2)}, u32[]{:S(2)}) collective-permute-start(f32[136,128]{1,0:T(8,128)S(1)} %get-tuple-element.57), channel_id=1, source_target_pairs={{1,4},{3,6},{5,8},{7,10},{9,12},{11,14},{13,16},{15,18},{17,20},{1... | collective-permute-start | bytes 208904 | tf_op jit(solution)/shard_map/ppermute | solution.py:465
  49.0 11.5 %collective-permute-start.9 = (f32[136,128]{1,0:T(8,128)S(1)}, f32[136,128]{1,0:T(8,128)S(1)}, u32[]{:S(2)}, u32[]{:S(2)}) collective-permute-start(f32[136,128]{1,0:T(8,128)S(1)} %get-tuple-element.58), channel_id=1, source_target_pairs={{0,3},{2,5},{4,7},{6,9},{8,11},{10,13},{12,15},{14,17},{16,19},{18... | collective-permute-start | bytes 208904 | tf_op jit(solution)/shard_map/ppermute | solution.py:465
  60.8 1.7 %collective-permute-done.9.second = f32[136,128]{1,0:T(8,128)S(1)} collective-permute-done((f32[136,128]{1,0:T(8,128)S(1)}, f32[136,128]{1,0:T(8,128)S(1)}, u32[]{:S(2)}, u32[]{:S(2)}) %collective-permute-start.9) | collective-permute-done | bytes 69664 | tf_op jit(solution)/shard_map/ppermute | solution.py:465
  62.5 1.4 %shard_map.48 = (f32[128,128]{1,0:T(8,128)S(1)}, f32[32,128]{1,0:T(8,128)S(1)}, f32[32,128]{1,0:T(8,128)S(1)}) custom-call(s32[1]{0:T(128)} %bitcast.me, f32[136,128]{1,0:T(8,128)S(1)} %collective-permute-done.8.first, f32[10,24,128]{2,1,0:T(8,128)S(1)} %get-tuple-element.56.here, f32[136,128]{1,0:T(8,128)S(1)} %collective-permute-done.9.second, ...), custom_call_target="tpu_custom_call" | custom-call | tf_op jit(solution)/shard_map/pallas_call | solution.py:447
  64.1 0.4 collective-permute-start.11
  64.5 0.3 shard_map.49
  64.8 0.4 collective-permute-done.10.v_low
  65.2 2.4 %collective-permute-done.11.v_high = f32[32,128]{1,0:T(8,128)S(1)} collective-permute-done((f32[32,128]{1,0:T(8,128)S(1)}, f32[32,128]{1,0:T(8,128)S(1)}, u32[]{:S(2)}, u32[]{:S(2)}) %collective-permute-start.11) | collective-permute-done | bytes 16416 | tf_op jit(solution)/shard_map/ppermute | solution.py:459
  67.6 1.8 %shard_map.50 = (f32[8,8,512]{2,1,0:T(8,128)}, f32[8,8,512]{2,1,0:T(8,128)}) custom-call(f32[128,128]{1,0:T(8,128)S(1)} %get-tuple-element.65.v_here, f32[32,128]{1,0:T(8,128)S(1)} %collective-permute-done.10.v_low, f32[32,128]{1,0:T(8,128)S(1)} %collective-permute-done.11.v_high, f32[14,4,16,128]{3,2,1,0:T(8,128)S(1)} %get-tuple-element.70.u0, ...), custom_call_target="tpu_custom_call" | custom-call | tf_op jit(solution)/shard_map/pallas_call | solution.py:447
  (16 shorter events, 1.0 us)
Async XLA Ops:
  2.0 12.2 %collective-permute-start = (f32[14,4,8,128]{3,2,1,0:T(8,128)S(1)}, f32[14,4,8,128]{3,2,1,0:T(8,128)S(1)}, u32[]{:S(2)}, u32[]{:S(2)}) collective-permute-start(f32[14,4,8,128]{3,2,1,0:T(8,128)S(1)} %get-tuple-element.40), channel_id=1, source_target_pairs={{32,64},{96,128},{160,192},{224,256},{288,320},{352,384},{416,448}... | collective-permute-start | bytes 688136 | tf_op jit(solution)/shard_map/ppermute | solution.py:465
  9.7 7.9 %collective-permute-start.1 = (f32[14,4,8,128]{3,2,1,0:T(8,128)S(1)}, f32[14,4,8,128]{3,2,1,0:T(8,128)S(1)}, u32[]{:S(2)}, u32[]{:S(2)}) collective-permute-start(f32[14,4,8,128]{3,2,1,0:T(8,128)S(1)} %get-tuple-element.41), channel_id=1, source_target_pairs={{0,32},{64,96},{128,160},{192,224},{256,288},{320,352},{384,416},{... | collective-permute-start | bytes 688136 | tf_op jit(solution)/shard_map/ppermute | solution.py:465
  11.7 9.8 %collective-permute-start.2 = (f32[416,128]{1,0:T(8,128)S(1)}, f32[416,128]{1,0:T(8,128)S(1)}, u32[]{:S(2)}, u32[]{:S(2)}) collective-permute-start(f32[416,128]{1,0:T(8,128)S(1)} %get-tuple-element.43), channel_id=1, source_target_pairs={{0,1},{1,2},{2,3},{3,4},{4,5},{5,6},{6,7},{7,8},{8,9},{9,10},{10,1... | collective-permute-start | bytes 638984 | tf_op jit(solution)/shard_map/ppermute | solution.py:459
  14.2 7.3 %collective-permute-start.3 = (f32[416,128]{1,0:T(8,128)S(1)}, f32[416,128]{1,0:T(8,128)S(1)}, u32[]{:S(2)}, u32[]{:S(2)}) collective-permute-start(f32[416,128]{1,0:T(8,128)S(1)} %get-tuple-element.44), channel_id=1, source_target_pairs={{0,31},{1,0},{2,1},{3,2},{4,3},{5,4},{6,5},{7,6},{8,7},{9,8},{10,9... | collective-permute-start | bytes 638984 | tf_op jit(solution)/shard_map/ppermute | solution.py:459
  17.7 5.8 %collective-permute-start.4 = (f32[304,128]{1,0:T(8,128)S(1)}, f32[304,128]{1,0:T(8,128)S(1)}, u32[]{:S(2)}, u32[]{:S(2)}) collective-permute-start(f32[304,128]{1,0:T(8,128)S(1)} %get-tuple-element.45), channel_id=1, source_target_pairs={{0,1},{1,2},{2,3},{3,4},{4,5},{5,6},{6,7},{7,8},{8,9},{9,10},{10,1... | collective-permute-start | bytes 466952 | tf_op jit(solution)/shard_map/ppermute | solution.py:459
  21.3 4.7 %collective-permute-start.5 = (f32[304,128]{1,0:T(8,128)S(1)}, f32[304,128]{1,0:T(8,128)S(1)}, u32[]{:S(2)}, u32[]{:S(2)}) collective-permute-start(f32[304,128]{1,0:T(8,128)S(1)} %get-tuple-element.46), channel_id=1, source_target_pairs={{0,31},{1,0},{2,1},{3,2},{4,3},{5,4},{6,5},{7,6},{8,7},{9,8},{10,9... | collective-permute-start | bytes 466952 | tf_op jit(solution)/shard_map/ppermute | solution.py:459
  38.7 0.7 copy-start
  39.3 7.1 %collective-permute-start.6 = (f32[10,24,128]{2,1,0:T(8,128)S(1)}, f32[10,24,128]{2,1,0:T(8,128)S(1)}, u32[]{:S(2)}, u32[]{:S(2)}) collective-permute-start(f32[10,24,128]{2,1,0:T(8,128)S(1)} %get-tuple-element.56.here), channel_id=1, source_target_pairs={{0,1},{1,2},{2,3},{3,4},{4,5},{5,6},{6,7},{7,8},{8,9},{9,10},{10,1... | collective-permute-start | bytes 368648 | tf_op jit(solution)/shard_map/ppermute | solution.py:459
  41.4 5.1 %collective-permute-start.7 = (f32[10,24,128]{2,1,0:T(8,128)S(1)}, f32[10,24,128]{2,1,0:T(8,128)S(1)}, u32[]{:S(2)}, u32[]{:S(2)}) collective-permute-start(f32[10,24,128]{2,1,0:T(8,128)S(1)} %get-tuple-element.56.here), channel_id=1, source_target_pairs={{0,31},{1,0},{2,1},{3,2},{4,3},{5,4},{6,5},{7,6},{8,7},{9,8},{10,9... | collective-permute-start | bytes 368648 | tf_op jit(solution)/shard_map/ppermute | solution.py:459
  45.6 17.0 %copy-start.1 = (f32[352,128]{1,0:T(8,128)S(1)}, f32[352,128]{1,0:T(8,128)}, u32[]{:S(2)}) copy-start(f32[352,128]{1,0:T(8,128)} %copy-done) | copy-start | bytes 540676
  46.6 14.2 %collective-permute-start.8 = (f32[136,128]{1,0:T(8,128)S(1)}, f32[136,128]{1,0:T(8,128)S(1)}, u32[]{:S(2)}, u32[]{:S(2)}) collective-permute-start(f32[136,128]{1,0:T(8,128)S(1)} %get-tuple-element.57), channel_id=1, source_target_pairs={{1,4},{3,6},{5,8},{7,10},{9,12},{11,14},{13,16},{15,18},{17,20},{1... | collective-permute-start | bytes 208904 | tf_op jit(solution)/shard_map/ppermute | solution.py:465
  49.0 13.5 %collective-permute-start.9 = (f32[136,128]{1,0:T(8,128)S(1)}, f32[136,128]{1,0:T(8,128)S(1)}, u32[]{:S(2)}, u32[]{:S(2)}) collective-permute-start(f32[136,128]{1,0:T(8,128)S(1)} %get-tuple-element.58), channel_id=1, source_target_pairs={{0,3},{2,5},{4,7},{6,9},{8,11},{10,13},{12,15},{14,17},{16,19},{18... | collective-permute-start | bytes 208904 | tf_op jit(solution)/shard_map/ppermute | solution.py:465
  64.0 1.2 %collective-permute-start.10 = (f32[32,128]{1,0:T(8,128)S(1)}, f32[32,128]{1,0:T(8,128)S(1)}, u32[]{:S(2)}, u32[]{:S(2)}) collective-permute-start(f32[32,128]{1,0:T(8,128)S(1)} %get-tuple-element.66), channel_id=1, source_target_pairs={{0,1},{1,2},{2,3},{3,4},{4,5},{5,6},{6,7},{7,8},{8,9},{9,10},{10,1... | collective-permute-start | bytes 49160 | tf_op jit(solution)/shard_map/ppermute | solution.py:459
  64.1 3.5 %collective-permute-start.11 = (f32[32,128]{1,0:T(8,128)S(1)}, f32[32,128]{1,0:T(8,128)S(1)}, u32[]{:S(2)}, u32[]{:S(2)}) collective-permute-start(f32[32,128]{1,0:T(8,128)S(1)} %get-tuple-element.67), channel_id=1, source_target_pairs={{0,31},{1,0},{2,1},{3,2},{4,3},{5,4},{6,5},{7,6},{8,7},{9,8},{10,9... | collective-permute-start | bytes 49160 | tf_op jit(solution)/shard_map/ppermute | solution.py:459

commit v6 on v5

--- a/solution.py
+++ b/solution.py
@@ -43,7 +43,7 @@
 
     def at(self, i):
         size = self.parts * self.rows
-        return pl.ds(pl.multiple_of(i * size, 8), size)
+        return pl.ds(i * size, size)
 
     def __getitem__(self, i):
         return self.flat[self.at(i), :].reshape(self.parts, self.rows, LANES)
@@ -60,46 +60,58 @@
             self.flat[pl.ds((self.parts * i + r) * self.rows + start, value.shape[1]), :] = value[r]
 
 
-def loop(count, body, carry, unroll):
-    return lax.fori_loop(0, count, body, carry, unroll=unroll)
-
-
-def face_pass(count, k_ref, fx, fy, fz, w, scale, unroll, k_at=0):
+class Parted:
+    def __init__(self, inner, outer, start, stop):
+        self.inner, self.outer, self.start, self.stop = inner, outer, start, stop
+
+    def place(self, i):
+        if self.start <= i < self.stop:
+            return self.inner, i - self.start
+        return self.outer, i if i < self.start else i - (self.stop - self.start)
+
+    def __getitem__(self, i):
+        buffer, at = self.place(i)
+        return buffer[at]
+
+    def __setitem__(self, i, value):
+        buffer, at = self.place(i)
+        buffer[at] = value
+
+    def part(self, i, start, size):
+        buffer, at = self.place(i)
+        if isinstance(buffer, (Parted, Slabs)):
+            return buffer.part(at, start, size)
+        return buffer[at, :, start : start + size, :]
+
+
+def face_pass(count, k_ref, fx, fy, fz, w, scale, k_at=0, done=()):
     half = 0.5 * scale
-    k0, k1 = k_ref[k_at], k_ref[k_at + 1]
-    low = half * (k0 + k1)
-    fx[0] = low
-
-    def body(i, carry):
-        k, low = carry
-        k_next = k_ref[k_at + 2 + i]
-        high = half * (k + k_next)
+    for i in range(count + 1):
+        if i not in done or i - 1 not in done:
+            fx[i] = half * (k_ref[k_at + i] + k_ref[k_at + 1 + i])
+        if i == 0 or i - 1 in done:
+            continue
+        k = k_ref[k_at + i]
         face_y = half * (k + y_next(k))
         face_z = half * (k + z_next(k))
-        diag = ABSORPTION + (high + low + face_y + y_prev(face_y) + face_z + z_prev(face_z))
-        fx[i + 1] = high
-        fy[i] = face_y
-        fz[i] = face_z
-        w[i] = DAMPING / diag
-        return k_next, high
-
-    loop(count, body, (k1, low), unroll)
-
-
-def sweep_pass(count, u_ref, u_at, faces_at, g_ref, g_at, fx, fy, fz, w, out, out_at, unroll, last=False):
-    u0, u1 = u_ref[u_at], u_ref[u_at + 1]
-    low = fx[faces_at] * (u0 - u1)
-
-    def body(i, carry):
-        u, low = carry
-        u_next = u_ref[u_at + 2 + i]
-        f = faces_at + i
-        applied, high = flux_sum(u, u_next, low, fx[f + 1], fy[f], fz[f])
+        diag = ABSORPTION + (fx[i] + fx[i - 1] + face_y + y_prev(face_y) + face_z + z_prev(face_z))
+        fy[i - 1] = face_y
+        fz[i - 1] = face_z
+        w[i - 1] = DAMPING / diag
+
+
+def sweep_pass(count, u_ref, u_at, faces_at, g_ref, g_at, fx, fy, fz, w, out, out_at, last=False, done=()):
+    low = None
+    for i in range(count):
+        if i in done:
+            low = None
+            continue
+        u, u_next, f = u_ref[u_at + 1 + i], u_ref[u_at + 2 + i], faces_at + i
+        if low is None:
+            low = fx[f] * (u_ref[u_at + i] - u)
+        applied, low = flux_sum(u, u_next, low, fx[f + 1], fy[f], fz[f])
         rest = g_ref[g_at + i] - applied
         out[out_at + i] = rest if last else u + w[f] * rest
-        return u_next, high
-
-    loop(count, body, (u1, low), unroll)
 
 
 def permutation(inverse):
@@ -192,29 +204,46 @@
         to_low[at : at + size] = flat[pl.ds(base + d - 1, size, 8), :]
 
 
-def fine_kernel(me, own, low, high, low_corners, high_corners, piece, u0, g_flat, k_flat, u1, rhs, fx, fy, fz, w, uf, res, s1, sc,
+def early_kernel(own, low, high, g_flat, k_flat, fx, fy, fz, w, uf, u0, res):
+    own, flats = Slabs(own, 8), (g_flat, k_flat)
+    g, k = Slabs(g_flat, 24), Slabs(k_flat, 24)
+    for i in range(8):
+        g.put(i, 8, own[i])
+        k.put(i, 8, own[8 + i])
+    for i, (array, d, _, _) in enumerate(row_parts()):
+        flats[array][pl.ds(8 - d, 32, 24), :] = low[32 * i : 32 * i + 32]
+        flats[array][pl.ds(15 + d, 32, 24), :] = high[32 * i : 32 * i + 32]
+    face_pass(6, k, fx, fy, fz, w, 1.0)
+    for i in range(6):
+        uf[i] = w[i] * g[1 + i]
+    sweep_pass(4, uf, 0, 1, g, 2, fx, fy, fz, w, u0, 0)
+    sweep_pass(2, u0, 0, 2, g, 3, fx, fy, fz, w, res, 0, last=True)
+
+
+def fine_kernel(me, wide, low_corners, high_corners, g_early, k_early, fx_early, fy_early, fz_early, w_early, uf_early,
+                u0_early, res_early, piece, u0_kept, g_flat, k_flat, u1, rhs, u0_edge, fx, fy, fz, w, uf, res, s1, sc,
                 mx, my, mz, mw, mf, mr, ck):
     flats = g_flat, k_flat
-    own, g, k = Slabs(own, 8), Slabs(g_flat, 24), Slabs(k_flat, 24)
-    for i in range(G_SLABS):
-        g.put(i, 8, own[i])
-    for i in range(K_SLABS):
-        k.put(i, 8, own[G_SLABS + i])
-    for i, (array, d, _, border) in enumerate(row_parts()):
-        flats[array][pl.ds(border * 96 + 8 - d, 32, 24), :] = low[32 * i : 32 * i + 32]
-        flats[array][pl.ds(border * 96 + 15 + d, 32, 24), :] = high[32 * i : 32 * i + 32]
+    wide, g, k = Slabs(wide, 8), Slabs(g_flat, 24), Slabs(k_flat, 24)
+    for i in range(12):
+        g.put(i, 8, wide[i if i < 6 else i + 8])
+    for i in range(16):
+        k.put(i, 8, wide[G_SLABS + (i if i < 8 else i + 8)])
     for array, d, column, size, at in corners():
-        flats[array][pl.ds(column * 96 + 8 - d, size, 24), :] = low_corners[at : at + size]
-        flats[array][pl.ds(column * 96 + 15 + d, size, 24), :] = high_corners[at : at + size]
-    face_pass(20, k, fx, fy, fz, w, 1.0, 20, k_at=1)
-
-    def first(i, carry):
-        uf[i] = w[i] * g[i]
-        return carry
-
-    loop(20, first, 0, 20)
-    sweep_pass(18, uf, 0, 1, g, 1, fx, fy, fz, w, u0, 0, 18)
-    sweep_pass(16, u0, 0, 2, g, 2, fx, fy, fz, w, res, 0, 16, last=True)
+        slab = column if column < (G_BORDER, K_BORDER)[array] else column - 8
+        flats[array][pl.ds(slab * 96 + 8 - d, size, 24), :] = low_corners[at : at + size]
+        flats[array][pl.ds(slab * 96 + 15 + d, size, 24), :] = high_corners[at : at + size]
+    g, k = Parted(Slabs(g_early, 24), g, 6, 14), Parted(Slabs(k_early, 24), k, 8, 16)
+    fx = Parted(fx_early, fx, 7, 14)
+    fy, fz, w, uf = [Parted(*pair, 7, 13) for pair in ((fy_early, fy), (fz_early, fz), (w_early, w), (uf_early, uf))]
+    u0 = Parted(Parted(u0_early, u0_kept, 5, 9), u0_edge, 2, 16)
+    res = Parted(res_early, res, 7, 9)
+    face_pass(20, k, fx, fy, fz, w, 1.0, k_at=1, done=range(7, 13))
+    for i in range(20):
+        if not 7 <= i < 13:
+            uf[i] = w[i] * g[i]
+    sweep_pass(18, uf, 0, 1, g, 1, fx, fy, fz, w, u0, 0, done=range(7, 11))
+    sweep_pass(16, u0, 0, 2, g, 2, fx, fy, fz, w, res, 0, last=True, done=range(7, 9))
     for x in range(8):
         both = res[2 * x] + res[2 * x + 1]
         s1[x, 0] = both[0] + both[1]
@@ -244,8 +273,8 @@
         mw[x] = DAMPING / diag
         rhs[x] = rows(s1, x, 4)
         mf[x] = mw[x] * rhs[x]
-    sweep_pass(6, mf, 0, 1, rhs, 1, mx, my, mz, mw, u1, 0, 6)
-    sweep_pass(4, u1, 0, 2, rhs, 2, mx, my, mz, mw, mr, 0, 4, last=True)
+    sweep_pass(6, mf, 0, 1, rhs, 1, mx, my, mz, mw, u1, 0)
+    sweep_pass(4, u1, 0, 2, rhs, 2, mx, my, mz, mw, mr, 0, last=True)
     for x in range(4):
         both = k_mid[2 * x + 1] + k_mid[2 * x + 2]
         ck[x] = both[0] + both[1]
@@ -277,34 +306,38 @@
             piece[to, 32 + 4 * r : 36 + 4 * r, :] = rhs[column + 3, r, 2:6, :]
 
 
-def prepare_middle_kernel(k_flat, fx, fy, fz, w, k_mid, sums):
-    k = Slabs(k_flat, 24)
+def prepare_middle_kernel(k_early, k_flat, fx, fy, fz, w, k_mid, sums):
+    k = Parted(Slabs(k_early, 24), Slabs(k_flat, 24), 8, 16)
     for x in range(12):
         both = k[2 * x] + k[2 * x + 1]
         for r in range(2):
             sums[r] = both[2 * r] + both[2 * r + 1]
             k_mid[x, r] = (sums[r, pl.ds(4, 8, 2), :] + sums[r, pl.ds(5, 8, 2), :]) * 0.125
-    face_pass(10, k_mid, fx, fy, fz, w, 0.25, 10)
-
-
-def prepare_kernel(u0, g_flat, k_flat, u_out, g_out, fx, fy, fz, w, k_rows):
-    g, k = Slabs(g_flat, 24), Slabs(k_flat, 24)
+    face_pass(10, k_mid, fx, fy, fz, w, 0.25)
+
+
+def prepare_kernel(u0_early, u0, g_early, g_flat, k_early, k_flat, u_out, g_out, fx, fy, fz, w, k_rows):
+    g, k = Parted(Slabs(g_early, 24), Slabs(g_flat, 24), 6, 14), Parted(Slabs(k_early, 24), Slabs(k_flat, 24), 8, 16)
+    u0 = Parted(u0_early, u0, 5, 9)
     for i in range(14):
-        u_out[i] = u0[i + 2, :, 4:20, :]
+        u_out[i] = u0.part(i, 4, 16)
         k_rows[i] = k.part(i + 5, 4, 16)
     for i in range(12):
         g_out[i] = g.part(i + 4, 4, 16)
-    face_pass(12, k_rows, fx, fy, fz, w, 1.0, 12)
-
-
-def middle_kernel(me, gathered, u1, rhs, send, level_1):
+    face_pass(12, k_rows, fx, fy, fz, w, 1.0)
+
+
+EDGE_ROWS = 4 * 20 + 2 * 20 + 16
+
+
+def middle_kernel(me, gathered, u1, rhs, here, to_high, to_low, level_1):
     count = gathered.shape[0]
     for block in range(11):
         source = lax.rem(me[0] + (block - 5 + count * 5), count)
         for j in range(2):
             for array in range(2):
                 at = 4 * array + 2 * j
-                send[2 * j + array, 2 * block : 2 * block + 2, :] = gathered[source, at : at + 2, :]
+                here[2 * j + array, 2 * block : 2 * block + 2, :] = gathered[source, at : at + 2, :]
     u_flat, r_flat = level_1.at[0:192], level_1.at[192:352]
     u, g = Slabs(u_flat, 8, 2), Slabs(r_flat, 8, 2)
     for x in range(6):
@@ -319,10 +352,12 @@
                 u_flat[to : to + 4, :] = gathered[source, at : at + 4, :]
             to = 8 * (2 * edge + r) + 2
             r_flat[to : to + 4, :] = gathered[source, 32 + 4 * r : 36 + 4 * r, :]
-    for row in range(4):
-        send[4 + row] = u_flat[pl.ds(2 + row, 24, 8), :]
-    send[8, 0:20] = r_flat[pl.ds(2, 20, 8), :]
-    send[9, 0:20] = r_flat[pl.ds(5, 20, 8), :]
+    for out, row, rhs_row in ((to_high, 4, 5), (to_low, 2, 2)):
+        for slab in range(4):
+            out[20 * slab : 20 * slab + 20] = here[slab, 1:21]
+        for i in range(2):
+            out[80 + 20 * i : 100 + 20 * i] = level_1[pl.ds(16 + row + i, 20, 8), :]
+        out[120:136] = level_1[pl.ds(192 + 16 + rhs_row, 16, 8), :]
 
 
 SPREAD = (16, 14, 12, 10, 8, 6)
@@ -344,7 +379,12 @@
                 for out, upward in ((to_high, False), (to_low, True)):
                     start, size, at = spread(j, upward)
                     for array in range(2):
-                        out[at + size * array : at + size * array + size] = source[2 * (j % 2) + array, start : start + size]
+                        slab = 2 * (j % 2) + array
+                        if source is here:
+                            values = here[slab, start : start + size]
+                        else:
+                            values = source[20 * slab + start - 1 : 20 * slab + start - 1 + size]
+                        out[at + size * array : at + size * array + size] = values
 
 
 def coarse_kernel(me, first, here, second, left, right, level_1, fx, fy, fz, w, v_flat_out, to_high, to_low,
@@ -360,9 +400,13 @@
                     start[y, column : column + size] = source[at : at + size]
                     c[y, column : column + size] = source[at + size : at + 2 * size]
     for j in range(6):
-        block = (left, here, right)[j // 2]
-        start[6 + j] = block[2 * (j % 2)]
-        c[6 + j] = block[2 * (j % 2) + 1]
+        block, slab = (left, here, right)[j // 2], 2 * (j % 2)
+        if block is here:
+            start[6 + j] = here[slab]
+            c[6 + j] = here[slab + 1]
+        else:
+            start[6 + j, 1:21] = block[20 * slab : 20 * slab + 20]
+            c[6 + j, 1:21] = block[20 * slab + 20 : 20 * slab + 40]
     cy[0] = half * (c[0] + c[1])
     for y in range(18):
         u[y] = start[y]
@@ -387,10 +431,10 @@
             before, now = now, later
     v_flat[...] = level_1[0:192]
     r_flat[...] = level_1[192:352]
-    for source, row, slab, rhs_row, rhs_slab in ((left, 0, 6, 1, 9), (right, 6, 4, 6, 8)):
-        v_flat[pl.ds(row, 24, 8), :] = source[slab]
-        v_flat[pl.ds(row + 1, 24, 8), :] = source[slab + 1]
-        r_flat[pl.ds(rhs_row, 20, 8), :] = source[rhs_slab, 0:20]
+    for source, row, rhs_row in ((left, 0, 1), (right, 6, 6)):
+        for i in range(2):
+            v_flat[pl.ds(16 + row + i, 20, 8), :] = source[80 + 20 * i : 100 + 20 * i]
+        r_flat[pl.ds(16 + rhs_row, 16, 8), :] = source[120:136]
     v, rhs = Slabs(v_flat, 8, 2), Slabs(r_flat, 8, 2)
     for x in range(6):
         rows = jnp.concatenate(
@@ -398,8 +442,8 @@
         )
         for twin in range(2):
             v[2 * x + twin] = v[2 * x + twin] + rows[None]
-    sweep_pass(10, v, 0, 0, rhs, 0, fx, fy, fz, w, va, 0, 10)
-    sweep_pass(8, va, 0, 1, rhs, 1, fx, fy, fz, w, Slabs(v_flat_out, 8, 2), 0, 8)
+    sweep_pass(10, v, 0, 0, rhs, 0, fx, fy, fz, w, va, 0)
+    sweep_pass(8, va, 0, 1, rhs, 1, fx, fy, fz, w, Slabs(v_flat_out, 8, 2), 0)
     for out, row in ((to_high, 4), (to_low, 2)):
         for i in range(2):
             out[16 * i : 16 * i + 16] = v_flat_out[pl.ds(row + i, 16, 8), :]
@@ -418,8 +462,8 @@
     for i in range(14):
         fine = wide[(i + 1) // 2]
         ua[i] = u0[i] + jnp.stack([fine[0], fine[0], fine[1], fine[1]])
-    sweep_pass(12, ua, 0, 0, g, 0, fx, fy, fz, w, ub, 0, 12)
-    sweep_pass(10, ub, 0, 1, g, 1, fx, fy, fz, w, ua, 0, 10)
+    sweep_pass(12, ua, 0, 0, g, 0, fx, fy, fz, w, ub, 0)
+    sweep_pass(10, ub, 0, 1, g, 1, fx, fy, fz, w, ua, 0)
     matrix = permutation(True)
 
     def leave(index, source, at, out):
@@ -432,7 +476,7 @@
         return copy
 
     first = leave(0, ua, 1, correction)
-    sweep_pass(8, ua, 0, 2, g, 2, fx, fy, fz, w, res, 0, 8, last=True)
+    sweep_pass(8, ua, 0, 2, g, 2, fx, fy, fz, w, res, 0, last=True)
     second = leave(1, res, 0, residual)
     first.wait()
     second.wait()
@@ -482,24 +526,30 @@
     )
     low_corners, high_corners = shift(high_corners, "gy", 1), shift(low_corners, "gy", -1)
     fine, mid, last = (4, 24, 128), (2, 8, 128), (4, 16, 128)
+    early = call(
+        early_kernel,
+        [(8 * 96, 128), (8 * 96, 128), (7, *fine), (6, *fine), (6, *fine), (6, *fine), (6, *fine), (4, *fine), (2, *fine)],
+        [], own, low, high,
+    )
+    g_early, k_early, u0_early = early[0], early[1], early[7]
     piece, u0, g, k, u1, rhs = call(
         fine_kernel,
-        [(count, 40, 128), (18, *fine), (G_SLABS * 96, 128), (K_SLABS * 96, 128), (6, *mid), (8, *mid)],
-        [(21, *fine), (20, *fine), (20, *fine), (20, *fine), (20, *fine), (16, *fine), (8, 2, 24, 128), (10, 2, 24, 128),
+        [(count, 40, 128), (10, *fine), (12 * 96, 128), (16 * 96, 128), (6, *mid), (8, *mid)],
+        [(4, *fine), (14, *fine), (14, *fine), (14, *fine), (14, *fine), (14, *fine), (14, *fine), (8, 2, 24, 128), (10, 2, 24, 128),
          (9, *mid), (8, *mid), (8, *mid), (8, *mid), (8, *mid), (4, *mid), (4, 8, 128)],
-        me_x, wide, low, high, low_corners, high_corners, scalars=1,
+        me_x, wide, low_corners, high_corners, *early, scalars=1,
     )
     piece, u0, g, k, u1, rhs = lax.optimization_barrier((piece, u0, g, k, u1, rhs))
     gathered = lax.all_to_all(piece, "gx", 0, 0)
     gathered, u0, g, k, u1, rhs = lax.optimization_barrier((gathered, u0, g, k, u1, rhs))
-    here, level_1 = call(
-        middle_kernel, [(10, 24, 128), (352, 128)], [], me_x, gathered, u1, rhs, scalars=1
-    )
-    low, high = shift(here, "gy", 1), shift(here, "gy", -1)
+    here, high, low, level_1 = call(
+        middle_kernel, [(4, 24, 128), (EDGE_ROWS, 128), (EDGE_ROWS, 128), (352, 128)], [], me_x, gathered, u1, rhs, scalars=1
+    )
+    low, high = shift(high, "gy", 1), shift(low, "gy", -1)
     first, second = call(three_kernel, [(136, 128), (136, 128)], [], me_y, here, low, high, scalars=1)
     first, second = swap(first, "gy", 1, 3), swap(second, "gy", 0, 3)
     faces = call(
-        prepare_middle_kernel, [(11, *mid), (10, *mid), (10, *mid), (10, *mid)], [(12, *mid), (2, 24, 128)], k
+        prepare_middle_kernel, [(11, *mid), (10, *mid), (10, *mid), (10, *mid)], [(12, *mid), (2, 24, 128)], k_early, k
     )
     rows = (18, 24, 128)
     v1, high_rows, low_rows = call(
@@ -508,7 +558,8 @@
         me_y, first, here, second, low, high, level_1, *faces, scalars=1,
     )
     u0, g, *faces = call(
-        prepare_kernel, [(14, *last), (12, *last), (13, *last), (12, *last), (12, *last), (12, *last)], [(14, *last)], u0, g, k
+        prepare_kernel, [(14, *last), (12, *last), (13, *last), (12, *last), (12, *last), (12, *last)], [(14, *last)],
+        u0_early, u0, g_early, g, k_early, k,
     )
     low, high = shift(high_rows, "gy", 1), shift(low_rows, "gy", -1)
     return tuple(call(

time: 69.6 us -> 67.9 us (0.976)
    pallas_call x10 -> x11, Pallas kernels: 6.8 us -> 6.84 us  [call(): pl.pallas_call(kernel, out_shape=[jax.ShapeDtypeStruct(shape, F32) for sh...]
  transfers between devices with their start and end apart: 12 -> 12, of which waited for: 8 -> 8; matrix products, arithmetic and copies ran while one was open for 0% -> 0% of each run, Pallas kernels for 1% -> 2%
where the time goes in v6:
time: 67.9 us; the launch traced here: 67.7 us
  starting transfers between devices  36.2 us (53%)
  waiting for transfers between devices  12.7 us (19%)
  blocking collectives  10.3 us (15%)
  Pallas kernels  6.84 us (10%)
  other arithmetic  0.99 us (1%)
  between operations  0.74 us (1%)
    ppermute x4, starting transfers between devices, swap(): return lax.ppermute(array, axis, pairs + [(j, i) for i, j in pairs])  23 us
    ppermute x8, starting transfers between devices, shift(): lax.ppermute(array, axis, [(i, (i + by) % count) for i in range(count)])  13.1 us
    all_to_all x1, blocking collectives, per_device(): gathered = lax.all_to_all(piece, 'gx', 0, 0)  10.3 us
    ppermute x8, waiting for transfers between devices, shift(): lax.ppermute(array, axis, [(i, (i + by) % count) for i in range(count)])  7.58 us
    pallas_call x11, Pallas kernels, call(): pl.pallas_call(kernel, out_shape=[jax.ShapeDtypeStruct(shape, F32) for sh...  6.84 us
    ppermute x4, waiting for transfers between devices, swap(): return lax.ppermute(array, axis, pairs + [(j, i) for i, j in pairs])  5.1 us
  transfers between devices with their start and end apart: 12, of which 8 were waited for; matrix products, arithmetic and copies ran while one was open for 0% of the time, Pallas kernels for 2%

profile of v6, /device:TPU:1, one launch (start us, length us, event | category | flops | bytes accessed | tf_op | source)
XLA Modules:
  0.0 67.7 jit_solution(2546347395914010828)
XLA Ops:
  0.6 1.0 %pad_maximum_fusion.held = f32[2,8,8,512]{3,2,1,0:T(8,128)S(1)} fusion(f32[1,8,8,512]{3,2,1,0:T(8,128)} %bitcast.4, f32[1,8,8,512]{3,2,1,0:T(8,128)} %bitcast.5), kind=kLoop, calls=%fused_computation | loop fusion | flops 65536 | bytes 524288 | tf_op jit(solution)/shard_map/stack | solution.py:518
  1.6 0.4 shard_map.41
  2.0 7.7 %collective-permute-start = (f32[14,4,8,128]{3,2,1,0:T(8,128)S(1)}, f32[14,4,8,128]{3,2,1,0:T(8,128)S(1)}, u32[]{:S(2)}, u32[]{:S(2)}) collective-permute-start(f32[14,4,8,128]{3,2,1,0:T(8,128)S(1)} %get-tuple-element.51), channel_id=1, source_target_pairs={{32,64},{96,128},{160,192},{224,256},{288,320},{352,384},{416,448}... | collective-permute-start | bytes 688136 | tf_op jit(solution)/shard_map/ppermute | solution.py:509
  9.7 1.9 %collective-permute-start.1 = (f32[14,4,8,128]{3,2,1,0:T(8,128)S(1)}, f32[14,4,8,128]{3,2,1,0:T(8,128)S(1)}, u32[]{:S(2)}, u32[]{:S(2)}) collective-permute-start(f32[14,4,8,128]{3,2,1,0:T(8,128)S(1)} %get-tuple-element.52), channel_id=1, source_target_pairs={{0,32},{64,96},{128,160},{192,224},{256,288},{320,352},{384,416},{... | collective-permute-start | bytes 688136 | tf_op jit(solution)/shard_map/ppermute | solution.py:509
  11.7 2.5 %collective-permute-start.4 = (f32[416,128]{1,0:T(8,128)S(1)}, f32[416,128]{1,0:T(8,128)S(1)}, u32[]{:S(2)}, u32[]{:S(2)}) collective-permute-start(f32[416,128]{1,0:T(8,128)S(1)} %get-tuple-element.56), channel_id=1, source_target_pairs={{0,1},{1,2},{2,3},{3,4},{4,5},{5,6},{6,7},{7,8},{8,9},{9,10},{10,1... | collective-permute-start | bytes 638984 | tf_op jit(solution)/shard_map/ppermute | solution.py:503
  14.2 3.4 %collective-permute-done.1.second = f32[14,4,8,128]{3,2,1,0:T(8,128)S(1)} collective-permute-done((f32[14,4,8,128]{3,2,1,0:T(8,128)S(1)}, f32[14,4,8,128]{3,2,1,0:T(8,128)S(1)}, u32[]{:S(2)}, u32[]{:S(2)}) %collective-permute-start.1) | collective-permute-done | bytes 229408 | tf_op jit(solution)/shard_map/ppermute | solution.py:509
  17.7 3.6 %collective-permute-start.2 = (f32[304,128]{1,0:T(8,128)S(1)}, f32[304,128]{1,0:T(8,128)S(1)}, u32[]{:S(2)}, u32[]{:S(2)}) collective-permute-start(f32[304,128]{1,0:T(8,128)S(1)} %get-tuple-element.54), channel_id=1, source_target_pairs={{0,1},{1,2},{2,3},{3,4},{4,5},{5,6},{6,7},{7,8},{8,9},{9,10},{10,1... | collective-permute-start | bytes 466952 | tf_op jit(solution)/shard_map/ppermute | solution.py:503
  21.5 0.5 shard_map.44
  22.1 1.4 %collective-permute-done.2.low_corners = f32[304,128]{1,0:T(8,128)S(1)} collective-permute-done((f32[304,128]{1,0:T(8,128)S(1)}, f32[304,128]{1,0:T(8,128)S(1)}, u32[]{:S(2)}, u32[]{:S(2)}) %collective-permute-start.2) | collective-permute-done | bytes 155680 | tf_op jit(solution)/shard_map/ppermute | solution.py:503
  23.5 2.5 %collective-permute-done.3.high_corners = f32[304,128]{1,0:T(8,128)S(1)} collective-permute-done((f32[304,128]{1,0:T(8,128)S(1)}, f32[304,128]{1,0:T(8,128)S(1)}, u32[]{:S(2)}, u32[]{:S(2)}) %collective-permute-start.3) | collective-permute-done | bytes 155680 | tf_op jit(solution)/shard_map/ppermute | solution.py:503
  25.9 1.9 %shard_map.45 = (f32[16,40,128]{2,1,0:T(8,128)S(1)}, f32[10,4,24,128]{3,2,1,0:T(8,128)S(1)}, f32[1152,128]{1,0:T(8,128)S(1)}, f32[1536,128]{1,0:T(8,128)S(1)}, f...) custom-call(s32[1]{0:T(128)} %bitcast.1.me, f32[1408,128]{1,0:T(8,128)S(1)} %get-tuple-element.53.wide, ...), custom_call_target="tpu_custom_call" | custom-call | tf_op jit(solution)/shard_map/pallas_call | solution.py:491
  27.9 10.3 %all_to_all.5.gathered = f32[16,40,128]{2,1,0:T(8,128)S(1)} all-to-all(f32[16,40,128]{2,1,0:T(8,128)S(1)} %get-tuple-element.67), channel_id=1, replica_groups=mesh['gx'=16,'gy'=32] {'gx'}, dimensions={0} | all-to-all | bytes 655360 | tf_op jit(solution)/shard_map/all_to_all | solution.py:543
  38.2 2.1 %collective-permute-start.6 = (f32[136,128]{1,0:T(8,128)S(1)}, f32[136,128]{1,0:T(8,128)S(1)}, u32[]{:S(2)}, u32[]{:S(2)}) collective-permute-start(f32[136,128]{1,0:T(8,128)S(1)} %get-tuple-element.77), channel_id=1, source_target_pairs={{0,1},{1,2},{2,3},{3,4},{4,5},{5,6},{6,7},{7,8},{8,9},{9,10},{10,1... | collective-permute-start | bytes 208904 | tf_op jit(solution)/shard_map/ppermute | solution.py:503
  40.3 4.2 %collective-permute-start.7 = (f32[136,128]{1,0:T(8,128)S(1)}, f32[136,128]{1,0:T(8,128)S(1)}, u32[]{:S(2)}, u32[]{:S(2)}) collective-permute-start(f32[136,128]{1,0:T(8,128)S(1)} %get-tuple-element.78), channel_id=1, source_target_pairs={{0,31},{1,0},{2,1},{3,2},{4,3},{5,4},{6,5},{7,6},{8,7},{9,8},{10,9... | collective-permute-start | bytes 208904 | tf_op jit(solution)/shard_map/ppermute | solution.py:503
  44.4 0.7 %collective-permute-done.6.low.left = f32[136,128]{1,0:T(8,128)S(1)} collective-permute-done((f32[136,128]{1,0:T(8,128)S(1)}, f32[136,128]{1,0:T(8,128)S(1)}, u32[]{:S(2)}, u32[]{:S(2)}) %collective-permute-start.6) | collective-permute-done | bytes 69664 | tf_op jit(solution)/shard_map/ppermute | solution.py:503
  45.4 1.9 %collective-permute-start.8 = (f32[136,128]{1,0:T(8,128)S(1)}, f32[136,128]{1,0:T(8,128)S(1)}, u32[]{:S(2)}, u32[]{:S(2)}) collective-permute-start(f32[136,128]{1,0:T(8,128)S(1)} %get-tuple-element.79), channel_id=1, source_target_pairs={{1,4},{3,6},{5,8},{7,10},{9,12},{11,14},{13,16},{15,18},{17,20},{1... | collective-permute-start | bytes 208904 | tf_op jit(solution)/shard_map/ppermute | solution.py:509
  47.3 11.5 %collective-permute-start.9 = (f32[136,128]{1,0:T(8,128)S(1)}, f32[136,128]{1,0:T(8,128)S(1)}, u32[]{:S(2)}, u32[]{:S(2)}) collective-permute-start(f32[136,128]{1,0:T(8,128)S(1)} %get-tuple-element.80), channel_id=1, source_target_pairs={{0,3},{2,5},{4,7},{6,9},{8,11},{10,13},{12,15},{14,17},{16,19},{18... | collective-permute-start | bytes 208904 | tf_op jit(solution)/shard_map/ppermute | solution.py:509
  59.1 1.7 %collective-permute-done.9.second = f32[136,128]{1,0:T(8,128)S(1)} collective-permute-done((f32[136,128]{1,0:T(8,128)S(1)}, f32[136,128]{1,0:T(8,128)S(1)}, u32[]{:S(2)}, u32[]{:S(2)}) %collective-permute-start.9) | collective-permute-done | bytes 69664 | tf_op jit(solution)/shard_map/ppermute | solution.py:509
  60.8 1.4 %shard_map.49 = (f32[128,128]{1,0:T(8,128)S(1)}, f32[32,128]{1,0:T(8,128)S(1)}, f32[32,128]{1,0:T(8,128)S(1)}) custom-call(s32[1]{0:T(128)} %bitcast.me, f32[136,128]{1,0:T(8,128)S(1)} %collective-permute-done.8.first, f32[4,24,128]{2,1,0:T(8,128)S(1)} %get-tuple-element.76.here, f32[136,128]{1,0:T(8,128)S(1)} %collective-permute-done.9.second, ...), custom_call_target="tpu_custom_call" | custom-call | tf_op jit(solution)/shard_map/pallas_call | solution.py:491
  62.4 0.4 collective-permute-start.11
  62.8 0.3 shard_map.50
  63.0 0.4 collective-permute-done.10.v_low
  63.4 2.4 %collective-permute-done.11.v_high = f32[32,128]{1,0:T(8,128)S(1)} collective-permute-done((f32[32,128]{1,0:T(8,128)S(1)}, f32[32,128]{1,0:T(8,128)S(1)}, u32[]{:S(2)}, u32[]{:S(2)}) %collective-permute-start.11) | collective-permute-done | bytes 16416 | tf_op jit(solution)/shard_map/ppermute | solution.py:503
  65.8 1.8 %shard_map.51 = (f32[8,8,512]{2,1,0:T(8,128)}, f32[8,8,512]{2,1,0:T(8,128)}) custom-call(f32[128,128]{1,0:T(8,128)S(1)} %get-tuple-element.87.v_here, f32[32,128]{1,0:T(8,128)S(1)} %collective-permute-done.10.v_low, f32[32,128]{1,0:T(8,128)S(1)} %collective-permute-done.11.v_high, f32[14,4,16,128]{3,2,1,0:T(8,128)S(1)} %get-tuple-element.92.u0, ...), custom_call_target="tpu_custom_call" | custom-call | tf_op jit(solution)/shard_map/pallas_call | solution.py:491
  (13 shorter events, 1.0 us)
Async XLA Ops:
  2.0 12.2 %collective-permute-start = (f32[14,4,8,128]{3,2,1,0:T(8,128)S(1)}, f32[14,4,8,128]{3,2,1,0:T(8,128)S(1)}, u32[]{:S(2)}, u32[]{:S(2)}) collective-permute-start(f32[14,4,8,128]{3,2,1,0:T(8,128)S(1)} %get-tuple-element.51), channel_id=1, source_target_pairs={{32,64},{96,128},{160,192},{224,256},{288,320},{352,384},{416,448}... | collective-permute-start | bytes 688136 | tf_op jit(solution)/shard_map/ppermute | solution.py:509
  9.7 7.8 %collective-permute-start.1 = (f32[14,4,8,128]{3,2,1,0:T(8,128)S(1)}, f32[14,4,8,128]{3,2,1,0:T(8,128)S(1)}, u32[]{:S(2)}, u32[]{:S(2)}) collective-permute-start(f32[14,4,8,128]{3,2,1,0:T(8,128)S(1)} %get-tuple-element.52), channel_id=1, source_target_pairs={{0,32},{64,96},{128,160},{192,224},{256,288},{320,352},{384,416},{... | collective-permute-start | bytes 688136 | tf_op jit(solution)/shard_map/ppermute | solution.py:509
  11.7 9.8 %collective-permute-start.4 = (f32[416,128]{1,0:T(8,128)S(1)}, f32[416,128]{1,0:T(8,128)S(1)}, u32[]{:S(2)}, u32[]{:S(2)}) collective-permute-start(f32[416,128]{1,0:T(8,128)S(1)} %get-tuple-element.56), channel_id=1, source_target_pairs={{0,1},{1,2},{2,3},{3,4},{4,5},{5,6},{6,7},{7,8},{8,9},{9,10},{10,1... | collective-permute-start | bytes 638984 | tf_op jit(solution)/shard_map/ppermute | solution.py:503
  14.2 7.3 %collective-permute-start.5 = (f32[416,128]{1,0:T(8,128)S(1)}, f32[416,128]{1,0:T(8,128)S(1)}, u32[]{:S(2)}, u32[]{:S(2)}) collective-permute-start(f32[416,128]{1,0:T(8,128)S(1)} %get-tuple-element.57), channel_id=1, source_target_pairs={{0,31},{1,0},{2,1},{3,2},{4,3},{5,4},{6,5},{7,6},{8,7},{9,8},{10,9... | collective-permute-start | bytes 638984 | tf_op jit(solution)/shard_map/ppermute | solution.py:503
  17.7 5.8 %collective-permute-start.2 = (f32[304,128]{1,0:T(8,128)S(1)}, f32[304,128]{1,0:T(8,128)S(1)}, u32[]{:S(2)}, u32[]{:S(2)}) collective-permute-start(f32[304,128]{1,0:T(8,128)S(1)} %get-tuple-element.54), channel_id=1, source_target_pairs={{0,1},{1,2},{2,3},{3,4},{4,5},{5,6},{6,7},{7,8},{8,9},{9,10},{10,1... | collective-permute-start | bytes 466952 | tf_op jit(solution)/shard_map/ppermute | solution.py:503
  21.3 4.7 %collective-permute-start.3 = (f32[304,128]{1,0:T(8,128)S(1)}, f32[304,128]{1,0:T(8,128)S(1)}, u32[]{:S(2)}, u32[]{:S(2)}) collective-permute-start(f32[304,128]{1,0:T(8,128)S(1)} %get-tuple-element.55), channel_id=1, source_target_pairs={{0,31},{1,0},{2,1},{3,2},{4,3},{5,4},{6,5},{7,6},{8,7},{9,8},{10,9... | collective-permute-start | bytes 466952 | tf_op jit(solution)/shard_map/ppermute | solution.py:503
  38.2 7.0 %collective-permute-start.6 = (f32[136,128]{1,0:T(8,128)S(1)}, f32[136,128]{1,0:T(8,128)S(1)}, u32[]{:S(2)}, u32[]{:S(2)}) collective-permute-start(f32[136,128]{1,0:T(8,128)S(1)} %get-tuple-element.77), channel_id=1, source_target_pairs={{0,1},{1,2},{2,3},{3,4},{4,5},{5,6},{6,7},{7,8},{8,9},{9,10},{10,1... | collective-permute-start | bytes 208904 | tf_op jit(solution)/shard_map/ppermute | solution.py:503
  40.3 5.1 %collective-permute-start.7 = (f32[136,128]{1,0:T(8,128)S(1)}, f32[136,128]{1,0:T(8,128)S(1)}, u32[]{:S(2)}, u32[]{:S(2)}) collective-permute-start(f32[136,128]{1,0:T(8,128)S(1)} %get-tuple-element.78), channel_id=1, source_target_pairs={{0,31},{1,0},{2,1},{3,2},{4,3},{5,4},{6,5},{7,6},{8,7},{9,8},{10,9... | collective-permute-start | bytes 208904 | tf_op jit(solution)/shard_map/ppermute | solution.py:503
  45.4 13.7 %collective-permute-start.8 = (f32[136,128]{1,0:T(8,128)S(1)}, f32[136,128]{1,0:T(8,128)S(1)}, u32[]{:S(2)}, u32[]{:S(2)}) collective-permute-start(f32[136,128]{1,0:T(8,128)S(1)} %get-tuple-element.79), channel_id=1, source_target_pairs={{1,4},{3,6},{5,8},{7,10},{9,12},{11,14},{13,16},{15,18},{17,20},{1... | collective-permute-start | bytes 208904 | tf_op jit(solution)/shard_map/ppermute | solution.py:509
  47.3 13.5 %collective-permute-start.9 = (f32[136,128]{1,0:T(8,128)S(1)}, f32[136,128]{1,0:T(8,128)S(1)}, u32[]{:S(2)}, u32[]{:S(2)}) collective-permute-start(f32[136,128]{1,0:T(8,128)S(1)} %get-tuple-element.80), channel_id=1, source_target_pairs={{0,3},{2,5},{4,7},{6,9},{8,11},{10,13},{12,15},{14,17},{16,19},{18... | collective-permute-start | bytes 208904 | tf_op jit(solution)/shard_map/ppermute | solution.py:509
  62.2 1.2 %collective-permute-start.10 = (f32[32,128]{1,0:T(8,128)S(1)}, f32[32,128]{1,0:T(8,128)S(1)}, u32[]{:S(2)}, u32[]{:S(2)}) collective-permute-start(f32[32,128]{1,0:T(8,128)S(1)} %get-tuple-element.88), channel_id=1, source_target_pairs={{0,1},{1,2},{2,3},{3,4},{4,5},{5,6},{6,7},{7,8},{8,9},{9,10},{10,1... | collective-permute-start | bytes 49160 | tf_op jit(solution)/shard_map/ppermute | solution.py:503
  62.4 3.5 %collective-permute-start.11 = (f32[32,128]{1,0:T(8,128)S(1)}, f32[32,128]{1,0:T(8,128)S(1)}, u32[]{:S(2)}, u32[]{:S(2)}) collective-permute-start(f32[32,128]{1,0:T(8,128)S(1)} %get-tuple-element.89), channel_id=1, source_target_pairs={{0,31},{1,0},{2,1},{3,2},{4,3},{5,4},{6,5},{7,6},{8,7},{9,8},{10,9... | collective-permute-start | bytes 49160 | tf_op jit(solution)/shard_map/ppermute | solution.py:503

commit v7 on v6

--- a/solution.py
+++ b/solution.py
@@ -84,34 +84,56 @@
         return buffer[at, :, start : start + size, :]
 
 
-def face_pass(count, k_ref, fx, fy, fz, w, scale, k_at=0, done=()):
+def get(ref, i, rows):
+    if rows is None:
+        return ref[i]
+    return ref.part(i, *rows) if hasattr(ref, "part") else ref[i, :, rows[0] : rows[0] + rows[1], :]
+
+
+def put(ref, i, rows, value):
+    if isinstance(ref, Parted):
+        put(*ref.place(i), rows, value)
+    elif rows is None:
+        ref[i] = value
+    else:
+        ref[i, :, rows[0] : rows[0] + rows[1], :] = value
+
+
+def every_row(i):
+    return None
+
+
+def face_pass(count, k_ref, fx, fy, fz, w, scale, k_at=0, done=(), rows=every_row):
     half = 0.5 * scale
     for i in range(count + 1):
         if i not in done or i - 1 not in done:
             fx[i] = half * (k_ref[k_at + i] + k_ref[k_at + 1 + i])
         if i == 0 or i - 1 in done:
             continue
-        k = k_ref[k_at + i]
+        some = rows(i - 1)
+        k = get(k_ref, k_at + i, some)
         face_y = half * (k + y_next(k))
         face_z = half * (k + z_next(k))
-        diag = ABSORPTION + (fx[i] + fx[i - 1] + face_y + y_prev(face_y) + face_z + z_prev(face_z))
-        fy[i - 1] = face_y
-        fz[i - 1] = face_z
-        w[i - 1] = DAMPING / diag
-
-
-def sweep_pass(count, u_ref, u_at, faces_at, g_ref, g_at, fx, fy, fz, w, out, out_at, last=False, done=()):
-    low = None
+        diag = ABSORPTION + (get(fx, i, some) + get(fx, i - 1, some) + face_y + y_prev(face_y) + face_z + z_prev(face_z))
+        put(fy, i - 1, some, face_y)
+        put(fz, i - 1, some, face_z)
+        put(w, i - 1, some, DAMPING / diag)
+
+
+def sweep_pass(count, u_ref, u_at, faces_at, g_ref, g_at, fx, fy, fz, w, out, out_at, last=False, done=(), rows=every_row):
+    low, low_rows = None, None
     for i in range(count):
         if i in done:
             low = None
             continue
-        u, u_next, f = u_ref[u_at + 1 + i], u_ref[u_at + 2 + i], faces_at + i
-        if low is None:
-            low = fx[f] * (u_ref[u_at + i] - u)
-        applied, low = flux_sum(u, u_next, low, fx[f + 1], fy[f], fz[f])
-        rest = g_ref[g_at + i] - applied
-        out[out_at + i] = rest if last else u + w[f] * rest
+        some, f = rows(i), faces_at + i
+        u, u_next = get(u_ref, u_at + 1 + i, some), get(u_ref, u_at + 2 + i, some)
+        if low is None or low_rows != some:
+            low = get(fx, f, some) * (get(u_ref, u_at + i, some) - u)
+        applied, low = flux_sum(u, u_next, low, get(fx, f + 1, some), get(fy, f, some), get(fz, f, some))
+        low_rows = some
+        rest = get(g_ref, g_at + i, some) - applied
+        put(out, out_at + i, some, rest if last else u + get(w, f, some) * rest)
 
 
 def permutation(inverse):
@@ -238,12 +260,16 @@
     fy, fz, w, uf = [Parted(*pair, 7, 13) for pair in ((fy_early, fy), (fz_early, fz), (w_early, w), (uf_early, uf))]
     u0 = Parted(Parted(u0_early, u0_kept, 5, 9), u0_edge, 2, 16)
     res = Parted(res_early, res, 7, 9)
-    face_pass(20, k, fx, fy, fz, w, 1.0, k_at=1, done=range(7, 13))
+    def beside(first_x, border):
+        return lambda i: (4, 16) if first_x + i <= -border or first_x + i >= 7 + border else None
+
+    face_pass(20, k, fx, fy, fz, w, 1.0, k_at=1, done=range(7, 13), rows=beside(-6, 3))
     for i in range(20):
         if not 7 <= i < 13:
-            uf[i] = w[i] * g[i]
-    sweep_pass(18, uf, 0, 1, g, 1, fx, fy, fz, w, u0, 0, done=range(7, 11))
-    sweep_pass(16, u0, 0, 2, g, 2, fx, fy, fz, w, res, 0, last=True, done=range(7, 9))
+            some = beside(-6, 3)(i)
+            put(uf, i, some, get(w, i, some) * get(g, i, some))
+    sweep_pass(18, uf, 0, 1, g, 1, fx, fy, fz, w, u0, 0, done=range(7, 11), rows=beside(-5, 2))
+    sweep_pass(16, u0, 0, 2, g, 2, fx, fy, fz, w, res, 0, last=True, done=range(7, 9), rows=beside(-4, 1))
     for x in range(8):
         both = res[2 * x] + res[2 * x + 1]
         s1[x, 0] = both[0] + both[1]
@@ -387,8 +413,12 @@
                         out[at + size * array : at + size * array + size] = values
 
 
+def window(reach):
+    return (7, 8) if reach <= 3 else (3, 16) if reach <= 7 else (1, 24)
+
+
 def coarse_kernel(me, first, here, second, left, right, level_1, fx, fy, fz, w, v_flat_out, to_high, to_low,
-                  u, c, start, cy, weights, v_flat, r_flat, va):
+                  u, other, c, start, weights, v_flat, r_flat, va):
     half = 0.5 * 0.0625
     even = lax.rem(me[0], 2) == 0
     for take, below, above in ((even, first, second), (jnp.logical_not(even), second, first)):
@@ -402,33 +432,43 @@
     for j in range(6):
         block, slab = (left, here, right)[j // 2], 2 * (j % 2)
         if block is here:
-            start[6 + j] = here[slab]
-            c[6 + j] = here[slab + 1]
+            start[6 + j, 0:24] = here[slab]
+            c[6 + j, 0:24] = here[slab + 1]
         else:
             start[6 + j, 1:21] = block[20 * slab : 20 * slab + 20]
             c[6 + j, 1:21] = block[20 * slab + 20 : 20 * slab + 40]
-    cy[0] = half * (c[0] + c[1])
-    for y in range(18):
-        u[y] = start[y]
+
+    def reach(y, step):
+        return 9 - step - max(0, 7 - y, y - 10)
+
+    def at(ref, y, lo, size):
+        return ref[y, lo : lo + size]
+
     for y in range(1, 17):
-        k = c[y]
-        right_x = half * (k + pltpu.roll(k, 23, 0))
-        right_z = half * (k + pltpu.roll(k, LANES - 1, 1))
-        right_y = half * (k + c[y + 1])
-        left_x, left_z, left_y = pltpu.roll(right_x, 1, 0), pltpu.roll(right_z, 1, 1), cy[y - 1]
-        cy[y] = right_y
-        scale = DAMPING / (ABSORPTION + (right_x + left_x + right_y + left_y + right_z + left_z))
-        for i, face in enumerate((right_x, left_x, right_y, left_y, right_z, left_z)):
-            weights[i, y] = scale * face
+        lo, size = window(reach(y, 1))
+        k = at(c, y, lo, size)
+        face_z = half * (k + pltpu.roll(k, LANES - 1, 1))
+        faces = [half * (k + at(c, y, lo + 1, size)), half * (k + at(c, y, lo - 1, size))]
+        faces += [half * (k + at(c, y + 1, lo, size)), half * (k + at(c, y - 1, lo, size))]
+        faces += [face_z, pltpu.roll(face_z, 1, 1)]
+        scale = DAMPING / (ABSORPTION + ((faces[0] + faces[1]) + (faces[2] + faces[3]) + (faces[4] + faces[5])))
+        for i, face in enumerate(faces):
+            weights[i, y, lo : lo + size] = scale * face
+    old = start
     for step in range(1, 8):
-        before, now = u[step - 1], u[step]
+        new = (u, other)[step % 2]
         for y in range(step, 18 - step):
-            later = u[y + 1]
-            along_x = weights[0, y] * pltpu.roll(now, 23, 0) + weights[1, y] * pltpu.roll(now, 1, 0)
-            along_y = weights[2, y] * later + weights[3, y] * before
-            along_z = weights[4, y] * pltpu.roll(now, LANES - 1, 1) + weights[5, y] * pltpu.roll(now, 1, 1)
-            u[y] = ((1.0 - DAMPING) * now + start[y]) + along_y + (along_x + along_z)
-            before, now = now, later
+            lo, size = window(reach(y, step))
+            now = at(old, y, lo, size)
+            along_x = at(weights.at[0], y, lo, size) * at(old, y, lo + 1, size) + at(weights.at[1], y, lo, size) * at(old, y, lo - 1, size)
+            along_y = at(weights.at[2], y, lo, size) * at(old, y + 1, lo, size) + at(weights.at[3], y, lo, size) * at(old, y - 1, lo, size)
+            along_z = (
+                at(weights.at[4], y, lo, size) * pltpu.roll(now, LANES - 1, 1)
+                + at(weights.at[5], y, lo, size) * pltpu.roll(now, 1, 1)
+            )
+            new[y, lo : lo + size] = ((1.0 - DAMPING) * now + at(start, y, lo, size)) + along_y + (along_x + along_z)
+        old = new
+    u = old
     v_flat[...] = level_1[0:192]
     r_flat[...] = level_1[192:352]
     for source, row, rhs_row in ((left, 0, 1), (right, 6, 6)):
@@ -551,7 +591,7 @@
     faces = call(
         prepare_middle_kernel, [(11, *mid), (10, *mid), (10, *mid), (10, *mid)], [(12, *mid), (2, 24, 128)], k_early, k
     )
-    rows = (18, 24, 128)
+    rows = (18, 32, 128)
     v1, high_rows, low_rows = call(
         coarse_kernel, [(128, 128), (32, 128), (32, 128)],
         [rows, rows, rows, rows, (6, *rows), (192, 128), (160, 128), (10, *mid)],

time: 67.9 us -> 67.1 us (0.988)
  Pallas kernels: 6.84 us -> 6.04 us
    pallas_call x11, Pallas kernels: 6.84 us -> 6.04 us  [call(): pl.pallas_call(kernel, out_shape=[jax.ShapeDtypeStruct(shape, F32) for sh...]
where the time goes in v7:
time: 67.1 us; the launch traced here: 66.9 us
  starting transfers between devices  36.2 us (54%)
  waiting for transfers between devices  12.7 us (19%)
  blocking collectives  10.3 us (15%)
  Pallas kernels  6.04 us (9%)
  other arithmetic  0.99 us (1%)
  between operations  0.73 us (1%)
    ppermute x4, starting transfers between devices, swap(): return lax.ppermute(array, axis, pairs + [(j, i) for i, j in pairs])  23 us
    ppermute x8, starting transfers between devices, shift(): lax.ppermute(array, axis, [(i, (i + by) % count) for i in range(count)])  13.1 us
    all_to_all x1, blocking collectives, per_device(): gathered = lax.all_to_all(piece, 'gx', 0, 0)  10.3 us
    ppermute x8, waiting for transfers between devices, shift(): lax.ppermute(array, axis, [(i, (i + by) % count) for i in range(count)])  7.58 us
    pallas_call x11, Pallas kernels, call(): pl.pallas_call(kernel, out_shape=[jax.ShapeDtypeStruct(shape, F32) for sh...  6.04 us
    ppermute x4, waiting for transfers between devices, swap(): return lax.ppermute(array, axis, pairs + [(j, i) for i, j in pairs])  5.1 us
  transfers between devices with their start and end apart: 12, of which 8 were waited for; matrix products, arithmetic and copies ran while one was open for 0% of the time, Pallas kernels for 2%

profile of v7, /device:TPU:1, one launch (start us, length us, event | category | flops | bytes accessed | tf_op | source)
XLA Modules:
  0.0 66.9 jit_solution(16359627625609248703)
XLA Ops:
  0.6 1.0 %pad_maximum_fusion.held = f32[2,8,8,512]{3,2,1,0:T(8,128)S(1)} fusion(f32[1,8,8,512]{3,2,1,0:T(8,128)} %bitcast.4, f32[1,8,8,512]{3,2,1,0:T(8,128)} %bitcast.5), kind=kLoop, calls=%fused_computation | loop fusion | flops 65536 | bytes 524288 | tf_op jit(solution)/shard_map/stack | solution.py:558
  1.6 0.4 shard_map.41
  2.0 7.7 %collective-permute-start = (f32[14,4,8,128]{3,2,1,0:T(8,128)S(1)}, f32[14,4,8,128]{3,2,1,0:T(8,128)S(1)}, u32[]{:S(2)}, u32[]{:S(2)}) collective-permute-start(f32[14,4,8,128]{3,2,1,0:T(8,128)S(1)} %get-tuple-element.51), channel_id=1, source_target_pairs={{32,64},{96,128},{160,192},{224,256},{288,320},{352,384},{416,448}... | collective-permute-start | bytes 688136 | tf_op jit(solution)/shard_map/ppermute | solution.py:549
  9.7 1.9 %collective-permute-start.1 = (f32[14,4,8,128]{3,2,1,0:T(8,128)S(1)}, f32[14,4,8,128]{3,2,1,0:T(8,128)S(1)}, u32[]{:S(2)}, u32[]{:S(2)}) collective-permute-start(f32[14,4,8,128]{3,2,1,0:T(8,128)S(1)} %get-tuple-element.52), channel_id=1, source_target_pairs={{0,32},{64,96},{128,160},{192,224},{256,288},{320,352},{384,416},{... | collective-permute-start | bytes 688136 | tf_op jit(solution)/shard_map/ppermute | solution.py:549
  11.7 2.5 %collective-permute-start.4 = (f32[416,128]{1,0:T(8,128)S(1)}, f32[416,128]{1,0:T(8,128)S(1)}, u32[]{:S(2)}, u32[]{:S(2)}) collective-permute-start(f32[416,128]{1,0:T(8,128)S(1)} %get-tuple-element.56), channel_id=1, source_target_pairs={{0,1},{1,2},{2,3},{3,4},{4,5},{5,6},{6,7},{7,8},{8,9},{9,10},{10,1... | collective-permute-start | bytes 638984 | tf_op jit(solution)/shard_map/ppermute | solution.py:543
  14.2 3.4 %collective-permute-done.1.second = f32[14,4,8,128]{3,2,1,0:T(8,128)S(1)} collective-permute-done((f32[14,4,8,128]{3,2,1,0:T(8,128)S(1)}, f32[14,4,8,128]{3,2,1,0:T(8,128)S(1)}, u32[]{:S(2)}, u32[]{:S(2)}) %collective-permute-start.1) | collective-permute-done | bytes 229408 | tf_op jit(solution)/shard_map/ppermute | solution.py:549
  17.7 3.6 %collective-permute-start.2 = (f32[304,128]{1,0:T(8,128)S(1)}, f32[304,128]{1,0:T(8,128)S(1)}, u32[]{:S(2)}, u32[]{:S(2)}) collective-permute-start(f32[304,128]{1,0:T(8,128)S(1)} %get-tuple-element.54), channel_id=1, source_target_pairs={{0,1},{1,2},{2,3},{3,4},{4,5},{5,6},{6,7},{7,8},{8,9},{9,10},{10,1... | collective-permute-start | bytes 466952 | tf_op jit(solution)/shard_map/ppermute | solution.py:543
  21.5 0.5 shard_map.44
  22.1 1.4 %collective-permute-done.2.low_corners = f32[304,128]{1,0:T(8,128)S(1)} collective-permute-done((f32[304,128]{1,0:T(8,128)S(1)}, f32[304,128]{1,0:T(8,128)S(1)}, u32[]{:S(2)}, u32[]{:S(2)}) %collective-permute-start.2) | collective-permute-done | bytes 155680 | tf_op jit(solution)/shard_map/ppermute | solution.py:543
  23.5 2.5 %collective-permute-done.3.high_corners = f32[304,128]{1,0:T(8,128)S(1)} collective-permute-done((f32[304,128]{1,0:T(8,128)S(1)}, f32[304,128]{1,0:T(8,128)S(1)}, u32[]{:S(2)}, u32[]{:S(2)}) %collective-permute-start.3) | collective-permute-done | bytes 155680 | tf_op jit(solution)/shard_map/ppermute | solution.py:543
  25.9 1.5 %shard_map.45 = (f32[16,40,128]{2,1,0:T(8,128)S(1)}, f32[10,4,24,128]{3,2,1,0:T(8,128)S(1)}, f32[1152,128]{1,0:T(8,128)S(1)}, f32[1536,128]{1,0:T(8,128)S(1)}, f...) custom-call(s32[1]{0:T(128)} %bitcast.1.me, f32[1408,128]{1,0:T(8,128)S(1)} %get-tuple-element.53.wide, ...), custom_call_target="tpu_custom_call" | custom-call | tf_op jit(solution)/shard_map/pallas_call | solution.py:531
  27.4 10.3 %all_to_all.5.gathered = f32[16,40,128]{2,1,0:T(8,128)S(1)} all-to-all(f32[16,40,128]{2,1,0:T(8,128)S(1)} %get-tuple-element.67), channel_id=1, replica_groups=mesh['gx'=16,'gy'=32] {'gx'}, dimensions={0} | all-to-all | bytes 655360 | tf_op jit(solution)/shard_map/all_to_all | solution.py:583
  37.7 2.1 %collective-permute-start.6 = (f32[136,128]{1,0:T(8,128)S(1)}, f32[136,128]{1,0:T(8,128)S(1)}, u32[]{:S(2)}, u32[]{:S(2)}) collective-permute-start(f32[136,128]{1,0:T(8,128)S(1)} %get-tuple-element.77), channel_id=1, source_target_pairs={{0,1},{1,2},{2,3},{3,4},{4,5},{5,6},{6,7},{7,8},{8,9},{9,10},{10,1... | collective-permute-start | bytes 208904 | tf_op jit(solution)/shard_map/ppermute | solution.py:543
  39.8 4.2 %collective-permute-start.7 = (f32[136,128]{1,0:T(8,128)S(1)}, f32[136,128]{1,0:T(8,128)S(1)}, u32[]{:S(2)}, u32[]{:S(2)}) collective-permute-start(f32[136,128]{1,0:T(8,128)S(1)} %get-tuple-element.78), channel_id=1, source_target_pairs={{0,31},{1,0},{2,1},{3,2},{4,3},{5,4},{6,5},{7,6},{8,7},{9,8},{10,9... | collective-permute-start | bytes 208904 | tf_op jit(solution)/shard_map/ppermute | solution.py:543
  44.0 0.7 %collective-permute-done.6.low.left = f32[136,128]{1,0:T(8,128)S(1)} collective-permute-done((f32[136,128]{1,0:T(8,128)S(1)}, f32[136,128]{1,0:T(8,128)S(1)}, u32[]{:S(2)}, u32[]{:S(2)}) %collective-permute-start.6) | collective-permute-done | bytes 69664 | tf_op jit(solution)/shard_map/ppermute | solution.py:543
  44.9 1.9 %collective-permute-start.8 = (f32[136,128]{1,0:T(8,128)S(1)}, f32[136,128]{1,0:T(8,128)S(1)}, u32[]{:S(2)}, u32[]{:S(2)}) collective-permute-start(f32[136,128]{1,0:T(8,128)S(1)} %get-tuple-element.79), channel_id=1, source_target_pairs={{1,4},{3,6},{5,8},{7,10},{9,12},{11,14},{13,16},{15,18},{17,20},{1... | collective-permute-start | bytes 208904 | tf_op jit(solution)/shard_map/ppermute | solution.py:549
  46.9 11.5 %collective-permute-start.9 = (f32[136,128]{1,0:T(8,128)S(1)}, f32[136,128]{1,0:T(8,128)S(1)}, u32[]{:S(2)}, u32[]{:S(2)}) collective-permute-start(f32[136,128]{1,0:T(8,128)S(1)} %get-tuple-element.80), channel_id=1, source_target_pairs={{0,3},{2,5},{4,7},{6,9},{8,11},{10,13},{12,15},{14,17},{16,19},{18... | collective-permute-start | bytes 208904 | tf_op jit(solution)/shard_map/ppermute | solution.py:549
  58.7 1.7 %collective-permute-done.9.second = f32[136,128]{1,0:T(8,128)S(1)} collective-permute-done((f32[136,128]{1,0:T(8,128)S(1)}, f32[136,128]{1,0:T(8,128)S(1)}, u32[]{:S(2)}, u32[]{:S(2)}) %collective-permute-start.9) | collective-permute-done | bytes 69664 | tf_op jit(solution)/shard_map/ppermute | solution.py:549
  60.4 1.0 %shard_map.49 = (f32[128,128]{1,0:T(8,128)S(1)}, f32[32,128]{1,0:T(8,128)S(1)}, f32[32,128]{1,0:T(8,128)S(1)}) custom-call(s32[1]{0:T(128)} %bitcast.me, f32[136,128]{1,0:T(8,128)S(1)} %collective-permute-done.8.first, f32[4,24,128]{2,1,0:T(8,128)S(1)} %get-tuple-element.76.here, f32[136,128]{1,0:T(8,128)S(1)} %collective-permute-done.9.second, ...), custom_call_target="tpu_custom_call" | custom-call | tf_op jit(solution)/shard_map/pallas_call | solution.py:531
  61.6 0.4 collective-permute-start.11
  62.0 0.3 shard_map.50
  62.2 0.4 collective-permute-done.10.v_low
  62.6 2.4 %collective-permute-done.11.v_high = f32[32,128]{1,0:T(8,128)S(1)} collective-permute-done((f32[32,128]{1,0:T(8,128)S(1)}, f32[32,128]{1,0:T(8,128)S(1)}, u32[]{:S(2)}, u32[]{:S(2)}) %collective-permute-start.11) | collective-permute-done | bytes 16416 | tf_op jit(solution)/shard_map/ppermute | solution.py:543
  65.0 1.8 %shard_map.51 = (f32[8,8,512]{2,1,0:T(8,128)}, f32[8,8,512]{2,1,0:T(8,128)}) custom-call(f32[128,128]{1,0:T(8,128)S(1)} %get-tuple-element.87.v_here, f32[32,128]{1,0:T(8,128)S(1)} %collective-permute-done.10.v_low, f32[32,128]{1,0:T(8,128)S(1)} %collective-permute-done.11.v_high, f32[14,4,16,128]{3,2,1,0:T(8,128)S(1)} %get-tuple-element.92.u0, ...), custom_call_target="tpu_custom_call" | custom-call | tf_op jit(solution)/shard_map/pallas_call | solution.py:531
  (13 shorter events, 1.0 us)
Async XLA Ops:
  2.0 12.2 %collective-permute-start = (f32[14,4,8,128]{3,2,1,0:T(8,128)S(1)}, f32[14,4,8,128]{3,2,1,0:T(8,128)S(1)}, u32[]{:S(2)}, u32[]{:S(2)}) collective-permute-start(f32[14,4,8,128]{3,2,1,0:T(8,128)S(1)} %get-tuple-element.51), channel_id=1, source_target_pairs={{32,64},{96,128},{160,192},{224,256},{288,320},{352,384},{416,448}... | collective-permute-start | bytes 688136 | tf_op jit(solution)/shard_map/ppermute | solution.py:549
  9.7 7.8 %collective-permute-start.1 = (f32[14,4,8,128]{3,2,1,0:T(8,128)S(1)}, f32[14,4,8,128]{3,2,1,0:T(8,128)S(1)}, u32[]{:S(2)}, u32[]{:S(2)}) collective-permute-start(f32[14,4,8,128]{3,2,1,0:T(8,128)S(1)} %get-tuple-element.52), channel_id=1, source_target_pairs={{0,32},{64,96},{128,160},{192,224},{256,288},{320,352},{384,416},{... | collective-permute-start | bytes 688136 | tf_op jit(solution)/shard_map/ppermute | solution.py:549
  11.7 9.8 %collective-permute-start.4 = (f32[416,128]{1,0:T(8,128)S(1)}, f32[416,128]{1,0:T(8,128)S(1)}, u32[]{:S(2)}, u32[]{:S(2)}) collective-permute-start(f32[416,128]{1,0:T(8,128)S(1)} %get-tuple-element.56), channel_id=1, source_target_pairs={{0,1},{1,2},{2,3},{3,4},{4,5},{5,6},{6,7},{7,8},{8,9},{9,10},{10,1... | collective-permute-start | bytes 638984 | tf_op jit(solution)/shard_map/ppermute | solution.py:543
  14.2 7.3 %collective-permute-start.5 = (f32[416,128]{1,0:T(8,128)S(1)}, f32[416,128]{1,0:T(8,128)S(1)}, u32[]{:S(2)}, u32[]{:S(2)}) collective-permute-start(f32[416,128]{1,0:T(8,128)S(1)} %get-tuple-element.57), channel_id=1, source_target_pairs={{0,31},{1,0},{2,1},{3,2},{4,3},{5,4},{6,5},{7,6},{8,7},{9,8},{10,9... | collective-permute-start | bytes 638984 | tf_op jit(solution)/shard_map/ppermute | solution.py:543
  17.7 5.8 %collective-permute-start.2 = (f32[304,128]{1,0:T(8,128)S(1)}, f32[304,128]{1,0:T(8,128)S(1)}, u32[]{:S(2)}, u32[]{:S(2)}) collective-permute-start(f32[304,128]{1,0:T(8,128)S(1)} %get-tuple-element.54), channel_id=1, source_target_pairs={{0,1},{1,2},{2,3},{3,4},{4,5},{5,6},{6,7},{7,8},{8,9},{9,10},{10,1... | collective-permute-start | bytes 466952 | tf_op jit(solution)/shard_map/ppermute | solution.py:543
  21.3 4.7 %collective-permute-start.3 = (f32[304,128]{1,0:T(8,128)S(1)}, f32[304,128]{1,0:T(8,128)S(1)}, u32[]{:S(2)}, u32[]{:S(2)}) collective-permute-start(f32[304,128]{1,0:T(8,128)S(1)} %get-tuple-element.55), channel_id=1, source_target_pairs={{0,31},{1,0},{2,1},{3,2},{4,3},{5,4},{6,5},{7,6},{8,7},{9,8},{10,9... | collective-permute-start | bytes 466952 | tf_op jit(solution)/shard_map/ppermute | solution.py:543
  37.7 7.0 %collective-permute-start.6 = (f32[136,128]{1,0:T(8,128)S(1)}, f32[136,128]{1,0:T(8,128)S(1)}, u32[]{:S(2)}, u32[]{:S(2)}) collective-permute-start(f32[136,128]{1,0:T(8,128)S(1)} %get-tuple-element.77), channel_id=1, source_target_pairs={{0,1},{1,2},{2,3},{3,4},{4,5},{5,6},{6,7},{7,8},{8,9},{9,10},{10,1... | collective-permute-start | bytes 208904 | tf_op jit(solution)/shard_map/ppermute | solution.py:543
  39.8 5.1 %collective-permute-start.7 = (f32[136,128]{1,0:T(8,128)S(1)}, f32[136,128]{1,0:T(8,128)S(1)}, u32[]{:S(2)}, u32[]{:S(2)}) collective-permute-start(f32[136,128]{1,0:T(8,128)S(1)} %get-tuple-element.78), channel_id=1, source_target_pairs={{0,31},{1,0},{2,1},{3,2},{4,3},{5,4},{6,5},{7,6},{8,7},{9,8},{10,9... | collective-permute-start | bytes 208904 | tf_op jit(solution)/shard_map/ppermute | solution.py:543
  44.9 13.7 %collective-permute-start.8 = (f32[136,128]{1,0:T(8,128)S(1)}, f32[136,128]{1,0:T(8,128)S(1)}, u32[]{:S(2)}, u32[]{:S(2)}) collective-permute-start(f32[136,128]{1,0:T(8,128)S(1)} %get-tuple-element.79), channel_id=1, source_target_pairs={{1,4},{3,6},{5,8},{7,10},{9,12},{11,14},{13,16},{15,18},{17,20},{1... | collective-permute-start | bytes 208904 | tf_op jit(solution)/shard_map/ppermute | solution.py:549
  46.9 13.5 %collective-permute-start.9 = (f32[136,128]{1,0:T(8,128)S(1)}, f32[136,128]{1,0:T(8,128)S(1)}, u32[]{:S(2)}, u32[]{:S(2)}) collective-permute-start(f32[136,128]{1,0:T(8,128)S(1)} %get-tuple-element.80), channel_id=1, source_target_pairs={{0,3},{2,5},{4,7},{6,9},{8,11},{10,13},{12,15},{14,17},{16,19},{18... | collective-permute-start | bytes 208904 | tf_op jit(solution)/shard_map/ppermute | solution.py:549
  61.4 1.2 %collective-permute-start.10 = (f32[32,128]{1,0:T(8,128)S(1)}, f32[32,128]{1,0:T(8,128)S(1)}, u32[]{:S(2)}, u32[]{:S(2)}) collective-permute-start(f32[32,128]{1,0:T(8,128)S(1)} %get-tuple-element.88), channel_id=1, source_target_pairs={{0,1},{1,2},{2,3},{3,4},{4,5},{5,6},{6,7},{7,8},{8,9},{9,10},{10,1... | collective-permute-start | bytes 49160 | tf_op jit(solution)/shard_map/ppermute | solution.py:543
  61.6 3.5 %collective-permute-start.11 = (f32[32,128]{1,0:T(8,128)S(1)}, f32[32,128]{1,0:T(8,128)S(1)}, u32[]{:S(2)}, u32[]{:S(2)}) collective-permute-start(f32[32,128]{1,0:T(8,128)S(1)} %get-tuple-element.89), channel_id=1, source_target_pairs={{0,31},{1,0},{2,1},{3,2},{4,3},{5,4},{6,5},{7,6},{8,7},{9,8},{10,9... | collective-permute-start | bytes 49160 | tf_op jit(solution)/shard_map/ppermute | solution.py:543

commit v8 on v7

--- a/solution.py
+++ b/solution.py
@@ -1,5 +1,7 @@
 import jax
 import jax.numpy as jnp
+import ml_dtypes
+import numpy as np
 from jax import lax
 from jax.experimental import pallas as pl
 from jax.experimental.pallas import tpu as pltpu
@@ -134,6 +136,11 @@
         low_rows = some
         rest = get(g_ref, g_at + i, some) - applied
         put(out, out_at + i, some, rest if last else u + get(w, f, some) * rest)
+
+
+def inverse_permutation():
+    z, at = np.arange(512)[None, :], np.arange(512)[:, None]
+    return jnp.asarray((z == 4 * (at % LANES) + at // LANES).astype(ml_dtypes.bfloat16))
 
 
 def permutation(inverse):
@@ -489,7 +496,7 @@
             out[16 * i : 16 * i + 16] = v_flat_out[pl.ds(row + i, 16, 8), :]
 
 
-def last_kernel(v_here, v_low, v_high, u0, g, fx, fy, fz, w, correction, residual, v_flat, wide, ua, ub, res, held, left):
+def last_kernel(v_here, v_low, v_high, u0, g, fx, fy, fz, w, matrix, correction, residual, v_flat, wide, ua, ub, res, held, left):
     v_flat[...] = v_here[...]
     for source, row in ((v_low, 0), (v_high, 6)):
         for i in range(2):
@@ -504,22 +511,25 @@
         ua[i] = u0[i] + jnp.stack([fine[0], fine[0], fine[1], fine[1]])
     sweep_pass(12, ua, 0, 0, g, 0, fx, fy, fz, w, ub, 0)
     sweep_pass(10, ub, 0, 1, g, 1, fx, fy, fz, w, ua, 0)
-    matrix = permutation(True)
-
-    def leave(index, source, at, out):
+    copies = []
+
+    def leave(index, source, at, out, start, size):
         rows = [
-            jnp.concatenate([source[at + x, r, 4:12, :] for r in range(4)], axis=1) for x in range(8)
+            jnp.concatenate([source[at + x, r, 4:12, :] for r in range(4)], axis=1) for x in range(start, start + size)
         ]
-        held[index] = rearrange(jnp.concatenate(rows, axis=0), matrix).reshape(8, 8, 512)
-        copy = pltpu.make_async_copy(held.at[index], out, left.at[index])
+        held[index, start : start + size] = rearrange(jnp.concatenate(rows, axis=0), matrix[...]).reshape(size, 8, 512)
+        part = pl.ds(start, size)
+        copy = pltpu.make_async_copy(held.at[index, part], out.at[part], left.at[len(copies)])
         copy.start()
-        return copy
-
-    first = leave(0, ua, 1, correction)
-    sweep_pass(8, ua, 0, 2, g, 2, fx, fy, fz, w, res, 0, last=True)
-    second = leave(1, res, 0, residual)
-    first.wait()
-    second.wait()
+        copies.append(copy)
+
+    leave(0, ua, 1, correction, 0, 8)
+    sweep_pass(4, ua, 0, 2, g, 2, fx, fy, fz, w, res, 0, last=True)
+    leave(1, res, 0, residual, 0, 4)
+    sweep_pass(4, ua, 4, 6, g, 6, fx, fy, fz, w, res, 4, last=True)
+    leave(1, res, 0, residual, 4, 4)
+    for copy in copies:
+        copy.wait()
 
 
 VMEM = pl.BlockSpec(memory_space=pltpu.VMEM)
@@ -605,7 +615,7 @@
     return tuple(call(
         last_kernel, [(8, 8, 512), (8, 8, 512)],
         [(128, 128), (8, 2, 16, 128), (14, *last), (12, *last), (8, *last), (2, 8, 8, 512)],
-        v1, low, high, u0, g, *faces, to_hbm=True, extra=[pltpu.SemaphoreType.DMA((2,))],
+        v1, low, high, u0, g, *faces, inverse_permutation(), to_hbm=True, extra=[pltpu.SemaphoreType.DMA((3,))],
     ))
 
 

time: 67.1 us -> 66.9 us (level)
  no operation moved by 1% of the time
where the time goes in v8:
time: 66.9 us; the launch traced here: 66.7 us
  starting transfers between devices  36.2 us (54%)
  waiting for transfers between devices  12.7 us (19%)
  blocking collectives  10.3 us (15%)
  Pallas kernels  5.83 us (9%)
  other arithmetic  0.99 us (1%)
  between operations  0.73 us (1%)
    ppermute x4, starting transfers between devices, swap(): return lax.ppermute(array, axis, pairs + [(j, i) for i, j in pairs])  23 us
    ppermute x8, starting transfers between devices, shift(): lax.ppermute(array, axis, [(i, (i + by) % count) for i in range(count)])  13.1 us
    all_to_all x1, blocking collectives, per_device(): gathered = lax.all_to_all(piece, 'gx', 0, 0)  10.3 us
    ppermute x8, waiting for transfers between devices, shift(): lax.ppermute(array, axis, [(i, (i + by) % count) for i in range(count)])  7.58 us
    pallas_call x11, Pallas kernels, call(): pl.pallas_call(kernel, out_shape=[jax.ShapeDtypeStruct(shape, F32) for sh...  5.83 us
    ppermute x4, waiting for transfers between devices, swap(): return lax.ppermute(array, axis, pairs + [(j, i) for i, j in pairs])  5.1 us
  transfers between devices with their start and end apart: 12, of which 8 were waited for; matrix products, arithmetic and copies ran while one was open for 0% of the time, Pallas kernels for 2%

profile of v8, /device:TPU:1, one launch (start us, length us, event | category | flops | bytes accessed | tf_op | source)
XLA Modules:
  0.0 66.7 jit_solution(11866254410762935480)
XLA Ops:
  0.6 1.0 %pad_maximum_fusion.held = f32[2,8,8,512]{3,2,1,0:T(8,128)S(1)} fusion(f32[1,8,8,512]{3,2,1,0:T(8,128)} %bitcast.4, f32[1,8,8,512]{3,2,1,0:T(8,128)} %bitcast.5), kind=kLoop, calls=%fused_computation | loop fusion | flops 65536 | bytes 524288 | tf_op jit(solution)/shard_map/stack | solution.py:568
  1.6 0.4 shard_map.50
  2.0 7.7 %collective-permute-start = (f32[14,4,8,128]{3,2,1,0:T(8,128)S(1)}, f32[14,4,8,128]{3,2,1,0:T(8,128)S(1)}, u32[]{:S(2)}, u32[]{:S(2)}) collective-permute-start(f32[14,4,8,128]{3,2,1,0:T(8,128)S(1)} %get-tuple-element.51), channel_id=1, source_target_pairs={{32,64},{96,128},{160,192},{224,256},{288,320},{352,384},{416,448}... | collective-permute-start | bytes 688136 | tf_op jit(solution)/shard_map/ppermute | solution.py:559
  9.7 1.9 %collective-permute-start.1 = (f32[14,4,8,128]{3,2,1,0:T(8,128)S(1)}, f32[14,4,8,128]{3,2,1,0:T(8,128)S(1)}, u32[]{:S(2)}, u32[]{:S(2)}) collective-permute-start(f32[14,4,8,128]{3,2,1,0:T(8,128)S(1)} %get-tuple-element.52), channel_id=1, source_target_pairs={{0,32},{64,96},{128,160},{192,224},{256,288},{320,352},{384,416},{... | collective-permute-start | bytes 688136 | tf_op jit(solution)/shard_map/ppermute | solution.py:559
  11.7 2.5 %collective-permute-start.4 = (f32[416,128]{1,0:T(8,128)S(1)}, f32[416,128]{1,0:T(8,128)S(1)}, u32[]{:S(2)}, u32[]{:S(2)}) collective-permute-start(f32[416,128]{1,0:T(8,128)S(1)} %get-tuple-element.56), channel_id=1, source_target_pairs={{0,1},{1,2},{2,3},{3,4},{4,5},{5,6},{6,7},{7,8},{8,9},{9,10},{10,1... | collective-permute-start | bytes 638984 | tf_op jit(solution)/shard_map/ppermute | solution.py:553
  14.2 3.4 %collective-permute-done.1.second = f32[14,4,8,128]{3,2,1,0:T(8,128)S(1)} collective-permute-done((f32[14,4,8,128]{3,2,1,0:T(8,128)S(1)}, f32[14,4,8,128]{3,2,1,0:T(8,128)S(1)}, u32[]{:S(2)}, u32[]{:S(2)}) %collective-permute-start.1) | collective-permute-done | bytes 229408 | tf_op jit(solution)/shard_map/ppermute | solution.py:559
  17.7 3.6 %collective-permute-start.2 = (f32[304,128]{1,0:T(8,128)S(1)}, f32[304,128]{1,0:T(8,128)S(1)}, u32[]{:S(2)}, u32[]{:S(2)}) collective-permute-start(f32[304,128]{1,0:T(8,128)S(1)} %get-tuple-element.54), channel_id=1, source_target_pairs={{0,1},{1,2},{2,3},{3,4},{4,5},{5,6},{6,7},{7,8},{8,9},{9,10},{10,1... | collective-permute-start | bytes 466952 | tf_op jit(solution)/shard_map/ppermute | solution.py:553
  21.5 0.5 shard_map.53
  22.1 1.4 %collective-permute-done.2.low_corners = f32[304,128]{1,0:T(8,128)S(1)} collective-permute-done((f32[304,128]{1,0:T(8,128)S(1)}, f32[304,128]{1,0:T(8,128)S(1)}, u32[]{:S(2)}, u32[]{:S(2)}) %collective-permute-start.2) | collective-permute-done | bytes 155680 | tf_op jit(solution)/shard_map/ppermute | solution.py:553
  23.5 2.5 %collective-permute-done.3.high_corners = f32[304,128]{1,0:T(8,128)S(1)} collective-permute-done((f32[304,128]{1,0:T(8,128)S(1)}, f32[304,128]{1,0:T(8,128)S(1)}, u32[]{:S(2)}, u32[]{:S(2)}) %collective-permute-start.3) | collective-permute-done | bytes 155680 | tf_op jit(solution)/shard_map/ppermute | solution.py:553
  25.9 1.5 %shard_map.54 = (f32[16,40,128]{2,1,0:T(8,128)S(1)}, f32[10,4,24,128]{3,2,1,0:T(8,128)S(1)}, f32[1152,128]{1,0:T(8,128)S(1)}, f32[1536,128]{1,0:T(8,128)S(1)}, f...) custom-call(s32[1]{0:T(128)} %bitcast.1.me, f32[1408,128]{1,0:T(8,128)S(1)} %get-tuple-element.53.wide, ...), custom_call_target="tpu_custom_call" | custom-call | tf_op jit(solution)/shard_map/pallas_call | solution.py:541
  27.4 10.3 %all_to_all.5.gathered = f32[16,40,128]{2,1,0:T(8,128)S(1)} all-to-all(f32[16,40,128]{2,1,0:T(8,128)S(1)} %get-tuple-element.67), channel_id=1, replica_groups=mesh['gx'=16,'gy'=32] {'gx'}, dimensions={0} | all-to-all | bytes 655360 | tf_op jit(solution)/shard_map/all_to_all | solution.py:593
  37.7 2.1 %collective-permute-start.6 = (f32[136,128]{1,0:T(8,128)S(1)}, f32[136,128]{1,0:T(8,128)S(1)}, u32[]{:S(2)}, u32[]{:S(2)}) collective-permute-start(f32[136,128]{1,0:T(8,128)S(1)} %get-tuple-element.77), channel_id=1, source_target_pairs={{0,1},{1,2},{2,3},{3,4},{4,5},{5,6},{6,7},{7,8},{8,9},{9,10},{10,1... | collective-permute-start | bytes 208904 | tf_op jit(solution)/shard_map/ppermute | solution.py:553
  39.8 4.2 %collective-permute-start.7 = (f32[136,128]{1,0:T(8,128)S(1)}, f32[136,128]{1,0:T(8,128)S(1)}, u32[]{:S(2)}, u32[]{:S(2)}) collective-permute-start(f32[136,128]{1,0:T(8,128)S(1)} %get-tuple-element.78), channel_id=1, source_target_pairs={{0,31},{1,0},{2,1},{3,2},{4,3},{5,4},{6,5},{7,6},{8,7},{9,8},{10,9... | collective-permute-start | bytes 208904 | tf_op jit(solution)/shard_map/ppermute | solution.py:553
  44.0 0.7 %collective-permute-done.6.low.left = f32[136,128]{1,0:T(8,128)S(1)} collective-permute-done((f32[136,128]{1,0:T(8,128)S(1)}, f32[136,128]{1,0:T(8,128)S(1)}, u32[]{:S(2)}, u32[]{:S(2)}) %collective-permute-start.6) | collective-permute-done | bytes 69664 | tf_op jit(solution)/shard_map/ppermute | solution.py:553
  44.9 1.9 %collective-permute-start.8 = (f32[136,128]{1,0:T(8,128)S(1)}, f32[136,128]{1,0:T(8,128)S(1)}, u32[]{:S(2)}, u32[]{:S(2)}) collective-permute-start(f32[136,128]{1,0:T(8,128)S(1)} %get-tuple-element.79), channel_id=1, source_target_pairs={{1,4},{3,6},{5,8},{7,10},{9,12},{11,14},{13,16},{15,18},{17,20},{1... | collective-permute-start | bytes 208904 | tf_op jit(solution)/shard_map/ppermute | solution.py:559
  46.9 11.5 %collective-permute-start.9 = (f32[136,128]{1,0:T(8,128)S(1)}, f32[136,128]{1,0:T(8,128)S(1)}, u32[]{:S(2)}, u32[]{:S(2)}) collective-permute-start(f32[136,128]{1,0:T(8,128)S(1)} %get-tuple-element.80), channel_id=1, source_target_pairs={{0,3},{2,5},{4,7},{6,9},{8,11},{10,13},{12,15},{14,17},{16,19},{18... | collective-permute-start | bytes 208904 | tf_op jit(solution)/shard_map/ppermute | solution.py:559
  58.7 1.7 %collective-permute-done.9.second = f32[136,128]{1,0:T(8,128)S(1)} collective-permute-done((f32[136,128]{1,0:T(8,128)S(1)}, f32[136,128]{1,0:T(8,128)S(1)}, u32[]{:S(2)}, u32[]{:S(2)}) %collective-permute-start.9) | collective-permute-done | bytes 69664 | tf_op jit(solution)/shard_map/ppermute | solution.py:559
  60.4 1.0 %shard_map.58 = (f32[128,128]{1,0:T(8,128)S(1)}, f32[32,128]{1,0:T(8,128)S(1)}, f32[32,128]{1,0:T(8,128)S(1)}) custom-call(s32[1]{0:T(128)} %bitcast.me, f32[136,128]{1,0:T(8,128)S(1)} %collective-permute-done.8.first, f32[4,24,128]{2,1,0:T(8,128)S(1)} %get-tuple-element.76.here, f32[136,128]{1,0:T(8,128)S(1)} %collective-permute-done.9.second, ...), custom_call_target="tpu_custom_call" | custom-call | tf_op jit(solution)/shard_map/pallas_call | solution.py:541
  61.6 0.4 collective-permute-start.11
  62.0 0.3 shard_map.59
  62.2 0.4 collective-permute-done.10.v_low
  62.6 2.4 %collective-permute-done.11.v_high = f32[32,128]{1,0:T(8,128)S(1)} collective-permute-done((f32[32,128]{1,0:T(8,128)S(1)}, f32[32,128]{1,0:T(8,128)S(1)}, u32[]{:S(2)}, u32[]{:S(2)}) %collective-permute-start.11) | collective-permute-done | bytes 16416 | tf_op jit(solution)/shard_map/ppermute | solution.py:553
  65.0 1.6 %shard_map.60 = (f32[8,8,512]{2,1,0:T(8,128)}, f32[8,8,512]{2,1,0:T(8,128)}) custom-call(f32[128,128]{1,0:T(8,128)S(1)} %get-tuple-element.87.v_here, f32[32,128]{1,0:T(8,128)S(1)} %collective-permute-done.10.v_low, f32[32,128]{1,0:T(8,128)S(1)} %collective-permute-done.11.v_high, f32[14,4,16,128]{3,2,1,0:T(8,128)S(1)} %get-tuple-element.92.u0, ...), custom_call_target="tpu_custom_call" | custom-call | tf_op jit(solution)/shard_map/pallas_call | solution.py:541
  (15 shorter events, 1.0 us)
Async XLA Ops:
  2.0 12.2 %collective-permute-start = (f32[14,4,8,128]{3,2,1,0:T(8,128)S(1)}, f32[14,4,8,128]{3,2,1,0:T(8,128)S(1)}, u32[]{:S(2)}, u32[]{:S(2)}) collective-permute-start(f32[14,4,8,128]{3,2,1,0:T(8,128)S(1)} %get-tuple-element.51), channel_id=1, source_target_pairs={{32,64},{96,128},{160,192},{224,256},{288,320},{352,384},{416,448}... | collective-permute-start | bytes 688136 | tf_op jit(solution)/shard_map/ppermute | solution.py:559
  9.7 7.8 %collective-permute-start.1 = (f32[14,4,8,128]{3,2,1,0:T(8,128)S(1)}, f32[14,4,8,128]{3,2,1,0:T(8,128)S(1)}, u32[]{:S(2)}, u32[]{:S(2)}) collective-permute-start(f32[14,4,8,128]{3,2,1,0:T(8,128)S(1)} %get-tuple-element.52), channel_id=1, source_target_pairs={{0,32},{64,96},{128,160},{192,224},{256,288},{320,352},{384,416},{... | collective-permute-start | bytes 688136 | tf_op jit(solution)/shard_map/ppermute | solution.py:559
  11.7 9.8 %collective-permute-start.4 = (f32[416,128]{1,0:T(8,128)S(1)}, f32[416,128]{1,0:T(8,128)S(1)}, u32[]{:S(2)}, u32[]{:S(2)}) collective-permute-start(f32[416,128]{1,0:T(8,128)S(1)} %get-tuple-element.56), channel_id=1, source_target_pairs={{0,1},{1,2},{2,3},{3,4},{4,5},{5,6},{6,7},{7,8},{8,9},{9,10},{10,1... | collective-permute-start | bytes 638984 | tf_op jit(solution)/shard_map/ppermute | solution.py:553
  14.2 7.3 %collective-permute-start.5 = (f32[416,128]{1,0:T(8,128)S(1)}, f32[416,128]{1,0:T(8,128)S(1)}, u32[]{:S(2)}, u32[]{:S(2)}) collective-permute-start(f32[416,128]{1,0:T(8,128)S(1)} %get-tuple-element.57), channel_id=1, source_target_pairs={{0,31},{1,0},{2,1},{3,2},{4,3},{5,4},{6,5},{7,6},{8,7},{9,8},{10,9... | collective-permute-start | bytes 638984 | tf_op jit(solution)/shard_map/ppermute | solution.py:553
  17.7 5.8 %collective-permute-start.2 = (f32[304,128]{1,0:T(8,128)S(1)}, f32[304,128]{1,0:T(8,128)S(1)}, u32[]{:S(2)}, u32[]{:S(2)}) collective-permute-start(f32[304,128]{1,0:T(8,128)S(1)} %get-tuple-element.54), channel_id=1, source_target_pairs={{0,1},{1,2},{2,3},{3,4},{4,5},{5,6},{6,7},{7,8},{8,9},{9,10},{10,1... | collective-permute-start | bytes 466952 | tf_op jit(solution)/shard_map/ppermute | solution.py:553
  21.3 4.7 %collective-permute-start.3 = (f32[304,128]{1,0:T(8,128)S(1)}, f32[304,128]{1,0:T(8,128)S(1)}, u32[]{:S(2)}, u32[]{:S(2)}) collective-permute-start(f32[304,128]{1,0:T(8,128)S(1)} %get-tuple-element.55), channel_id=1, source_target_pairs={{0,31},{1,0},{2,1},{3,2},{4,3},{5,4},{6,5},{7,6},{8,7},{9,8},{10,9... | collective-permute-start | bytes 466952 | tf_op jit(solution)/shard_map/ppermute | solution.py:553
  37.7 7.0 %collective-permute-start.6 = (f32[136,128]{1,0:T(8,128)S(1)}, f32[136,128]{1,0:T(8,128)S(1)}, u32[]{:S(2)}, u32[]{:S(2)}) collective-permute-start(f32[136,128]{1,0:T(8,128)S(1)} %get-tuple-element.77), channel_id=1, source_target_pairs={{0,1},{1,2},{2,3},{3,4},{4,5},{5,6},{6,7},{7,8},{8,9},{9,10},{10,1... | collective-permute-start | bytes 208904 | tf_op jit(solution)/shard_map/ppermute | solution.py:553
  39.8 5.1 %collective-permute-start.7 = (f32[136,128]{1,0:T(8,128)S(1)}, f32[136,128]{1,0:T(8,128)S(1)}, u32[]{:S(2)}, u32[]{:S(2)}) collective-permute-start(f32[136,128]{1,0:T(8,128)S(1)} %get-tuple-element.78), channel_id=1, source_target_pairs={{0,31},{1,0},{2,1},{3,2},{4,3},{5,4},{6,5},{7,6},{8,7},{9,8},{10,9... | collective-permute-start | bytes 208904 | tf_op jit(solution)/shard_map/ppermute | solution.py:553
  44.9 13.7 %collective-permute-start.8 = (f32[136,128]{1,0:T(8,128)S(1)}, f32[136,128]{1,0:T(8,128)S(1)}, u32[]{:S(2)}, u32[]{:S(2)}) collective-permute-start(f32[136,128]{1,0:T(8,128)S(1)} %get-tuple-element.79), channel_id=1, source_target_pairs={{1,4},{3,6},{5,8},{7,10},{9,12},{11,14},{13,16},{15,18},{17,20},{1... | collective-permute-start | bytes 208904 | tf_op jit(solution)/shard_map/ppermute | solution.py:559
  46.9 13.5 %collective-permute-start.9 = (f32[136,128]{1,0:T(8,128)S(1)}, f32[136,128]{1,0:T(8,128)S(1)}, u32[]{:S(2)}, u32[]{:S(2)}) collective-permute-start(f32[136,128]{1,0:T(8,128)S(1)} %get-tuple-element.80), channel_id=1, source_target_pairs={{0,3},{2,5},{4,7},{6,9},{8,11},{10,13},{12,15},{14,17},{16,19},{18... | collective-permute-start | bytes 208904 | tf_op jit(solution)/shard_map/ppermute | solution.py:559
  61.4 1.2 %collective-permute-start.10 = (f32[32,128]{1,0:T(8,128)S(1)}, f32[32,128]{1,0:T(8,128)S(1)}, u32[]{:S(2)}, u32[]{:S(2)}) collective-permute-start(f32[32,128]{1,0:T(8,128)S(1)} %get-tuple-element.88), channel_id=1, source_target_pairs={{0,1},{1,2},{2,3},{3,4},{4,5},{5,6},{6,7},{7,8},{8,9},{9,10},{10,1... | collective-permute-start | bytes 49160 | tf_op jit(solution)/shard_map/ppermute | solution.py:553
  61.6 3.5 %copy-start = (bf16[512,512]{1,0:T(8,128)(2,1)S(1)}, bf16[512,512]{1,0:T(8,128)(2,1)}, u32[]{:S(2)}) copy-start(bf16[512,512]{1,0:T(8,128)(2,1)} %constant.11.clone.matrix) | copy-start | bytes 1572868
  61.6 3.5 %collective-permute-start.11 = (f32[32,128]{1,0:T(8,128)S(1)}, f32[32,128]{1,0:T(8,128)S(1)}, u32[]{:S(2)}, u32[]{:S(2)}) collective-permute-start(f32[32,128]{1,0:T(8,128)S(1)} %get-tuple-element.89), channel_id=1, source_target_pairs={{0,31},{1,0},{2,1},{3,2},{4,3},{5,4},{6,5},{7,6},{8,7},{9,8},{10,9... | collective-permute-start | bytes 49160 | tf_op jit(solution)/shard_map/ppermute | solution.py:553

commit v9 on v8

--- a/solution.py
+++ b/solution.py
@@ -192,7 +192,7 @@
 
 
 FACE_ROWS = 32 * (len(G_REACH) + len(K_REACH))
-CORNER_ROWS = 8 * (sum(G_REACH) + sum(K_REACH))
+CORNER_ROWS = 8 * (sum(G_REACH) + sum(K_REACH)) + 8
 
 
 def face_kernel(own, to_high, to_low):
@@ -251,7 +251,7 @@
 
 def fine_kernel(me, wide, low_corners, high_corners, g_early, k_early, fx_early, fy_early, fz_early, w_early, uf_early,
                 u0_early, res_early, piece, u0_kept, g_flat, k_flat, u1, rhs, u0_edge, fx, fy, fz, w, uf, res, s1, sc,
-                mx, my, mz, mw, mf, mr, ck):
+                mx, my, mz, mw, mf, mr, ck, near):
     flats = g_flat, k_flat
     wide, g, k = Slabs(wide, 8), Slabs(g_flat, 24), Slabs(k_flat, 24)
     for i in range(12):
@@ -310,7 +310,7 @@
     sweep_pass(4, u1, 0, 2, rhs, 2, mx, my, mz, mw, mr, 0, last=True)
     for x in range(4):
         both = k_mid[2 * x + 1] + k_mid[2 * x + 2]
-        ck[x] = both[0] + both[1]
+        ck[x, 0:8] = both[0] + both[1]
     k2 = [(ck[x, pl.ds(0, 4, 2), :] + ck[x, pl.ds(1, 4, 2), :]) * 0.125 for x in range(4)]
     half = 0.5 * 0.0625
     for x in range(2):
@@ -322,21 +322,22 @@
             + face_z + pltpu.roll(face_z, 1, 1)
         )
         both = mr[2 * x] + mr[2 * x + 1]
-        ck[x] = both[0] + both[1]
+        ck[x, 0:8] = both[0] + both[1]
         first_sweep = DAMPING / diag * ((ck[x, pl.ds(2, 2, 2), :] + ck[x, pl.ds(3, 2, 2), :]) * 0.125)
         for j in range(2):
             ck[3, 2 * j + x : 2 * j + x + 1, :] = first_sweep[j : j + 1]
             ck[3, 4 + 2 * j + x : 5 + 2 * j + x, :] = here[j : j + 1]
-    level_2 = ck[3]
+    level_2 = ck[3, 0:8]
     for to in range(piece.shape[0]):
         piece[to, 0:8, :] = level_2
     count = piece.shape[0]
     for to, column in ((lax.rem(me[0] + 1, count), 0), (lax.rem(me[0] + count - 1, count), 1)):
         for r in range(2):
             for x in range(3):
-                at = 8 + 4 * (2 * x + r)
-                piece[to, at : at + 4, :] = u1[column + x + 1, r, 2:6, :]
-            piece[to, 32 + 4 * r : 36 + 4 * r, :] = rhs[column + 3, r, 2:6, :]
+                at = 4 * (2 * x + r)
+                near[column, at : at + 4, :] = u1[column + x + 1, r, 2:6, :]
+            near[column, 24 + 4 * r : 28 + 4 * r, :] = rhs[column + 3, r, 2:6, :]
+        piece[to, 8:40, :] = near[column, 0:32, :]
 
 
 def prepare_middle_kernel(k_early, k_flat, fx, fy, fz, w, k_mid, sums):
@@ -371,7 +372,7 @@
             for array in range(2):
                 at = 4 * array + 2 * j
                 here[2 * j + array, 2 * block : 2 * block + 2, :] = gathered[source, at : at + 2, :]
-    u_flat, r_flat = level_1.at[0:192], level_1.at[192:352]
+    u_flat, r_flat = level_1.at[0:192], level_1.at[192:360]
     u, g = Slabs(u_flat, 8, 2), Slabs(r_flat, 8, 2)
     for x in range(6):
         u[3 + x] = u1[x]
@@ -439,8 +440,8 @@
     for j in range(6):
         block, slab = (left, here, right)[j // 2], 2 * (j % 2)
         if block is here:
-            start[6 + j, 0:24] = here[slab]
-            c[6 + j, 0:24] = here[slab + 1]
+            start[6 + j, 0:24] = here[slab, 0:24]
+            c[6 + j, 0:24] = here[slab + 1, 0:24]
         else:
             start[6 + j, 1:21] = block[20 * slab : 20 * slab + 20]
             c[6 + j, 1:21] = block[20 * slab + 20 : 20 * slab + 40]
@@ -476,8 +477,8 @@
             new[y, lo : lo + size] = ((1.0 - DAMPING) * now + at(start, y, lo, size)) + along_y + (along_x + along_z)
         old = new
     u = old
-    v_flat[...] = level_1[0:192]
-    r_flat[...] = level_1[192:352]
+    v_flat[0:192] = level_1[0:192]
+    r_flat[0:160] = level_1[192:352]
     for source, row, rhs_row in ((left, 0, 1), (right, 6, 6)):
         for i in range(2):
             v_flat[pl.ds(16 + row + i, 20, 8), :] = source[80 + 20 * i : 100 + 20 * i]
@@ -586,14 +587,14 @@
         fine_kernel,
         [(count, 40, 128), (10, *fine), (12 * 96, 128), (16 * 96, 128), (6, *mid), (8, *mid)],
         [(4, *fine), (14, *fine), (14, *fine), (14, *fine), (14, *fine), (14, *fine), (14, *fine), (8, 2, 24, 128), (10, 2, 24, 128),
-         (9, *mid), (8, *mid), (8, *mid), (8, *mid), (8, *mid), (4, *mid), (4, 8, 128)],
+         (9, *mid), (8, *mid), (8, *mid), (8, *mid), (8, *mid), (4, *mid), (4, 16, 128), (2, 40, 128)],
         me_x, wide, low_corners, high_corners, *early, scalars=1,
     )
     piece, u0, g, k, u1, rhs = lax.optimization_barrier((piece, u0, g, k, u1, rhs))
     gathered = lax.all_to_all(piece, "gx", 0, 0)
     gathered, u0, g, k, u1, rhs = lax.optimization_barrier((gathered, u0, g, k, u1, rhs))
     here, high, low, level_1 = call(
-        middle_kernel, [(4, 24, 128), (EDGE_ROWS, 128), (EDGE_ROWS, 128), (352, 128)], [], me_x, gathered, u1, rhs, scalars=1
+        middle_kernel, [(4, 32, 128), (EDGE_ROWS, 128), (EDGE_ROWS, 128), (360, 128)], [], me_x, gathered, u1, rhs, scalars=1
     )
     low, high = shift(high, "gy", 1), shift(low, "gy", -1)
     first, second = call(three_kernel, [(136, 128), (136, 128)], [], me_y, here, low, high, scalars=1)
@@ -604,7 +605,7 @@
     rows = (18, 32, 128)
     v1, high_rows, low_rows = call(
         coarse_kernel, [(128, 128), (32, 128), (32, 128)],
-        [rows, rows, rows, rows, (6, *rows), (192, 128), (160, 128), (10, *mid)],
+        [rows, rows, rows, rows, (6, *rows), (216, 128), (168, 128), (10, *mid)],
         me_y, first, here, second, low, high, level_1, *faces, scalars=1,
     )
     u0, g, *faces = call(

time: 66.9 us -> 67 us (level)
  no operation moved by 1% of the time
where the time goes in v9:
time: 67 us; the launch traced here: 66.7 us
  starting transfers between devices  36.2 us (54%)
  waiting for transfers between devices  12.7 us (19%)
  blocking collectives  10.3 us (15%)
  Pallas kernels  5.85 us (9%)
  other arithmetic  0.99 us (1%)
  between operations  0.73 us (1%)
    ppermute x4, starting transfers between devices, swap(): return lax.ppermute(array, axis, pairs + [(j, i) for i, j in pairs])  23 us
    ppermute x8, starting transfers between devices, shift(): lax.ppermute(array, axis, [(i, (i + by) % count) for i in range(count)])  13.1 us
    all_to_all x1, blocking collectives, per_device(): gathered = lax.all_to_all(piece, 'gx', 0, 0)  10.3 us
    ppermute x8, waiting for transfers between devices, shift(): lax.ppermute(array, axis, [(i, (i + by) % count) for i in range(count)])  7.63 us
    pallas_call x11, Pallas kernels, call(): pl.pallas_call(kernel, out_shape=[jax.ShapeDtypeStruct(shape, F32) for sh...  5.85 us
    ppermute x4, waiting for transfers between devices, swap(): return lax.ppermute(array, axis, pairs + [(j, i) for i, j in pairs])  5.11 us
  transfers between devices with their start and end apart: 12, of which 8 were waited for; matrix products, arithmetic and copies ran while one was open for 0% of the time, Pallas kernels for 2%

profile of v9, /device:TPU:1, one launch (start us, length us, event | category | flops | bytes accessed | tf_op | source)
XLA Modules:
  0.0 66.7 jit_solution(18023942955773058552)
XLA Ops:
  0.6 1.0 %pad_maximum_fusion.held = f32[2,8,8,512]{3,2,1,0:T(8,128)S(1)} fusion(f32[1,8,8,512]{3,2,1,0:T(8,128)} %bitcast.4, f32[1,8,8,512]{3,2,1,0:T(8,128)} %bitcast.5), kind=kLoop, calls=%fused_computation | loop fusion | flops 65536 | bytes 524288 | tf_op jit(solution)/shard_map/stack | solution.py:569
  1.6 0.4 shard_map.50
  2.0 7.7 %collective-permute-start = (f32[14,4,8,128]{3,2,1,0:T(8,128)S(1)}, f32[14,4,8,128]{3,2,1,0:T(8,128)S(1)}, u32[]{:S(2)}, u32[]{:S(2)}) collective-permute-start(f32[14,4,8,128]{3,2,1,0:T(8,128)S(1)} %get-tuple-element.51), channel_id=1, source_target_pairs={{32,64},{96,128},{160,192},{224,256},{288,320},{352,384},{416,448}... | collective-permute-start | bytes 688136 | tf_op jit(solution)/shard_map/ppermute | solution.py:560
  9.7 1.9 %collective-permute-start.1 = (f32[14,4,8,128]{3,2,1,0:T(8,128)S(1)}, f32[14,4,8,128]{3,2,1,0:T(8,128)S(1)}, u32[]{:S(2)}, u32[]{:S(2)}) collective-permute-start(f32[14,4,8,128]{3,2,1,0:T(8,128)S(1)} %get-tuple-element.52), channel_id=1, source_target_pairs={{0,32},{64,96},{128,160},{192,224},{256,288},{320,352},{384,416},{... | collective-permute-start | bytes 688136 | tf_op jit(solution)/shard_map/ppermute | solution.py:560
  11.7 2.5 %collective-permute-start.4 = (f32[416,128]{1,0:T(8,128)S(1)}, f32[416,128]{1,0:T(8,128)S(1)}, u32[]{:S(2)}, u32[]{:S(2)}) collective-permute-start(f32[416,128]{1,0:T(8,128)S(1)} %get-tuple-element.56), channel_id=1, source_target_pairs={{0,1},{1,2},{2,3},{3,4},{4,5},{5,6},{6,7},{7,8},{8,9},{9,10},{10,1... | collective-permute-start | bytes 638984 | tf_op jit(solution)/shard_map/ppermute | solution.py:554
  14.2 3.4 %collective-permute-done.1.second = f32[14,4,8,128]{3,2,1,0:T(8,128)S(1)} collective-permute-done((f32[14,4,8,128]{3,2,1,0:T(8,128)S(1)}, f32[14,4,8,128]{3,2,1,0:T(8,128)S(1)}, u32[]{:S(2)}, u32[]{:S(2)}) %collective-permute-start.1) | collective-permute-done | bytes 229408 | tf_op jit(solution)/shard_map/ppermute | solution.py:560
  17.7 3.6 %collective-permute-start.2 = (f32[312,128]{1,0:T(8,128)S(1)}, f32[312,128]{1,0:T(8,128)S(1)}, u32[]{:S(2)}, u32[]{:S(2)}) collective-permute-start(f32[312,128]{1,0:T(8,128)S(1)} %get-tuple-element.54), channel_id=1, source_target_pairs={{0,1},{1,2},{2,3},{3,4},{4,5},{5,6},{6,7},{7,8},{8,9},{9,10},{10,1... | collective-permute-start | bytes 479240 | tf_op jit(solution)/shard_map/ppermute | solution.py:554
  21.5 0.5 shard_map.53
  22.1 1.4 %collective-permute-done.2.low_corners = f32[312,128]{1,0:T(8,128)S(1)} collective-permute-done((f32[312,128]{1,0:T(8,128)S(1)}, f32[312,128]{1,0:T(8,128)S(1)}, u32[]{:S(2)}, u32[]{:S(2)}) %collective-permute-start.2) | collective-permute-done | bytes 159776 | tf_op jit(solution)/shard_map/ppermute | solution.py:554
  23.5 2.5 %collective-permute-done.3.high_corners = f32[312,128]{1,0:T(8,128)S(1)} collective-permute-done((f32[312,128]{1,0:T(8,128)S(1)}, f32[312,128]{1,0:T(8,128)S(1)}, u32[]{:S(2)}, u32[]{:S(2)}) %collective-permute-start.3) | collective-permute-done | bytes 159776 | tf_op jit(solution)/shard_map/ppermute | solution.py:554
  26.0 1.5 %shard_map.54 = (f32[16,40,128]{2,1,0:T(8,128)S(1)}, f32[10,4,24,128]{3,2,1,0:T(8,128)S(1)}, f32[1152,128]{1,0:T(8,128)S(1)}, f32[1536,128]{1,0:T(8,128)S(1)}, f...) custom-call(s32[1]{0:T(128)} %bitcast.1.me, f32[1408,128]{1,0:T(8,128)S(1)} %get-tuple-element.53.wide, ...), custom_call_target="tpu_custom_call" | custom-call | tf_op jit(solution)/shard_map/pallas_call | solution.py:542
  27.5 10.3 %all_to_all.5.gathered = f32[16,40,128]{2,1,0:T(8,128)S(1)} all-to-all(f32[16,40,128]{2,1,0:T(8,128)S(1)} %get-tuple-element.67), channel_id=1, replica_groups=mesh['gx'=16,'gy'=32] {'gx'}, dimensions={0} | all-to-all | bytes 655360 | tf_op jit(solution)/shard_map/all_to_all | solution.py:594
  37.8 2.1 %collective-permute-start.6 = (f32[136,128]{1,0:T(8,128)S(1)}, f32[136,128]{1,0:T(8,128)S(1)}, u32[]{:S(2)}, u32[]{:S(2)}) collective-permute-start(f32[136,128]{1,0:T(8,128)S(1)} %get-tuple-element.77), channel_id=1, source_target_pairs={{0,1},{1,2},{2,3},{3,4},{4,5},{5,6},{6,7},{7,8},{8,9},{9,10},{10,1... | collective-permute-start | bytes 208904 | tf_op jit(solution)/shard_map/ppermute | solution.py:554
  39.9 4.2 %collective-permute-start.7 = (f32[136,128]{1,0:T(8,128)S(1)}, f32[136,128]{1,0:T(8,128)S(1)}, u32[]{:S(2)}, u32[]{:S(2)}) collective-permute-start(f32[136,128]{1,0:T(8,128)S(1)} %get-tuple-element.78), channel_id=1, source_target_pairs={{0,31},{1,0},{2,1},{3,2},{4,3},{5,4},{6,5},{7,6},{8,7},{9,8},{10,9... | collective-permute-start | bytes 208904 | tf_op jit(solution)/shard_map/ppermute | solution.py:554
  44.1 0.7 %collective-permute-done.6.low.left = f32[136,128]{1,0:T(8,128)S(1)} collective-permute-done((f32[136,128]{1,0:T(8,128)S(1)}, f32[136,128]{1,0:T(8,128)S(1)}, u32[]{:S(2)}, u32[]{:S(2)}) %collective-permute-start.6) | collective-permute-done | bytes 69664 | tf_op jit(solution)/shard_map/ppermute | solution.py:554
  45.0 1.9 %collective-permute-start.8 = (f32[136,128]{1,0:T(8,128)S(1)}, f32[136,128]{1,0:T(8,128)S(1)}, u32[]{:S(2)}, u32[]{:S(2)}) collective-permute-start(f32[136,128]{1,0:T(8,128)S(1)} %get-tuple-element.79), channel_id=1, source_target_pairs={{1,4},{3,6},{5,8},{7,10},{9,12},{11,14},{13,16},{15,18},{17,20},{1... | collective-permute-start | bytes 208904 | tf_op jit(solution)/shard_map/ppermute | solution.py:560
  46.9 11.5 %collective-permute-start.9 = (f32[136,128]{1,0:T(8,128)S(1)}, f32[136,128]{1,0:T(8,128)S(1)}, u32[]{:S(2)}, u32[]{:S(2)}) collective-permute-start(f32[136,128]{1,0:T(8,128)S(1)} %get-tuple-element.80), channel_id=1, source_target_pairs={{0,3},{2,5},{4,7},{6,9},{8,11},{10,13},{12,15},{14,17},{16,19},{18... | collective-permute-start | bytes 208904 | tf_op jit(solution)/shard_map/ppermute | solution.py:560
  58.7 1.7 %collective-permute-done.9.second = f32[136,128]{1,0:T(8,128)S(1)} collective-permute-done((f32[136,128]{1,0:T(8,128)S(1)}, f32[136,128]{1,0:T(8,128)S(1)}, u32[]{:S(2)}, u32[]{:S(2)}) %collective-permute-start.9) | collective-permute-done | bytes 69664 | tf_op jit(solution)/shard_map/ppermute | solution.py:560
  60.5 1.0 %shard_map.58 = (f32[128,128]{1,0:T(8,128)S(1)}, f32[32,128]{1,0:T(8,128)S(1)}, f32[32,128]{1,0:T(8,128)S(1)}) custom-call(s32[1]{0:T(128)} %bitcast.me, f32[136,128]{1,0:T(8,128)S(1)} %collective-permute-done.8.first, f32[4,32,128]{2,1,0:T(8,128)S(1)} %get-tuple-element.76.here, f32[136,128]{1,0:T(8,128)S(1)} %collective-permute-done.9.second, ...), custom_call_target="tpu_custom_call" | custom-call | tf_op jit(solution)/shard_map/pallas_call | solution.py:542
  61.6 0.4 collective-permute-start.11
  62.0 0.3 shard_map.59
  62.3 0.4 collective-permute-done.10.v_low
  62.7 2.4 %collective-permute-done.11.v_high = f32[32,128]{1,0:T(8,128)S(1)} collective-permute-done((f32[32,128]{1,0:T(8,128)S(1)}, f32[32,128]{1,0:T(8,128)S(1)}, u32[]{:S(2)}, u32[]{:S(2)}) %collective-permute-start.11) | collective-permute-done | bytes 16416 | tf_op jit(solution)/shard_map/ppermute | solution.py:554
  65.1 1.6 %shard_map.60 = (f32[8,8,512]{2,1,0:T(8,128)}, f32[8,8,512]{2,1,0:T(8,128)}) custom-call(f32[128,128]{1,0:T(8,128)S(1)} %get-tuple-element.87.v_here, f32[32,128]{1,0:T(8,128)S(1)} %collective-permute-done.10.v_low, f32[32,128]{1,0:T(8,128)S(1)} %collective-permute-done.11.v_high, f32[14,4,16,128]{3,2,1,0:T(8,128)S(1)} %get-tuple-element.92.u0, ...), custom_call_target="tpu_custom_call" | custom-call | tf_op jit(solution)/shard_map/pallas_call | solution.py:542
  (15 shorter events, 1.0 us)
Async XLA Ops:
  2.0 12.2 %collective-permute-start = (f32[14,4,8,128]{3,2,1,0:T(8,128)S(1)}, f32[14,4,8,128]{3,2,1,0:T(8,128)S(1)}, u32[]{:S(2)}, u32[]{:S(2)}) collective-permute-start(f32[14,4,8,128]{3,2,1,0:T(8,128)S(1)} %get-tuple-element.51), channel_id=1, source_target_pairs={{32,64},{96,128},{160,192},{224,256},{288,320},{352,384},{416,448}... | collective-permute-start | bytes 688136 | tf_op jit(solution)/shard_map/ppermute | solution.py:560
  9.7 7.9 %collective-permute-start.1 = (f32[14,4,8,128]{3,2,1,0:T(8,128)S(1)}, f32[14,4,8,128]{3,2,1,0:T(8,128)S(1)}, u32[]{:S(2)}, u32[]{:S(2)}) collective-permute-start(f32[14,4,8,128]{3,2,1,0:T(8,128)S(1)} %get-tuple-element.52), channel_id=1, source_target_pairs={{0,32},{64,96},{128,160},{192,224},{256,288},{320,352},{384,416},{... | collective-permute-start | bytes 688136 | tf_op jit(solution)/shard_map/ppermute | solution.py:560
  11.7 9.8 %collective-permute-start.4 = (f32[416,128]{1,0:T(8,128)S(1)}, f32[416,128]{1,0:T(8,128)S(1)}, u32[]{:S(2)}, u32[]{:S(2)}) collective-permute-start(f32[416,128]{1,0:T(8,128)S(1)} %get-tuple-element.56), channel_id=1, source_target_pairs={{0,1},{1,2},{2,3},{3,4},{4,5},{5,6},{6,7},{7,8},{8,9},{9,10},{10,1... | collective-permute-start | bytes 638984 | tf_op jit(solution)/shard_map/ppermute | solution.py:554
  14.2 7.3 %collective-permute-start.5 = (f32[416,128]{1,0:T(8,128)S(1)}, f32[416,128]{1,0:T(8,128)S(1)}, u32[]{:S(2)}, u32[]{:S(2)}) collective-permute-start(f32[416,128]{1,0:T(8,128)S(1)} %get-tuple-element.57), channel_id=1, source_target_pairs={{0,31},{1,0},{2,1},{3,2},{4,3},{5,4},{6,5},{7,6},{8,7},{9,8},{10,9... | collective-permute-start | bytes 638984 | tf_op jit(solution)/shard_map/ppermute | solution.py:554
  17.7 5.8 %collective-permute-start.2 = (f32[312,128]{1,0:T(8,128)S(1)}, f32[312,128]{1,0:T(8,128)S(1)}, u32[]{:S(2)}, u32[]{:S(2)}) collective-permute-start(f32[312,128]{1,0:T(8,128)S(1)} %get-tuple-element.54), channel_id=1, source_target_pairs={{0,1},{1,2},{2,3},{3,4},{4,5},{5,6},{6,7},{7,8},{8,9},{9,10},{10,1... | collective-permute-start | bytes 479240 | tf_op jit(solution)/shard_map/ppermute | solution.py:554
  21.3 4.7 %collective-permute-start.3 = (f32[312,128]{1,0:T(8,128)S(1)}, f32[312,128]{1,0:T(8,128)S(1)}, u32[]{:S(2)}, u32[]{:S(2)}) collective-permute-start(f32[312,128]{1,0:T(8,128)S(1)} %get-tuple-element.55), channel_id=1, source_target_pairs={{0,31},{1,0},{2,1},{3,2},{4,3},{5,4},{6,5},{7,6},{8,7},{9,8},{10,9... | collective-permute-start | bytes 479240 | tf_op jit(solution)/shard_map/ppermute | solution.py:554
  37.8 7.0 %collective-permute-start.6 = (f32[136,128]{1,0:T(8,128)S(1)}, f32[136,128]{1,0:T(8,128)S(1)}, u32[]{:S(2)}, u32[]{:S(2)}) collective-permute-start(f32[136,128]{1,0:T(8,128)S(1)} %get-tuple-element.77), channel_id=1, source_target_pairs={{0,1},{1,2},{2,3},{3,4},{4,5},{5,6},{6,7},{7,8},{8,9},{9,10},{10,1... | collective-permute-start | bytes 208904 | tf_op jit(solution)/shard_map/ppermute | solution.py:554
  39.9 5.1 %collective-permute-start.7 = (f32[136,128]{1,0:T(8,128)S(1)}, f32[136,128]{1,0:T(8,128)S(1)}, u32[]{:S(2)}, u32[]{:S(2)}) collective-permute-start(f32[136,128]{1,0:T(8,128)S(1)} %get-tuple-element.78), channel_id=1, source_target_pairs={{0,31},{1,0},{2,1},{3,2},{4,3},{5,4},{6,5},{7,6},{8,7},{9,8},{10,9... | collective-permute-start | bytes 208904 | tf_op jit(solution)/shard_map/ppermute | solution.py:554
  45.0 13.7 %collective-permute-start.8 = (f32[136,128]{1,0:T(8,128)S(1)}, f32[136,128]{1,0:T(8,128)S(1)}, u32[]{:S(2)}, u32[]{:S(2)}) collective-permute-start(f32[136,128]{1,0:T(8,128)S(1)} %get-tuple-element.79), channel_id=1, source_target_pairs={{1,4},{3,6},{5,8},{7,10},{9,12},{11,14},{13,16},{15,18},{17,20},{1... | collective-permute-start | bytes 208904 | tf_op jit(solution)/shard_map/ppermute | solution.py:560
  46.9 13.5 %collective-permute-start.9 = (f32[136,128]{1,0:T(8,128)S(1)}, f32[136,128]{1,0:T(8,128)S(1)}, u32[]{:S(2)}, u32[]{:S(2)}) collective-permute-start(f32[136,128]{1,0:T(8,128)S(1)} %get-tuple-element.80), channel_id=1, source_target_pairs={{0,3},{2,5},{4,7},{6,9},{8,11},{10,13},{12,15},{14,17},{16,19},{18... | collective-permute-start | bytes 208904 | tf_op jit(solution)/shard_map/ppermute | solution.py:560
  61.5 1.2 %collective-permute-start.10 = (f32[32,128]{1,0:T(8,128)S(1)}, f32[32,128]{1,0:T(8,128)S(1)}, u32[]{:S(2)}, u32[]{:S(2)}) collective-permute-start(f32[32,128]{1,0:T(8,128)S(1)} %get-tuple-element.88), channel_id=1, source_target_pairs={{0,1},{1,2},{2,3},{3,4},{4,5},{5,6},{6,7},{7,8},{8,9},{9,10},{10,1... | collective-permute-start | bytes 49160 | tf_op jit(solution)/shard_map/ppermute | solution.py:554
  61.6 3.5 %copy-start = (bf16[512,512]{1,0:T(8,128)(2,1)S(1)}, bf16[512,512]{1,0:T(8,128)(2,1)}, u32[]{:S(2)}) copy-start(bf16[512,512]{1,0:T(8,128)(2,1)} %constant.11.clone.matrix) | copy-start | bytes 1572868
  61.6 3.5 %collective-permute-start.11 = (f32[32,128]{1,0:T(8,128)S(1)}, f32[32,128]{1,0:T(8,128)S(1)}, u32[]{:S(2)}, u32[]{:S(2)}) collective-permute-start(f32[32,128]{1,0:T(8,128)S(1)} %get-tuple-element.89), channel_id=1, source_target_pairs={{0,31},{1,0},{2,1},{3,2},{4,3},{5,4},{6,5},{7,6},{8,7},{9,8},{10,9... | collective-permute-start | bytes 49160 | tf_op jit(solution)/shard_map/ppermute | solution.py:554

commit v10 on v9

--- a/solution.py
+++ b/solution.py
@@ -136,6 +136,16 @@
         low_rows = some
         rest = get(g_ref, g_at + i, some) - applied
         put(out, out_at + i, some, rest if last else u + get(w, f, some) * rest)
+
+
+def neighbour_sweep(count, u_ref, g_ref, at, fx, fy, fz, w, out):
+    for i in range(count):
+        f, u = at + i, u_ref[1 + i]
+        face_y, face_z = fy[f], fz[f]
+        along_x = fx[f + 1] * u_ref[2 + i] + fx[f] * u_ref[i]
+        along_y = face_y * y_next(u) + y_prev(face_y) * y_prev(u)
+        along_z = face_z * z_next(u) + z_prev(face_z) * z_prev(u)
+        out[i] = (1.0 - DAMPING) * u + w[f] * ((g_ref[f] + along_x) + (along_y + along_z))
 
 
 def inverse_permutation():
@@ -490,8 +500,8 @@
         )
         for twin in range(2):
             v[2 * x + twin] = v[2 * x + twin] + rows[None]
-    sweep_pass(10, v, 0, 0, rhs, 0, fx, fy, fz, w, va, 0)
-    sweep_pass(8, va, 0, 1, rhs, 1, fx, fy, fz, w, Slabs(v_flat_out, 8, 2), 0)
+    neighbour_sweep(10, v, rhs, 0, fx, fy, fz, w, va)
+    neighbour_sweep(8, va, rhs, 1, fx, fy, fz, w, Slabs(v_flat_out, 8, 2))
     for out, row in ((to_high, 4), (to_low, 2)):
         for i in range(2):
             out[16 * i : 16 * i + 16] = v_flat_out[pl.ds(row + i, 16, 8), :]

time: 67 us -> 66.9 us (level)
  no operation moved by 1% of the time
where the time goes in v10:
time: 66.9 us; the launch traced here: 66.6 us
  starting transfers between devices  36.2 us (54%)
  waiting for transfers between devices  12.7 us (19%)
  blocking collectives  10.3 us (15%)
  Pallas kernels  5.73 us (9%)
  other arithmetic  0.99 us (1%)
  between operations  0.73 us (1%)
    ppermute x4, starting transfers between devices, swap(): return lax.ppermute(array, axis, pairs + [(j, i) for i, j in pairs])  23 us
    ppermute x8, starting transfers between devices, shift(): lax.ppermute(array, axis, [(i, (i + by) % count) for i in range(count)])  13.1 us
    all_to_all x1, blocking collectives, per_device(): gathered = lax.all_to_all(piece, 'gx', 0, 0)  10.3 us
    ppermute x8, waiting for transfers between devices, shift(): lax.ppermute(array, axis, [(i, (i + by) % count) for i in range(count)])  7.63 us
    pallas_call x11, Pallas kernels, call(): pl.pallas_call(kernel, out_shape=[jax.ShapeDtypeStruct(shape, F32) for sh...  5.73 us
    ppermute x4, waiting for transfers between devices, swap(): return lax.ppermute(array, axis, pairs + [(j, i) for i, j in pairs])  5.11 us
  transfers between devices with their start and end apart: 12, of which 8 were waited for; matrix products, arithmetic and copies ran while one was open for 0% of the time, Pallas kernels for 2%

profile of v10, /device:TPU:1, one launch (start us, length us, event | category | flops | bytes accessed | tf_op | source)
XLA Modules:
  0.0 66.6 jit_solution(444231237676152207)
XLA Ops:
  0.6 1.0 %pad_maximum_fusion.held = f32[2,8,8,512]{3,2,1,0:T(8,128)S(1)} fusion(f32[1,8,8,512]{3,2,1,0:T(8,128)} %bitcast.4, f32[1,8,8,512]{3,2,1,0:T(8,128)} %bitcast.5), kind=kLoop, calls=%fused_computation | loop fusion | flops 65536 | bytes 524288 | tf_op jit(solution)/shard_map/stack | solution.py:579
  1.6 0.4 shard_map.50
  2.0 7.7 %collective-permute-start = (f32[14,4,8,128]{3,2,1,0:T(8,128)S(1)}, f32[14,4,8,128]{3,2,1,0:T(8,128)S(1)}, u32[]{:S(2)}, u32[]{:S(2)}) collective-permute-start(f32[14,4,8,128]{3,2,1,0:T(8,128)S(1)} %get-tuple-element.51), channel_id=1, source_target_pairs={{32,64},{96,128},{160,192},{224,256},{288,320},{352,384},{416,448}... | collective-permute-start | bytes 688136 | tf_op jit(solution)/shard_map/ppermute | solution.py:570
  9.7 1.9 %collective-permute-start.1 = (f32[14,4,8,128]{3,2,1,0:T(8,128)S(1)}, f32[14,4,8,128]{3,2,1,0:T(8,128)S(1)}, u32[]{:S(2)}, u32[]{:S(2)}) collective-permute-start(f32[14,4,8,128]{3,2,1,0:T(8,128)S(1)} %get-tuple-element.52), channel_id=1, source_target_pairs={{0,32},{64,96},{128,160},{192,224},{256,288},{320,352},{384,416},{... | collective-permute-start | bytes 688136 | tf_op jit(solution)/shard_map/ppermute | solution.py:570
  11.7 2.5 %collective-permute-start.4 = (f32[416,128]{1,0:T(8,128)S(1)}, f32[416,128]{1,0:T(8,128)S(1)}, u32[]{:S(2)}, u32[]{:S(2)}) collective-permute-start(f32[416,128]{1,0:T(8,128)S(1)} %get-tuple-element.56), channel_id=1, source_target_pairs={{0,1},{1,2},{2,3},{3,4},{4,5},{5,6},{6,7},{7,8},{8,9},{9,10},{10,1... | collective-permute-start | bytes 638984 | tf_op jit(solution)/shard_map/ppermute | solution.py:564
  14.2 3.4 %collective-permute-done.1.second = f32[14,4,8,128]{3,2,1,0:T(8,128)S(1)} collective-permute-done((f32[14,4,8,128]{3,2,1,0:T(8,128)S(1)}, f32[14,4,8,128]{3,2,1,0:T(8,128)S(1)}, u32[]{:S(2)}, u32[]{:S(2)}) %collective-permute-start.1) | collective-permute-done | bytes 229408 | tf_op jit(solution)/shard_map/ppermute | solution.py:570
  17.7 3.6 %collective-permute-start.2 = (f32[312,128]{1,0:T(8,128)S(1)}, f32[312,128]{1,0:T(8,128)S(1)}, u32[]{:S(2)}, u32[]{:S(2)}) collective-permute-start(f32[312,128]{1,0:T(8,128)S(1)} %get-tuple-element.54), channel_id=1, source_target_pairs={{0,1},{1,2},{2,3},{3,4},{4,5},{5,6},{6,7},{7,8},{8,9},{9,10},{10,1... | collective-permute-start | bytes 479240 | tf_op jit(solution)/shard_map/ppermute | solution.py:564
  21.5 0.5 shard_map.53
  22.1 1.4 %collective-permute-done.2.low_corners = f32[312,128]{1,0:T(8,128)S(1)} collective-permute-done((f32[312,128]{1,0:T(8,128)S(1)}, f32[312,128]{1,0:T(8,128)S(1)}, u32[]{:S(2)}, u32[]{:S(2)}) %collective-permute-start.2) | collective-permute-done | bytes 159776 | tf_op jit(solution)/shard_map/ppermute | solution.py:564
  23.5 2.5 %collective-permute-done.3.high_corners = f32[312,128]{1,0:T(8,128)S(1)} collective-permute-done((f32[312,128]{1,0:T(8,128)S(1)}, f32[312,128]{1,0:T(8,128)S(1)}, u32[]{:S(2)}, u32[]{:S(2)}) %collective-permute-start.3) | collective-permute-done | bytes 159776 | tf_op jit(solution)/shard_map/ppermute | solution.py:564
  26.0 1.5 %shard_map.54 = (f32[16,40,128]{2,1,0:T(8,128)S(1)}, f32[10,4,24,128]{3,2,1,0:T(8,128)S(1)}, f32[1152,128]{1,0:T(8,128)S(1)}, f32[1536,128]{1,0:T(8,128)S(1)}, f...) custom-call(s32[1]{0:T(128)} %bitcast.1.me, f32[1408,128]{1,0:T(8,128)S(1)} %get-tuple-element.53.wide, ...), custom_call_target="tpu_custom_call" | custom-call | tf_op jit(solution)/shard_map/pallas_call | solution.py:552
  27.5 10.3 %all_to_all.5.gathered = f32[16,40,128]{2,1,0:T(8,128)S(1)} all-to-all(f32[16,40,128]{2,1,0:T(8,128)S(1)} %get-tuple-element.67), channel_id=1, replica_groups=mesh['gx'=16,'gy'=32] {'gx'}, dimensions={0} | all-to-all | bytes 655360 | tf_op jit(solution)/shard_map/all_to_all | solution.py:604
  37.8 2.1 %collective-permute-start.6 = (f32[136,128]{1,0:T(8,128)S(1)}, f32[136,128]{1,0:T(8,128)S(1)}, u32[]{:S(2)}, u32[]{:S(2)}) collective-permute-start(f32[136,128]{1,0:T(8,128)S(1)} %get-tuple-element.77), channel_id=1, source_target_pairs={{0,1},{1,2},{2,3},{3,4},{4,5},{5,6},{6,7},{7,8},{8,9},{9,10},{10,1... | collective-permute-start | bytes 208904 | tf_op jit(solution)/shard_map/ppermute | solution.py:564
  39.9 4.2 %collective-permute-start.7 = (f32[136,128]{1,0:T(8,128)S(1)}, f32[136,128]{1,0:T(8,128)S(1)}, u32[]{:S(2)}, u32[]{:S(2)}) collective-permute-start(f32[136,128]{1,0:T(8,128)S(1)} %get-tuple-element.78), channel_id=1, source_target_pairs={{0,31},{1,0},{2,1},{3,2},{4,3},{5,4},{6,5},{7,6},{8,7},{9,8},{10,9... | collective-permute-start | bytes 208904 | tf_op jit(solution)/shard_map/ppermute | solution.py:564
  44.1 0.7 %collective-permute-done.6.low.left = f32[136,128]{1,0:T(8,128)S(1)} collective-permute-done((f32[136,128]{1,0:T(8,128)S(1)}, f32[136,128]{1,0:T(8,128)S(1)}, u32[]{:S(2)}, u32[]{:S(2)}) %collective-permute-start.6) | collective-permute-done | bytes 69664 | tf_op jit(solution)/shard_map/ppermute | solution.py:564
  45.0 1.9 %collective-permute-start.8 = (f32[136,128]{1,0:T(8,128)S(1)}, f32[136,128]{1,0:T(8,128)S(1)}, u32[]{:S(2)}, u32[]{:S(2)}) collective-permute-start(f32[136,128]{1,0:T(8,128)S(1)} %get-tuple-element.79), channel_id=1, source_target_pairs={{1,4},{3,6},{5,8},{7,10},{9,12},{11,14},{13,16},{15,18},{17,20},{1... | collective-permute-start | bytes 208904 | tf_op jit(solution)/shard_map/ppermute | solution.py:570
  46.9 11.5 %collective-permute-start.9 = (f32[136,128]{1,0:T(8,128)S(1)}, f32[136,128]{1,0:T(8,128)S(1)}, u32[]{:S(2)}, u32[]{:S(2)}) collective-permute-start(f32[136,128]{1,0:T(8,128)S(1)} %get-tuple-element.80), channel_id=1, source_target_pairs={{0,3},{2,5},{4,7},{6,9},{8,11},{10,13},{12,15},{14,17},{16,19},{18... | collective-permute-start | bytes 208904 | tf_op jit(solution)/shard_map/ppermute | solution.py:570
  58.7 1.7 %collective-permute-done.9.second = f32[136,128]{1,0:T(8,128)S(1)} collective-permute-done((f32[136,128]{1,0:T(8,128)S(1)}, f32[136,128]{1,0:T(8,128)S(1)}, u32[]{:S(2)}, u32[]{:S(2)}) %collective-permute-start.9) | collective-permute-done | bytes 69664 | tf_op jit(solution)/shard_map/ppermute | solution.py:570
  60.5 0.9 %shard_map.58 = (f32[128,128]{1,0:T(8,128)S(1)}, f32[32,128]{1,0:T(8,128)S(1)}, f32[32,128]{1,0:T(8,128)S(1)}) custom-call(s32[1]{0:T(128)} %bitcast.me, f32[136,128]{1,0:T(8,128)S(1)} %collective-permute-done.8.first, f32[4,32,128]{2,1,0:T(8,128)S(1)} %get-tuple-element.76.here, f32[136,128]{1,0:T(8,128)S(1)} %collective-permute-done.9.second, ...), custom_call_target="tpu_custom_call" | custom-call | tf_op jit(solution)/shard_map/pallas_call | solution.py:552
  61.5 0.4 collective-permute-start.11
  61.9 0.3 shard_map.59
  62.2 0.4 collective-permute-done.10.v_low
  62.6 2.4 %collective-permute-done.11.v_high = f32[32,128]{1,0:T(8,128)S(1)} collective-permute-done((f32[32,128]{1,0:T(8,128)S(1)}, f32[32,128]{1,0:T(8,128)S(1)}, u32[]{:S(2)}, u32[]{:S(2)}) %collective-permute-start.11) | collective-permute-done | bytes 16416 | tf_op jit(solution)/shard_map/ppermute | solution.py:564
  65.0 1.6 %shard_map.60 = (f32[8,8,512]{2,1,0:T(8,128)}, f32[8,8,512]{2,1,0:T(8,128)}) custom-call(f32[128,128]{1,0:T(8,128)S(1)} %get-tuple-element.87.v_here, f32[32,128]{1,0:T(8,128)S(1)} %collective-permute-done.10.v_low, f32[32,128]{1,0:T(8,128)S(1)} %collective-permute-done.11.v_high, f32[14,4,16,128]{3,2,1,0:T(8,128)S(1)} %get-tuple-element.92.u0, ...), custom_call_target="tpu_custom_call" | custom-call | tf_op jit(solution)/shard_map/pallas_call | solution.py:552
  (15 shorter events, 1.0 us)
Async XLA Ops:
  2.0 12.2 %collective-permute-start = (f32[14,4,8,128]{3,2,1,0:T(8,128)S(1)}, f32[14,4,8,128]{3,2,1,0:T(8,128)S(1)}, u32[]{:S(2)}, u32[]{:S(2)}) collective-permute-start(f32[14,4,8,128]{3,2,1,0:T(8,128)S(1)} %get-tuple-element.51), channel_id=1, source_target_pairs={{32,64},{96,128},{160,192},{224,256},{288,320},{352,384},{416,448}... | collective-permute-start | bytes 688136 | tf_op jit(solution)/shard_map/ppermute | solution.py:570
  9.7 7.9 %collective-permute-start.1 = (f32[14,4,8,128]{3,2,1,0:T(8,128)S(1)}, f32[14,4,8,128]{3,2,1,0:T(8,128)S(1)}, u32[]{:S(2)}, u32[]{:S(2)}) collective-permute-start(f32[14,4,8,128]{3,2,1,0:T(8,128)S(1)} %get-tuple-element.52), channel_id=1, source_target_pairs={{0,32},{64,96},{128,160},{192,224},{256,288},{320,352},{384,416},{... | collective-permute-start | bytes 688136 | tf_op jit(solution)/shard_map/ppermute | solution.py:570
  11.7 9.8 %collective-permute-start.4 = (f32[416,128]{1,0:T(8,128)S(1)}, f32[416,128]{1,0:T(8,128)S(1)}, u32[]{:S(2)}, u32[]{:S(2)}) collective-permute-start(f32[416,128]{1,0:T(8,128)S(1)} %get-tuple-element.56), channel_id=1, source_target_pairs={{0,1},{1,2},{2,3},{3,4},{4,5},{5,6},{6,7},{7,8},{8,9},{9,10},{10,1... | collective-permute-start | bytes 638984 | tf_op jit(solution)/shard_map/ppermute | solution.py:564
  14.2 7.3 %collective-permute-start.5 = (f32[416,128]{1,0:T(8,128)S(1)}, f32[416,128]{1,0:T(8,128)S(1)}, u32[]{:S(2)}, u32[]{:S(2)}) collective-permute-start(f32[416,128]{1,0:T(8,128)S(1)} %get-tuple-element.57), channel_id=1, source_target_pairs={{0,31},{1,0},{2,1},{3,2},{4,3},{5,4},{6,5},{7,6},{8,7},{9,8},{10,9... | collective-permute-start | bytes 638984 | tf_op jit(solution)/shard_map/ppermute | solution.py:564
  17.7 5.8 %collective-permute-start.2 = (f32[312,128]{1,0:T(8,128)S(1)}, f32[312,128]{1,0:T(8,128)S(1)}, u32[]{:S(2)}, u32[]{:S(2)}) collective-permute-start(f32[312,128]{1,0:T(8,128)S(1)} %get-tuple-element.54), channel_id=1, source_target_pairs={{0,1},{1,2},{2,3},{3,4},{4,5},{5,6},{6,7},{7,8},{8,9},{9,10},{10,1... | collective-permute-start | bytes 479240 | tf_op jit(solution)/shard_map/ppermute | solution.py:564
  21.3 4.7 %collective-permute-start.3 = (f32[312,128]{1,0:T(8,128)S(1)}, f32[312,128]{1,0:T(8,128)S(1)}, u32[]{:S(2)}, u32[]{:S(2)}) collective-permute-start(f32[312,128]{1,0:T(8,128)S(1)} %get-tuple-element.55), channel_id=1, source_target_pairs={{0,31},{1,0},{2,1},{3,2},{4,3},{5,4},{6,5},{7,6},{8,7},{9,8},{10,9... | collective-permute-start | bytes 479240 | tf_op jit(solution)/shard_map/ppermute | solution.py:564
  37.8 7.0 %collective-permute-start.6 = (f32[136,128]{1,0:T(8,128)S(1)}, f32[136,128]{1,0:T(8,128)S(1)}, u32[]{:S(2)}, u32[]{:S(2)}) collective-permute-start(f32[136,128]{1,0:T(8,128)S(1)} %get-tuple-element.77), channel_id=1, source_target_pairs={{0,1},{1,2},{2,3},{3,4},{4,5},{5,6},{6,7},{7,8},{8,9},{9,10},{10,1... | collective-permute-start | bytes 208904 | tf_op jit(solution)/shard_map/ppermute | solution.py:564
  39.9 5.1 %collective-permute-start.7 = (f32[136,128]{1,0:T(8,128)S(1)}, f32[136,128]{1,0:T(8,128)S(1)}, u32[]{:S(2)}, u32[]{:S(2)}) collective-permute-start(f32[136,128]{1,0:T(8,128)S(1)} %get-tuple-element.78), channel_id=1, source_target_pairs={{0,31},{1,0},{2,1},{3,2},{4,3},{5,4},{6,5},{7,6},{8,7},{9,8},{10,9... | collective-permute-start | bytes 208904 | tf_op jit(solution)/shard_map/ppermute | solution.py:564
  45.0 13.7 %collective-permute-start.8 = (f32[136,128]{1,0:T(8,128)S(1)}, f32[136,128]{1,0:T(8,128)S(1)}, u32[]{:S(2)}, u32[]{:S(2)}) collective-permute-start(f32[136,128]{1,0:T(8,128)S(1)} %get-tuple-element.79), channel_id=1, source_target_pairs={{1,4},{3,6},{5,8},{7,10},{9,12},{11,14},{13,16},{15,18},{17,20},{1... | collective-permute-start | bytes 208904 | tf_op jit(solution)/shard_map/ppermute | solution.py:570
  46.9 13.5 %collective-permute-start.9 = (f32[136,128]{1,0:T(8,128)S(1)}, f32[136,128]{1,0:T(8,128)S(1)}, u32[]{:S(2)}, u32[]{:S(2)}) collective-permute-start(f32[136,128]{1,0:T(8,128)S(1)} %get-tuple-element.80), channel_id=1, source_target_pairs={{0,3},{2,5},{4,7},{6,9},{8,11},{10,13},{12,15},{14,17},{16,19},{18... | collective-permute-start | bytes 208904 | tf_op jit(solution)/shard_map/ppermute | solution.py:570
  61.4 1.2 %collective-permute-start.10 = (f32[32,128]{1,0:T(8,128)S(1)}, f32[32,128]{1,0:T(8,128)S(1)}, u32[]{:S(2)}, u32[]{:S(2)}) collective-permute-start(f32[32,128]{1,0:T(8,128)S(1)} %get-tuple-element.88), channel_id=1, source_target_pairs={{0,1},{1,2},{2,3},{3,4},{4,5},{5,6},{6,7},{7,8},{8,9},{9,10},{10,1... | collective-permute-start | bytes 49160 | tf_op jit(solution)/shard_map/ppermute | solution.py:564
  61.5 3.5 %copy-start = (bf16[512,512]{1,0:T(8,128)(2,1)S(1)}, bf16[512,512]{1,0:T(8,128)(2,1)}, u32[]{:S(2)}) copy-start(bf16[512,512]{1,0:T(8,128)(2,1)} %constant.11.clone.matrix) | copy-start | bytes 1572868
  61.5 3.5 %collective-permute-start.11 = (f32[32,128]{1,0:T(8,128)S(1)}, f32[32,128]{1,0:T(8,128)S(1)}, u32[]{:S(2)}, u32[]{:S(2)}) collective-permute-start(f32[32,128]{1,0:T(8,128)S(1)} %get-tuple-element.89), channel_id=1, source_target_pairs={{0,31},{1,0},{2,1},{3,2},{4,3},{5,4},{6,5},{7,6},{8,7},{9,8},{10,9... | collective-permute-start | bytes 49160 | tf_op jit(solution)/shard_map/ppermute | solution.py:564

commit v11 on v10

--- a/solution.py
+++ b/solution.py
@@ -316,7 +316,7 @@
         mw[x] = DAMPING / diag
         rhs[x] = rows(s1, x, 4)
         mf[x] = mw[x] * rhs[x]
-    sweep_pass(6, mf, 0, 1, rhs, 1, mx, my, mz, mw, u1, 0)
+    neighbour_sweep(6, mf, rhs, 1, mx, my, mz, mw, u1)
     sweep_pass(4, u1, 0, 2, rhs, 2, mx, my, mz, mw, mr, 0, last=True)
     for x in range(4):
         both = k_mid[2 * x + 1] + k_mid[2 * x + 2]

time: 66.9 us -> 66.9 us (level)
  no operation moved by 1% of the time
where the time goes in v11:
time: 66.9 us; the launch traced here: 66.6 us
  starting transfers between devices  36.2 us (54%)
  waiting for transfers between devices  12.7 us (19%)
  blocking collectives  10.3 us (15%)
  Pallas kernels  5.74 us (9%)
  other arithmetic  0.99 us (1%)
  between operations  0.73 us (1%)
    ppermute x4, starting transfers between devices, swap(): return lax.ppermute(array, axis, pairs + [(j, i) for i, j in pairs])  23 us
    ppermute x8, starting transfers between devices, shift(): lax.ppermute(array, axis, [(i, (i + by) % count) for i in range(count)])  13.1 us
    all_to_all x1, blocking collectives, per_device(): gathered = lax.all_to_all(piece, 'gx', 0, 0)  10.3 us
    ppermute x8, waiting for transfers between devices, shift(): lax.ppermute(array, axis, [(i, (i + by) % count) for i in range(count)])  7.63 us
    pallas_call x11, Pallas kernels, call(): pl.pallas_call(kernel, out_shape=[jax.ShapeDtypeStruct(shape, F32) for sh...  5.74 us
    ppermute x4, waiting for transfers between devices, swap(): return lax.ppermute(array, axis, pairs + [(j, i) for i, j in pairs])  5.11 us
  transfers between devices with their start and end apart: 12, of which 8 were waited for; matrix products, arithmetic and copies ran while one was open for 0% of the time, Pallas kernels for 2%

profile of v11, /device:TPU:1, one launch (start us, length us, event | category | flops | bytes accessed | tf_op | source)
XLA Modules:
  0.0 66.6 jit_solution(17331385085908363604)
XLA Ops:
  0.6 1.0 %pad_maximum_fusion.held = f32[2,8,8,512]{3,2,1,0:T(8,128)S(1)} fusion(f32[1,8,8,512]{3,2,1,0:T(8,128)} %bitcast.4, f32[1,8,8,512]{3,2,1,0:T(8,128)} %bitcast.5), kind=kLoop, calls=%fused_computation | loop fusion | flops 65536 | bytes 524288 | tf_op jit(solution)/shard_map/stack | solution.py:579
  1.6 0.4 shard_map.50
  2.0 7.7 %collective-permute-start = (f32[14,4,8,128]{3,2,1,0:T(8,128)S(1)}, f32[14,4,8,128]{3,2,1,0:T(8,128)S(1)}, u32[]{:S(2)}, u32[]{:S(2)}) collective-permute-start(f32[14,4,8,128]{3,2,1,0:T(8,128)S(1)} %get-tuple-element.51), channel_id=1, source_target_pairs={{32,64},{96,128},{160,192},{224,256},{288,320},{352,384},{416,448}... | collective-permute-start | bytes 688136 | tf_op jit(solution)/shard_map/ppermute | solution.py:570
  9.7 1.9 %collective-permute-start.1 = (f32[14,4,8,128]{3,2,1,0:T(8,128)S(1)}, f32[14,4,8,128]{3,2,1,0:T(8,128)S(1)}, u32[]{:S(2)}, u32[]{:S(2)}) collective-permute-start(f32[14,4,8,128]{3,2,1,0:T(8,128)S(1)} %get-tuple-element.52), channel_id=1, source_target_pairs={{0,32},{64,96},{128,160},{192,224},{256,288},{320,352},{384,416},{... | collective-permute-start | bytes 688136 | tf_op jit(solution)/shard_map/ppermute | solution.py:570
  11.7 2.5 %collective-permute-start.4 = (f32[416,128]{1,0:T(8,128)S(1)}, f32[416,128]{1,0:T(8,128)S(1)}, u32[]{:S(2)}, u32[]{:S(2)}) collective-permute-start(f32[416,128]{1,0:T(8,128)S(1)} %get-tuple-element.56), channel_id=1, source_target_pairs={{0,1},{1,2},{2,3},{3,4},{4,5},{5,6},{6,7},{7,8},{8,9},{9,10},{10,1... | collective-permute-start | bytes 638984 | tf_op jit(solution)/shard_map/ppermute | solution.py:564
  14.2 3.4 %collective-permute-done.1.second = f32[14,4,8,128]{3,2,1,0:T(8,128)S(1)} collective-permute-done((f32[14,4,8,128]{3,2,1,0:T(8,128)S(1)}, f32[14,4,8,128]{3,2,1,0:T(8,128)S(1)}, u32[]{:S(2)}, u32[]{:S(2)}) %collective-permute-start.1) | collective-permute-done | bytes 229408 | tf_op jit(solution)/shard_map/ppermute | solution.py:570
  17.7 3.6 %collective-permute-start.2 = (f32[312,128]{1,0:T(8,128)S(1)}, f32[312,128]{1,0:T(8,128)S(1)}, u32[]{:S(2)}, u32[]{:S(2)}) collective-permute-start(f32[312,128]{1,0:T(8,128)S(1)} %get-tuple-element.54), channel_id=1, source_target_pairs={{0,1},{1,2},{2,3},{3,4},{4,5},{5,6},{6,7},{7,8},{8,9},{9,10},{10,1... | collective-permute-start | bytes 479240 | tf_op jit(solution)/shard_map/ppermute | solution.py:564
  21.5 0.5 shard_map.53
  22.1 1.4 %collective-permute-done.2.low_corners = f32[312,128]{1,0:T(8,128)S(1)} collective-permute-done((f32[312,128]{1,0:T(8,128)S(1)}, f32[312,128]{1,0:T(8,128)S(1)}, u32[]{:S(2)}, u32[]{:S(2)}) %collective-permute-start.2) | collective-permute-done | bytes 159776 | tf_op jit(solution)/shard_map/ppermute | solution.py:564
  23.5 2.5 %collective-permute-done.3.high_corners = f32[312,128]{1,0:T(8,128)S(1)} collective-permute-done((f32[312,128]{1,0:T(8,128)S(1)}, f32[312,128]{1,0:T(8,128)S(1)}, u32[]{:S(2)}, u32[]{:S(2)}) %collective-permute-start.3) | collective-permute-done | bytes 159776 | tf_op jit(solution)/shard_map/ppermute | solution.py:564
  26.0 1.5 %shard_map.54 = (f32[16,40,128]{2,1,0:T(8,128)S(1)}, f32[10,4,24,128]{3,2,1,0:T(8,128)S(1)}, f32[1152,128]{1,0:T(8,128)S(1)}, f32[1536,128]{1,0:T(8,128)S(1)}, f...) custom-call(s32[1]{0:T(128)} %bitcast.1.me, f32[1408,128]{1,0:T(8,128)S(1)} %get-tuple-element.53.wide, ...), custom_call_target="tpu_custom_call" | custom-call | tf_op jit(solution)/shard_map/pallas_call | solution.py:552
  27.5 10.3 %all_to_all.5.gathered = f32[16,40,128]{2,1,0:T(8,128)S(1)} all-to-all(f32[16,40,128]{2,1,0:T(8,128)S(1)} %get-tuple-element.67), channel_id=1, replica_groups=mesh['gx'=16,'gy'=32] {'gx'}, dimensions={0} | all-to-all | bytes 655360 | tf_op jit(solution)/shard_map/all_to_all | solution.py:604
  37.8 2.1 %collective-permute-start.6 = (f32[136,128]{1,0:T(8,128)S(1)}, f32[136,128]{1,0:T(8,128)S(1)}, u32[]{:S(2)}, u32[]{:S(2)}) collective-permute-start(f32[136,128]{1,0:T(8,128)S(1)} %get-tuple-element.77), channel_id=1, source_target_pairs={{0,1},{1,2},{2,3},{3,4},{4,5},{5,6},{6,7},{7,8},{8,9},{9,10},{10,1... | collective-permute-start | bytes 208904 | tf_op jit(solution)/shard_map/ppermute | solution.py:564
  39.9 4.2 %collective-permute-start.7 = (f32[136,128]{1,0:T(8,128)S(1)}, f32[136,128]{1,0:T(8,128)S(1)}, u32[]{:S(2)}, u32[]{:S(2)}) collective-permute-start(f32[136,128]{1,0:T(8,128)S(1)} %get-tuple-element.78), channel_id=1, source_target_pairs={{0,31},{1,0},{2,1},{3,2},{4,3},{5,4},{6,5},{7,6},{8,7},{9,8},{10,9... | collective-permute-start | bytes 208904 | tf_op jit(solution)/shard_map/ppermute | solution.py:564
  44.1 0.7 %collective-permute-done.6.low.left = f32[136,128]{1,0:T(8,128)S(1)} collective-permute-done((f32[136,128]{1,0:T(8,128)S(1)}, f32[136,128]{1,0:T(8,128)S(1)}, u32[]{:S(2)}, u32[]{:S(2)}) %collective-permute-start.6) | collective-permute-done | bytes 69664 | tf_op jit(solution)/shard_map/ppermute | solution.py:564
  45.0 1.9 %collective-permute-start.8 = (f32[136,128]{1,0:T(8,128)S(1)}, f32[136,128]{1,0:T(8,128)S(1)}, u32[]{:S(2)}, u32[]{:S(2)}) collective-permute-start(f32[136,128]{1,0:T(8,128)S(1)} %get-tuple-element.79), channel_id=1, source_target_pairs={{1,4},{3,6},{5,8},{7,10},{9,12},{11,14},{13,16},{15,18},{17,20},{1... | collective-permute-start | bytes 208904 | tf_op jit(solution)/shard_map/ppermute | solution.py:570
  46.9 11.5 %collective-permute-start.9 = (f32[136,128]{1,0:T(8,128)S(1)}, f32[136,128]{1,0:T(8,128)S(1)}, u32[]{:S(2)}, u32[]{:S(2)}) collective-permute-start(f32[136,128]{1,0:T(8,128)S(1)} %get-tuple-element.80), channel_id=1, source_target_pairs={{0,3},{2,5},{4,7},{6,9},{8,11},{10,13},{12,15},{14,17},{16,19},{18... | collective-permute-start | bytes 208904 | tf_op jit(solution)/shard_map/ppermute | solution.py:570
  58.7 1.7 %collective-permute-done.9.second = f32[136,128]{1,0:T(8,128)S(1)} collective-permute-done((f32[136,128]{1,0:T(8,128)S(1)}, f32[136,128]{1,0:T(8,128)S(1)}, u32[]{:S(2)}, u32[]{:S(2)}) %collective-permute-start.9) | collective-permute-done | bytes 69664 | tf_op jit(solution)/shard_map/ppermute | solution.py:570
  60.5 0.9 %shard_map.58 = (f32[128,128]{1,0:T(8,128)S(1)}, f32[32,128]{1,0:T(8,128)S(1)}, f32[32,128]{1,0:T(8,128)S(1)}) custom-call(s32[1]{0:T(128)} %bitcast.me, f32[136,128]{1,0:T(8,128)S(1)} %collective-permute-done.8.first, f32[4,32,128]{2,1,0:T(8,128)S(1)} %get-tuple-element.76.here, f32[136,128]{1,0:T(8,128)S(1)} %collective-permute-done.9.second, ...), custom_call_target="tpu_custom_call" | custom-call | tf_op jit(solution)/shard_map/pallas_call | solution.py:552
  61.5 0.4 collective-permute-start.11
  61.9 0.3 shard_map.59
  62.2 0.4 collective-permute-done.10.v_low
  62.6 2.4 %collective-permute-done.11.v_high = f32[32,128]{1,0:T(8,128)S(1)} collective-permute-done((f32[32,128]{1,0:T(8,128)S(1)}, f32[32,128]{1,0:T(8,128)S(1)}, u32[]{:S(2)}, u32[]{:S(2)}) %collective-permute-start.11) | collective-permute-done | bytes 16416 | tf_op jit(solution)/shard_map/ppermute | solution.py:564
  65.0 1.6 %shard_map.60 = (f32[8,8,512]{2,1,0:T(8,128)}, f32[8,8,512]{2,1,0:T(8,128)}) custom-call(f32[128,128]{1,0:T(8,128)S(1)} %get-tuple-element.87.v_here, f32[32,128]{1,0:T(8,128)S(1)} %collective-permute-done.10.v_low, f32[32,128]{1,0:T(8,128)S(1)} %collective-permute-done.11.v_high, f32[14,4,16,128]{3,2,1,0:T(8,128)S(1)} %get-tuple-element.92.u0, ...), custom_call_target="tpu_custom_call" | custom-call | tf_op jit(solution)/shard_map/pallas_call | solution.py:552
  (15 shorter events, 1.0 us)
Async XLA Ops:
  2.0 12.2 %collective-permute-start = (f32[14,4,8,128]{3,2,1,0:T(8,128)S(1)}, f32[14,4,8,128]{3,2,1,0:T(8,128)S(1)}, u32[]{:S(2)}, u32[]{:S(2)}) collective-permute-start(f32[14,4,8,128]{3,2,1,0:T(8,128)S(1)} %get-tuple-element.51), channel_id=1, source_target_pairs={{32,64},{96,128},{160,192},{224,256},{288,320},{352,384},{416,448}... | collective-permute-start | bytes 688136 | tf_op jit(solution)/shard_map/ppermute | solution.py:570
  9.7 7.9 %collective-permute-start.1 = (f32[14,4,8,128]{3,2,1,0:T(8,128)S(1)}, f32[14,4,8,128]{3,2,1,0:T(8,128)S(1)}, u32[]{:S(2)}, u32[]{:S(2)}) collective-permute-start(f32[14,4,8,128]{3,2,1,0:T(8,128)S(1)} %get-tuple-element.52), channel_id=1, source_target_pairs={{0,32},{64,96},{128,160},{192,224},{256,288},{320,352},{384,416},{... | collective-permute-start | bytes 688136 | tf_op jit(solution)/shard_map/ppermute | solution.py:570
  11.7 9.8 %collective-permute-start.4 = (f32[416,128]{1,0:T(8,128)S(1)}, f32[416,128]{1,0:T(8,128)S(1)}, u32[]{:S(2)}, u32[]{:S(2)}) collective-permute-start(f32[416,128]{1,0:T(8,128)S(1)} %get-tuple-element.56), channel_id=1, source_target_pairs={{0,1},{1,2},{2,3},{3,4},{4,5},{5,6},{6,7},{7,8},{8,9},{9,10},{10,1... | collective-permute-start | bytes 638984 | tf_op jit(solution)/shard_map/ppermute | solution.py:564
  14.2 7.3 %collective-permute-start.5 = (f32[416,128]{1,0:T(8,128)S(1)}, f32[416,128]{1,0:T(8,128)S(1)}, u32[]{:S(2)}, u32[]{:S(2)}) collective-permute-start(f32[416,128]{1,0:T(8,128)S(1)} %get-tuple-element.57), channel_id=1, source_target_pairs={{0,31},{1,0},{2,1},{3,2},{4,3},{5,4},{6,5},{7,6},{8,7},{9,8},{10,9... | collective-permute-start | bytes 638984 | tf_op jit(solution)/shard_map/ppermute | solution.py:564
  17.7 5.8 %collective-permute-start.2 = (f32[312,128]{1,0:T(8,128)S(1)}, f32[312,128]{1,0:T(8,128)S(1)}, u32[]{:S(2)}, u32[]{:S(2)}) collective-permute-start(f32[312,128]{1,0:T(8,128)S(1)} %get-tuple-element.54), channel_id=1, source_target_pairs={{0,1},{1,2},{2,3},{3,4},{4,5},{5,6},{6,7},{7,8},{8,9},{9,10},{10,1... | collective-permute-start | bytes 479240 | tf_op jit(solution)/shard_map/ppermute | solution.py:564
  21.3 4.7 %collective-permute-start.3 = (f32[312,128]{1,0:T(8,128)S(1)}, f32[312,128]{1,0:T(8,128)S(1)}, u32[]{:S(2)}, u32[]{:S(2)}) collective-permute-start(f32[312,128]{1,0:T(8,128)S(1)} %get-tuple-element.55), channel_id=1, source_target_pairs={{0,31},{1,0},{2,1},{3,2},{4,3},{5,4},{6,5},{7,6},{8,7},{9,8},{10,9... | collective-permute-start | bytes 479240 | tf_op jit(solution)/shard_map/ppermute | solution.py:564
  37.8 7.0 %collective-permute-start.6 = (f32[136,128]{1,0:T(8,128)S(1)}, f32[136,128]{1,0:T(8,128)S(1)}, u32[]{:S(2)}, u32[]{:S(2)}) collective-permute-start(f32[136,128]{1,0:T(8,128)S(1)} %get-tuple-element.77), channel_id=1, source_target_pairs={{0,1},{1,2},{2,3},{3,4},{4,5},{5,6},{6,7},{7,8},{8,9},{9,10},{10,1... | collective-permute-start | bytes 208904 | tf_op jit(solution)/shard_map/ppermute | solution.py:564
  39.9 5.1 %collective-permute-start.7 = (f32[136,128]{1,0:T(8,128)S(1)}, f32[136,128]{1,0:T(8,128)S(1)}, u32[]{:S(2)}, u32[]{:S(2)}) collective-permute-start(f32[136,128]{1,0:T(8,128)S(1)} %get-tuple-element.78), channel_id=1, source_target_pairs={{0,31},{1,0},{2,1},{3,2},{4,3},{5,4},{6,5},{7,6},{8,7},{9,8},{10,9... | collective-permute-start | bytes 208904 | tf_op jit(solution)/shard_map/ppermute | solution.py:564
  45.0 13.7 %collective-permute-start.8 = (f32[136,128]{1,0:T(8,128)S(1)}, f32[136,128]{1,0:T(8,128)S(1)}, u32[]{:S(2)}, u32[]{:S(2)}) collective-permute-start(f32[136,128]{1,0:T(8,128)S(1)} %get-tuple-element.79), channel_id=1, source_target_pairs={{1,4},{3,6},{5,8},{7,10},{9,12},{11,14},{13,16},{15,18},{17,20},{1... | collective-permute-start | bytes 208904 | tf_op jit(solution)/shard_map/ppermute | solution.py:570
  46.9 13.5 %collective-permute-start.9 = (f32[136,128]{1,0:T(8,128)S(1)}, f32[136,128]{1,0:T(8,128)S(1)}, u32[]{:S(2)}, u32[]{:S(2)}) collective-permute-start(f32[136,128]{1,0:T(8,128)S(1)} %get-tuple-element.80), channel_id=1, source_target_pairs={{0,3},{2,5},{4,7},{6,9},{8,11},{10,13},{12,15},{14,17},{16,19},{18... | collective-permute-start | bytes 208904 | tf_op jit(solution)/shard_map/ppermute | solution.py:570
  61.4 1.2 %collective-permute-start.10 = (f32[32,128]{1,0:T(8,128)S(1)}, f32[32,128]{1,0:T(8,128)S(1)}, u32[]{:S(2)}, u32[]{:S(2)}) collective-permute-start(f32[32,128]{1,0:T(8,128)S(1)} %get-tuple-element.88), channel_id=1, source_target_pairs={{0,1},{1,2},{2,3},{3,4},{4,5},{5,6},{6,7},{7,8},{8,9},{9,10},{10,1... | collective-permute-start | bytes 49160 | tf_op jit(solution)/shard_map/ppermute | solution.py:564
  61.5 3.5 %copy-start = (bf16[512,512]{1,0:T(8,128)(2,1)S(1)}, bf16[512,512]{1,0:T(8,128)(2,1)}, u32[]{:S(2)}) copy-start(bf16[512,512]{1,0:T(8,128)(2,1)} %constant.11.clone.matrix) | copy-start | bytes 1572868
  61.5 3.5 %collective-permute-start.11 = (f32[32,128]{1,0:T(8,128)S(1)}, f32[32,128]{1,0:T(8,128)S(1)}, u32[]{:S(2)}, u32[]{:S(2)}) collective-permute-start(f32[32,128]{1,0:T(8,128)S(1)} %get-tuple-element.89), channel_id=1, source_target_pairs={{0,31},{1,0},{2,1},{3,2},{4,3},{5,4},{6,5},{7,6},{8,7},{9,8},{10,9... | collective-permute-start | bytes 49160 | tf_op jit(solution)/shard_map/ppermute | solution.py:564

commit v12 on v11

--- a/solution.py
+++ b/solution.py
@@ -261,7 +261,7 @@
 
 def fine_kernel(me, wide, low_corners, high_corners, g_early, k_early, fx_early, fy_early, fz_early, w_early, uf_early,
                 u0_early, res_early, piece, u0_kept, g_flat, k_flat, u1, rhs, u0_edge, fx, fy, fz, w, uf, res, s1, sc,
-                mx, my, mz, mw, mf, mr, ck, near):
+                mx, my, mz, mw, mf, mr, ck, near, md):
     flats = g_flat, k_flat
     wide, g, k = Slabs(wide, 8), Slabs(g_flat, 24), Slabs(k_flat, 24)
     for i in range(12):
@@ -314,10 +314,16 @@
         )
         mx[x + 1], my[x], mz[x] = face_x, face_y, face_z
         mw[x] = DAMPING / diag
+        md[x] = diag
         rhs[x] = rows(s1, x, 4)
         mf[x] = mw[x] * rhs[x]
     neighbour_sweep(6, mf, rhs, 1, mx, my, mz, mw, u1)
-    sweep_pass(4, u1, 0, 2, rhs, 2, mx, my, mz, mw, mr, 0, last=True)
+    for i in range(4):
+        f, u = 2 + i, u1[1 + i]
+        along_x = mx[f + 1] * u1[2 + i] + mx[f] * u1[i]
+        along_y = my[f] * y_next(u) + y_prev(my[f]) * y_prev(u)
+        along_z = mz[f] * z_next(u) + z_prev(mz[f]) * z_prev(u)
+        mr[i] = (rhs[f] - md[f] * u) + (along_x + (along_y + along_z))
     for x in range(4):
         both = k_mid[2 * x + 1] + k_mid[2 * x + 2]
         ck[x, 0:8] = both[0] + both[1]
@@ -597,7 +603,7 @@
         fine_kernel,
         [(count, 40, 128), (10, *fine), (12 * 96, 128), (16 * 96, 128), (6, *mid), (8, *mid)],
         [(4, *fine), (14, *fine), (14, *fine), (14, *fine), (14, *fine), (14, *fine), (14, *fine), (8, 2, 24, 128), (10, 2, 24, 128),
-         (9, *mid), (8, *mid), (8, *mid), (8, *mid), (8, *mid), (4, *mid), (4, 16, 128), (2, 40, 128)],
+         (9, *mid), (8, *mid), (8, *mid), (8, *mid), (8, *mid), (4, *mid), (4, 16, 128), (2, 40, 128), (8, *mid)],
         me_x, wide, low_corners, high_corners, *early, scalars=1,
     )
     piece, u0, g, k, u1, rhs = lax.optimization_barrier((piece, u0, g, k, u1, rhs))

time: 66.9 us -> 66.8 us (level)
  no operation moved by 1% of the time
where the time goes in v12:
time: 66.8 us; the launch traced here: 66.6 us
  starting transfers between devices  36.2 us (54%)
  waiting for transfers between devices  12.7 us (19%)
  blocking collectives  10.3 us (15%)
  Pallas kernels  5.71 us (9%)
  other arithmetic  0.99 us (1%)
  between operations  0.73 us (1%)
    ppermute x4, starting transfers between devices, swap(): return lax.ppermute(array, axis, pairs + [(j, i) for i, j in pairs])  23 us
    ppermute x8, starting transfers between devices, shift(): lax.ppermute(array, axis, [(i, (i + by) % count) for i in range(count)])  13.1 us
    all_to_all x1, blocking collectives, per_device(): gathered = lax.all_to_all(piece, 'gx', 0, 0)  10.3 us
    ppermute x8, waiting for transfers between devices, shift(): lax.ppermute(array, axis, [(i, (i + by) % count) for i in range(count)])  7.63 us
    pallas_call x11, Pallas kernels, call(): pl.pallas_call(kernel, out_shape=[jax.ShapeDtypeStruct(shape, F32) for sh...  5.71 us
    ppermute x4, waiting for transfers between devices, swap(): return lax.ppermute(array, axis, pairs + [(j, i) for i, j in pairs])  5.11 us
  transfers between devices with their start and end apart: 12, of which 8 were waited for; matrix products, arithmetic and copies ran while one was open for 0% of the time, Pallas kernels for 2%

profile of v12, /device:TPU:1, one launch (start us, length us, event | category | flops | bytes accessed | tf_op | source)
XLA Modules:
  0.0 66.6 jit_solution(7571794639653643883)
XLA Ops:
  0.6 1.0 %pad_maximum_fusion.held = f32[2,8,8,512]{3,2,1,0:T(8,128)S(1)} fusion(f32[1,8,8,512]{3,2,1,0:T(8,128)} %bitcast.4, f32[1,8,8,512]{3,2,1,0:T(8,128)} %bitcast.5), kind=kLoop, calls=%fused_computation | loop fusion | flops 65536 | bytes 524288 | tf_op jit(solution)/shard_map/stack | solution.py:585
  1.6 0.4 shard_map.50
  2.0 7.7 %collective-permute-start = (f32[14,4,8,128]{3,2,1,0:T(8,128)S(1)}, f32[14,4,8,128]{3,2,1,0:T(8,128)S(1)}, u32[]{:S(2)}, u32[]{:S(2)}) collective-permute-start(f32[14,4,8,128]{3,2,1,0:T(8,128)S(1)} %get-tuple-element.51), channel_id=1, source_target_pairs={{32,64},{96,128},{160,192},{224,256},{288,320},{352,384},{416,448}... | collective-permute-start | bytes 688136 | tf_op jit(solution)/shard_map/ppermute | solution.py:576
  9.7 1.9 %collective-permute-start.1 = (f32[14,4,8,128]{3,2,1,0:T(8,128)S(1)}, f32[14,4,8,128]{3,2,1,0:T(8,128)S(1)}, u32[]{:S(2)}, u32[]{:S(2)}) collective-permute-start(f32[14,4,8,128]{3,2,1,0:T(8,128)S(1)} %get-tuple-element.52), channel_id=1, source_target_pairs={{0,32},{64,96},{128,160},{192,224},{256,288},{320,352},{384,416},{... | collective-permute-start | bytes 688136 | tf_op jit(solution)/shard_map/ppermute | solution.py:576
  11.7 2.5 %collective-permute-start.4 = (f32[416,128]{1,0:T(8,128)S(1)}, f32[416,128]{1,0:T(8,128)S(1)}, u32[]{:S(2)}, u32[]{:S(2)}) collective-permute-start(f32[416,128]{1,0:T(8,128)S(1)} %get-tuple-element.56), channel_id=1, source_target_pairs={{0,1},{1,2},{2,3},{3,4},{4,5},{5,6},{6,7},{7,8},{8,9},{9,10},{10,1... | collective-permute-start | bytes 638984 | tf_op jit(solution)/shard_map/ppermute | solution.py:570
  14.2 3.4 %collective-permute-done.1.second = f32[14,4,8,128]{3,2,1,0:T(8,128)S(1)} collective-permute-done((f32[14,4,8,128]{3,2,1,0:T(8,128)S(1)}, f32[14,4,8,128]{3,2,1,0:T(8,128)S(1)}, u32[]{:S(2)}, u32[]{:S(2)}) %collective-permute-start.1) | collective-permute-done | bytes 229408 | tf_op jit(solution)/shard_map/ppermute | solution.py:576
  17.7 3.6 %collective-permute-start.2 = (f32[312,128]{1,0:T(8,128)S(1)}, f32[312,128]{1,0:T(8,128)S(1)}, u32[]{:S(2)}, u32[]{:S(2)}) collective-permute-start(f32[312,128]{1,0:T(8,128)S(1)} %get-tuple-element.54), channel_id=1, source_target_pairs={{0,1},{1,2},{2,3},{3,4},{4,5},{5,6},{6,7},{7,8},{8,9},{9,10},{10,1... | collective-permute-start | bytes 479240 | tf_op jit(solution)/shard_map/ppermute | solution.py:570
  21.5 0.5 shard_map.53
  22.1 1.4 %collective-permute-done.2.low_corners = f32[312,128]{1,0:T(8,128)S(1)} collective-permute-done((f32[312,128]{1,0:T(8,128)S(1)}, f32[312,128]{1,0:T(8,128)S(1)}, u32[]{:S(2)}, u32[]{:S(2)}) %collective-permute-start.2) | collective-permute-done | bytes 159776 | tf_op jit(solution)/shard_map/ppermute | solution.py:570
  23.5 2.5 %collective-permute-done.3.high_corners = f32[312,128]{1,0:T(8,128)S(1)} collective-permute-done((f32[312,128]{1,0:T(8,128)S(1)}, f32[312,128]{1,0:T(8,128)S(1)}, u32[]{:S(2)}, u32[]{:S(2)}) %collective-permute-start.3) | collective-permute-done | bytes 159776 | tf_op jit(solution)/shard_map/ppermute | solution.py:570
  26.0 1.5 %shard_map.54 = (f32[16,40,128]{2,1,0:T(8,128)S(1)}, f32[10,4,24,128]{3,2,1,0:T(8,128)S(1)}, f32[1152,128]{1,0:T(8,128)S(1)}, f32[1536,128]{1,0:T(8,128)S(1)}, f...) custom-call(s32[1]{0:T(128)} %bitcast.1.me, f32[1408,128]{1,0:T(8,128)S(1)} %get-tuple-element.53.wide, ...), custom_call_target="tpu_custom_call" | custom-call | tf_op jit(solution)/shard_map/pallas_call | solution.py:558
  27.5 10.3 %all_to_all.5.gathered = f32[16,40,128]{2,1,0:T(8,128)S(1)} all-to-all(f32[16,40,128]{2,1,0:T(8,128)S(1)} %get-tuple-element.67), channel_id=1, replica_groups=mesh['gx'=16,'gy'=32] {'gx'}, dimensions={0} | all-to-all | bytes 655360 | tf_op jit(solution)/shard_map/all_to_all | solution.py:610
  37.8 2.1 %collective-permute-start.6 = (f32[136,128]{1,0:T(8,128)S(1)}, f32[136,128]{1,0:T(8,128)S(1)}, u32[]{:S(2)}, u32[]{:S(2)}) collective-permute-start(f32[136,128]{1,0:T(8,128)S(1)} %get-tuple-element.77), channel_id=1, source_target_pairs={{0,1},{1,2},{2,3},{3,4},{4,5},{5,6},{6,7},{7,8},{8,9},{9,10},{10,1... | collective-permute-start | bytes 208904 | tf_op jit(solution)/shard_map/ppermute | solution.py:570
  39.9 4.2 %collective-permute-start.7 = (f32[136,128]{1,0:T(8,128)S(1)}, f32[136,128]{1,0:T(8,128)S(1)}, u32[]{:S(2)}, u32[]{:S(2)}) collective-permute-start(f32[136,128]{1,0:T(8,128)S(1)} %get-tuple-element.78), channel_id=1, source_target_pairs={{0,31},{1,0},{2,1},{3,2},{4,3},{5,4},{6,5},{7,6},{8,7},{9,8},{10,9... | collective-permute-start | bytes 208904 | tf_op jit(solution)/shard_map/ppermute | solution.py:570
  44.1 0.7 %collective-permute-done.6.low.left = f32[136,128]{1,0:T(8,128)S(1)} collective-permute-done((f32[136,128]{1,0:T(8,128)S(1)}, f32[136,128]{1,0:T(8,128)S(1)}, u32[]{:S(2)}, u32[]{:S(2)}) %collective-permute-start.6) | collective-permute-done | bytes 69664 | tf_op jit(solution)/shard_map/ppermute | solution.py:570
  45.0 1.9 %collective-permute-start.8 = (f32[136,128]{1,0:T(8,128)S(1)}, f32[136,128]{1,0:T(8,128)S(1)}, u32[]{:S(2)}, u32[]{:S(2)}) collective-permute-start(f32[136,128]{1,0:T(8,128)S(1)} %get-tuple-element.79), channel_id=1, source_target_pairs={{1,4},{3,6},{5,8},{7,10},{9,12},{11,14},{13,16},{15,18},{17,20},{1... | collective-permute-start | bytes 208904 | tf_op jit(solution)/shard_map/ppermute | solution.py:576
  46.9 11.5 %collective-permute-start.9 = (f32[136,128]{1,0:T(8,128)S(1)}, f32[136,128]{1,0:T(8,128)S(1)}, u32[]{:S(2)}, u32[]{:S(2)}) collective-permute-start(f32[136,128]{1,0:T(8,128)S(1)} %get-tuple-element.80), channel_id=1, source_target_pairs={{0,3},{2,5},{4,7},{6,9},{8,11},{10,13},{12,15},{14,17},{16,19},{18... | collective-permute-start | bytes 208904 | tf_op jit(solution)/shard_map/ppermute | solution.py:576
  58.7 1.7 %collective-permute-done.9.second = f32[136,128]{1,0:T(8,128)S(1)} collective-permute-done((f32[136,128]{1,0:T(8,128)S(1)}, f32[136,128]{1,0:T(8,128)S(1)}, u32[]{:S(2)}, u32[]{:S(2)}) %collective-permute-start.9) | collective-permute-done | bytes 69664 | tf_op jit(solution)/shard_map/ppermute | solution.py:576
  60.4 0.9 %shard_map.58 = (f32[128,128]{1,0:T(8,128)S(1)}, f32[32,128]{1,0:T(8,128)S(1)}, f32[32,128]{1,0:T(8,128)S(1)}) custom-call(s32[1]{0:T(128)} %bitcast.me, f32[136,128]{1,0:T(8,128)S(1)} %collective-permute-done.8.first, f32[4,32,128]{2,1,0:T(8,128)S(1)} %get-tuple-element.76.here, f32[136,128]{1,0:T(8,128)S(1)} %collective-permute-done.9.second, ...), custom_call_target="tpu_custom_call" | custom-call | tf_op jit(solution)/shard_map/pallas_call | solution.py:558
  61.5 0.4 collective-permute-start.11
  61.9 0.3 shard_map.59
  62.2 0.4 collective-permute-done.10.v_low
  62.6 2.4 %collective-permute-done.11.v_high = f32[32,128]{1,0:T(8,128)S(1)} collective-permute-done((f32[32,128]{1,0:T(8,128)S(1)}, f32[32,128]{1,0:T(8,128)S(1)}, u32[]{:S(2)}, u32[]{:S(2)}) %collective-permute-start.11) | collective-permute-done | bytes 16416 | tf_op jit(solution)/shard_map/ppermute | solution.py:570
  65.0 1.6 %shard_map.60 = (f32[8,8,512]{2,1,0:T(8,128)}, f32[8,8,512]{2,1,0:T(8,128)}) custom-call(f32[128,128]{1,0:T(8,128)S(1)} %get-tuple-element.87.v_here, f32[32,128]{1,0:T(8,128)S(1)} %collective-permute-done.10.v_low, f32[32,128]{1,0:T(8,128)S(1)} %collective-permute-done.11.v_high, f32[14,4,16,128]{3,2,1,0:T(8,128)S(1)} %get-tuple-element.92.u0, ...), custom_call_target="tpu_custom_call" | custom-call | tf_op jit(solution)/shard_map/pallas_call | solution.py:558
  (15 shorter events, 1.0 us)
Async XLA Ops:
  2.0 12.2 %collective-permute-start = (f32[14,4,8,128]{3,2,1,0:T(8,128)S(1)}, f32[14,4,8,128]{3,2,1,0:T(8,128)S(1)}, u32[]{:S(2)}, u32[]{:S(2)}) collective-permute-start(f32[14,4,8,128]{3,2,1,0:T(8,128)S(1)} %get-tuple-element.51), channel_id=1, source_target_pairs={{32,64},{96,128},{160,192},{224,256},{288,320},{352,384},{416,448}... | collective-permute-start | bytes 688136 | tf_op jit(solution)/shard_map/ppermute | solution.py:576
  9.7 7.9 %collective-permute-start.1 = (f32[14,4,8,128]{3,2,1,0:T(8,128)S(1)}, f32[14,4,8,128]{3,2,1,0:T(8,128)S(1)}, u32[]{:S(2)}, u32[]{:S(2)}) collective-permute-start(f32[14,4,8,128]{3,2,1,0:T(8,128)S(1)} %get-tuple-element.52), channel_id=1, source_target_pairs={{0,32},{64,96},{128,160},{192,224},{256,288},{320,352},{384,416},{... | collective-permute-start | bytes 688136 | tf_op jit(solution)/shard_map/ppermute | solution.py:576
  11.7 9.8 %collective-permute-start.4 = (f32[416,128]{1,0:T(8,128)S(1)}, f32[416,128]{1,0:T(8,128)S(1)}, u32[]{:S(2)}, u32[]{:S(2)}) collective-permute-start(f32[416,128]{1,0:T(8,128)S(1)} %get-tuple-element.56), channel_id=1, source_target_pairs={{0,1},{1,2},{2,3},{3,4},{4,5},{5,6},{6,7},{7,8},{8,9},{9,10},{10,1... | collective-permute-start | bytes 638984 | tf_op jit(solution)/shard_map/ppermute | solution.py:570
  14.2 7.3 %collective-permute-start.5 = (f32[416,128]{1,0:T(8,128)S(1)}, f32[416,128]{1,0:T(8,128)S(1)}, u32[]{:S(2)}, u32[]{:S(2)}) collective-permute-start(f32[416,128]{1,0:T(8,128)S(1)} %get-tuple-element.57), channel_id=1, source_target_pairs={{0,31},{1,0},{2,1},{3,2},{4,3},{5,4},{6,5},{7,6},{8,7},{9,8},{10,9... | collective-permute-start | bytes 638984 | tf_op jit(solution)/shard_map/ppermute | solution.py:570
  17.7 5.8 %collective-permute-start.2 = (f32[312,128]{1,0:T(8,128)S(1)}, f32[312,128]{1,0:T(8,128)S(1)}, u32[]{:S(2)}, u32[]{:S(2)}) collective-permute-start(f32[312,128]{1,0:T(8,128)S(1)} %get-tuple-element.54), channel_id=1, source_target_pairs={{0,1},{1,2},{2,3},{3,4},{4,5},{5,6},{6,7},{7,8},{8,9},{9,10},{10,1... | collective-permute-start | bytes 479240 | tf_op jit(solution)/shard_map/ppermute | solution.py:570
  21.3 4.7 %collective-permute-start.3 = (f32[312,128]{1,0:T(8,128)S(1)}, f32[312,128]{1,0:T(8,128)S(1)}, u32[]{:S(2)}, u32[]{:S(2)}) collective-permute-start(f32[312,128]{1,0:T(8,128)S(1)} %get-tuple-element.55), channel_id=1, source_target_pairs={{0,31},{1,0},{2,1},{3,2},{4,3},{5,4},{6,5},{7,6},{8,7},{9,8},{10,9... | collective-permute-start | bytes 479240 | tf_op jit(solution)/shard_map/ppermute | solution.py:570
  37.8 7.0 %collective-permute-start.6 = (f32[136,128]{1,0:T(8,128)S(1)}, f32[136,128]{1,0:T(8,128)S(1)}, u32[]{:S(2)}, u32[]{:S(2)}) collective-permute-start(f32[136,128]{1,0:T(8,128)S(1)} %get-tuple-element.77), channel_id=1, source_target_pairs={{0,1},{1,2},{2,3},{3,4},{4,5},{5,6},{6,7},{7,8},{8,9},{9,10},{10,1... | collective-permute-start | bytes 208904 | tf_op jit(solution)/shard_map/ppermute | solution.py:570
  39.9 5.1 %collective-permute-start.7 = (f32[136,128]{1,0:T(8,128)S(1)}, f32[136,128]{1,0:T(8,128)S(1)}, u32[]{:S(2)}, u32[]{:S(2)}) collective-permute-start(f32[136,128]{1,0:T(8,128)S(1)} %get-tuple-element.78), channel_id=1, source_target_pairs={{0,31},{1,0},{2,1},{3,2},{4,3},{5,4},{6,5},{7,6},{8,7},{9,8},{10,9... | collective-permute-start | bytes 208904 | tf_op jit(solution)/shard_map/ppermute | solution.py:570
  45.0 13.7 %collective-permute-start.8 = (f32[136,128]{1,0:T(8,128)S(1)}, f32[136,128]{1,0:T(8,128)S(1)}, u32[]{:S(2)}, u32[]{:S(2)}) collective-permute-start(f32[136,128]{1,0:T(8,128)S(1)} %get-tuple-element.79), channel_id=1, source_target_pairs={{1,4},{3,6},{5,8},{7,10},{9,12},{11,14},{13,16},{15,18},{17,20},{1... | collective-permute-start | bytes 208904 | tf_op jit(solution)/shard_map/ppermute | solution.py:576
  46.9 13.5 %collective-permute-start.9 = (f32[136,128]{1,0:T(8,128)S(1)}, f32[136,128]{1,0:T(8,128)S(1)}, u32[]{:S(2)}, u32[]{:S(2)}) collective-permute-start(f32[136,128]{1,0:T(8,128)S(1)} %get-tuple-element.80), channel_id=1, source_target_pairs={{0,3},{2,5},{4,7},{6,9},{8,11},{10,13},{12,15},{14,17},{16,19},{18... | collective-permute-start | bytes 208904 | tf_op jit(solution)/shard_map/ppermute | solution.py:576
  61.4 1.2 %collective-permute-start.10 = (f32[32,128]{1,0:T(8,128)S(1)}, f32[32,128]{1,0:T(8,128)S(1)}, u32[]{:S(2)}, u32[]{:S(2)}) collective-permute-start(f32[32,128]{1,0:T(8,128)S(1)} %get-tuple-element.88), channel_id=1, source_target_pairs={{0,1},{1,2},{2,3},{3,4},{4,5},{5,6},{6,7},{7,8},{8,9},{9,10},{10,1... | collective-permute-start | bytes 49160 | tf_op jit(solution)/shard_map/ppermute | solution.py:570
  61.5 3.5 %copy-start = (bf16[512,512]{1,0:T(8,128)(2,1)S(1)}, bf16[512,512]{1,0:T(8,128)(2,1)}, u32[]{:S(2)}) copy-start(bf16[512,512]{1,0:T(8,128)(2,1)} %constant.11.clone.matrix) | copy-start | bytes 1572868
  61.5 3.5 %collective-permute-start.11 = (f32[32,128]{1,0:T(8,128)S(1)}, f32[32,128]{1,0:T(8,128)S(1)}, u32[]{:S(2)}, u32[]{:S(2)}) collective-permute-start(f32[32,128]{1,0:T(8,128)S(1)} %get-tuple-element.89), channel_id=1, source_target_pairs={{0,31},{1,0},{2,1},{3,2},{4,3},{5,4},{6,5},{7,6},{8,7},{9,8},{10,9... | collective-permute-start | bytes 49160 | tf_op jit(solution)/shard_map/ppermute | solution.py:570
